TPU v7x, 256 devices: a whole 4x4x8 slice. The times are simulated.
256 devices in a mesh: ctx: 16 (over x_hi, z), resp: 16 (over y, x_lo, core).
Axes of the slice: x: 4 (x_hi: 2, x_lo: 2; x = x_hi * 2 + x_lo), y: 4, z: 8, core: 2. Of those that a mesh axis runs over, the one named last changes fastest.
Arguments:
- q_resp: bfloat16 [16, 2048, 2048], P('resp', 'ctx'), may hold values from -8 to 8
- k_resp: bfloat16 [16, 2048, 512], P('resp', 'ctx'), may hold values from -6 to 6
- v_resp: bfloat16 [16, 2048, 512], P('resp', 'ctx'), may hold values from -6 to 6
- k_prompt: bfloat16 [1024, 512], P('ctx'), may hold values from -8 to 8
- v_prompt: bfloat16 [1024, 512], P('ctx'), may hold values from -6 to 6
- d_out: bfloat16 [16, 2048, 2048], P('resp', 'ctx'), may hold values from -4 to 4
- lengths: int32 [16], P('resp'), may hold values from 512 to 2048, as said below
- counts: int32 [16], P('resp'), may hold values from 256 to 2048, as said below
Outputs:
- attn_out: bfloat16 [16, 2048, 2048], P('resp', 'ctx')
- d_query: bfloat16 [16, 2048, 2048], P('resp', 'ctx')
- d_key_resp: bfloat16 [16, 2048, 512], P('resp', 'ctx')
- d_value_resp: bfloat16 [16, 2048, 512], P('resp', 'ctx')
- d_key_prompt: bfloat16 [1024, 512], P('ctx')
- d_value_prompt: bfloat16 [1024, 512], P('ctx')
Inputs may be any that keep to these rules, and one draw needn't show every extreme that they name: Rows of response r from lengths[r] on are padding; some response has 2048 real tokens. The first counts[r] tokens of response r enter the loss; (lengths[r] + 1) // 2 <= counts[r] <= lengths[r].
All inputs are finite; a program needn't handle non-finite values.
Results may differ from a plain program's by a relative error of at most 0.035.
Values may be sent and summed in bfloat16 or wider, within the bound.
No kernel may reach another device: no remote copies, remote signals or barrier semaphores. Data moves between devices by JAX's collectives and lax.ppermute only.
A program may use at most 128 MiB of HBM per device.

v0:
```python
import math

import jax
import jax.numpy as jnp
from jax import lax
from jax.experimental import pallas as pl
from jax.experimental.pallas import tpu as pltpu
from jax.sharding import Mesh
from jax.sharding import PartitionSpec as P

HEADS = 16
KV_HEADS = 4
HEAD_DIM = 128
GROUP = HEADS // KV_HEADS
RESP_LEN = 2048
PROMPT_LEN = 1024
CTX = ("xh", "z")
LOCAL = ("xh", "z", "core")
RESP = ("y", "xl", "core")
ROWS = 128
PROWS = 64
BOTH = ROWS + PROWS
CHUNK = 256
SPAN = 3 * CHUNK
TILE_SPANS = (2 * CHUNK, 3 * CHUNK)
TILE_STARTS = (0, 2 * CHUNK)
PROBS = 5 * CHUNK
HALF = GROUP * ROWS
LANES = 2 * HALF
WIDE = 2 * HEAD_DIM
SCALE = HEAD_DIM**-0.5
SCALE2 = SCALE * math.log2(math.e)
NEG = -1e30
F32 = jnp.float32
BF16 = jnp.bfloat16
VMEM = pl.BlockSpec(memory_space=pltpu.VMEM)
SMEM = pl.BlockSpec(memory_space=pltpu.SMEM)


def dot(a, b):
    return jnp.dot(a, b, preferred_element_type=F32)


def head_at(h, width=HEAD_DIM):
    return slice(h * width, (h + 1) * width)


def lanes_at(j, h):
    return slice(j * HALF + h * HEAD_DIM, j * HALF + (h + 1) * HEAD_DIM)


def block_of(member, quad, core):
    return (member // 2) * 8 + ((quad * 2 + (member & 1) + core) & 7)


def run_copies(pairs, sems):
    copies = [
        pltpu.make_async_copy(source, to, sems.at[i]) for i, (source, to) in enumerate(pairs)
    ]
    for copy in copies:
        copy.start()
    for copy in copies:
        copy.wait()


def pack_kv_kernel(info, k, v, kp, vp, kv0, kv1, kv2, kv3, sems):
    mine = info[0]
    pairs = []
    for d, kv in enumerate((kv0, kv1, kv2, kv3)):
        at = pl.ds(pl.multiple_of((mine ^ d) * HEAD_DIM, HEAD_DIM), HEAD_DIM)
        pairs += [
            (k.at[:, at], kv.at[:ROWS, :HEAD_DIM]),
            (v.at[:, at], kv.at[:ROWS, HEAD_DIM:]),
            (kp.at[:, at], kv.at[ROWS:, :HEAD_DIM]),
            (vp.at[:, at], kv.at[ROWS:, HEAD_DIM:]),
        ]
    run_copies(pairs, sems)


def pack_qd_kernel(info, q, do, qd0, qd1, qd2, qd3, sems):
    mine = info[0]
    pairs = []
    for d, qd in enumerate((qd0, qd1, qd2, qd3)):
        at = pl.ds(pl.multiple_of((mine ^ d) * HALF, HALF), HALF)
        pairs += [(q.at[:, at], qd.at[:, :HALF]), (do.at[:, at], qd.at[:, HALF:])]
    run_copies(pairs, sems)


def rows_at(mine, d):
    return pl.ds(pl.multiple_of(CHUNK + (mine ^ d) // 2 * CHUNK + (d & 1) * ROWS, ROWS), ROWS)


def load_keys(mine, g, kvs, k_s, v_s):
    for d, kv in enumerate(kvs):
        k_s[g, rows_at(mine, d), :] = kv[:ROWS, :HEAD_DIM]
        v_s[g, rows_at(mine, d), :] = kv[:ROWS, HEAD_DIM:]
        k_s[g, head_at(d, PROWS), :] = kv[ROWS:, :HEAD_DIM]
        v_s[g, head_at(d, PROWS), :] = kv[ROWS:, HEAD_DIM:]


def query_rows(info, x):
    mine, quad, core = info[0], info[1], info[2]
    rows = []
    for j in range(2):
        start = block_of(x * 2 + ((mine & 1) ^ j), quad, core) * ROWS
        rows += [start + lax.broadcasted_iota(jnp.int32, (1, ROWS), 1)] * GROUP
    return jnp.concatenate(rows, axis=1)


def key_rows(info, x, quad):
    mine, core = info[0], info[2]
    rows = []
    for j in range(2):
        start = block_of(x * 2 + ((mine & 1) ^ j), quad, core) * ROWS
        rows.append(start + lax.broadcasted_iota(jnp.int32, (ROWS, 1), 0))
    return jnp.concatenate(rows, axis=0)


def fold(x, op):
    return op(x.reshape(x.shape[0] // 8, 8, LANES), axis=0)


def each(count, step, carry):
    return step(0, carry) if count == 1 else lax.fori_loop(0, count, step, carry)


def forward(info, quads, count, k_s, v_s, qt, before, score_s, probs, vt_s, shift, total, acc):
    def turn_values(g, carry):
        vt_s[g] = v_s[g].T
        return carry

    each(count, turn_values, 0)
    for x in range(2):
        place = query_rows(info, x)
        start, span = TILE_STARTS[x], TILE_SPANS[x]

        def score_step(g, running):
            for c in range(span // CHUNK):
                at = slice(c * CHUNK, (c + 1) * CHUNK)
                score = dot(k_s[g, at, :], qt[x])
                if c > 0:
                    score = jnp.where(key_rows(info, c - 1, quads(g)) <= place, score, NEG)
                score_s[g, at, :] = score
                running = jnp.maximum(running, fold(score, jnp.max))
            return running

        running = each(count, score_step, jnp.full((8, LANES), NEG, F32))
        now = jnp.max(running, axis=0, keepdims=True) * SCALE2
        if before is not None:
            now = jnp.maximum(now, before[0][x])
            factor = jnp.exp2(before[0][x] - now)
            acc[x] = before[2][x] * factor

        def prob_step(g, running):
            for c in range(span // CHUNK):
                prob = jnp.exp2(score_s[g, c * CHUNK : (c + 1) * CHUNK, :] * SCALE2 - now)
                running = running + fold(prob, jnp.sum)
                probs[g, start + c * CHUNK : start + (c + 1) * CHUNK, :] = prob.astype(BF16)
            part = dot(vt_s[g, :, :span], probs[g, start : start + span, :])
            if before is None:
                acc[x] = part
            else:
                acc[x] += part
            return running

        running = each(count, prob_step, jnp.zeros((8, LANES), F32))
        sums = jnp.sum(running, axis=0, keepdims=True)
        if before is not None:
            sums = sums + before[1][x] * factor
        shift[x], total[x] = now, sums


def backward(count, k_s, v_s, kt_s, q, uplt, upl, delta, probs, factors, grad_s, before, dqt):
    for x in range(2):
        dqt[x] = jnp.zeros((HEAD_DIM, LANES), F32) if before is None else before[x]

    def chunk(g, c, tiles):
        at = pl.ds(pl.multiple_of(c * CHUNK, CHUNK), CHUNK)
        dk, dv = None, None
        for x in tiles:
            here = pl.ds(pl.multiple_of(TILE_STARTS[x] + c * CHUNK, CHUNK), CHUNK)
            low = probs[g, here, :]
            if factors is not None:
                low = (low.astype(F32) * factors[x]).astype(BF16)
            prob_grad = dot(v_s[g, at, :], uplt[x])
            grad = (low.astype(F32) * (prob_grad - delta[x])).astype(BF16)
            grad_s[here, :] = grad
            dv_part = dot(low, upl[x])
            dk_part = dot(grad, q[x])
            dv = dv_part if dv is None else dv + dv_part
            dk = dk_part if dk is None else dk + dk_part
        k_s[g, at, :] = (dk * SCALE).astype(BF16)
        v_s[g, at, :] = dv.astype(BF16)

    def step(g, carry):
        kt_s[...] = k_s[g].T

        def two_tiles(c, carry):
            chunk(g, c, (0, 1))
            return carry

        lax.fori_loop(0, 2, two_tiles, 0)
        chunk(g, 2, (1,))
        for x in range(2):
            start, span = TILE_STARTS[x], TILE_SPANS[x]
            dqt[x] += dot(kt_s[:, :span], grad_s[start : start + span, :])
        return carry

    each(count, step, 0)


def store_grads(mine, g, k_s, v_s, outs):
    for d, out in enumerate(outs):
        out[:ROWS, :HEAD_DIM] = k_s[g, rows_at(mine, d), :]
        out[:ROWS, HEAD_DIM:] = v_s[g, rows_at(mine, d), :]
        out[ROWS:, :HEAD_DIM] = k_s[g, head_at(d, PROWS), :]
        out[ROWS:, HEAD_DIM:] = v_s[g, head_at(d, PROWS), :]


def pieces(*parts):
    return [part.at[d] for part in parts for d in range(part.shape[0])]


def first_kernel(
    info, weight, qd0, qd1, qd2, qd3, own,
    qt, q, upt, probs, shift, total, acc,
    k_s, v_s, vt_s, score_s,
):
    mine, quad, core, count = info[0], info[1], info[2], info[4]
    load_keys(mine, 0, pieces(own), k_s, v_s)
    for d, qd in enumerate((qd0, qd1, qd2, qd3)):
        x = (mine ^ d) // 2
        row = block_of(mine ^ d, quad, core) * ROWS
        row = row + lax.broadcasted_iota(jnp.int32, (1, ROWS), 1)
        row_weight = jnp.where(row < count, weight[0], 0.0)
        for h in range(GROUP):
            cols = lanes_at(d & 1, h)
            q_head = qd[:, head_at(h)]
            q[x, cols, :] = q_head
            qt[x, :, cols] = q_head.T
            grad = qd[:, HALF + h * HEAD_DIM : HALF + (h + 1) * HEAD_DIM]
            upt[x, :, cols] = (grad.T.astype(F32) * row_weight).astype(BF16)
    forward(
        info, lambda g: quad, 1, k_s, v_s, qt, None, score_s, probs, vt_s, shift, total, acc
    )


def side_kernel(
    info, qt, left, right, shift0, total0, acc0,
    probs, shift, total, acc,
    k_s, v_s, vt_s, score_s,
):
    mine, quad = info[0], info[1]
    load_keys(mine, 0, pieces(left), k_s, v_s)
    load_keys(mine, 1, pieces(right), k_s, v_s)
    forward(
        info, lambda g: (quad + 3 + 2 * g) & 3, 2, k_s, v_s, qt, (shift0, total0, acc0),
        score_s, probs, vt_s, shift, total, acc,
    )


def far_kernel(
    info, qt, q, upt, far_a, far_b, shift0, total0, acc0,
    shift, uplt, upl, delta, dqt, attn, out_a, out_b,
    k_s, v_s, vt_s, kt_s, score_s, probs, grad_s, acc, total,
):
    mine, quad, length = info[0], info[1], info[3]
    load_keys(mine, 0, pieces(far_a, far_b), k_s, v_s)
    forward(
        info, lambda g: (quad + 2) & 3, 1, k_s, v_s, qt, (shift0, total0, acc0),
        score_s, probs, vt_s, shift, total, acc,
    )
    for x in range(2):
        inverse = 1.0 / total[x]
        valid = jnp.where(query_rows(info, x) < length, 1.0, 0.0)
        out_t = (acc[x] * (inverse * valid)).astype(BF16)
        up_low = (upt[x].astype(F32) * inverse).astype(BF16)
        uplt[x] = up_low
        delta[x] = jnp.sum(up_low.astype(F32) * out_t.astype(F32), axis=0, keepdims=True)
        attn[x] = out_t
        for j in range(2):
            for h in range(GROUP):
                upl[x, lanes_at(j, h), :] = up_low[:, lanes_at(j, h)].T
    backward(
        1, k_s, v_s, kt_s, q, uplt, upl, delta, probs, None, grad_s, None, dqt
    )
    store_grads(mine, 0, k_s, v_s, pieces(out_a, out_b))


def back_side_kernel(
    info, q, uplt, upl, delta, shift_then, shift_last, probs,
    left, right, dqt0,
    dqt, out_l, out_r,
    k_s, v_s, kt_s, grad_s,
):
    mine = info[0]
    factors = [jnp.exp2(shift_then[x] - shift_last[x]) for x in range(2)]
    load_keys(mine, 0, pieces(left), k_s, v_s)
    load_keys(mine, 1, pieces(right), k_s, v_s)
    backward(
        2, k_s, v_s, kt_s, q, uplt, upl, delta, probs, factors, grad_s, dqt0, dqt
    )
    store_grads(mine, 0, k_s, v_s, pieces(out_l))
    store_grads(mine, 1, k_s, v_s, pieces(out_r))


def back_own_kernel(
    info, q, uplt, upl, delta, shift_then, shift_last, probs, own, dqt0, attn,
    out, od0, od1, od2, od3,
    k_s, v_s, kt_s, grad_s, dqt, dq_s,
):
    mine = info[0]
    factors = [jnp.exp2(shift_then[x] - shift_last[x]) for x in range(2)]
    load_keys(mine, 0, pieces(own), k_s, v_s)
    backward(
        1, k_s, v_s, kt_s, q, uplt, upl, delta, probs, factors, grad_s, dqt0, dqt
    )
    store_grads(mine, 0, k_s, v_s, pieces(out))
    for x in range(2):
        dq_s[x] = (dqt[x] * SCALE).astype(BF16)
    for d, od in enumerate((od0, od1, od2, od3)):
        x = (mine ^ d) // 2
        for h in range(GROUP):
            od[:, head_at(h)] = attn[x, :, lanes_at(d & 1, h)].T
            od[:, HALF + h * HEAD_DIM : HALF + (h + 1) * HEAD_DIM] = dq_s[
                x, :, lanes_at(d & 1, h)
            ].T


def unpack_kernel(info, od0, od1, od2, od3, attended, query_grad):
    mine = info[0]
    for d, od in enumerate((od0, od1, od2, od3)):
        at = pl.ds(pl.multiple_of((mine ^ d) * HALF, HALF), HALF)
        attended[:, at] = od[:, :HALF]
        query_grad[:, at] = od[:, HALF:]


def both(a, b):
    return (a.astype(F32) + b.astype(F32)).astype(BF16)


def add_kernel(side_l, side_r, far_a, far_b, out_l, out_r):
    out_r[:2] = both(side_r[:2], far_a[...])
    out_r[2:] = side_r[2:]
    out_l[:2] = side_l[:2]
    out_l[2:] = both(side_l[2:], far_b[...])


def sum_kernel(own, left, right, *outs):
    for d, out in enumerate(outs):
        total = own[d].astype(F32) + left[d].astype(F32) + right[d].astype(F32)
        out[...] = total.astype(BF16)


def finish_kernel(info, g0, g1, g2, g3, key_grad, value_grad, share):
    mine = info[0]
    for d, g in enumerate((g0, g1, g2, g3)):
        at = pl.ds(pl.multiple_of((mine ^ d) * HEAD_DIM, HEAD_DIM), HEAD_DIM)
        key_grad[:, at] = g[:ROWS, :HEAD_DIM]
        value_grad[:, at] = g[:ROWS, HEAD_DIM:]
        share[:, at] = g[ROWS:, :HEAD_DIM]
        at = pl.ds(pl.multiple_of(KV_HEADS * HEAD_DIM + (mine ^ d) * HEAD_DIM, HEAD_DIM), HEAD_DIM)
        share[:, at] = g[ROWS:, HEAD_DIM:]


def bf16(*shape):
    return jax.ShapeDtypeStruct(shape, BF16)


def f32(*shape):
    return jax.ShapeDtypeStruct(shape, F32)


def call(kernel, outs, scratch, scalars, *operands, copies=0):
    place = pl.BlockSpec(memory_space=pl.ANY) if copies else VMEM
    scratch = [pltpu.VMEM(shape, dtype) for shape, dtype in scratch]
    if copies:
        scratch.append(pltpu.SemaphoreType.DMA((copies,)))
    return pl.pallas_call(
        kernel,
        out_shape=tuple(outs),
        in_specs=[SMEM] * len(scalars) + [place] * len(operands),
        out_specs=(VMEM,) * len(outs),
        scratch_shapes=scratch,
        compiler_params=pltpu.CompilerParams(vmem_limit_bytes=(60 if copies else 32) * 2**20),
        cost_estimate=pl.CostEstimate(flops=0, bytes_accessed=0, transcendentals=0),
    )(*scalars, *operands)


def swap(x, axis):
    return lax.ppermute(x, axis, [(0, 1), (1, 0)])


def turn(x, axis, step):
    size = lax.axis_size(axis)
    return lax.ppermute(x, axis, [(i, (i + step) % size) for i in range(size)])


def local_permute(x, place):
    pairs = []
    for i in range(32):
        xh, z, core = i // 16, i // 2 % 8, i % 2
        xh, z = place(xh, (z - core) % 8)
        pairs.append((i, (xh * 8 + (z + core) % 8) * 2 + core))
    return lax.ppermute(x, LOCAL, pairs)


def partner(x, d):
    return local_permute(x, lambda xh, z: (xh ^ (d // 2), z ^ (d & 1)))


def quad_turn(x, step):
    return local_permute(x, lambda xh, z: (xh, (z + 2 * step) % 8))


def rounded(x):
    return lax.optimization_barrier(x.astype(BF16))


def body(q_resp, k_resp, v_resp, k_prompt, v_prompt, d_out, lengths, counts):
    core = lax.axis_index("core")
    z = (lax.axis_index("z") - core) & 7
    mine = lax.axis_index("xh") * 2 + (z & 1)
    info = jnp.stack([mine, z // 2, core, lengths[0], counts[0]]).astype(jnp.int32)
    weight = (RESP_LEN / counts[0].astype(F32)).reshape(1)
    kv = list(
        call(
            pack_kv_kernel,
            (bf16(BOTH, WIDE),) * 4,
            (),
            (info,),
            k_resp[0], v_resp[0], k_prompt, v_prompt,
            copies=16,
        )
    )
    qd = list(call(pack_qd_kernel, (bf16(ROWS, LANES),) * 4, (), (info,), q_resp[0], d_out[0], copies=8))
    for d in (1, 2, 3):
        kv[d] = partner(kv[d], d)
    for d in (1, 2, 3):
        qd[d] = partner(qd[d], d)
    own = jnp.stack(kv)
    left, right = quad_turn(own, 1), quad_turn(own, -1)
    far_a, far_b = quad_turn(left[:2], 1), quad_turn(right[2:], -1)

    tiles = (2, HEAD_DIM, LANES)
    line = f32(2, 1, LANES)

    def keys(count):
        return [((count, SPAN, HEAD_DIM), BF16)] * 2

    def forward_scratch(count):
        return keys(count) + [((count, HEAD_DIM, SPAN), BF16), ((count, SPAN, LANES), F32)]

    turned = ((HEAD_DIM, SPAN), BF16)
    grad_s = ((PROBS, LANES), BF16)
    whole, pair = bf16(4, BOTH, WIDE), bf16(2, BOTH, WIDE)
    qt, q, upt, probs1, shift1, total1, acc1 = call(
        first_kernel,
        (bf16(*tiles), bf16(2, LANES, HEAD_DIM), bf16(*tiles), bf16(1, PROBS, LANES), line, line, f32(*tiles)),
        forward_scratch(1),
        (info, weight),
        *qd, own,
    )
    probs2, shift2, total2, acc2 = call(
        side_kernel,
        (bf16(2, PROBS, LANES), line, line, f32(*tiles)),
        forward_scratch(2),
        (info,),
        qt, left, right, shift1, total1, acc1,
    )
    shift3, uplt, upl, delta, dqt, attn, far_ga, far_gb = call(
        far_kernel,
        (line, bf16(*tiles), bf16(2, LANES, HEAD_DIM), line, f32(*tiles), bf16(*tiles), pair, pair),
        keys(1) + [((1, HEAD_DIM, SPAN), BF16), turned, ((1, SPAN, LANES), F32)]
        + [((1, PROBS, LANES), BF16), grad_s, (tiles, F32), ((2, 1, LANES), F32)],
        (info,),
        qt, q, upt, far_a, far_b, shift2, total2, acc2,
    )
    far_ga, far_gb = quad_turn(far_ga, 1), quad_turn(far_gb, -1)
    dqt, left_g, right_g = call(
        back_side_kernel,
        (f32(*tiles), whole, whole),
        keys(2) + [turned, grad_s],
        (info,),
        q, uplt, upl, delta, shift2, shift3, probs2,
        left, right, dqt,
    )
    left_g, right_g = call(add_kernel, (whole, whole), (), (), left_g, right_g, far_ga, far_gb)
    left_g, right_g = quad_turn(left_g, -1), quad_turn(right_g, 1)
    own_g, *od = call(
        back_own_kernel,
        (whole,) + (bf16(ROWS, LANES),) * 4,
        keys(1) + [turned, grad_s, (tiles, F32), (tiles, BF16)],
        (info,),
        q, uplt, upl, delta, shift1, shift3, probs1, own, dqt, attn,
    )
    for d in (1, 2, 3):
        od[d] = partner(od[d], d)
    grads = list(call(sum_kernel, (bf16(BOTH, WIDE),) * 4, (), (), own_g, left_g, right_g))
    for d in (1, 2, 3):
        grads[d] = partner(grads[d], d)
    tied = lax.optimization_barrier((*grads, *od))
    grads, od = tied[:4], tied[4:]
    width = KV_HEADS * HEAD_DIM
    rows = bf16(ROWS, HEADS * HEAD_DIM)
    key_grad, value_grad, share = call(
        finish_kernel,
        (bf16(ROWS, width), bf16(ROWS, width), bf16(PROWS, 2 * width)),
        (),
        (info,),
        *grads,
    )
    for axis in ("core", "xl"):
        share = rounded(share.astype(F32) + swap(share, axis).astype(F32))
    across = share.astype(F32) + turn(share, "y", 2).astype(F32)
    beside = turn(share, "y", 1).astype(F32) + turn(share, "y", 3).astype(F32)
    share = (across + beside).astype(BF16)
    attended, query_grad = call(unpack_kernel, (rows, rows), (), (info,), *od)
    return (
        attended[None],
        query_grad[None],
        key_grad[None],
        value_grad[None],
        share[:, :width],
        share[:, width:],
    )


def solution(mesh):
    split = Mesh(mesh.devices.reshape(2, 8, 4, 2, 2), CTX + RESP)
    rows = P(RESP, CTX, None)
    prompt = P(CTX, None)
    return jax.shard_map(
        body,
        mesh=split,
        in_specs=(rows, rows, rows, prompt, prompt, rows, P(RESP), P(RESP)),
        out_specs=(rows, rows, rows, rows, prompt, prompt),
        check_vma=False,
    )
```

profile of v0, /device:TPU:1, one launch (start us, length us, event | category | flops | bytes accessed | tf_op | source)
XLA Modules:
  0.0 136.5 jit_solution(10643331931100623238)
XLA Ops:
  2.6 2.5 %shard_map.128 = (bf16[192,256]{1,0:T(8,128)(2,1)}, bf16[192,256]{1,0:T(8,128)(2,1)}, bf16[192,256]{1,0:T(8,128)(2,1)}, bf16[192,256]{1,0:T(8,128)(2,1)}) custom-call(s32[5]{0:T(128)} %stack.30.info, bf16[128,512]{1,0:T(8,128)(2,1)} %bitcast.17, bf16[128,512]{1,0:T(8,128)(2,1)} %bitcast.18, bf16[64,512]{1,0:T(8,128)(2,1)} %kp.1, bf16[64,512]{1,0:T(8,128)(2,1)} %vp.1), custom_call_target="tpu_custom_call" | custom-call | tf_op jit(solution)/shard_map/pallas_call | solution.py:379
  5.1 6.5 %collective-permute-start.3 = (bf16[192,256]{1,0:T(8,128)(2,1)}, bf16[192,256]{1,0:T(8,128)(2,1)S(1)}, u32[]{:S(2)}, u32[]{:S(2)}) collective-permute-start(bf16[192,256]{1,0:T(8,128)(2,1)} %get-tuple-element.65), channel_id=1, source_target_pairs={{0,16},{1,113},{16,0},{17,33},{32,48},{33,17},{48,32},{49,65},{64,... | collective-permute-start | bytes 294920 | tf_op jit(solution)/shard_map/ppermute | solution.py:405
  11.6 2.7 %collective-permute-start.4 = (bf16[192,256]{1,0:T(8,128)(2,1)}, bf16[192,256]{1,0:T(8,128)(2,1)S(1)}, u32[]{:S(2)}, u32[]{:S(2)}) collective-permute-start(bf16[192,256]{1,0:T(8,128)(2,1)} %get-tuple-element.66), channel_id=1, source_target_pairs={{0,128},{1,129},{16,144},{17,145},{32,160},{33,161},{48,176},{49,1... | collective-permute-start | bytes 294920 | tf_op jit(solution)/shard_map/ppermute | solution.py:405
  14.4 2.4 %collective-permute-done.4 = bf16[192,256]{1,0:T(8,128)(2,1)S(1)} collective-permute-done((bf16[192,256]{1,0:T(8,128)(2,1)}, bf16[192,256]{1,0:T(8,128)(2,1)S(1)}, u32[]{:S(2)}, u32[]{:S(2)}) %collective-permute-start.4) | collective-permute-done | bytes 98336 | tf_op jit(solution)/shard_map/ppermute | solution.py:405
  16.7 4.9 %collective-permute-done.5 = bf16[192,256]{1,0:T(8,128)(2,1)S(1)} collective-permute-done((bf16[192,256]{1,0:T(8,128)(2,1)}, bf16[192,256]{1,0:T(8,128)(2,1)S(1)}, u32[]{:S(2)}, u32[]{:S(2)}) %collective-permute-start.5) | collective-permute-done | bytes 98336 | tf_op jit(solution)/shard_map/ppermute | solution.py:405
  22.6 2.4 %collective-permute-start.6 = (bf16[4,192,256]{2,1,0:T(8,128)(2,1)S(1)}, bf16[4,192,256]{2,1,0:T(8,128)(2,1)S(1)}, u32[]{:S(2)}, u32[]{:S(2)}) collective-permute-start(bf16[4,192,256]{2,1,0:T(8,128)(2,1)S(1)} %pad_maximum_fusion.own), channel_id=1, source_target_pairs={{0,32},{1,33},{16,48},{17,49},{32,64},{33,65},{48,80},{49,81},{64,... | collective-permute-start | bytes 1179656 | tf_op jit(solution)/shard_map/ppermute | solution.py:405
  25.0 3.0 %shard_map.127 = (bf16[128,1024]{1,0:T(8,128)(2,1)}, bf16[128,1024]{1,0:T(8,128)(2,1)}, bf16[128,1024]{1,0:T(8,128)(2,1)}, bf16[128,1024]{1,0:T(8,128)(2,1)}) custom-call(s32[5]{0:T(128)} %stack.30.info, bf16[128,2048]{1,0:T(8,128)(2,1)} %bitcast.15, bf16[128,2048]{1,0:T(8,128)(2,1)} %bitcast.16), custom_call_target="tpu_custom_call" | custom-call | tf_op jit(solution)/shard_map/pallas_call | solution.py:379
  28.0 1.4 %collective-permute-start = (bf16[128,1024]{1,0:T(8,128)(2,1)}, bf16[128,1024]{1,0:T(8,128)(2,1)S(1)}, u32[]{:S(2)}, u32[]{:S(2)}) collective-permute-start(bf16[128,1024]{1,0:T(8,128)(2,1)} %get-tuple-element.61), channel_id=1, source_target_pairs={{0,16},{1,113},{16,0},{17,33},{32,48},{33,17},{48,32},{49,65},{64,... | collective-permute-start | bytes 786440 | tf_op jit(solution)/shard_map/ppermute | solution.py:405
  29.7 3.7 %collective-permute-start.2 = (bf16[128,1024]{1,0:T(8,128)(2,1)}, bf16[128,1024]{1,0:T(8,128)(2,1)S(1)}, u32[]{:S(2)}, u32[]{:S(2)}) collective-permute-start(bf16[128,1024]{1,0:T(8,128)(2,1)} %get-tuple-element.63), channel_id=1, source_target_pairs={{0,144},{1,241},{16,128},{17,161},{32,176},{33,145},{48,160},{49,1... | collective-permute-start | bytes 786440 | tf_op jit(solution)/shard_map/ppermute | solution.py:405
  33.4 7.1 %collective-permute-done.8.right = bf16[4,192,256]{2,1,0:T(8,128)(2,1)S(1)} collective-permute-done((bf16[4,192,256]{2,1,0:T(8,128)(2,1)S(1)}, bf16[4,192,256]{2,1,0:T(8,128)(2,1)S(1)}, u32[]{:S(2)}, u32[]{:S(2)}) %collective-permute-start.8) | collective-permute-done | bytes 393248 | tf_op jit(solution)/shard_map/ppermute | solution.py:405
  40.9 2.3 %collective-permute-start.7 = (bf16[2,192,256]{2,1,0:T(8,128)(2,1)S(1)}, bf16[2,192,256]{2,1,0:T(8,128)(2,1)S(1)}, u32[]{:S(2)}, u32[]{:S(2)}) collective-permute-start(bf16[2,192,256]{2,1,0:T(8,128)(2,1)S(1)} %slice.16), channel_id=1, source_target_pairs={{0,32},{1,33},{16,48},{17,49},{32,64},{33,65},{48,80},{49,81},{64,... | collective-permute-start | bytes 589832 | tf_op jit(solution)/shard_map/ppermute | solution.py:405
  43.3 5.1 %collective-permute-done.qd1 = bf16[128,1024]{1,0:T(8,128)(2,1)S(1)} collective-permute-done((bf16[128,1024]{1,0:T(8,128)(2,1)}, bf16[128,1024]{1,0:T(8,128)(2,1)S(1)}, u32[]{:S(2)}, u32[]{:S(2)}) %collective-permute-start) | collective-permute-done | bytes 262176 | tf_op jit(solution)/shard_map/ppermute | solution.py:405
  48.4 5.9 %collective-permute-done.2.qd3 = bf16[128,1024]{1,0:T(8,128)(2,1)S(1)} collective-permute-done((bf16[128,1024]{1,0:T(8,128)(2,1)}, bf16[128,1024]{1,0:T(8,128)(2,1)S(1)}, u32[]{:S(2)}, u32[]{:S(2)}) %collective-permute-start.2) | collective-permute-done | bytes 262176 | tf_op jit(solution)/shard_map/ppermute | solution.py:405
  55.9 3.4 %shard_map.129 = (bf16[2,128,1024]{2,1,0:T(8,128)(2,1)S(1)}, bf16[2,1024,128]{2,1,0:T(8,128)(2,1)S(1)}, bf16[2,128,1024]{2,1,0:T(8,128)(2,1)S(1)}, bf16[1,1280,1...) custom-call(s32[5]{0:T(128)S(1)} %copy-done.1, ...), custom_call_target="tpu_custom_call" | custom-call | tf_op jit(solution)/shard_map/pallas_call | solution.py:379
  59.3 5.7 %shard_map.130 = (bf16[2,1280,1024]{2,1,0:T(8,128)(2,1)S(1)}, f32[2,1,1024]{2,1,0:T(1,128)S(1)}, f32[2,1,1024]{2,1,0:T(1,128)S(1)}, f32[2,128,1024]{2,1,0:T(8,128)S(1)}) custom-call(s32[5]{0:T(128)S(1)} %copy-done.1, bf16[2,128,1024]{2,1,0:T(8,128)(2,1)S(1)} %get-tuple-element.69.qt, bf16[4,192,256]{2,1,0:T(8,128)(2,1)S(1)} %collective-permute-done.6.left, ...), custom_call_target="tpu_custom_call" | custom-call | tf_op jit(solution)/shard_map/pallas_call | solution.py:379
  65.0 6.4 %shard_map.131 = (f32[2,1,1024]{2,1,0:T(1,128)S(1)}, bf16[2,128,1024]{2,1,0:T(8,128)(2,1)S(1)}, bf16[2,1024,128]{2,1,0:T(8,128)(2,1)S(1)}, f32[2,1,1024]{2,1,0:T...) custom-call(s32[5]{0:T(128)S(1)} %copy-done.1, ...), custom_call_target="tpu_custom_call" | custom-call | tf_op jit(solution)/shard_map/pallas_call | solution.py:379
  71.5 3.6 %collective-permute-start.11 = (bf16[2,192,256]{2,1,0:T(8,128)(2,1)S(1)}, bf16[2,192,256]{2,1,0:T(8,128)(2,1)S(1)}, u32[]{:S(2)}, u32[]{:S(2)}) collective-permute-start(bf16[2,192,256]{2,1,0:T(8,128)(2,1)S(1)} %get-tuple-element.90), channel_id=1, source_target_pairs={{0,96},{1,97},{16,112},{17,113},{32,0},{33,1},{48,16},{49,17},{64,... | collective-permute-start | bytes 589832 | tf_op jit(solution)/shard_map/ppermute | solution.py:405
  75.1 7.7 %shard_map.132 = (f32[2,128,1024]{2,1,0:T(8,128)S(1)}, bf16[4,192,256]{2,1,0:T(8,128)(2,1)S(1)}, bf16[4,192,256]{2,1,0:T(8,128)(2,1)S(1)}) custom-call(s32[5]{0:T(128)S(1)} %copy-done.1, bf16[2,1024,128]{2,1,0:T(8,128)(2,1)S(1)} %get-tuple-element.68.q, bf16[2,128,1024]{2,1,0:T(8,128)(2,1)S(1)} %get-tuple-element.77.uplt, ...), custom_call_target="tpu_custom_call" | custom-call | tf_op jit(solution)/shard_map/pallas_call | solution.py:379
  83.0 3.5 %collective-permute-start.12 = (bf16[4,192,256]{2,1,0:T(8,128)(2,1)S(1)}, bf16[4,192,256]{2,1,0:T(8,128)(2,1)S(1)}, u32[]{:S(2)}, u32[]{:S(2)}) collective-permute-start(bf16[4,192,256]{2,1,0:T(8,128)(2,1)S(1)} %get-tuple-element.91), channel_id=1, source_target_pairs={{0,96},{1,97},{16,112},{17,113},{32,0},{33,1},{48,16},{49,17},{64,... | collective-permute-start | bytes 1179656 | tf_op jit(solution)/shard_map/ppermute | solution.py:405
  86.4 4.4 %shard_map.133 = (bf16[4,192,256]{2,1,0:T(8,128)(2,1)S(1)}, bf16[128,1024]{1,0:T(8,128)(2,1)S(1)}, bf16[128,1024]{1,0:T(8,128)(2,1)S(1)}, bf16[128,1024]{1,0:T(8,128)(2,1)S(1)}, bf16[128,1024]{1,0:T(8,128)(2,1)S(1)}) custom-call(s32[5]{0:T(128)S(1)} %copy-done.1, bf16[2,1024,128]{2,1,0:T(8,128)(2,1)S(1)} %get-tuple-element.68.q, ...), custom_call_target="tpu_custom_call" | custom-call | tf_op jit(solution)/shard_map/pallas_call | solution.py:379
  91.0 2.9 %collective-permute-start.18 = (bf16[128,1024]{1,0:T(8,128)(2,1)S(1)}, bf16[128,1024]{1,0:T(8,128)(2,1)S(1)}, u32[]{:S(2)}, u32[]{:S(2)}) collective-permute-start(bf16[128,1024]{1,0:T(8,128)(2,1)S(1)} %get-tuple-element.99), channel_id=1, source_target_pairs={{0,128},{1,129},{16,144},{17,145},{32,160},{33,161},{48,176},{49,1... | collective-permute-start | bytes 786440 | tf_op jit(solution)/shard_map/ppermute | solution.py:405
  93.9 2.4 %collective-permute-start.19 = (bf16[128,1024]{1,0:T(8,128)(2,1)S(1)}, bf16[128,1024]{1,0:T(8,128)(2,1)S(1)}, u32[]{:S(2)}, u32[]{:S(2)}) collective-permute-start(bf16[128,1024]{1,0:T(8,128)(2,1)S(1)} %get-tuple-element.100), channel_id=1, source_target_pairs={{0,144},{1,241},{16,128},{17,161},{32,176},{33,145},{48,160},{49,1... | collective-permute-start | bytes 786440 | tf_op jit(solution)/shard_map/ppermute | solution.py:405
  96.3 6.1 %collective-permute-done.12.left = bf16[4,192,256]{2,1,0:T(8,128)(2,1)S(1)} collective-permute-done((bf16[4,192,256]{2,1,0:T(8,128)(2,1)S(1)}, bf16[4,192,256]{2,1,0:T(8,128)(2,1)S(1)}, u32[]{:S(2)}, u32[]{:S(2)}) %collective-permute-start.12) | collective-permute-done | bytes 393248 | tf_op jit(solution)/shard_map/ppermute | solution.py:405
  102.4 1.7 %collective-permute-done.13.right = bf16[4,192,256]{2,1,0:T(8,128)(2,1)S(1)} collective-permute-done((bf16[4,192,256]{2,1,0:T(8,128)(2,1)S(1)}, bf16[4,192,256]{2,1,0:T(8,128)(2,1)S(1)}, u32[]{:S(2)}, u32[]{:S(2)}) %collective-permute-start.13) | collective-permute-done | bytes 393248 | tf_op jit(solution)/shard_map/ppermute | solution.py:405
  104.4 4.4 %collective-permute-start.15 = (bf16[192,256]{1,0:T(8,128)(2,1)S(1)}, bf16[192,256]{1,0:T(8,128)(2,1)S(1)}, u32[]{:S(2)}, u32[]{:S(2)}) collective-permute-start(bf16[192,256]{1,0:T(8,128)(2,1)S(1)} %get-tuple-element.95), channel_id=1, source_target_pairs={{0,128},{1,129},{16,144},{17,145},{32,160},{33,161},{48,176},{49,1... | collective-permute-start | bytes 294920 | tf_op jit(solution)/shard_map/ppermute | solution.py:405
  108.8 2.3 %collective-permute-start.16 = (bf16[192,256]{1,0:T(8,128)(2,1)S(1)}, bf16[192,256]{1,0:T(8,128)(2,1)S(1)}, u32[]{:S(2)}, u32[]{:S(2)}) collective-permute-start(bf16[192,256]{1,0:T(8,128)(2,1)S(1)} %get-tuple-element.96), channel_id=1, source_target_pairs={{0,144},{1,241},{16,128},{17,161},{32,176},{33,145},{48,160},{49,1... | collective-permute-start | bytes 294920 | tf_op jit(solution)/shard_map/ppermute | solution.py:405
  111.2 5.6 %collective-permute-done.16.g3 = bf16[192,256]{1,0:T(8,128)(2,1)S(1)} collective-permute-done((bf16[192,256]{1,0:T(8,128)(2,1)S(1)}, bf16[192,256]{1,0:T(8,128)(2,1)S(1)}, u32[]{:S(2)}, u32[]{:S(2)}) %collective-permute-start.16) | collective-permute-done | bytes 98336 | tf_op jit(solution)/shard_map/ppermute | solution.py:405
  120.5 3.8 %collective-permute-done.21 = bf16[64,1024]{1,0:T(8,128)(2,1)S(1)} collective-permute-done((bf16[64,1024]{1,0:T(8,128)(2,1)S(1)}, bf16[64,1024]{1,0:T(8,128)(2,1)S(1)}, u32[]{:S(2)}, u32[]{:S(2)}) %collective-permute-start.21) | collective-permute-done | bytes 131104 | tf_op jit(solution)/shard_map/ppermute | solution.py:391
  124.4 2.8 %collective-permute-start.24 = (bf16[64,1024]{1,0:T(8,128)(2,1)S(1)}, bf16[64,1024]{1,0:T(8,128)(2,1)S(1)}, u32[]{:S(2)}, u32[]{:S(2)}) collective-permute-start(bf16[64,1024]{1,0:T(8,128)(2,1)S(1)} %add_convert_fusion.1), channel_id=1, source_target_pairs={{0,12},{4,0},{8,4},{12,8},{1,13},{5,1},{9,5},{13,9},{2,14},{6,2},{... | collective-permute-start | bytes 393224 | tf_op jit(solution)/shard_map/ppermute | solution.py:396
  127.2 1.6 %collective-permute-start.22 = (bf16[64,1024]{1,0:T(8,128)(2,1)S(1)}, bf16[64,1024]{1,0:T(8,128)(2,1)S(1)}, u32[]{:S(2)}, u32[]{:S(2)}) collective-permute-start(bf16[64,1024]{1,0:T(8,128)(2,1)S(1)} %add_convert_fusion.1), channel_id=1, source_target_pairs={{0,8},{4,12},{8,0},{12,4},{1,9},{5,13},{9,1},{13,5},{2,10},{6,14},... | collective-permute-start | bytes 393224 | tf_op jit(solution)/shard_map/ppermute | solution.py:396
  128.8 1.6 %shard_map.136 = (bf16[128,2048]{1,0:T(8,128)(2,1)}, bf16[128,2048]{1,0:T(8,128)(2,1)}) custom-call(s32[5]{0:T(128)S(1)} %copy-done.1, bf16[128,1024]{1,0:T(8,128)(2,1)S(1)} %get-tuple-element.101.od0, bf16[128,1024]{1,0:T(8,128)(2,1)S(1)} %collective-permute-done.17.od1, bf16[128,1024]{1,0:T(8,128)(2,1)S(1)} %collective-permute-done.18.od2, ...), custom_call_target="tpu_custom_call" | custom-call | tf_op jit(solution)/shard_map/pallas_call | solution.py:379
  130.4 5.4 %collective-permute-done.23 = bf16[64,1024]{1,0:T(8,128)(2,1)S(1)} collective-permute-done((bf16[64,1024]{1,0:T(8,128)(2,1)S(1)}, bf16[64,1024]{1,0:T(8,128)(2,1)S(1)}, u32[]{:S(2)}, u32[]{:S(2)}) %collective-permute-start.23) | collective-permute-done | bytes 131104 | tf_op jit(solution)/shard_map/ppermute | solution.py:396
  (41 shorter events, 9.1 us)
Async XLA Ops:
  5.1 9.3 %collective-permute-start.3 = (bf16[192,256]{1,0:T(8,128)(2,1)}, bf16[192,256]{1,0:T(8,128)(2,1)S(1)}, u32[]{:S(2)}, u32[]{:S(2)}) collective-permute-start(bf16[192,256]{1,0:T(8,128)(2,1)} %get-tuple-element.65), channel_id=1, source_target_pairs={{0,16},{1,113},{16,0},{17,33},{32,48},{33,17},{48,32},{49,65},{64,... | collective-permute-start | bytes 294920 | tf_op jit(solution)/shard_map/ppermute | solution.py:405
  11.6 5.2 %collective-permute-start.4 = (bf16[192,256]{1,0:T(8,128)(2,1)}, bf16[192,256]{1,0:T(8,128)(2,1)S(1)}, u32[]{:S(2)}, u32[]{:S(2)}) collective-permute-start(bf16[192,256]{1,0:T(8,128)(2,1)} %get-tuple-element.66), channel_id=1, source_target_pairs={{0,128},{1,129},{16,144},{17,145},{32,160},{33,161},{48,176},{49,1... | collective-permute-start | bytes 294920 | tf_op jit(solution)/shard_map/ppermute | solution.py:405
  14.3 7.3 %collective-permute-start.5 = (bf16[192,256]{1,0:T(8,128)(2,1)}, bf16[192,256]{1,0:T(8,128)(2,1)S(1)}, u32[]{:S(2)}, u32[]{:S(2)}) collective-permute-start(bf16[192,256]{1,0:T(8,128)(2,1)} %get-tuple-element.67), channel_id=1, source_target_pairs={{0,144},{1,241},{16,128},{17,161},{32,176},{33,145},{48,160},{49,1... | collective-permute-start | bytes 294920 | tf_op jit(solution)/shard_map/ppermute | solution.py:405
  22.5 18.0 %collective-permute-start.8 = (bf16[4,192,256]{2,1,0:T(8,128)(2,1)S(1)}, bf16[4,192,256]{2,1,0:T(8,128)(2,1)S(1)}, u32[]{:S(2)}, u32[]{:S(2)}) collective-permute-start(bf16[4,192,256]{2,1,0:T(8,128)(2,1)S(1)} %pad_maximum_fusion.own), channel_id=1, source_target_pairs={{0,96},{1,97},{16,112},{17,113},{32,0},{33,1},{48,16},{49,17},{64,... | collective-permute-start | bytes 1179656 | tf_op jit(solution)/shard_map/ppermute | solution.py:405
  22.6 18.3 %collective-permute-start.6 = (bf16[4,192,256]{2,1,0:T(8,128)(2,1)S(1)}, bf16[4,192,256]{2,1,0:T(8,128)(2,1)S(1)}, u32[]{:S(2)}, u32[]{:S(2)}) collective-permute-start(bf16[4,192,256]{2,1,0:T(8,128)(2,1)S(1)} %pad_maximum_fusion.own), channel_id=1, source_target_pairs={{0,32},{1,33},{16,48},{17,49},{32,64},{33,65},{48,80},{49,81},{64,... | collective-permute-start | bytes 1179656 | tf_op jit(solution)/shard_map/ppermute | solution.py:405
  28.0 20.4 %collective-permute-start = (bf16[128,1024]{1,0:T(8,128)(2,1)}, bf16[128,1024]{1,0:T(8,128)(2,1)S(1)}, u32[]{:S(2)}, u32[]{:S(2)}) collective-permute-start(bf16[128,1024]{1,0:T(8,128)(2,1)} %get-tuple-element.61), channel_id=1, source_target_pairs={{0,16},{1,113},{16,0},{17,33},{32,48},{33,17},{48,32},{49,65},{64,... | collective-permute-start | bytes 786440 | tf_op jit(solution)/shard_map/ppermute | solution.py:405
  29.4 19.0 %collective-permute-start.1 = (bf16[128,1024]{1,0:T(8,128)(2,1)}, bf16[128,1024]{1,0:T(8,128)(2,1)S(1)}, u32[]{:S(2)}, u32[]{:S(2)}) collective-permute-start(bf16[128,1024]{1,0:T(8,128)(2,1)} %get-tuple-element.62), channel_id=1, source_target_pairs={{0,128},{1,129},{16,144},{17,145},{32,160},{33,161},{48,176},{49,1... | collective-permute-start | bytes 786440 | tf_op jit(solution)/shard_map/ppermute | solution.py:405
  29.7 24.6 %collective-permute-start.2 = (bf16[128,1024]{1,0:T(8,128)(2,1)}, bf16[128,1024]{1,0:T(8,128)(2,1)S(1)}, u32[]{:S(2)}, u32[]{:S(2)}) collective-permute-start(bf16[128,1024]{1,0:T(8,128)(2,1)} %get-tuple-element.63), channel_id=1, source_target_pairs={{0,144},{1,241},{16,128},{17,161},{32,176},{33,145},{48,160},{49,1... | collective-permute-start | bytes 786440 | tf_op jit(solution)/shard_map/ppermute | solution.py:405
  40.5 24.5 %collective-permute-start.9 = (bf16[2,192,256]{2,1,0:T(8,128)(2,1)S(1)}, bf16[2,192,256]{2,1,0:T(8,128)(2,1)S(1)}, u32[]{:S(2)}, u32[]{:S(2)}) collective-permute-start(bf16[2,192,256]{2,1,0:T(8,128)(2,1)S(1)} %slice.17), channel_id=1, source_target_pairs={{0,96},{1,97},{16,112},{17,113},{32,0},{33,1},{48,16},{49,17},{64,... | collective-permute-start | bytes 589832 | tf_op jit(solution)/shard_map/ppermute | solution.py:405
  40.9 24.1 %collective-permute-start.7 = (bf16[2,192,256]{2,1,0:T(8,128)(2,1)S(1)}, bf16[2,192,256]{2,1,0:T(8,128)(2,1)S(1)}, u32[]{:S(2)}, u32[]{:S(2)}) collective-permute-start(bf16[2,192,256]{2,1,0:T(8,128)(2,1)S(1)} %slice.16), channel_id=1, source_target_pairs={{0,32},{1,33},{16,48},{17,49},{32,64},{33,65},{48,80},{49,81},{64,... | collective-permute-start | bytes 589832 | tf_op jit(solution)/shard_map/ppermute | solution.py:405
  54.3 1.0 copy-start
  55.3 0.6 copy-start.1
  71.4 11.4 %collective-permute-start.10 = (bf16[2,192,256]{2,1,0:T(8,128)(2,1)S(1)}, bf16[2,192,256]{2,1,0:T(8,128)(2,1)S(1)}, u32[]{:S(2)}, u32[]{:S(2)}) collective-permute-start(bf16[2,192,256]{2,1,0:T(8,128)(2,1)S(1)} %get-tuple-element.89), channel_id=1, source_target_pairs={{0,32},{1,33},{16,48},{17,49},{32,64},{33,65},{48,80},{49,81},{64,... | collective-permute-start | bytes 589832 | tf_op jit(solution)/shard_map/ppermute | solution.py:405
  71.5 11.3 %collective-permute-start.11 = (bf16[2,192,256]{2,1,0:T(8,128)(2,1)S(1)}, bf16[2,192,256]{2,1,0:T(8,128)(2,1)S(1)}, u32[]{:S(2)}, u32[]{:S(2)}) collective-permute-start(bf16[2,192,256]{2,1,0:T(8,128)(2,1)S(1)} %get-tuple-element.90), channel_id=1, source_target_pairs={{0,96},{1,97},{16,112},{17,113},{32,0},{33,1},{48,16},{49,17},{64,... | collective-permute-start | bytes 589832 | tf_op jit(solution)/shard_map/ppermute | solution.py:405
  83.0 19.5 %collective-permute-start.12 = (bf16[4,192,256]{2,1,0:T(8,128)(2,1)S(1)}, bf16[4,192,256]{2,1,0:T(8,128)(2,1)S(1)}, u32[]{:S(2)}, u32[]{:S(2)}) collective-permute-start(bf16[4,192,256]{2,1,0:T(8,128)(2,1)S(1)} %get-tuple-element.91), channel_id=1, source_target_pairs={{0,96},{1,97},{16,112},{17,113},{32,0},{33,1},{48,16},{49,17},{64,... | collective-permute-start | bytes 1179656 | tf_op jit(solution)/shard_map/ppermute | solution.py:405
  86.4 17.7 %collective-permute-start.13 = (bf16[4,192,256]{2,1,0:T(8,128)(2,1)S(1)}, bf16[4,192,256]{2,1,0:T(8,128)(2,1)S(1)}, u32[]{:S(2)}, u32[]{:S(2)}) collective-permute-start(bf16[4,192,256]{2,1,0:T(8,128)(2,1)S(1)} %get-tuple-element.92), channel_id=1, source_target_pairs={{0,32},{1,33},{16,48},{17,49},{32,64},{33,65},{48,80},{49,81},{64,... | collective-permute-start | bytes 1179656 | tf_op jit(solution)/shard_map/ppermute | solution.py:405
  90.9 18.0 %collective-permute-start.17 = (bf16[128,1024]{1,0:T(8,128)(2,1)S(1)}, bf16[128,1024]{1,0:T(8,128)(2,1)S(1)}, u32[]{:S(2)}, u32[]{:S(2)}) collective-permute-start(bf16[128,1024]{1,0:T(8,128)(2,1)S(1)} %get-tuple-element.98), channel_id=1, source_target_pairs={{0,16},{1,113},{16,0},{17,33},{32,48},{33,17},{48,32},{49,65},{64,... | collective-permute-start | bytes 786440 | tf_op jit(solution)/shard_map/ppermute | solution.py:405
  91.0 20.2 %collective-permute-start.18 = (bf16[128,1024]{1,0:T(8,128)(2,1)S(1)}, bf16[128,1024]{1,0:T(8,128)(2,1)S(1)}, u32[]{:S(2)}, u32[]{:S(2)}) collective-permute-start(bf16[128,1024]{1,0:T(8,128)(2,1)S(1)} %get-tuple-element.99), channel_id=1, source_target_pairs={{0,128},{1,129},{16,144},{17,145},{32,160},{33,161},{48,176},{49,1... | collective-permute-start | bytes 786440 | tf_op jit(solution)/shard_map/ppermute | solution.py:405
  93.9 17.3 %collective-permute-start.19 = (bf16[128,1024]{1,0:T(8,128)(2,1)S(1)}, bf16[128,1024]{1,0:T(8,128)(2,1)S(1)}, u32[]{:S(2)}, u32[]{:S(2)}) collective-permute-start(bf16[128,1024]{1,0:T(8,128)(2,1)S(1)} %get-tuple-element.100), channel_id=1, source_target_pairs={{0,144},{1,241},{16,128},{17,161},{32,176},{33,145},{48,160},{49,1... | collective-permute-start | bytes 786440 | tf_op jit(solution)/shard_map/ppermute | solution.py:405
  104.3 6.8 %collective-permute-start.14 = (bf16[192,256]{1,0:T(8,128)(2,1)S(1)}, bf16[192,256]{1,0:T(8,128)(2,1)S(1)}, u32[]{:S(2)}, u32[]{:S(2)}) collective-permute-start(bf16[192,256]{1,0:T(8,128)(2,1)S(1)} %get-tuple-element.94), channel_id=1, source_target_pairs={{0,16},{1,113},{16,0},{17,33},{32,48},{33,17},{48,32},{49,65},{64,... | collective-permute-start | bytes 294920 | tf_op jit(solution)/shard_map/ppermute | solution.py:405
  104.4 6.7 %collective-permute-start.15 = (bf16[192,256]{1,0:T(8,128)(2,1)S(1)}, bf16[192,256]{1,0:T(8,128)(2,1)S(1)}, u32[]{:S(2)}, u32[]{:S(2)}) collective-permute-start(bf16[192,256]{1,0:T(8,128)(2,1)S(1)} %get-tuple-element.95), channel_id=1, source_target_pairs={{0,128},{1,129},{16,144},{17,145},{32,160},{33,161},{48,176},{49,1... | collective-permute-start | bytes 294920 | tf_op jit(solution)/shard_map/ppermute | solution.py:405
  108.8 7.9 %collective-permute-start.16 = (bf16[192,256]{1,0:T(8,128)(2,1)S(1)}, bf16[192,256]{1,0:T(8,128)(2,1)S(1)}, u32[]{:S(2)}, u32[]{:S(2)}) collective-permute-start(bf16[192,256]{1,0:T(8,128)(2,1)S(1)} %get-tuple-element.96), channel_id=1, source_target_pairs={{0,144},{1,241},{16,128},{17,161},{32,176},{33,145},{48,160},{49,1... | collective-permute-start | bytes 294920 | tf_op jit(solution)/shard_map/ppermute | solution.py:405
  118.0 1.4 %collective-permute-start.20 = (bf16[64,1024]{1,0:T(8,128)(2,1)S(1)}, bf16[64,1024]{1,0:T(8,128)(2,1)S(1)}, u32[]{:S(2)}, u32[]{:S(2)}) collective-permute-start(bf16[64,1024]{1,0:T(8,128)(2,1)S(1)} %get-tuple-element.113), channel_id=1, source_target_pairs={{0,1},{1,0},{2,3},{3,2},{4,5},{5,4},{6,7},{7,6},{8,9},{9,8},{10,11... | collective-permute-start | bytes 393224 | tf_op jit(solution)/shard_map/ppermute | solution.py:391
  119.5 4.8 %collective-permute-start.21 = (bf16[64,1024]{1,0:T(8,128)(2,1)S(1)}, bf16[64,1024]{1,0:T(8,128)(2,1)S(1)}, u32[]{:S(2)}, u32[]{:S(2)}) collective-permute-start(bf16[64,1024]{1,0:T(8,128)(2,1)S(1)} %add_convert_fusion.2), channel_id=1, source_target_pairs={{0,2},{2,0},{1,3},{3,1},{4,6},{6,4},{5,7},{7,5},{8,10},{10,8},{9,1... | collective-permute-start | bytes 393224 | tf_op jit(solution)/shard_map/ppermute | solution.py:391
  124.4 6.0 %collective-permute-start.24 = (bf16[64,1024]{1,0:T(8,128)(2,1)S(1)}, bf16[64,1024]{1,0:T(8,128)(2,1)S(1)}, u32[]{:S(2)}, u32[]{:S(2)}) collective-permute-start(bf16[64,1024]{1,0:T(8,128)(2,1)S(1)} %add_convert_fusion.1), channel_id=1, source_target_pairs={{0,12},{4,0},{8,4},{12,8},{1,13},{5,1},{9,5},{13,9},{2,14},{6,2},{... | collective-permute-start | bytes 393224 | tf_op jit(solution)/shard_map/ppermute | solution.py:396
  127.2 8.6 %collective-permute-start.23 = (bf16[64,1024]{1,0:T(8,128)(2,1)S(1)}, bf16[64,1024]{1,0:T(8,128)(2,1)S(1)}, u32[]{:S(2)}, u32[]{:S(2)}) collective-permute-start(bf16[64,1024]{1,0:T(8,128)(2,1)S(1)} %add_convert_fusion.1), channel_id=1, source_target_pairs={{0,4},{4,8},{8,12},{12,0},{1,5},{5,9},{9,13},{13,1},{2,6},{6,10},{... | collective-permute-start | bytes 393224 | tf_op jit(solution)/shard_map/ppermute | solution.py:396
  127.2 8.6 %collective-permute-start.22 = (bf16[64,1024]{1,0:T(8,128)(2,1)S(1)}, bf16[64,1024]{1,0:T(8,128)(2,1)S(1)}, u32[]{:S(2)}, u32[]{:S(2)}) collective-permute-start(bf16[64,1024]{1,0:T(8,128)(2,1)S(1)} %add_convert_fusion.1), channel_id=1, source_target_pairs={{0,8},{4,12},{8,0},{12,4},{1,9},{5,13},{9,1},{13,5},{2,10},{6,14},... | collective-permute-start | bytes 393224 | tf_op jit(solution)/shard_map/ppermute | solution.py:396
where the time goes:
time: 137 us
  waiting for transfers between devices  49 us (36%)
  starting transfers between devices  45.1 us (33%)
  Pallas kernels  36.3 us (26%)
  local copies, waits for them, and re-layouts  2.88 us (2%)
  between operations  2.16 us (2%)
    ppermute x20, starting transfers between devices, local_permute(): return lax.ppermute(x, LOCAL, pairs)  39.2 us
    ppermute x20, waiting for transfers between devices, local_permute(): return lax.ppermute(x, LOCAL, pairs)  38.8 us
    pallas_call x11, Pallas kernels, call(): pl.pallas_call(kernel, out_shape=tuple(outs), in_specs=[SMEM] * len(scala...  36.3 us
    ppermute x3, waiting for transfers between devices, turn(): return lax.ppermute(x, axis, [(i, (i + step) % size) for i in range(size)])  5.38 us
    ppermute x2, waiting for transfers between devices, swap(): return lax.ppermute(x, axis, [(0, 1), (1, 0)])  4.83 us
    ppermute x3, starting transfers between devices, turn(): return lax.ppermute(x, axis, [(i, (i + step) % size) for i in range(size)])  4.45 us
  transfers between devices with their start and end apart: 25, of which 11 were waited for; matrix products, arithmetic and copies ran while one was open for 0% of the time, Pallas kernels for 19%

commit v1 on v0

--- a/solution.py
+++ b/solution.py
@@ -222,12 +222,12 @@
 
 
 def first_kernel(
-    info, weight, qd0, qd1, qd2, qd3, own,
+    info, weight, qd0, qd1, qd2, qd3, own_a, own_b,
     qt, q, upt, probs, shift, total, acc,
     k_s, v_s, vt_s, score_s,
 ):
     mine, quad, core, count = info[0], info[1], info[2], info[4]
-    load_keys(mine, 0, pieces(own), k_s, v_s)
+    load_keys(mine, 0, pieces(own_a, own_b), k_s, v_s)
     for d, qd in enumerate((qd0, qd1, qd2, qd3)):
         x = (mine ^ d) // 2
         row = block_of(mine ^ d, quad, core) * ROWS
@@ -246,13 +246,13 @@
 
 
 def side_kernel(
-    info, qt, left, right, shift0, total0, acc0,
+    info, qt, left_a, left_b, right_a, right_b, shift0, total0, acc0,
     probs, shift, total, acc,
     k_s, v_s, vt_s, score_s,
 ):
     mine, quad = info[0], info[1]
-    load_keys(mine, 0, pieces(left), k_s, v_s)
-    load_keys(mine, 1, pieces(right), k_s, v_s)
+    load_keys(mine, 0, pieces(left_a, left_b), k_s, v_s)
+    load_keys(mine, 1, pieces(right_a, right_b), k_s, v_s)
     forward(
         info, lambda g: (quad + 3 + 2 * g) & 3, 2, k_s, v_s, qt, (shift0, total0, acc0),
         score_s, probs, vt_s, shift, total, acc,
@@ -289,14 +289,14 @@
 
 def back_side_kernel(
     info, q, uplt, upl, delta, shift_then, shift_last, probs,
-    left, right, dqt0,
+    left_a, left_b, right_a, right_b, dqt0,
     dqt, out_l, out_r,
     k_s, v_s, kt_s, grad_s,
 ):
     mine = info[0]
     factors = [jnp.exp2(shift_then[x] - shift_last[x]) for x in range(2)]
-    load_keys(mine, 0, pieces(left), k_s, v_s)
-    load_keys(mine, 1, pieces(right), k_s, v_s)
+    load_keys(mine, 0, pieces(left_a, left_b), k_s, v_s)
+    load_keys(mine, 1, pieces(right_a, right_b), k_s, v_s)
     backward(
         2, k_s, v_s, kt_s, q, uplt, upl, delta, probs, factors, grad_s, dqt0, dqt
     )
@@ -305,13 +305,13 @@
 
 
 def back_own_kernel(
-    info, q, uplt, upl, delta, shift_then, shift_last, probs, own, dqt0, attn,
+    info, q, uplt, upl, delta, shift_then, shift_last, probs, own_a, own_b, dqt0, attn,
     out, od0, od1, od2, od3,
     k_s, v_s, kt_s, grad_s, dqt, dq_s,
 ):
     mine = info[0]
     factors = [jnp.exp2(shift_then[x] - shift_last[x]) for x in range(2)]
-    load_keys(mine, 0, pieces(own), k_s, v_s)
+    load_keys(mine, 0, pieces(own_a, own_b), k_s, v_s)
     backward(
         1, k_s, v_s, kt_s, q, uplt, upl, delta, probs, factors, grad_s, dqt0, dqt
     )
@@ -371,7 +371,7 @@
     return jax.ShapeDtypeStruct(shape, F32)
 
 
-def call(kernel, outs, scratch, scalars, *operands, copies=0):
+def call(kernel, outs, scratch, scalars, *operands, copies=0, products=0):
     place = pl.BlockSpec(memory_space=pl.ANY) if copies else VMEM
     scratch = [pltpu.VMEM(shape, dtype) for shape, dtype in scratch]
     if copies:
@@ -382,8 +382,12 @@
         in_specs=[SMEM] * len(scalars) + [place] * len(operands),
         out_specs=(VMEM,) * len(outs),
         scratch_shapes=scratch,
-        compiler_params=pltpu.CompilerParams(vmem_limit_bytes=(60 if copies else 32) * 2**20),
-        cost_estimate=pl.CostEstimate(flops=0, bytes_accessed=0, transcendentals=0),
+        compiler_params=pltpu.CompilerParams(vmem_limit_bytes=(56 if copies == 16 else 32) * 2**20),
+        cost_estimate=pl.CostEstimate(
+            flops=products * PROBS * LANES * HEAD_DIM * 4,
+            bytes_accessed=1_000_000,
+            transcendentals=0,
+        ),
     )(*scalars, *operands)
 
 
@@ -438,9 +442,10 @@
         kv[d] = partner(kv[d], d)
     for d in (1, 2, 3):
         qd[d] = partner(qd[d], d)
-    own = jnp.stack(kv)
-    left, right = quad_turn(own, 1), quad_turn(own, -1)
-    far_a, far_b = quad_turn(left[:2], 1), quad_turn(right[2:], -1)
+    own_a, own_b = jnp.stack(kv[:2]), jnp.stack(kv[2:])
+    left_a, right_b = quad_turn(own_a, 1), quad_turn(own_b, -1)
+    left_b, right_a = quad_turn(own_b, 1), quad_turn(own_a, -1)
+    far_a, far_b = quad_turn(left_a, 1), quad_turn(right_b, -1)
 
     tiles = (2, HEAD_DIM, LANES)
     line = f32(2, 1, LANES)
@@ -459,14 +464,16 @@
         (bf16(*tiles), bf16(2, LANES, HEAD_DIM), bf16(*tiles), bf16(1, PROBS, LANES), line, line, f32(*tiles)),
         forward_scratch(1),
         (info, weight),
-        *qd, own,
+        *qd, own_a, own_b,
+        products=2,
     )
     probs2, shift2, total2, acc2 = call(
         side_kernel,
         (bf16(2, PROBS, LANES), line, line, f32(*tiles)),
         forward_scratch(2),
         (info,),
-        qt, left, right, shift1, total1, acc1,
+        qt, left_a, left_b, right_a, right_b, shift1, total1, acc1,
+        products=4,
     )
     shift3, uplt, upl, delta, dqt, attn, far_ga, far_gb = call(
         far_kernel,
@@ -475,6 +482,7 @@
         + [((1, PROBS, LANES), BF16), grad_s, (tiles, F32), ((2, 1, LANES), F32)],
         (info,),
         qt, q, upt, far_a, far_b, shift2, total2, acc2,
+        products=6,
     )
     far_ga, far_gb = quad_turn(far_ga, 1), quad_turn(far_gb, -1)
     dqt, left_g, right_g = call(
@@ -483,7 +491,8 @@
         keys(2) + [turned, grad_s],
         (info,),
         q, uplt, upl, delta, shift2, shift3, probs2,
-        left, right, dqt,
+        left_a, left_b, right_a, right_b, dqt,
+        products=8,
     )
     left_g, right_g = call(add_kernel, (whole, whole), (), (), left_g, right_g, far_ga, far_gb)
     left_g, right_g = quad_turn(left_g, -1), quad_turn(right_g, 1)
@@ -492,7 +501,8 @@
         (whole,) + (bf16(ROWS, LANES),) * 4,
         keys(1) + [turned, grad_s, (tiles, F32), (tiles, BF16)],
         (info,),
-        q, uplt, upl, delta, shift1, shift3, probs1, own, dqt, attn,
+        q, uplt, upl, delta, shift1, shift3, probs1, own_a, own_b, dqt, attn,
+        products=4,
     )
     for d in (1, 2, 3):
         od[d] = partner(od[d], d)

time: 137 us -> 130 us (0.949)
  waiting for transfers between devices: 49 us -> 32.8 us
  starting transfers between devices: 45.1 us -> 55.6 us
  Pallas kernels: 36.3 us -> 34 us
    ppermute x20 -> x22, waiting for transfers between devices: 38.8 us -> 23.3 us  [local_permute(): return lax.ppermute(x, LOCAL, pairs)]
    ppermute x20 -> x22, starting transfers between devices: 39.2 us -> 48.6 us  [local_permute(): return lax.ppermute(x, LOCAL, pairs)]
    ppermute x2, starting transfers between devices: 1.42 us -> 3.91 us  [swap(): return lax.ppermute(x, axis, [(0, 1), (1, 0)])]
    pallas_call x11, Pallas kernels: 36.3 us -> 34 us  [call(): pl.pallas_call(kernel, out_shape=tuple(outs), in_specs=[SMEM] * len(scala...]
    ppermute x3, waiting for transfers between devices: 5.38 us -> 3.83 us  [turn(): return lax.ppermute(x, axis, [(i, (i + step) % size) for i in range(size)])]
    ppermute x3, starting transfers between devices: 4.45 us -> 3.04 us  [turn(): return lax.ppermute(x, axis, [(i, (i + step) % size) for i in range(size)])]
  transfers between devices with their start and end apart: 25 -> 27, of which waited for: 11 -> 10; matrix products, arithmetic and copies ran while one was open for 0% -> 1% of each run, Pallas kernels for 19% -> 18%
where the time goes in v1:
time: 130 us
  starting transfers between devices  55.6 us (43%)
  Pallas kernels  34 us (26%)
  waiting for transfers between devices  32.8 us (25%)
  local copies, waits for them, and re-layouts  4 us (3%)
  between operations  2.17 us (2%)
    ppermute x22, starting transfers between devices, local_permute(): return lax.ppermute(x, LOCAL, pairs)  48.6 us
    pallas_call x11, Pallas kernels, call(): pl.pallas_call(kernel, out_shape=tuple(outs), in_specs=[SMEM] * len(scala...  34 us
    ppermute x22, waiting for transfers between devices, local_permute(): return lax.ppermute(x, LOCAL, pairs)  23.3 us
    ppermute x2, waiting for transfers between devices, swap(): return lax.ppermute(x, axis, [(0, 1), (1, 0)])  5.69 us
    ppermute x2, starting transfers between devices, swap(): return lax.ppermute(x, axis, [(0, 1), (1, 0)])  3.91 us
    ppermute x3, waiting for transfers between devices, turn(): return lax.ppermute(x, axis, [(i, (i + step) % size) for i in range(size)])  3.83 us
    ppermute x3, starting transfers between devices, turn(): return lax.ppermute(x, axis, [(i, (i + step) % size) for i in range(size)])  3.04 us
    unnamed x6, local copies, waits for them, and re-layouts  2.71 us
  transfers between devices with their start and end apart: 27, of which 10 were waited for; matrix products, arithmetic and copies ran while one was open for 1% of the time, Pallas kernels for 18%

profile of v1, /device:TPU:1, one launch (start us, length us, event | category | flops | bytes accessed | tf_op | source)
XLA Modules:
  0.0 129.7 jit_solution(5630155862737053182)
XLA Ops:
  2.6 2.5 %shard_map.128 = (bf16[192,256]{1,0:T(8,128)(2,1)}, bf16[192,256]{1,0:T(8,128)(2,1)}, bf16[192,256]{1,0:T(8,128)(2,1)}, bf16[192,256]{1,0:T(8,128)(2,1)}) custom-call(s32[5]{0:T(128)} %stack.33.info, bf16[128,512]{1,0:T(8,128)(2,1)} %bitcast.17, bf16[128,512]{1,0:T(8,128)(2,1)} %bitcast.18, bf16[64,512]{1,0:T(8,128)(2,1)} %kp.1, bf16[64,512]{1,0:T(8,128)(2,1)} %vp.1), custom_call_target="tpu_custom_call" | custom-call | bytes 1000000 | tf_op jit(solution)/shard_map/pallas_call | solution.py:379
  5.1 3.7 %collective-permute-start.4 = (bf16[192,256]{1,0:T(8,128)(2,1)}, bf16[192,256]{1,0:T(8,128)(2,1)S(1)}, u32[]{:S(2)}, u32[]{:S(2)}) collective-permute-start(bf16[192,256]{1,0:T(8,128)(2,1)} %get-tuple-element.66), channel_id=1, source_target_pairs={{0,128},{1,129},{16,144},{17,145},{32,160},{33,161},{48,176},{49,1... | collective-permute-start | bytes 294920 | tf_op jit(solution)/shard_map/ppermute | solution.py:409
  8.7 5.5 %collective-permute-start.5 = (bf16[192,256]{1,0:T(8,128)(2,1)}, bf16[192,256]{1,0:T(8,128)(2,1)S(1)}, u32[]{:S(2)}, u32[]{:S(2)}) collective-permute-start(bf16[192,256]{1,0:T(8,128)(2,1)} %get-tuple-element.67), channel_id=1, source_target_pairs={{0,144},{1,241},{16,128},{17,161},{32,176},{33,145},{48,160},{49,1... | collective-permute-start | bytes 294920 | tf_op jit(solution)/shard_map/ppermute | solution.py:409
  17.9 2.8 %collective-permute-start.1 = (bf16[128,1024]{1,0:T(8,128)(2,1)S(1)}, bf16[128,1024]{1,0:T(8,128)(2,1)S(1)}, u32[]{:S(2)}, u32[]{:S(2)}) collective-permute-start(bf16[128,1024]{1,0:T(8,128)(2,1)S(1)} %get-tuple-element.62), channel_id=1, source_target_pairs={{0,128},{1,129},{16,144},{17,145},{32,160},{33,161},{48,176},{49,1... | collective-permute-start | bytes 786440 | tf_op jit(solution)/shard_map/ppermute | solution.py:409
  20.7 2.6 %collective-permute-start.3 = (bf16[192,256]{1,0:T(8,128)(2,1)}, bf16[192,256]{1,0:T(8,128)(2,1)S(1)}, u32[]{:S(2)}, u32[]{:S(2)}) collective-permute-start(bf16[192,256]{1,0:T(8,128)(2,1)} %get-tuple-element.65), channel_id=1, source_target_pairs={{0,16},{1,113},{16,0},{17,33},{32,48},{33,17},{48,32},{49,65},{64,... | collective-permute-start | bytes 294920 | tf_op jit(solution)/shard_map/ppermute | solution.py:409
  24.0 1.9 %collective-permute-done.3 = bf16[192,256]{1,0:T(8,128)(2,1)S(1)} collective-permute-done((bf16[192,256]{1,0:T(8,128)(2,1)}, bf16[192,256]{1,0:T(8,128)(2,1)S(1)}, u32[]{:S(2)}, u32[]{:S(2)}) %collective-permute-start.3) | collective-permute-done | bytes 98336 | tf_op jit(solution)/shard_map/ppermute | solution.py:409
  26.9 4.2 %collective-permute-start.10 = (bf16[2,192,256]{2,1,0:T(8,128)(2,1)S(1)}, bf16[2,192,256]{2,1,0:T(8,128)(2,1)S(1)}, u32[]{:S(2)}, u32[]{:S(2)}) collective-permute-start(bf16[2,192,256]{2,1,0:T(8,128)(2,1)S(1)} %pad_maximum_fusion.1.own_b), channel_id=1, source_target_pairs={{0,32},{1,33},{16,48},{17,49},{32,64},{33,65},{48,80},{49,81},{64,... | collective-permute-start | bytes 589832 | tf_op jit(solution)/shard_map/ppermute | solution.py:409
  31.1 1.5 %collective-permute-done.1.qd2 = bf16[128,1024]{1,0:T(8,128)(2,1)S(1)} collective-permute-done((bf16[128,1024]{1,0:T(8,128)(2,1)S(1)}, bf16[128,1024]{1,0:T(8,128)(2,1)S(1)}, u32[]{:S(2)}, u32[]{:S(2)}) %collective-permute-start.1) | collective-permute-done | bytes 262176 | tf_op jit(solution)/shard_map/ppermute | solution.py:409
  32.7 3.4 %shard_map.129 = (bf16[2,128,1024]{2,1,0:T(8,128)(2,1)S(1)}, bf16[2,1024,128]{2,1,0:T(8,128)(2,1)S(1)}, bf16[2,128,1024]{2,1,0:T(8,128)(2,1)S(1)}, bf16[1,1280,1...) custom-call(s32[5]{0:T(128)S(1)} %copy-done.2, ...), custom_call_target="tpu_custom_call" | custom-call | flops 1342177280 | bytes 1000000 | tf_op jit(solution)/shard_map/pallas_call | solution.py:379
  36.1 1.3 collective-permute-done.8.right_b
  37.4 4.8 %collective-permute-start.9 = (bf16[2,192,256]{2,1,0:T(8,128)(2,1)S(1)}, bf16[2,192,256]{2,1,0:T(8,128)(2,1)S(1)}, u32[]{:S(2)}, u32[]{:S(2)}) collective-permute-start(bf16[2,192,256]{2,1,0:T(8,128)(2,1)S(1)} %collective-permute-done.8.right_b), channel_id=1, source_target_pairs={{0,96},{1,97},{16,112},{17,113},{32,0},{33,1},{48,16},{49,17},{64,... | collective-permute-start | bytes 589832 | tf_op jit(solution)/shard_map/ppermute | solution.py:409
  42.2 9.1 %collective-permute-done.10.left_b = bf16[2,192,256]{2,1,0:T(8,128)(2,1)S(1)} collective-permute-done((bf16[2,192,256]{2,1,0:T(8,128)(2,1)S(1)}, bf16[2,192,256]{2,1,0:T(8,128)(2,1)S(1)}, u32[]{:S(2)}, u32[]{:S(2)}) %collective-permute-start.10) | collective-permute-done | bytes 196640 | tf_op jit(solution)/shard_map/ppermute | solution.py:409
  51.3 5.7 %shard_map.130 = (bf16[2,1280,1024]{2,1,0:T(8,128)(2,1)S(1)}, f32[2,1,1024]{2,1,0:T(1,128)S(1)}, f32[2,1,1024]{2,1,0:T(1,128)S(1)}, f32[2,128,1024]{2,1,0:T(8,128)S(1)}) custom-call(s32[5]{0:T(128)S(1)} %copy-done.2, bf16[2,128,1024]{2,1,0:T(8,128)(2,1)S(1)} %get-tuple-element.69.qt, bf16[2,192,256]{2,1,0:T(8,128)(2,1)S(1)} %collective-permute-done.6.left_a, ...), custom_call_target="tpu_custom_call" | custom-call | flops 2684354560 | bytes 1000000 | tf_op jit(solution)/shard_map/pallas_call | solution.py:379
  57.0 6.4 %shard_map.131 = (f32[2,1,1024]{2,1,0:T(1,128)S(1)}, bf16[2,128,1024]{2,1,0:T(8,128)(2,1)S(1)}, bf16[2,1024,128]{2,1,0:T(8,128)(2,1)S(1)}, f32[2,1,1024]{2,1,0:T...) custom-call(s32[5]{0:T(128)S(1)} %copy-done.2, ...), custom_call_target="tpu_custom_call" | custom-call | flops 4026531840 | bytes 1000000 | tf_op jit(solution)/shard_map/pallas_call | solution.py:379
  63.5 3.6 %collective-permute-start.13 = (bf16[2,192,256]{2,1,0:T(8,128)(2,1)S(1)}, bf16[2,192,256]{2,1,0:T(8,128)(2,1)S(1)}, u32[]{:S(2)}, u32[]{:S(2)}) collective-permute-start(bf16[2,192,256]{2,1,0:T(8,128)(2,1)S(1)} %get-tuple-element.90), channel_id=1, source_target_pairs={{0,96},{1,97},{16,112},{17,113},{32,0},{33,1},{48,16},{49,17},{64,... | collective-permute-start | bytes 589832 | tf_op jit(solution)/shard_map/ppermute | solution.py:409
  67.1 7.7 %shard_map.132 = (f32[2,128,1024]{2,1,0:T(8,128)S(1)}, bf16[4,192,256]{2,1,0:T(8,128)(2,1)S(1)}, bf16[4,192,256]{2,1,0:T(8,128)(2,1)S(1)}) custom-call(s32[5]{0:T(128)S(1)} %copy-done.2, bf16[2,1024,128]{2,1,0:T(8,128)(2,1)S(1)} %get-tuple-element.68.q, bf16[2,128,1024]{2,1,0:T(8,128)(2,1)S(1)} %get-tuple-element.77.uplt, ...), custom_call_target="tpu_custom_call" | custom-call | flops 5368709120 | bytes 1000000 | tf_op jit(solution)/shard_map/pallas_call | solution.py:379
  75.3 2.0 %collective-permute-start.15 = (bf16[4,192,256]{2,1,0:T(8,128)(2,1)S(1)}, bf16[4,192,256]{2,1,0:T(8,128)(2,1)S(1)}, u32[]{:S(2)}, u32[]{:S(2)}) collective-permute-start(bf16[4,192,256]{2,1,0:T(8,128)(2,1)S(1)} %get-tuple-element.92), channel_id=1, source_target_pairs={{0,32},{1,33},{16,48},{17,49},{32,64},{33,65},{48,80},{49,81},{64,... | collective-permute-start | bytes 1179656 | tf_op jit(solution)/shard_map/ppermute | solution.py:409
  77.3 4.4 %shard_map.133 = (bf16[4,192,256]{2,1,0:T(8,128)(2,1)S(1)}, bf16[128,1024]{1,0:T(8,128)(2,1)S(1)}, bf16[128,1024]{1,0:T(8,128)(2,1)S(1)}, bf16[128,1024]{1,0:T(8,128)(2,1)S(1)}, bf16[128,1024]{1,0:T(8,128)(2,1)S(1)}) custom-call(s32[5]{0:T(128)S(1)} %copy-done.2, bf16[2,1024,128]{2,1,0:T(8,128)(2,1)S(1)} %get-tuple-element.68.q, ...), custom_call_target="tpu_custom_call" | custom-call | flops 2684354560 | bytes 1000000 | tf_op jit(solution)/shard_map/pallas_call | solution.py:379
  82.6 5.0 %collective-permute-start.20 = (bf16[128,1024]{1,0:T(8,128)(2,1)S(1)}, bf16[128,1024]{1,0:T(8,128)(2,1)S(1)}, u32[]{:S(2)}, u32[]{:S(2)}) collective-permute-start(bf16[128,1024]{1,0:T(8,128)(2,1)S(1)} %get-tuple-element.99), channel_id=1, source_target_pairs={{0,128},{1,129},{16,144},{17,145},{32,160},{33,161},{48,176},{49,1... | collective-permute-start | bytes 786440 | tf_op jit(solution)/shard_map/ppermute | solution.py:409
  87.6 1.4 %collective-permute-start.21 = (bf16[128,1024]{1,0:T(8,128)(2,1)S(1)}, bf16[128,1024]{1,0:T(8,128)(2,1)S(1)}, u32[]{:S(2)}, u32[]{:S(2)}) collective-permute-start(bf16[128,1024]{1,0:T(8,128)(2,1)S(1)} %get-tuple-element.100), channel_id=1, source_target_pairs={{0,144},{1,241},{16,128},{17,161},{32,176},{33,145},{48,160},{49,1... | collective-permute-start | bytes 786440 | tf_op jit(solution)/shard_map/ppermute | solution.py:409
  89.0 3.5 %collective-permute-done.14.left = bf16[4,192,256]{2,1,0:T(8,128)(2,1)S(1)} collective-permute-done((bf16[4,192,256]{2,1,0:T(8,128)(2,1)S(1)}, bf16[4,192,256]{2,1,0:T(8,128)(2,1)S(1)}, u32[]{:S(2)}, u32[]{:S(2)}) %collective-permute-start.14) | collective-permute-done | bytes 393248 | tf_op jit(solution)/shard_map/ppermute | solution.py:409
  92.7 7.8 %collective-permute-start.17 = (bf16[192,256]{1,0:T(8,128)(2,1)S(1)}, bf16[192,256]{1,0:T(8,128)(2,1)S(1)}, u32[]{:S(2)}, u32[]{:S(2)}) collective-permute-start(bf16[192,256]{1,0:T(8,128)(2,1)S(1)} %get-tuple-element.95), channel_id=1, source_target_pairs={{0,128},{1,129},{16,144},{17,145},{32,160},{33,161},{48,176},{49,1... | collective-permute-start | bytes 294920 | tf_op jit(solution)/shard_map/ppermute | solution.py:409
  100.6 2.9 %collective-permute-start.18 = (bf16[192,256]{1,0:T(8,128)(2,1)S(1)}, bf16[192,256]{1,0:T(8,128)(2,1)S(1)}, u32[]{:S(2)}, u32[]{:S(2)}) collective-permute-start(bf16[192,256]{1,0:T(8,128)(2,1)S(1)} %get-tuple-element.96), channel_id=1, source_target_pairs={{0,144},{1,241},{16,128},{17,161},{32,176},{33,145},{48,160},{49,1... | collective-permute-start | bytes 294920 | tf_op jit(solution)/shard_map/ppermute | solution.py:409
  103.5 3.2 %collective-permute-done.21.od3 = bf16[128,1024]{1,0:T(8,128)(2,1)S(1)} collective-permute-done((bf16[128,1024]{1,0:T(8,128)(2,1)S(1)}, bf16[128,1024]{1,0:T(8,128)(2,1)S(1)}, u32[]{:S(2)}, u32[]{:S(2)}) %collective-permute-start.21) | collective-permute-done | bytes 262176 | tf_op jit(solution)/shard_map/ppermute | solution.py:409
  106.7 2.8 %collective-permute-done.17.g2 = bf16[192,256]{1,0:T(8,128)(2,1)S(1)} collective-permute-done((bf16[192,256]{1,0:T(8,128)(2,1)S(1)}, bf16[192,256]{1,0:T(8,128)(2,1)S(1)}, u32[]{:S(2)}, u32[]{:S(2)}) %collective-permute-start.17) | collective-permute-done | bytes 98336 | tf_op jit(solution)/shard_map/ppermute | solution.py:409
  109.5 1.3 %shard_map.137 = (bf16[128,512]{1,0:T(8,128)(2,1)}, bf16[128,512]{1,0:T(8,128)(2,1)}, bf16[64,1024]{1,0:T(8,128)(2,1)S(1)}) custom-call(s32[5]{0:T(128)S(1)} %copy-done.2, bf16[192,256]{1,0:T(8,128)(2,1)S(1)} %get-tuple-element.107.g0, bf16[192,256]{1,0:T(8,128)(2,1)S(1)} %collective-permute-done.16.g1, bf16[192,256]{1,0:T(8,128)(2,1)S(1)} %collective-permute-done.17.g2, ...), custom_call_target="tpu_custom_call" | custom-call | bytes 1000000 | tf_op jit(solution)/shard_map/pallas_call | solution.py:379
  110.8 3.8 %collective-permute-start.22 = (bf16[64,1024]{1,0:T(8,128)(2,1)S(1)}, bf16[64,1024]{1,0:T(8,128)(2,1)S(1)}, u32[]{:S(2)}, u32[]{:S(2)}) collective-permute-start(bf16[64,1024]{1,0:T(8,128)(2,1)S(1)} %get-tuple-element.113), channel_id=1, source_target_pairs={{0,1},{1,0},{2,3},{3,2},{4,5},{5,4},{6,7},{7,6},{8,9},{9,8},{10,11... | collective-permute-start | bytes 393224 | tf_op jit(solution)/shard_map/ppermute | solution.py:395
  115.7 4.7 %collective-permute-done.23 = bf16[64,1024]{1,0:T(8,128)(2,1)S(1)} collective-permute-done((bf16[64,1024]{1,0:T(8,128)(2,1)S(1)}, bf16[64,1024]{1,0:T(8,128)(2,1)S(1)}, u32[]{:S(2)}, u32[]{:S(2)}) %collective-permute-start.23) | collective-permute-done | bytes 131104 | tf_op jit(solution)/shard_map/ppermute | solution.py:395
  120.5 1.4 %collective-permute-start.26 = (bf16[64,1024]{1,0:T(8,128)(2,1)S(1)}, bf16[64,1024]{1,0:T(8,128)(2,1)S(1)}, u32[]{:S(2)}, u32[]{:S(2)}) collective-permute-start(bf16[64,1024]{1,0:T(8,128)(2,1)S(1)} %add_convert_fusion.1), channel_id=1, source_target_pairs={{0,12},{4,0},{8,4},{12,8},{1,13},{5,1},{9,5},{13,9},{2,14},{6,2},{... | collective-permute-start | bytes 393224 | tf_op jit(solution)/shard_map/ppermute | solution.py:400
  122.0 1.5 %collective-permute-start.24 = (bf16[64,1024]{1,0:T(8,128)(2,1)S(1)}, bf16[64,1024]{1,0:T(8,128)(2,1)S(1)}, u32[]{:S(2)}, u32[]{:S(2)}) collective-permute-start(bf16[64,1024]{1,0:T(8,128)(2,1)S(1)} %add_convert_fusion.1), channel_id=1, source_target_pairs={{0,8},{4,12},{8,0},{12,4},{1,9},{5,13},{9,1},{13,5},{2,10},{6,14},... | collective-permute-start | bytes 393224 | tf_op jit(solution)/shard_map/ppermute | solution.py:400
  123.5 1.6 %shard_map.136 = (bf16[128,2048]{1,0:T(8,128)(2,1)}, bf16[128,2048]{1,0:T(8,128)(2,1)}) custom-call(s32[5]{0:T(128)S(1)} %copy-done.2, bf16[128,1024]{1,0:T(8,128)(2,1)S(1)} %get-tuple-element.101.od0, bf16[128,1024]{1,0:T(8,128)(2,1)S(1)} %collective-permute-done.19.od1, bf16[128,1024]{1,0:T(8,128)(2,1)S(1)} %collective-permute-done.20.od2, ...), custom_call_target="tpu_custom_call" | custom-call | bytes 1000000 | tf_op jit(solution)/shard_map/pallas_call | solution.py:379
  125.1 3.8 %collective-permute-done.25 = bf16[64,1024]{1,0:T(8,128)(2,1)S(1)} collective-permute-done((bf16[64,1024]{1,0:T(8,128)(2,1)S(1)}, bf16[64,1024]{1,0:T(8,128)(2,1)S(1)}, u32[]{:S(2)}, u32[]{:S(2)}) %collective-permute-start.25) | collective-permute-done | bytes 131104 | tf_op jit(solution)/shard_map/ppermute | solution.py:400
  (46 shorter events, 9.8 us)
Async XLA Ops:
  5.1 18.2 %collective-permute-start.4 = (bf16[192,256]{1,0:T(8,128)(2,1)}, bf16[192,256]{1,0:T(8,128)(2,1)S(1)}, u32[]{:S(2)}, u32[]{:S(2)}) collective-permute-start(bf16[192,256]{1,0:T(8,128)(2,1)} %get-tuple-element.66), channel_id=1, source_target_pairs={{0,128},{1,129},{16,144},{17,145},{32,160},{33,161},{48,176},{49,1... | collective-permute-start | bytes 294920 | tf_op jit(solution)/shard_map/ppermute | solution.py:409
  8.7 14.6 %collective-permute-start.5 = (bf16[192,256]{1,0:T(8,128)(2,1)}, bf16[192,256]{1,0:T(8,128)(2,1)S(1)}, u32[]{:S(2)}, u32[]{:S(2)}) collective-permute-start(bf16[192,256]{1,0:T(8,128)(2,1)} %get-tuple-element.67), channel_id=1, source_target_pairs={{0,144},{1,241},{16,128},{17,161},{32,176},{33,145},{48,160},{49,1... | collective-permute-start | bytes 294920 | tf_op jit(solution)/shard_map/ppermute | solution.py:409
  14.3 1.0 copy-start
  15.3 1.0 copy-start.1
  16.3 0.6 copy-start.2
  17.8 9.1 %collective-permute-start = (bf16[128,1024]{1,0:T(8,128)(2,1)S(1)}, bf16[128,1024]{1,0:T(8,128)(2,1)S(1)}, u32[]{:S(2)}, u32[]{:S(2)}) collective-permute-start(bf16[128,1024]{1,0:T(8,128)(2,1)S(1)} %get-tuple-element.61), channel_id=1, source_target_pairs={{0,16},{1,113},{16,0},{17,33},{32,48},{33,17},{48,32},{49,65},{64,... | collective-permute-start | bytes 786440 | tf_op jit(solution)/shard_map/ppermute | solution.py:409
  17.9 14.7 %collective-permute-start.1 = (bf16[128,1024]{1,0:T(8,128)(2,1)S(1)}, bf16[128,1024]{1,0:T(8,128)(2,1)S(1)}, u32[]{:S(2)}, u32[]{:S(2)}) collective-permute-start(bf16[128,1024]{1,0:T(8,128)(2,1)S(1)} %get-tuple-element.62), channel_id=1, source_target_pairs={{0,128},{1,129},{16,144},{17,145},{32,160},{33,161},{48,176},{49,1... | collective-permute-start | bytes 786440 | tf_op jit(solution)/shard_map/ppermute | solution.py:409
  20.7 5.2 %collective-permute-start.3 = (bf16[192,256]{1,0:T(8,128)(2,1)}, bf16[192,256]{1,0:T(8,128)(2,1)S(1)}, u32[]{:S(2)}, u32[]{:S(2)}) collective-permute-start(bf16[192,256]{1,0:T(8,128)(2,1)} %get-tuple-element.65), channel_id=1, source_target_pairs={{0,16},{1,113},{16,0},{17,33},{32,48},{33,17},{48,32},{49,65},{64,... | collective-permute-start | bytes 294920 | tf_op jit(solution)/shard_map/ppermute | solution.py:409
  23.3 9.4 %collective-permute-start.2 = (bf16[128,1024]{1,0:T(8,128)(2,1)S(1)}, bf16[128,1024]{1,0:T(8,128)(2,1)S(1)}, u32[]{:S(2)}, u32[]{:S(2)}) collective-permute-start(bf16[128,1024]{1,0:T(8,128)(2,1)S(1)} %get-tuple-element.63), channel_id=1, source_target_pairs={{0,144},{1,241},{16,128},{17,161},{32,176},{33,145},{48,160},{49,1... | collective-permute-start | bytes 786440 | tf_op jit(solution)/shard_map/ppermute | solution.py:409
  23.3 14.0 %collective-permute-start.8 = (bf16[2,192,256]{2,1,0:T(8,128)(2,1)S(1)}, bf16[2,192,256]{2,1,0:T(8,128)(2,1)S(1)}, u32[]{:S(2)}, u32[]{:S(2)}) collective-permute-start(bf16[2,192,256]{2,1,0:T(8,128)(2,1)S(1)} %pad_maximum_fusion.1.own_b), channel_id=1, source_target_pairs={{0,96},{1,97},{16,112},{17,113},{32,0},{33,1},{48,16},{49,17},{64,... | collective-permute-start | bytes 589832 | tf_op jit(solution)/shard_map/ppermute | solution.py:409
  26.8 15.4 %collective-permute-start.6 = (bf16[2,192,256]{2,1,0:T(8,128)(2,1)S(1)}, bf16[2,192,256]{2,1,0:T(8,128)(2,1)S(1)}, u32[]{:S(2)}, u32[]{:S(2)}) collective-permute-start(bf16[2,192,256]{2,1,0:T(8,128)(2,1)S(1)} %pad_maximum_fusion.own_a), channel_id=1, source_target_pairs={{0,32},{1,33},{16,48},{17,49},{32,64},{33,65},{48,80},{49,81},{64,... | collective-permute-start | bytes 589832 | tf_op jit(solution)/shard_map/ppermute | solution.py:409
  26.9 24.4 %collective-permute-start.10 = (bf16[2,192,256]{2,1,0:T(8,128)(2,1)S(1)}, bf16[2,192,256]{2,1,0:T(8,128)(2,1)S(1)}, u32[]{:S(2)}, u32[]{:S(2)}) collective-permute-start(bf16[2,192,256]{2,1,0:T(8,128)(2,1)S(1)} %pad_maximum_fusion.1.own_b), channel_id=1, source_target_pairs={{0,32},{1,33},{16,48},{17,49},{32,64},{33,65},{48,80},{49,81},{64,... | collective-permute-start | bytes 589832 | tf_op jit(solution)/shard_map/ppermute | solution.py:409
  32.6 18.7 %collective-permute-start.11 = (bf16[2,192,256]{2,1,0:T(8,128)(2,1)S(1)}, bf16[2,192,256]{2,1,0:T(8,128)(2,1)S(1)}, u32[]{:S(2)}, u32[]{:S(2)}) collective-permute-start(bf16[2,192,256]{2,1,0:T(8,128)(2,1)S(1)} %pad_maximum_fusion.own_a), channel_id=1, source_target_pairs={{0,96},{1,97},{16,112},{17,113},{32,0},{33,1},{48,16},{49,17},{64,... | collective-permute-start | bytes 589832 | tf_op jit(solution)/shard_map/ppermute | solution.py:409
  37.4 19.6 %collective-permute-start.9 = (bf16[2,192,256]{2,1,0:T(8,128)(2,1)S(1)}, bf16[2,192,256]{2,1,0:T(8,128)(2,1)S(1)}, u32[]{:S(2)}, u32[]{:S(2)}) collective-permute-start(bf16[2,192,256]{2,1,0:T(8,128)(2,1)S(1)} %collective-permute-done.8.right_b), channel_id=1, source_target_pairs={{0,96},{1,97},{16,112},{17,113},{32,0},{33,1},{48,16},{49,17},{64,... | collective-permute-start | bytes 589832 | tf_op jit(solution)/shard_map/ppermute | solution.py:409
  42.2 14.8 %collective-permute-start.7 = (bf16[2,192,256]{2,1,0:T(8,128)(2,1)S(1)}, bf16[2,192,256]{2,1,0:T(8,128)(2,1)S(1)}, u32[]{:S(2)}, u32[]{:S(2)}) collective-permute-start(bf16[2,192,256]{2,1,0:T(8,128)(2,1)S(1)} %collective-permute-done.6.left_a), channel_id=1, source_target_pairs={{0,32},{1,33},{16,48},{17,49},{32,64},{33,65},{48,80},{49,81},{64,... | collective-permute-start | bytes 589832 | tf_op jit(solution)/shard_map/ppermute | solution.py:409
  63.4 11.4 %collective-permute-start.12 = (bf16[2,192,256]{2,1,0:T(8,128)(2,1)S(1)}, bf16[2,192,256]{2,1,0:T(8,128)(2,1)S(1)}, u32[]{:S(2)}, u32[]{:S(2)}) collective-permute-start(bf16[2,192,256]{2,1,0:T(8,128)(2,1)S(1)} %get-tuple-element.89), channel_id=1, source_target_pairs={{0,32},{1,33},{16,48},{17,49},{32,64},{33,65},{48,80},{49,81},{64,... | collective-permute-start | bytes 589832 | tf_op jit(solution)/shard_map/ppermute | solution.py:409
  63.5 11.3 %collective-permute-start.13 = (bf16[2,192,256]{2,1,0:T(8,128)(2,1)S(1)}, bf16[2,192,256]{2,1,0:T(8,128)(2,1)S(1)}, u32[]{:S(2)}, u32[]{:S(2)}) collective-permute-start(bf16[2,192,256]{2,1,0:T(8,128)(2,1)S(1)} %get-tuple-element.90), channel_id=1, source_target_pairs={{0,96},{1,97},{16,112},{17,113},{32,0},{33,1},{48,16},{49,17},{64,... | collective-permute-start | bytes 589832 | tf_op jit(solution)/shard_map/ppermute | solution.py:409
  74.9 17.6 %collective-permute-start.14 = (bf16[4,192,256]{2,1,0:T(8,128)(2,1)S(1)}, bf16[4,192,256]{2,1,0:T(8,128)(2,1)S(1)}, u32[]{:S(2)}, u32[]{:S(2)}) collective-permute-start(bf16[4,192,256]{2,1,0:T(8,128)(2,1)S(1)} %get-tuple-element.91), channel_id=1, source_target_pairs={{0,96},{1,97},{16,112},{17,113},{32,0},{33,1},{48,16},{49,17},{64,... | collective-permute-start | bytes 1179656 | tf_op jit(solution)/shard_map/ppermute | solution.py:409
  75.3 17.2 %collective-permute-start.15 = (bf16[4,192,256]{2,1,0:T(8,128)(2,1)S(1)}, bf16[4,192,256]{2,1,0:T(8,128)(2,1)S(1)}, u32[]{:S(2)}, u32[]{:S(2)}) collective-permute-start(bf16[4,192,256]{2,1,0:T(8,128)(2,1)S(1)} %get-tuple-element.92), channel_id=1, source_target_pairs={{0,32},{1,33},{16,48},{17,49},{32,64},{33,65},{48,80},{49,81},{64,... | collective-permute-start | bytes 1179656 | tf_op jit(solution)/shard_map/ppermute | solution.py:409
  81.7 18.8 %collective-permute-start.19 = (bf16[128,1024]{1,0:T(8,128)(2,1)S(1)}, bf16[128,1024]{1,0:T(8,128)(2,1)S(1)}, u32[]{:S(2)}, u32[]{:S(2)}) collective-permute-start(bf16[128,1024]{1,0:T(8,128)(2,1)S(1)} %get-tuple-element.98), channel_id=1, source_target_pairs={{0,16},{1,113},{16,0},{17,33},{32,48},{33,17},{48,32},{49,65},{64,... | collective-permute-start | bytes 786440 | tf_op jit(solution)/shard_map/ppermute | solution.py:409
  82.6 20.9 %collective-permute-start.20 = (bf16[128,1024]{1,0:T(8,128)(2,1)S(1)}, bf16[128,1024]{1,0:T(8,128)(2,1)S(1)}, u32[]{:S(2)}, u32[]{:S(2)}) collective-permute-start(bf16[128,1024]{1,0:T(8,128)(2,1)S(1)} %get-tuple-element.99), channel_id=1, source_target_pairs={{0,128},{1,129},{16,144},{17,145},{32,160},{33,161},{48,176},{49,1... | collective-permute-start | bytes 786440 | tf_op jit(solution)/shard_map/ppermute | solution.py:409
  87.6 19.1 %collective-permute-start.21 = (bf16[128,1024]{1,0:T(8,128)(2,1)S(1)}, bf16[128,1024]{1,0:T(8,128)(2,1)S(1)}, u32[]{:S(2)}, u32[]{:S(2)}) collective-permute-start(bf16[128,1024]{1,0:T(8,128)(2,1)S(1)} %get-tuple-element.100), channel_id=1, source_target_pairs={{0,144},{1,241},{16,128},{17,161},{32,176},{33,145},{48,160},{49,1... | collective-permute-start | bytes 786440 | tf_op jit(solution)/shard_map/ppermute | solution.py:409
  92.6 14.1 %collective-permute-start.16 = (bf16[192,256]{1,0:T(8,128)(2,1)S(1)}, bf16[192,256]{1,0:T(8,128)(2,1)S(1)}, u32[]{:S(2)}, u32[]{:S(2)}) collective-permute-start(bf16[192,256]{1,0:T(8,128)(2,1)S(1)} %get-tuple-element.94), channel_id=1, source_target_pairs={{0,16},{1,113},{16,0},{17,33},{32,48},{33,17},{48,32},{49,65},{64,... | collective-permute-start | bytes 294920 | tf_op jit(solution)/shard_map/ppermute | solution.py:409
  92.7 16.7 %collective-permute-start.17 = (bf16[192,256]{1,0:T(8,128)(2,1)S(1)}, bf16[192,256]{1,0:T(8,128)(2,1)S(1)}, u32[]{:S(2)}, u32[]{:S(2)}) collective-permute-start(bf16[192,256]{1,0:T(8,128)(2,1)S(1)} %get-tuple-element.95), channel_id=1, source_target_pairs={{0,128},{1,129},{16,144},{17,145},{32,160},{33,161},{48,176},{49,1... | collective-permute-start | bytes 294920 | tf_op jit(solution)/shard_map/ppermute | solution.py:409
  100.6 8.9 %collective-permute-start.18 = (bf16[192,256]{1,0:T(8,128)(2,1)S(1)}, bf16[192,256]{1,0:T(8,128)(2,1)S(1)}, u32[]{:S(2)}, u32[]{:S(2)}) collective-permute-start(bf16[192,256]{1,0:T(8,128)(2,1)S(1)} %get-tuple-element.96), channel_id=1, source_target_pairs={{0,144},{1,241},{16,128},{17,161},{32,176},{33,145},{48,160},{49,1... | collective-permute-start | bytes 294920 | tf_op jit(solution)/shard_map/ppermute | solution.py:409
  110.8 4.8 %collective-permute-start.22 = (bf16[64,1024]{1,0:T(8,128)(2,1)S(1)}, bf16[64,1024]{1,0:T(8,128)(2,1)S(1)}, u32[]{:S(2)}, u32[]{:S(2)}) collective-permute-start(bf16[64,1024]{1,0:T(8,128)(2,1)S(1)} %get-tuple-element.113), channel_id=1, source_target_pairs={{0,1},{1,0},{2,3},{3,2},{4,5},{5,4},{6,7},{7,6},{8,9},{9,8},{10,11... | collective-permute-start | bytes 393224 | tf_op jit(solution)/shard_map/ppermute | solution.py:395
  115.6 4.8 %collective-permute-start.23 = (bf16[64,1024]{1,0:T(8,128)(2,1)S(1)}, bf16[64,1024]{1,0:T(8,128)(2,1)S(1)}, u32[]{:S(2)}, u32[]{:S(2)}) collective-permute-start(bf16[64,1024]{1,0:T(8,128)(2,1)S(1)} %add_convert_fusion.2), channel_id=1, source_target_pairs={{0,2},{2,0},{1,3},{3,1},{4,6},{6,4},{5,7},{7,5},{8,10},{10,8},{9,1... | collective-permute-start | bytes 393224 | tf_op jit(solution)/shard_map/ppermute | solution.py:395
  120.5 4.6 %collective-permute-start.26 = (bf16[64,1024]{1,0:T(8,128)(2,1)S(1)}, bf16[64,1024]{1,0:T(8,128)(2,1)S(1)}, u32[]{:S(2)}, u32[]{:S(2)}) collective-permute-start(bf16[64,1024]{1,0:T(8,128)(2,1)S(1)} %add_convert_fusion.1), channel_id=1, source_target_pairs={{0,12},{4,0},{8,4},{12,8},{1,13},{5,1},{9,5},{13,9},{2,14},{6,2},{... | collective-permute-start | bytes 393224 | tf_op jit(solution)/shard_map/ppermute | solution.py:400
  121.9 7.1 %collective-permute-start.25 = (bf16[64,1024]{1,0:T(8,128)(2,1)S(1)}, bf16[64,1024]{1,0:T(8,128)(2,1)S(1)}, u32[]{:S(2)}, u32[]{:S(2)}) collective-permute-start(bf16[64,1024]{1,0:T(8,128)(2,1)S(1)} %add_convert_fusion.1), channel_id=1, source_target_pairs={{0,4},{4,8},{8,12},{12,0},{1,5},{5,9},{9,13},{13,1},{2,6},{6,10},{... | collective-permute-start | bytes 393224 | tf_op jit(solution)/shard_map/ppermute | solution.py:400
  122.0 6.9 %collective-permute-start.24 = (bf16[64,1024]{1,0:T(8,128)(2,1)S(1)}, bf16[64,1024]{1,0:T(8,128)(2,1)S(1)}, u32[]{:S(2)}, u32[]{:S(2)}) collective-permute-start(bf16[64,1024]{1,0:T(8,128)(2,1)S(1)} %add_convert_fusion.1), channel_id=1, source_target_pairs={{0,8},{4,12},{8,0},{12,4},{1,9},{5,13},{9,1},{13,5},{2,10},{6,14},... | collective-permute-start | bytes 393224 | tf_op jit(solution)/shard_map/ppermute | solution.py:400

commit v2 on v1

v2 whole, which is shorter than its diff:
```python
import math

import jax
import jax.numpy as jnp
from jax import lax
from jax.experimental import pallas as pl
from jax.experimental.pallas import tpu as pltpu
from jax.sharding import Mesh
from jax.sharding import PartitionSpec as P

HEADS = 16
KV_HEADS = 4
HEAD_DIM = 128
GROUP = HEADS // KV_HEADS
RESP_LEN = 2048
PROMPT_LEN = 1024
CTX = ("xh", "z")
LOCAL = ("xh", "z", "core")
RESP = ("y", "xl", "core")
ROWS = 128
PROWS = 64
BOTH = ROWS + PROWS
CHUNK = 256
SPAN = 3 * CHUNK
TILE_SPANS = (2 * CHUNK, 3 * CHUNK)
TILE_STARTS = (0, 2 * CHUNK)
PROBS = 5 * CHUNK
HALF = GROUP * ROWS
LANES = 2 * HALF
WIDE = 2 * HEAD_DIM
SCALE = HEAD_DIM**-0.5
SCALE2 = SCALE * math.log2(math.e)
NEG = -1e30
F32 = jnp.float32
BF16 = jnp.bfloat16
VMEM = pl.BlockSpec(memory_space=pltpu.VMEM)
SMEM = pl.BlockSpec(memory_space=pltpu.SMEM)


def dot(a, b):
    return jnp.dot(a, b, preferred_element_type=F32)


def head_at(h, width=HEAD_DIM):
    return slice(h * width, (h + 1) * width)


def lanes_at(j, h):
    return slice(j * HALF + h * HEAD_DIM, j * HALF + (h + 1) * HEAD_DIM)


def block_of(member, quad, core):
    return (member // 2) * 8 + ((quad * 2 + (member & 1) + core) & 7)


def run_copies(pairs, sems):
    copies = [
        pltpu.make_async_copy(source, to, sems.at[i]) for i, (source, to) in enumerate(pairs)
    ]
    for copy in copies:
        copy.start()
    for copy in copies:
        copy.wait()


def pack_kv_kernel(k, v, kp, vp, kv, k_s, v_s, kp_s, vp_s, sems):
    run_copies(((k, k_s), (v, v_s), (kp, kp_s), (vp, vp_s)), sems)
    for m in range(4):
        kv[m, :ROWS, :HEAD_DIM] = k_s[:, head_at(m)]
        kv[m, :ROWS, HEAD_DIM:] = v_s[:, head_at(m)]
        kv[m, ROWS:, :HEAD_DIM] = kp_s[:, head_at(m)]
        kv[m, ROWS:, HEAD_DIM:] = vp_s[:, head_at(m)]


def pack_qd_kernel(q, do, qd, q_s, do_s, sems):
    run_copies(((q, q_s), (do, do_s)), sems)
    for m in range(4):
        qd[m, :, :HALF] = q_s[:, head_at(m, HALF)]
        qd[m, :, HALF:] = do_s[:, head_at(m, HALF)]


def rows_at(m):
    return slice(CHUNK + m * ROWS, CHUNK + (m + 1) * ROWS)


def load_keys(g, kvs, k_s, v_s):
    for m, kv in enumerate(kvs):
        k_s[g, rows_at(m), :] = kv[:ROWS, :HEAD_DIM]
        v_s[g, rows_at(m), :] = kv[:ROWS, HEAD_DIM:]
        k_s[g, head_at(m, PROWS), :] = kv[ROWS:, :HEAD_DIM]
        v_s[g, head_at(m, PROWS), :] = kv[ROWS:, HEAD_DIM:]


def query_rows(info, x):
    rows = []
    for j in range(2):
        start = block_of(x * 2 + j, info[0], info[1]) * ROWS
        rows += [start + lax.broadcasted_iota(jnp.int32, (1, ROWS), 1)] * GROUP
    return jnp.concatenate(rows, axis=1)


def key_rows(info, x, quad):
    rows = []
    for j in range(2):
        start = block_of(x * 2 + j, quad, info[1]) * ROWS
        rows.append(start + lax.broadcasted_iota(jnp.int32, (ROWS, 1), 0))
    return jnp.concatenate(rows, axis=0)


def fold(x, op):
    return op(x.reshape(x.shape[0] // 8, 8, LANES), axis=0)


def each(count, step, carry):
    return step(0, carry) if count == 1 else lax.fori_loop(0, count, step, carry)


def forward(info, quads, count, k_s, v_s, qt, before, score_s, probs, vt_s, shift, total, acc):
    def turn_values(g, carry):
        vt_s[g] = v_s[g].T
        return carry

    each(count, turn_values, 0)
    for x in range(2):
        place = query_rows(info, x)
        start, span = TILE_STARTS[x], TILE_SPANS[x]

        def score_step(g, running):
            for c in range(span // CHUNK):
                at = slice(c * CHUNK, (c + 1) * CHUNK)
                score = dot(k_s[g, at, :], qt[x])
                if c > 0:
                    score = jnp.where(key_rows(info, c - 1, quads(g)) <= place, score, NEG)
                score_s[g, at, :] = score
                running = jnp.maximum(running, fold(score, jnp.max))
            return running

        running = each(count, score_step, jnp.full((8, LANES), NEG, F32))
        now = jnp.max(running, axis=0, keepdims=True) * SCALE2
        if before is not None:
            now = jnp.maximum(now, before[0][x])
            factor = jnp.exp2(before[0][x] - now)
            acc[x] = before[2][x] * factor

        def prob_step(g, running):
            for c in range(span // CHUNK):
                prob = jnp.exp2(score_s[g, c * CHUNK : (c + 1) * CHUNK, :] * SCALE2 - now)
                running = running + fold(prob, jnp.sum)
                probs[g, start + c * CHUNK : start + (c + 1) * CHUNK, :] = prob.astype(BF16)
            part = dot(vt_s[g, :, :span], probs[g, start : start + span, :])
            if before is None:
                acc[x] = part
            else:
                acc[x] += part
            return running

        running = each(count, prob_step, jnp.zeros((8, LANES), F32))
        sums = jnp.sum(running, axis=0, keepdims=True)
        if before is not None:
            sums = sums + before[1][x] * factor
        shift[x], total[x] = now, sums


def backward(count, k_s, v_s, kt_s, q, uplt, upl, delta, probs, factors, grad_s, before, dqt):
    for x in range(2):
        dqt[x] = jnp.zeros((HEAD_DIM, LANES), F32) if before is None else before[x]

    def step(g, carry):
        kt_s[...] = k_s[g].T
        for c in range(3):
            at = slice(c * CHUNK, (c + 1) * CHUNK)
            dk, dv = None, None
            for x in range(c // 2, 2):
                here = slice(TILE_STARTS[x] + c * CHUNK, TILE_STARTS[x] + (c + 1) * CHUNK)
                low = probs[g, here, :]
                if factors is not None:
                    low = (low.astype(F32) * factors[x]).astype(BF16)
                prob_grad = dot(v_s[g, at, :], uplt[x])
                grad = (low.astype(F32) * (prob_grad - delta[x])).astype(BF16)
                grad_s[here, :] = grad
                dv_part = dot(low, upl[x])
                dk_part = dot(grad, q[x])
                dv = dv_part if dv is None else dv + dv_part
                dk = dk_part if dk is None else dk + dk_part
            k_s[g, at, :] = (dk * SCALE).astype(BF16)
            v_s[g, at, :] = dv.astype(BF16)
        for x in range(2):
            start, span = TILE_STARTS[x], TILE_SPANS[x]
            dqt[x] += dot(kt_s[:, :span], grad_s[start : start + span, :])
        return carry

    each(count, step, 0)


def store_grads(g, k_s, v_s, outs):
    for m, out in enumerate(outs):
        out[:ROWS, :HEAD_DIM] = k_s[g, rows_at(m), :]
        out[:ROWS, HEAD_DIM:] = v_s[g, rows_at(m), :]
        out[ROWS:, :HEAD_DIM] = k_s[g, head_at(m, PROWS), :]
        out[ROWS:, HEAD_DIM:] = v_s[g, head_at(m, PROWS), :]


def pieces(*parts):
    return [part.at[m] for part in parts for m in range(part.shape[0])]


def turn_rows(x, tile, out):
    for j in range(2):
        for h in range(GROUP):
            out[x * 2 + j, :, head_at(h)] = tile[:, lanes_at(j, h)].T


def first_kernel(
    info, weight, qd, own, qt, q, upt, probs, shift, total, acc, k_s, v_s, vt_s, score_s
):
    quad, core, count = info[0], info[1], info[3]
    load_keys(0, pieces(own), k_s, v_s)
    for m in range(4):
        row = block_of(m, quad, core) * ROWS
        row = row + lax.broadcasted_iota(jnp.int32, (1, ROWS), 1)
        row_weight = jnp.where(row < count, weight[0], 0.0)
        for h in range(GROUP):
            cols = lanes_at(m & 1, h)
            q_head = qd[m, :, head_at(h)]
            q[m // 2, cols, :] = q_head
            qt[m // 2, :, cols] = q_head.T
            grad = qd[m, :, HALF + h * HEAD_DIM : HALF + (h + 1) * HEAD_DIM]
            upt[m // 2, :, cols] = (grad.T.astype(F32) * row_weight).astype(BF16)
    forward(
        info, lambda g: quad, 1, k_s, v_s, qt, None, score_s, probs, vt_s, shift, total, acc
    )


def side_kernel(
    info, qt, left, right, shift0, total0, acc0,
    probs, shift, total, acc,
    k_s, v_s, vt_s, score_s,
):
    quad = info[0]
    load_keys(0, pieces(left), k_s, v_s)
    load_keys(1, pieces(right), k_s, v_s)
    forward(
        info, lambda g: (quad + 3 + 2 * g) & 3, 2, k_s, v_s, qt, (shift0, total0, acc0),
        score_s, probs, vt_s, shift, total, acc,
    )


def far_kernel(
    info, qt, q, upt, far_a, far_b, shift0, total0, acc0,
    shift, uplt, upl, delta, dqt, attn, out_a, out_b,
    k_s, v_s, vt_s, kt_s, score_s, probs, grad_s, acc, total,
):
    quad, length = info[0], info[2]
    load_keys(0, pieces(far_a, far_b), k_s, v_s)
    forward(
        info, lambda g: (quad + 2) & 3, 1, k_s, v_s, qt, (shift0, total0, acc0),
        score_s, probs, vt_s, shift, total, acc,
    )
    for x in range(2):
        inverse = 1.0 / total[x]
        valid = jnp.where(query_rows(info, x) < length, 1.0, 0.0)
        out_t = (acc[x] * (inverse * valid)).astype(BF16)
        up_low = (upt[x].astype(F32) * inverse).astype(BF16)
        uplt[x] = up_low
        delta[x] = jnp.sum(up_low.astype(F32) * out_t.astype(F32), axis=0, keepdims=True)
        turn_rows(x, out_t, attn)
        for j in range(2):
            for h in range(GROUP):
                upl[x, lanes_at(j, h), :] = up_low[:, lanes_at(j, h)].T
    backward(
        1, k_s, v_s, kt_s, q, uplt, upl, delta, probs, None, grad_s, None, dqt
    )
    store_grads(0, k_s, v_s, pieces(out_a, out_b))


def back_side_kernel(
    q, uplt, upl, delta, shift_then, shift_last, probs, left, right, dqt0,
    dqt, out_l, out_r,
    k_s, v_s, kt_s, grad_s,
):
    factors = [jnp.exp2(shift_then[x] - shift_last[x]) for x in range(2)]
    load_keys(0, pieces(left), k_s, v_s)
    load_keys(1, pieces(right), k_s, v_s)
    backward(
        2, k_s, v_s, kt_s, q, uplt, upl, delta, probs, factors, grad_s, dqt0, dqt
    )
    store_grads(0, k_s, v_s, pieces(out_l))
    store_grads(1, k_s, v_s, pieces(out_r))


def back_own_kernel(
    q, uplt, upl, delta, shift_then, shift_last, probs, own, dqt0,
    out, dq,
    k_s, v_s, kt_s, grad_s, dqt,
):
    factors = [jnp.exp2(shift_then[x] - shift_last[x]) for x in range(2)]
    load_keys(0, pieces(own), k_s, v_s)
    backward(
        1, k_s, v_s, kt_s, q, uplt, upl, delta, probs, factors, grad_s, dqt0, dqt
    )
    store_grads(0, k_s, v_s, pieces(out))
    for x in range(2):
        turn_rows(x, (dqt[x] * SCALE).astype(BF16), dq)


def unpack_kernel(attn, dq, attended, query_grad):
    for m in range(4):
        attended[:, head_at(m, HALF)] = attn[m]
        query_grad[:, head_at(m, HALF)] = dq[m]


def both(a, b):
    return (a.astype(F32) + b.astype(F32)).astype(BF16)


def add_kernel(side_l, side_r, far_a, far_b, out_l, out_r):
    out_r[:2] = both(side_r[:2], far_a[...])
    out_r[2:] = side_r[2:]
    out_l[:2] = side_l[:2]
    out_l[2:] = both(side_l[2:], far_b[...])


def sum_kernel(own, left, right, out):
    for m in range(4):
        total = own[m].astype(F32) + left[m].astype(F32) + right[m].astype(F32)
        out[m] = total.astype(BF16)


def finish_kernel(grads, key_grad, value_grad, share):
    for m in range(4):
        key_grad[:, head_at(m)] = grads[m, :ROWS, :HEAD_DIM]
        value_grad[:, head_at(m)] = grads[m, :ROWS, HEAD_DIM:]
        share[:, head_at(m)] = grads[m, ROWS:, :HEAD_DIM]
        share[:, head_at(KV_HEADS + m)] = grads[m, ROWS:, HEAD_DIM:]


def bf16(*shape):
    return jax.ShapeDtypeStruct(shape, BF16)


def f32(*shape):
    return jax.ShapeDtypeStruct(shape, F32)


def call(kernel, outs, scratch, scalars, *operands, copies=0, products=0):
    place = pl.BlockSpec(memory_space=pl.ANY) if copies else VMEM
    scratch = [pltpu.VMEM(shape, dtype) for shape, dtype in scratch]
    if copies:
        scratch.append(pltpu.SemaphoreType.DMA((copies,)))
    return pl.pallas_call(
        kernel,
        out_shape=tuple(outs),
        in_specs=[SMEM] * len(scalars) + [place] * len(operands),
        out_specs=(VMEM,) * len(outs),
        scratch_shapes=scratch,
        compiler_params=pltpu.CompilerParams(vmem_limit_bytes=(56 if copies else 32) * 2**20),
        cost_estimate=pl.CostEstimate(
            flops=products * PROBS * LANES * HEAD_DIM * 4,
            bytes_accessed=1_000_000,
            transcendentals=0,
        ),
    )(*scalars, *operands)


def swap(x, axis):
    return lax.ppermute(x, axis, [(0, 1), (1, 0)])


def turn(x, axis, step):
    size = lax.axis_size(axis)
    return lax.ppermute(x, axis, [(i, (i + step) % size) for i in range(size)])


def quad_groups():
    groups = []
    for core in range(2):
        for quad in range(4):
            groups.append([block_of(m, quad, core) * 2 + core for m in range(4)])
    return groups


def quad_exchange(x):
    return lax.all_to_all(x, LOCAL, 0, 0, axis_index_groups=quad_groups(), tiled=True)


def quad_turn(x, step):
    pairs = []
    for i in range(32):
        xh, z, core = i // 16, i // 2 % 8, i % 2
        pairs.append((i, (xh * 8 + (z + 2 * step) % 8) * 2 + core))
    return lax.ppermute(x, LOCAL, pairs)


def rounded(x):
    return lax.optimization_barrier(x.astype(BF16))


def body(q_resp, k_resp, v_resp, k_prompt, v_prompt, d_out, lengths, counts):
    core = lax.axis_index("core")
    quad = ((lax.axis_index("z") - core) & 7) // 2
    info = jnp.stack([quad, core, lengths[0], counts[0]]).astype(jnp.int32)
    weight = (RESP_LEN / counts[0].astype(F32)).reshape(1)
    width = KV_HEADS * HEAD_DIM
    (own,) = call(
        pack_kv_kernel,
        (bf16(4, BOTH, WIDE),),
        [((ROWS, width), BF16)] * 2 + [((PROWS, width), BF16)] * 2,
        (),
        k_resp[0], v_resp[0], k_prompt, v_prompt,
        copies=4,
    )
    (qd,) = call(
        pack_qd_kernel,
        (bf16(4, ROWS, LANES),),
        [((ROWS, HEADS * HEAD_DIM), BF16)] * 2,
        (),
        q_resp[0], d_out[0],
        copies=2,
    )
    own = quad_exchange(own)
    qd = quad_exchange(qd)
    left, right = quad_turn(own, 1), quad_turn(own, -1)
    far_a, far_b = quad_turn(left[:2], 1), quad_turn(right[2:], -1)

    tiles = (2, HEAD_DIM, LANES)
    line = f32(2, 1, LANES)

    def keys(count):
        return [((count, SPAN, HEAD_DIM), BF16)] * 2

    def forward_scratch(count):
        return keys(count) + [((count, HEAD_DIM, SPAN), BF16), ((count, SPAN, LANES), F32)]

    turned = ((HEAD_DIM, SPAN), BF16)
    grad_s = ((PROBS, LANES), BF16)
    whole, pair = bf16(4, BOTH, WIDE), bf16(2, BOTH, WIDE)
    quarter = bf16(4, ROWS, HALF)
    qt, q, upt, probs1, shift1, total1, acc1 = call(
        first_kernel,
        (bf16(*tiles), bf16(2, LANES, HEAD_DIM), bf16(*tiles), bf16(1, PROBS, LANES), line, line, f32(*tiles)),
        forward_scratch(1),
        (info, weight),
        qd, own,
        products=2,
    )
    probs2, shift2, total2, acc2 = call(
        side_kernel,
        (bf16(2, PROBS, LANES), line, line, f32(*tiles)),
        forward_scratch(2),
        (info,),
        qt, left, right, shift1, total1, acc1,
        products=4,
    )
    shift3, uplt, upl, delta, dqt, attn, far_ga, far_gb = call(
        far_kernel,
        (line, bf16(*tiles), bf16(2, LANES, HEAD_DIM), line, f32(*tiles), quarter, pair, pair),
        keys(1) + [((1, HEAD_DIM, SPAN), BF16), turned, ((1, SPAN, LANES), F32)]
        + [((1, PROBS, LANES), BF16), grad_s, (tiles, F32), ((2, 1, LANES), F32)],
        (info,),
        qt, q, upt, far_a, far_b, shift2, total2, acc2,
        products=6,
    )
    far_ga, far_gb = quad_turn(far_ga, 1), quad_turn(far_gb, -1)
    attn = quad_exchange(attn)
    dqt, left_g, right_g = call(
        back_side_kernel,
        (f32(*tiles), whole, whole),
        keys(2) + [turned, grad_s],
        (),
        q, uplt, upl, delta, shift2, shift3, probs2,
        left, right, dqt,
        products=8,
    )
    left_g, right_g = call(add_kernel, (whole, whole), (), (), left_g, right_g, far_ga, far_gb)
    left_g, right_g = quad_turn(left_g, -1), quad_turn(right_g, 1)
    own_g, dq = call(
        back_own_kernel,
        (whole, quarter),
        keys(1) + [turned, grad_s, (tiles, F32)],
        (),
        q, uplt, upl, delta, shift1, shift3, probs1, own, dqt,
        products=4,
    )
    dq = quad_exchange(dq)
    left_g, right_g, attn, dq = lax.optimization_barrier((left_g, right_g, attn, dq))
    (grads,) = call(sum_kernel, (whole,), (), (), own_g, left_g, right_g)
    grads = quad_exchange(grads)
    rows = bf16(ROWS, HEADS * HEAD_DIM)
    key_grad, value_grad, share = call(
        finish_kernel,
        (bf16(ROWS, width), bf16(ROWS, width), bf16(PROWS, 2 * width)),
        (),
        (),
        grads,
    )
    for axis in ("core", "xl"):
        share = rounded(share.astype(F32) + swap(share, axis).astype(F32))
    across = share.astype(F32) + turn(share, "y", 2).astype(F32)
    beside = turn(share, "y", 1).astype(F32) + turn(share, "y", 3).astype(F32)
    share = (across + beside).astype(BF16)
    attended, query_grad = call(unpack_kernel, (rows, rows), (), (), attn, dq)
    return (
        attended[None],
        query_grad[None],
        key_grad[None],
        value_grad[None],
        share[:, :width],
        share[:, width:],
    )


def solution(mesh):
    split = Mesh(mesh.devices.reshape(2, 8, 4, 2, 2), CTX + RESP)
    rows = P(RESP, CTX, None)
    prompt = P(CTX, None)
    return jax.shard_map(
        body,
        mesh=split,
        in_specs=(rows, rows, rows, prompt, prompt, rows, P(RESP), P(RESP)),
        out_specs=(rows, rows, rows, rows, prompt, prompt),
        check_vma=False,
    )
```

time: 130 us -> 172 us (1.32)
  blocking collectives: 0 us -> 30.3 us
  waiting for transfers between devices: 32.8 us -> 53.7 us
  local copies, waits for them, and re-layouts: 4 us -> 0.69 us
  Pallas kernels: 34 us -> 30.7 us
  starting transfers between devices: 55.6 us -> 53.4 us
    ppermute x22 -> x8, starting transfers between devices: 48.6 us -> 14.4 us  [quad_turn(): return lax.ppermute(x, LOCAL, pairs)]
    all_to_all x0 -> x2, blocking collectives: none -> 30.3 us  [quad_exchange(): lax.all_to_all(x, LOCAL, 0, 0, axis_index_groups=quad_groups(), tiled=True)]
    all_to_all x0 -> x3, starting transfers between devices: none -> 20.8 us  [quad_exchange(): lax.all_to_all(x, LOCAL, 0, 0, axis_index_groups=quad_groups(), tiled=True)]
    ppermute x22 -> x8, waiting for transfers between devices: 23.3 us -> 38.5 us  [quad_turn(): return lax.ppermute(x, LOCAL, pairs)]
    ppermute x2, starting transfers between devices: 3.91 us -> 13.7 us  [swap(): return lax.ppermute(x, axis, [(0, 1), (1, 0)])]
    all_to_all x0 -> x3, waiting for transfers between devices: none -> 3.64 us  [quad_exchange(): lax.all_to_all(x, LOCAL, 0, 0, axis_index_groups=quad_groups(), tiled=True)]
    pallas_call x11, Pallas kernels: 34 us -> 30.7 us  [call(): pl.pallas_call(kernel, out_shape=tuple(outs), in_specs=[SMEM] * len(scala...]
    unnamed x6 -> x0, local copies, waits for them, and re-layouts: 2.71 us -> none
  transfers between devices with their start and end apart: 27 -> 16, of which waited for: 10 -> 9; matrix products, arithmetic and copies ran while one was open for 1% -> 0% of each run, Pallas kernels for 18% -> 7%
where the time goes in v2:
time: 172 us; the launch traced here: 171 us
  waiting for transfers between devices  53.7 us (31%)
  starting transfers between devices  53.4 us (31%)
  Pallas kernels  30.7 us (18%)
  blocking collectives  30.3 us (18%)
  between operations  2.08 us (1%)
    ppermute x8, waiting for transfers between devices, quad_turn(): return lax.ppermute(x, LOCAL, pairs)  38.5 us
    pallas_call x11, Pallas kernels, call(): pl.pallas_call(kernel, out_shape=tuple(outs), in_specs=[SMEM] * len(scala...  30.7 us
    all_to_all x2, blocking collectives, quad_exchange(): lax.all_to_all(x, LOCAL, 0, 0, axis_index_groups=quad_groups(), tiled=True)  30.3 us
    all_to_all x3, starting transfers between devices, quad_exchange(): lax.all_to_all(x, LOCAL, 0, 0, axis_index_groups=quad_groups(), tiled=True)  20.8 us
    ppermute x8, starting transfers between devices, quad_turn(): return lax.ppermute(x, LOCAL, pairs)  14.4 us
    ppermute x2, starting transfers between devices, swap(): return lax.ppermute(x, axis, [(0, 1), (1, 0)])  13.7 us
    ppermute x3, waiting for transfers between devices, turn(): return lax.ppermute(x, axis, [(i, (i + step) % size) for i in range(size)])  5.93 us
    ppermute x2, waiting for transfers between devices, swap(): return lax.ppermute(x, axis, [(0, 1), (1, 0)])  5.65 us
  transfers between devices with their start and end apart: 16, of which 9 were waited for; matrix products, arithmetic and copies ran while one was open for 0% of the time, Pallas kernels for 7%

profile of v2, /device:TPU:1, one launch (start us, length us, event | category | flops | bytes accessed | tf_op | source)
XLA Modules:
  0.0 171.2 jit_solution(4799265746879497100)
XLA Ops:
  0.6 1.8 %shard_map.128 = bf16[4,192,256]{2,1,0:T(8,128)(2,1)} custom-call(bf16[128,512]{1,0:T(8,128)(2,1)} %bitcast.12, bf16[128,512]{1,0:T(8,128)(2,1)} %bitcast.13, bf16[64,512]{1,0:T(8,128)(2,1)} %kp.1, bf16[64,512]{1,0:T(8,128)(2,1)} %vp.1), custom_call_target="tpu_custom_call" | custom-call | bytes 1000000 | tf_op jit(solution)/shard_map/pallas_call | solution.py:350
  2.5 10.4 %all-to-all-start.1 = ((bf16[4,192,256]{2,1,0:T(8,128)(2,1)}), bf16[4,192,256]{2,1,0:T(8,128)(2,1)S(1)}, u32[]{:S(2)}, u32[]{:S(2)}) async-start(bf16[4,192,256]{2,1,0:T(8,128)(2,1)} %shard_map.128), calls=%async_computation.1 | async-start | bytes 786432 | tf_op jit(solution)/shard_map/all_to_all | solution.py:383
  12.9 2.3 %shard_map.127 = bf16[4,128,1024]{2,1,0:T(8,128)(2,1)} custom-call(bf16[128,2048]{1,0:T(8,128)(2,1)} %bitcast.10, bf16[128,2048]{1,0:T(8,128)(2,1)} %bitcast.11), custom_call_target="tpu_custom_call" | custom-call | bytes 1000000 | tf_op jit(solution)/shard_map/pallas_call | solution.py:350
  15.2 3.6 %all-to-all-done.1.own = bf16[4,192,256]{2,1,0:T(8,128)(2,1)S(1)} async-done(((bf16[4,192,256]{2,1,0:T(8,128)(2,1)}), bf16[4,192,256]{2,1,0:T(8,128)(2,1)S(1)}, u32[]{:S(2)}, u32[]{:S(2)}) %all-to-all-start.1) | async-done | bytes 393248 | tf_op jit(solution)/shard_map/all_to_all | solution.py:383
  18.9 4.9 %all-to-all-start = ((bf16[4,128,1024]{2,1,0:T(8,128)(2,1)}), bf16[4,128,1024]{2,1,0:T(8,128)(2,1)S(1)}, u32[]{:S(2)}, u32[]{:S(2)}) async-start(bf16[4,128,1024]{2,1,0:T(8,128)(2,1)} %shard_map.127), calls=%async_computation | async-start | bytes 2097152 | tf_op jit(solution)/shard_map/all_to_all | solution.py:383
  23.8 1.5 collective-permute-start.2
  25.3 0.8 collective-permute-start
  27.6 17.9 %collective-permute-done.2.right = bf16[4,192,256]{2,1,0:T(8,128)(2,1)S(1)} collective-permute-done((bf16[4,192,256]{2,1,0:T(8,128)(2,1)S(1)}, bf16[4,192,256]{2,1,0:T(8,128)(2,1)S(1)}, u32[]{:S(2)}, u32[]{:S(2)}) %collective-permute-start.2) | collective-permute-done | bytes 393248 | tf_op jit(solution)/shard_map/ppermute | solution.py:391
  45.5 3.8 %collective-permute-start.3 = (bf16[2,192,256]{2,1,0:T(8,128)(2,1)S(1)}, bf16[2,192,256]{2,1,0:T(8,128)(2,1)S(1)}, u32[]{:S(2)}, u32[]{:S(2)}) collective-permute-start(bf16[2,192,256]{2,1,0:T(8,128)(2,1)S(1)} %slice.17), channel_id=1, source_target_pairs={{0,96},{1,97},{16,112},{17,113},{32,0},{33,1},{48,16},{49,17},{64,... | collective-permute-start | bytes 589832 | tf_op jit(solution)/shard_map/ppermute | solution.py:391
  49.3 1.4 collective-permute-start.1
  50.8 3.1 %shard_map.129 = (bf16[2,128,1024]{2,1,0:T(8,128)(2,1)S(1)}, bf16[2,1024,128]{2,1,0:T(8,128)(2,1)S(1)}, bf16[2,128,1024]{2,1,0:T(8,128)(2,1)S(1)}, bf16[1,1280,1...) custom-call(s32[4]{0:T(128)S(1)} %pad_add_fusion.info, ...), custom_call_target="tpu_custom_call" | custom-call | flops 1342177280 | bytes 1000000 | tf_op jit(solution)/shard_map/pallas_call | solution.py:350
  53.9 5.9 %shard_map.130 = (bf16[2,1280,1024]{2,1,0:T(8,128)(2,1)S(1)}, f32[2,1,1024]{2,1,0:T(1,128)S(1)}, f32[2,1,1024]{2,1,0:T(1,128)S(1)}, f32[2,128,1024]{2,1,0:T(8,128)S(1)}) custom-call(s32[4]{0:T(128)S(1)} %pad_add_fusion.info, bf16[2,128,1024]{2,1,0:T(8,128)(2,1)S(1)} %get-tuple-element.42.qt, bf16[4,192,256]{2,1,0:T(8,128)(2,1)S(1)} %collective-permute-done.left, ...), custom_call_target="tpu_custom_call" | custom-call | flops 2684354560 | bytes 1000000 | tf_op jit(solution)/shard_map/pallas_call | solution.py:350
  59.7 6.6 %shard_map.131 = (f32[2,1,1024]{2,1,0:T(1,128)S(1)}, bf16[2,128,1024]{2,1,0:T(8,128)(2,1)S(1)}, bf16[2,1024,128]{2,1,0:T(8,128)(2,1)S(1)}, f32[2,1,1024]{2,1,0:T...) custom-call(s32[4]{0:T(128)S(1)} %pad_add_fusion.info, ...), custom_call_target="tpu_custom_call" | custom-call | flops 4026531840 | bytes 1000000 | tf_op jit(solution)/shard_map/pallas_call | solution.py:350
  66.3 6.1 %shard_map.132 = (f32[2,128,1024]{2,1,0:T(8,128)S(1)}, bf16[4,192,256]{2,1,0:T(8,128)(2,1)S(1)}, bf16[4,192,256]{2,1,0:T(8,128)(2,1)S(1)}) custom-call(bf16[2,1024,128]{2,1,0:T(8,128)(2,1)S(1)} %get-tuple-element.41.q, bf16[2,128,1024]{2,1,0:T(8,128)(2,1)S(1)} %get-tuple-element.50.uplt, bf16[2,1024,128]{2,1,0:T(8,128)(2,1)S(1)} %get-tuple-element.51.upl, ...), custom_call_target="tpu_custom_call" | custom-call | flops 5368709120 | bytes 1000000 | tf_op jit(solution)/shard_map/pallas_call | solution.py:350
  72.4 2.9 %shard_map.134 = (bf16[4,192,256]{2,1,0:T(8,128)(2,1)S(1)}, bf16[4,128,512]{2,1,0:T(8,128)(2,1)S(1)}) custom-call(bf16[2,1024,128]{2,1,0:T(8,128)(2,1)S(1)} %get-tuple-element.41.q, bf16[2,128,1024]{2,1,0:T(8,128)(2,1)S(1)} %get-tuple-element.50.uplt, bf16[2,1024,128]{2,1,0:T(8,128)(2,1)S(1)} %get-tuple-element.51.upl, ...), custom_call_target="tpu_custom_call" | custom-call | flops 2684354560 | bytes 1000000 | tf_op jit(solution)/shard_map/pallas_call | solution.py:350
  75.4 11.6 %all_to_all.25.dq = bf16[4,128,512]{2,1,0:T(8,128)(2,1)S(1)} all-to-all(bf16[4,128,512]{2,1,0:T(8,128)(2,1)S(1)} %get-tuple-element.65), channel_id=1, replica_groups={{0,16,128,144},{32,48,160,176},{64,80,192,208},{96,112,224,240},{17,33,..., dimensions={0} | all-to-all | bytes 1048576 | tf_op jit(solution)/shard_map/all_to_all | solution.py:383
  87.0 5.5 %all-to-all-start.2 = ((bf16[4,128,512]{2,1,0:T(8,128)(2,1)}), bf16[4,128,512]{2,1,0:T(8,128)(2,1)S(1)}, u32[]{:S(2)}, u32[]{:S(2)}) async-start(bf16[4,128,512]{2,1,0:T(8,128)(2,1)} %get-tuple-element.62), calls=%async_computation.2 | async-start | bytes 1048576 | tf_op jit(solution)/shard_map/all_to_all | solution.py:383
  93.0 3.0 %collective-permute-start.5 = (bf16[2,192,256]{2,1,0:T(8,128)(2,1)S(1)}, bf16[2,192,256]{2,1,0:T(8,128)(2,1)S(1)}, u32[]{:S(2)}, u32[]{:S(2)}) collective-permute-start(bf16[2,192,256]{2,1,0:T(8,128)(2,1)S(1)} %get-tuple-element.59), channel_id=1, source_target_pairs={{0,96},{1,97},{16,112},{17,113},{32,0},{33,1},{48,16},{49,17},{64,... | collective-permute-start | bytes 589832 | tf_op jit(solution)/shard_map/ppermute | solution.py:391
  96.0 3.7 %collective-permute-done.4.far_a = bf16[2,192,256]{2,1,0:T(8,128)(2,1)S(1)} collective-permute-done((bf16[2,192,256]{2,1,0:T(8,128)(2,1)S(1)}, bf16[2,192,256]{2,1,0:T(8,128)(2,1)S(1)}, u32[]{:S(2)}, u32[]{:S(2)}) %collective-permute-start.4) | collective-permute-done | bytes 196640 | tf_op jit(solution)/shard_map/ppermute | solution.py:391
  99.7 2.6 %collective-permute-done.5.far_b = bf16[2,192,256]{2,1,0:T(8,128)(2,1)S(1)} collective-permute-done((bf16[2,192,256]{2,1,0:T(8,128)(2,1)S(1)}, bf16[2,192,256]{2,1,0:T(8,128)(2,1)S(1)}, u32[]{:S(2)}, u32[]{:S(2)}) %collective-permute-start.5) | collective-permute-done | bytes 196640 | tf_op jit(solution)/shard_map/ppermute | solution.py:391
  102.4 2.0 %collective-permute-start.6 = (bf16[4,192,256]{2,1,0:T(8,128)(2,1)S(1)}, bf16[4,192,256]{2,1,0:T(8,128)(2,1)S(1)}, u32[]{:S(2)}, u32[]{:S(2)}) collective-permute-start(bf16[4,192,256]{2,1,0:T(8,128)(2,1)S(1)} %get-tuple-element.60), channel_id=1, source_target_pairs={{0,96},{1,97},{16,112},{17,113},{32,0},{33,1},{48,16},{49,17},{64,... | collective-permute-start | bytes 1179656 | tf_op jit(solution)/shard_map/ppermute | solution.py:391
  104.4 1.2 collective-permute-start.7
  105.6 10.3 %collective-permute-done.6.left = bf16[4,192,256]{2,1,0:T(8,128)(2,1)S(1)} collective-permute-done((bf16[4,192,256]{2,1,0:T(8,128)(2,1)S(1)}, bf16[4,192,256]{2,1,0:T(8,128)(2,1)S(1)}, u32[]{:S(2)}, u32[]{:S(2)}) %collective-permute-start.6) | collective-permute-done | bytes 393248 | tf_op jit(solution)/shard_map/ppermute | solution.py:391
  115.9 4.0 %collective-permute-done.7.right = bf16[4,192,256]{2,1,0:T(8,128)(2,1)S(1)} collective-permute-done((bf16[4,192,256]{2,1,0:T(8,128)(2,1)S(1)}, bf16[4,192,256]{2,1,0:T(8,128)(2,1)S(1)}, u32[]{:S(2)}, u32[]{:S(2)}) %collective-permute-start.7) | collective-permute-done | bytes 393248 | tf_op jit(solution)/shard_map/ppermute | solution.py:391
  120.1 18.7 %all_to_all.26.grads = bf16[4,192,256]{2,1,0:T(8,128)(2,1)S(1)} all-to-all(bf16[4,192,256]{2,1,0:T(8,128)(2,1)S(1)} %shard_map.136), channel_id=1, replica_groups={{0,16,128,144},{32,48,160,176},{64,80,192,208},{96,112,224,240},{17,33,..., dimensions={0} | all-to-all | bytes 786432 | tf_op jit(solution)/shard_map/all_to_all | solution.py:383
  139.6 13.6 %collective-permute-start.8 = (bf16[64,1024]{1,0:T(8,128)(2,1)S(1)}, bf16[64,1024]{1,0:T(8,128)(2,1)S(1)}, u32[]{:S(2)}, u32[]{:S(2)}) collective-permute-start(bf16[64,1024]{1,0:T(8,128)(2,1)S(1)} %get-tuple-element.75), channel_id=1, source_target_pairs={{0,1},{1,0},{2,3},{3,2},{4,5},{5,4},{6,7},{7,6},{8,9},{9,8},{10,11... | collective-permute-start | bytes 393224 | tf_op jit(solution)/shard_map/ppermute | solution.py:366
  153.2 1.0 collective-permute-done.8
  154.4 4.7 %collective-permute-done.9 = bf16[64,1024]{1,0:T(8,128)(2,1)S(1)} collective-permute-done((bf16[64,1024]{1,0:T(8,128)(2,1)S(1)}, bf16[64,1024]{1,0:T(8,128)(2,1)S(1)}, u32[]{:S(2)}, u32[]{:S(2)}) %collective-permute-start.9) | collective-permute-done | bytes 131104 | tf_op jit(solution)/shard_map/ppermute | solution.py:366
  159.1 2.8 %collective-permute-start.12 = (bf16[64,1024]{1,0:T(8,128)(2,1)S(1)}, bf16[64,1024]{1,0:T(8,128)(2,1)S(1)}, u32[]{:S(2)}, u32[]{:S(2)}) collective-permute-start(bf16[64,1024]{1,0:T(8,128)(2,1)S(1)} %add_convert_fusion.1), channel_id=1, source_target_pairs={{0,12},{4,0},{8,4},{12,8},{1,13},{5,1},{9,5},{13,9},{2,14},{6,2},{... | collective-permute-start | bytes 393224 | tf_op jit(solution)/shard_map/ppermute | solution.py:371
  161.9 1.6 collective-permute-start.10
  163.5 1.0 shard_map.135
  164.6 5.9 %collective-permute-done.11 = bf16[64,1024]{1,0:T(8,128)(2,1)S(1)} collective-permute-done((bf16[64,1024]{1,0:T(8,128)(2,1)S(1)}, bf16[64,1024]{1,0:T(8,128)(2,1)S(1)}, u32[]{:S(2)}, u32[]{:S(2)}) %collective-permute-start.11) | collective-permute-done | bytes 131104 | tf_op jit(solution)/shard_map/ppermute | solution.py:371
  (20 shorter events, 2.7 us)
Async XLA Ops:
  2.5 16.4 %all-to-all-start.1 = ((bf16[4,192,256]{2,1,0:T(8,128)(2,1)}), bf16[4,192,256]{2,1,0:T(8,128)(2,1)S(1)}, u32[]{:S(2)}, u32[]{:S(2)}) async-start(bf16[4,192,256]{2,1,0:T(8,128)(2,1)} %shard_map.128), calls=%async_computation.1 | async-start | bytes 786432 | tf_op jit(solution)/shard_map/all_to_all | solution.py:383
  18.9 31.9 %all-to-all-start = ((bf16[4,128,1024]{2,1,0:T(8,128)(2,1)}), bf16[4,128,1024]{2,1,0:T(8,128)(2,1)S(1)}, u32[]{:S(2)}, u32[]{:S(2)}) async-start(bf16[4,128,1024]{2,1,0:T(8,128)(2,1)} %shard_map.127), calls=%async_computation | async-start | bytes 2097152 | tf_op jit(solution)/shard_map/all_to_all | solution.py:383
  23.8 21.7 %collective-permute-start.2 = (bf16[4,192,256]{2,1,0:T(8,128)(2,1)S(1)}, bf16[4,192,256]{2,1,0:T(8,128)(2,1)S(1)}, u32[]{:S(2)}, u32[]{:S(2)}) collective-permute-start(bf16[4,192,256]{2,1,0:T(8,128)(2,1)S(1)} %all-to-all-done.1.own), channel_id=1, source_target_pairs={{0,96},{1,97},{16,112},{17,113},{32,0},{33,1},{48,16},{49,17},{64,... | collective-permute-start | bytes 1179656 | tf_op jit(solution)/shard_map/ppermute | solution.py:391
  25.3 24.0 %collective-permute-start = (bf16[4,192,256]{2,1,0:T(8,128)(2,1)S(1)}, bf16[4,192,256]{2,1,0:T(8,128)(2,1)S(1)}, u32[]{:S(2)}, u32[]{:S(2)}) collective-permute-start(bf16[4,192,256]{2,1,0:T(8,128)(2,1)S(1)} %all-to-all-done.1.own), channel_id=1, source_target_pairs={{0,32},{1,33},{16,48},{17,49},{32,64},{33,65},{48,80},{49,81},{64,... | collective-permute-start | bytes 1179656 | tf_op jit(solution)/shard_map/ppermute | solution.py:391
  45.5 14.2 %collective-permute-start.3 = (bf16[2,192,256]{2,1,0:T(8,128)(2,1)S(1)}, bf16[2,192,256]{2,1,0:T(8,128)(2,1)S(1)}, u32[]{:S(2)}, u32[]{:S(2)}) collective-permute-start(bf16[2,192,256]{2,1,0:T(8,128)(2,1)S(1)} %slice.17), channel_id=1, source_target_pairs={{0,96},{1,97},{16,112},{17,113},{32,0},{33,1},{48,16},{49,17},{64,... | collective-permute-start | bytes 589832 | tf_op jit(solution)/shard_map/ppermute | solution.py:391
  49.3 10.4 %collective-permute-start.1 = (bf16[2,192,256]{2,1,0:T(8,128)(2,1)S(1)}, bf16[2,192,256]{2,1,0:T(8,128)(2,1)S(1)}, u32[]{:S(2)}, u32[]{:S(2)}) collective-permute-start(bf16[2,192,256]{2,1,0:T(8,128)(2,1)S(1)} %slice.16), channel_id=1, source_target_pairs={{0,32},{1,33},{16,48},{17,49},{32,64},{33,65},{48,80},{49,81},{64,... | collective-permute-start | bytes 589832 | tf_op jit(solution)/shard_map/ppermute | solution.py:391
  87.0 33.0 %all-to-all-start.2 = ((bf16[4,128,512]{2,1,0:T(8,128)(2,1)}), bf16[4,128,512]{2,1,0:T(8,128)(2,1)S(1)}, u32[]{:S(2)}, u32[]{:S(2)}) async-start(bf16[4,128,512]{2,1,0:T(8,128)(2,1)} %get-tuple-element.62), calls=%async_computation.2 | async-start | bytes 1048576 | tf_op jit(solution)/shard_map/all_to_all | solution.py:383
  92.4 7.2 %collective-permute-start.4 = (bf16[2,192,256]{2,1,0:T(8,128)(2,1)S(1)}, bf16[2,192,256]{2,1,0:T(8,128)(2,1)S(1)}, u32[]{:S(2)}, u32[]{:S(2)}) collective-permute-start(bf16[2,192,256]{2,1,0:T(8,128)(2,1)S(1)} %get-tuple-element.58), channel_id=1, source_target_pairs={{0,32},{1,33},{16,48},{17,49},{32,64},{33,65},{48,80},{49,81},{64,... | collective-permute-start | bytes 589832 | tf_op jit(solution)/shard_map/ppermute | solution.py:391
  93.0 9.2 %collective-permute-start.5 = (bf16[2,192,256]{2,1,0:T(8,128)(2,1)S(1)}, bf16[2,192,256]{2,1,0:T(8,128)(2,1)S(1)}, u32[]{:S(2)}, u32[]{:S(2)}) collective-permute-start(bf16[2,192,256]{2,1,0:T(8,128)(2,1)S(1)} %get-tuple-element.59), channel_id=1, source_target_pairs={{0,96},{1,97},{16,112},{17,113},{32,0},{33,1},{48,16},{49,17},{64,... | collective-permute-start | bytes 589832 | tf_op jit(solution)/shard_map/ppermute | solution.py:391
  102.4 13.6 %collective-permute-start.6 = (bf16[4,192,256]{2,1,0:T(8,128)(2,1)S(1)}, bf16[4,192,256]{2,1,0:T(8,128)(2,1)S(1)}, u32[]{:S(2)}, u32[]{:S(2)}) collective-permute-start(bf16[4,192,256]{2,1,0:T(8,128)(2,1)S(1)} %get-tuple-element.60), channel_id=1, source_target_pairs={{0,96},{1,97},{16,112},{17,113},{32,0},{33,1},{48,16},{49,17},{64,... | collective-permute-start | bytes 1179656 | tf_op jit(solution)/shard_map/ppermute | solution.py:391
  104.4 15.5 %collective-permute-start.7 = (bf16[4,192,256]{2,1,0:T(8,128)(2,1)S(1)}, bf16[4,192,256]{2,1,0:T(8,128)(2,1)S(1)}, u32[]{:S(2)}, u32[]{:S(2)}) collective-permute-start(bf16[4,192,256]{2,1,0:T(8,128)(2,1)S(1)} %get-tuple-element.61), channel_id=1, source_target_pairs={{0,32},{1,33},{16,48},{17,49},{32,64},{33,65},{48,80},{49,81},{64,... | collective-permute-start | bytes 1179656 | tf_op jit(solution)/shard_map/ppermute | solution.py:391
  139.6 14.6 %collective-permute-start.8 = (bf16[64,1024]{1,0:T(8,128)(2,1)S(1)}, bf16[64,1024]{1,0:T(8,128)(2,1)S(1)}, u32[]{:S(2)}, u32[]{:S(2)}) collective-permute-start(bf16[64,1024]{1,0:T(8,128)(2,1)S(1)} %get-tuple-element.75), channel_id=1, source_target_pairs={{0,1},{1,0},{2,3},{3,2},{4,5},{5,4},{6,7},{7,6},{8,9},{9,8},{10,11... | collective-permute-start | bytes 393224 | tf_op jit(solution)/shard_map/ppermute | solution.py:366
  154.2 4.8 %collective-permute-start.9 = (bf16[64,1024]{1,0:T(8,128)(2,1)S(1)}, bf16[64,1024]{1,0:T(8,128)(2,1)S(1)}, u32[]{:S(2)}, u32[]{:S(2)}) collective-permute-start(bf16[64,1024]{1,0:T(8,128)(2,1)S(1)} %add_convert_fusion.2), channel_id=1, source_target_pairs={{0,2},{2,0},{1,3},{3,1},{4,6},{6,4},{5,7},{7,5},{8,10},{10,8},{9,1... | collective-permute-start | bytes 393224 | tf_op jit(solution)/shard_map/ppermute | solution.py:366
  159.1 5.5 %collective-permute-start.12 = (bf16[64,1024]{1,0:T(8,128)(2,1)S(1)}, bf16[64,1024]{1,0:T(8,128)(2,1)S(1)}, u32[]{:S(2)}, u32[]{:S(2)}) collective-permute-start(bf16[64,1024]{1,0:T(8,128)(2,1)S(1)} %add_convert_fusion.1), channel_id=1, source_target_pairs={{0,12},{4,0},{8,4},{12,8},{1,13},{5,1},{9,5},{13,9},{2,14},{6,2},{... | collective-permute-start | bytes 393224 | tf_op jit(solution)/shard_map/ppermute | solution.py:371
  161.9 8.6 %collective-permute-start.11 = (bf16[64,1024]{1,0:T(8,128)(2,1)S(1)}, bf16[64,1024]{1,0:T(8,128)(2,1)S(1)}, u32[]{:S(2)}, u32[]{:S(2)}) collective-permute-start(bf16[64,1024]{1,0:T(8,128)(2,1)S(1)} %add_convert_fusion.1), channel_id=1, source_target_pairs={{0,4},{4,8},{8,12},{12,0},{1,5},{5,9},{9,13},{13,1},{2,6},{6,10},{... | collective-permute-start | bytes 393224 | tf_op jit(solution)/shard_map/ppermute | solution.py:371
  161.9 8.6 %collective-permute-start.10 = (bf16[64,1024]{1,0:T(8,128)(2,1)S(1)}, bf16[64,1024]{1,0:T(8,128)(2,1)S(1)}, u32[]{:S(2)}, u32[]{:S(2)}) collective-permute-start(bf16[64,1024]{1,0:T(8,128)(2,1)S(1)} %add_convert_fusion.1), channel_id=1, source_target_pairs={{0,8},{4,12},{8,0},{12,4},{1,9},{5,13},{9,1},{13,5},{2,10},{6,14},... | collective-permute-start | bytes 393224 | tf_op jit(solution)/shard_map/ppermute | solution.py:371

commit v3 on v1

--- a/solution.py
+++ b/solution.py
@@ -63,27 +63,24 @@
         copy.wait()
 
 
-def pack_kv_kernel(info, k, v, kp, vp, kv0, kv1, kv2, kv3, sems):
+def pack_kv_kernel(info, k, v, kp, vp, kv0, kv1, kv2, kv3, k_s, v_s, kp_s, vp_s, sems):
     mine = info[0]
-    pairs = []
+    run_copies(((k, k_s), (v, v_s), (kp, kp_s), (vp, vp_s)), sems)
     for d, kv in enumerate((kv0, kv1, kv2, kv3)):
         at = pl.ds(pl.multiple_of((mine ^ d) * HEAD_DIM, HEAD_DIM), HEAD_DIM)
-        pairs += [
-            (k.at[:, at], kv.at[:ROWS, :HEAD_DIM]),
-            (v.at[:, at], kv.at[:ROWS, HEAD_DIM:]),
-            (kp.at[:, at], kv.at[ROWS:, :HEAD_DIM]),
-            (vp.at[:, at], kv.at[ROWS:, HEAD_DIM:]),
-        ]
-    run_copies(pairs, sems)
-
-
-def pack_qd_kernel(info, q, do, qd0, qd1, qd2, qd3, sems):
+        kv[:ROWS, :HEAD_DIM] = k_s[:, at]
+        kv[:ROWS, HEAD_DIM:] = v_s[:, at]
+        kv[ROWS:, :HEAD_DIM] = kp_s[:, at]
+        kv[ROWS:, HEAD_DIM:] = vp_s[:, at]
+
+
+def pack_qd_kernel(info, q, do, qd0, qd1, qd2, qd3, q_s, do_s, sems):
     mine = info[0]
-    pairs = []
+    run_copies(((q, q_s), (do, do_s)), sems)
     for d, qd in enumerate((qd0, qd1, qd2, qd3)):
         at = pl.ds(pl.multiple_of((mine ^ d) * HALF, HALF), HALF)
-        pairs += [(q.at[:, at], qd.at[:, :HALF]), (do.at[:, at], qd.at[:, HALF:])]
-    run_copies(pairs, sems)
+        qd[:, :HALF] = q_s[:, at]
+        qd[:, HALF:] = do_s[:, at]
 
 
 def rows_at(mine, d):
@@ -170,15 +167,21 @@
         shift[x], total[x] = now, sums
 
 
-def backward(count, k_s, v_s, kt_s, q, uplt, upl, delta, probs, factors, grad_s, before, dqt):
+def chunk_at(c, start):
+    if isinstance(c, int):
+        return slice(start + c * CHUNK, start + (c + 1) * CHUNK)
+    return pl.ds(pl.multiple_of(start + c * CHUNK, CHUNK), CHUNK)
+
+
+def backward(count, looped, k_s, v_s, kt_s, q, uplt, upl, delta, probs, factors, grad_s, before, dqt):
     for x in range(2):
         dqt[x] = jnp.zeros((HEAD_DIM, LANES), F32) if before is None else before[x]
 
     def chunk(g, c, tiles):
-        at = pl.ds(pl.multiple_of(c * CHUNK, CHUNK), CHUNK)
+        at = chunk_at(c, 0)
         dk, dv = None, None
         for x in tiles:
-            here = pl.ds(pl.multiple_of(TILE_STARTS[x] + c * CHUNK, CHUNK), CHUNK)
+            here = chunk_at(c, TILE_STARTS[x])
             low = probs[g, here, :]
             if factors is not None:
                 low = (low.astype(F32) * factors[x]).astype(BF16)
@@ -199,7 +202,11 @@
             chunk(g, c, (0, 1))
             return carry
 
-        lax.fori_loop(0, 2, two_tiles, 0)
+        if looped:
+            lax.fori_loop(0, 2, two_tiles, 0)
+        else:
+            two_tiles(0, 0)
+            two_tiles(1, 0)
         chunk(g, 2, (1,))
         for x in range(2):
             start, span = TILE_STARTS[x], TILE_SPANS[x]
@@ -282,7 +289,7 @@
             for h in range(GROUP):
                 upl[x, lanes_at(j, h), :] = up_low[:, lanes_at(j, h)].T
     backward(
-        1, k_s, v_s, kt_s, q, uplt, upl, delta, probs, None, grad_s, None, dqt
+        1, False, k_s, v_s, kt_s, q, uplt, upl, delta, probs, None, grad_s, None, dqt
     )
     store_grads(mine, 0, k_s, v_s, pieces(out_a, out_b))
 
@@ -298,7 +305,7 @@
     load_keys(mine, 0, pieces(left_a, left_b), k_s, v_s)
     load_keys(mine, 1, pieces(right_a, right_b), k_s, v_s)
     backward(
-        2, k_s, v_s, kt_s, q, uplt, upl, delta, probs, factors, grad_s, dqt0, dqt
+        2, False, k_s, v_s, kt_s, q, uplt, upl, delta, probs, factors, grad_s, dqt0, dqt
     )
     store_grads(mine, 0, k_s, v_s, pieces(out_l))
     store_grads(mine, 1, k_s, v_s, pieces(out_r))
@@ -313,7 +320,7 @@
     factors = [jnp.exp2(shift_then[x] - shift_last[x]) for x in range(2)]
     load_keys(mine, 0, pieces(own_a, own_b), k_s, v_s)
     backward(
-        1, k_s, v_s, kt_s, q, uplt, upl, delta, probs, factors, grad_s, dqt0, dqt
+        1, True, k_s, v_s, kt_s, q, uplt, upl, delta, probs, factors, grad_s, dqt0, dqt
     )
     store_grads(mine, 0, k_s, v_s, pieces(out))
     for x in range(2):
@@ -382,7 +389,7 @@
         in_specs=[SMEM] * len(scalars) + [place] * len(operands),
         out_specs=(VMEM,) * len(outs),
         scratch_shapes=scratch,
-        compiler_params=pltpu.CompilerParams(vmem_limit_bytes=(56 if copies == 16 else 32) * 2**20),
+        compiler_params=pltpu.CompilerParams(vmem_limit_bytes=(56 if copies else 32) * 2**20),
         cost_estimate=pl.CostEstimate(
             flops=products * PROBS * LANES * HEAD_DIM * 4,
             bytes_accessed=1_000_000,
@@ -427,17 +434,28 @@
     mine = lax.axis_index("xh") * 2 + (z & 1)
     info = jnp.stack([mine, z // 2, core, lengths[0], counts[0]]).astype(jnp.int32)
     weight = (RESP_LEN / counts[0].astype(F32)).reshape(1)
+    spot = mine.reshape(1).astype(jnp.int32)
+    width = KV_HEADS * HEAD_DIM
     kv = list(
         call(
             pack_kv_kernel,
             (bf16(BOTH, WIDE),) * 4,
-            (),
-            (info,),
+            [((ROWS, width), BF16)] * 2 + [((PROWS, width), BF16)] * 2,
+            (spot,),
             k_resp[0], v_resp[0], k_prompt, v_prompt,
-            copies=16,
+            copies=4,
         )
     )
-    qd = list(call(pack_qd_kernel, (bf16(ROWS, LANES),) * 4, (), (info,), q_resp[0], d_out[0], copies=8))
+    qd = list(
+        call(
+            pack_qd_kernel,
+            (bf16(ROWS, LANES),) * 4,
+            [((ROWS, HEADS * HEAD_DIM), BF16)] * 2,
+            (spot,),
+            q_resp[0], d_out[0],
+            copies=2,
+        )
+    )
     for d in (1, 2, 3):
         kv[d] = partner(kv[d], d)
     for d in (1, 2, 3):
@@ -504,14 +522,14 @@
         q, uplt, upl, delta, shift1, shift3, probs1, own_a, own_b, dqt, attn,
         products=4,
     )
-    for d in (1, 2, 3):
-        od[d] = partner(od[d], d)
+    od[1], od[2] = partner(od[1], 1), partner(od[2], 2)
+    left_g, right_g, od[3] = lax.optimization_barrier((left_g, right_g, od[3]))
+    od[3] = partner(od[3], 3)
     grads = list(call(sum_kernel, (bf16(BOTH, WIDE),) * 4, (), (), own_g, left_g, right_g))
     for d in (1, 2, 3):
         grads[d] = partner(grads[d], d)
-    tied = lax.optimization_barrier((*grads, *od))
-    grads, od = tied[:4], tied[4:]
-    width = KV_HEADS * HEAD_DIM
+    tied = lax.optimization_barrier((*grads, od[1], od[2]))
+    grads, od[1:3] = tied[:4], tied[4:]
     rows = bf16(ROWS, HEADS * HEAD_DIM)
     key_grad, value_grad, share = call(
         finish_kernel,
@@ -522,6 +540,7 @@
     )
     for axis in ("core", "xl"):
         share = rounded(share.astype(F32) + swap(share, axis).astype(F32))
+    share, od[3] = lax.optimization_barrier((share, od[3]))
     across = share.astype(F32) + turn(share, "y", 2).astype(F32)
     beside = turn(share, "y", 1).astype(F32) + turn(share, "y", 3).astype(F32)
     share = (across + beside).astype(BF16)

time: 130 us -> 131 us (level); the launches traced: 130 us -> 129 us
  waiting for transfers between devices: 32.8 us -> 43.4 us
  starting transfers between devices: 55.6 us -> 48 us
  local copies, waits for them, and re-layouts: 4 us -> 1.7 us
    ppermute x22, waiting for transfers between devices: 23.3 us -> 34.9 us  [local_permute(): return lax.ppermute(x, LOCAL, pairs)]
    ppermute x22, starting transfers between devices: 48.6 us -> 40.1 us  [local_permute(): return lax.ppermute(x, LOCAL, pairs)]
    unnamed x6 -> x2, local copies, waits for them, and re-layouts: 2.71 us -> 0.95 us
  transfers between devices with their start and end apart: 27 -> 27, of which waited for: 10 -> 12; matrix products, arithmetic and copies ran while one was open for 1% -> 1% of each run, Pallas kernels for 18% -> 18%
where the time goes in v3:
time: 131 us; the launch traced here: 129 us
  starting transfers between devices  48 us (37%)
  waiting for transfers between devices  43.4 us (33%)
  Pallas kernels  32.9 us (25%)
  between operations  2.16 us (2%)
  local copies, waits for them, and re-layouts  1.7 us (1%)
    ppermute x22, starting transfers between devices, local_permute(): return lax.ppermute(x, LOCAL, pairs)  40.1 us
    ppermute x22, waiting for transfers between devices, local_permute(): return lax.ppermute(x, LOCAL, pairs)  34.9 us
    pallas_call x11, Pallas kernels, call(): pl.pallas_call(kernel, out_shape=tuple(outs), in_specs=[SMEM] * len(scala...  32.9 us
    ppermute x2, starting transfers between devices, swap(): return lax.ppermute(x, axis, [(0, 1), (1, 0)])  5.06 us
    ppermute x2, waiting for transfers between devices, swap(): return lax.ppermute(x, axis, [(0, 1), (1, 0)])  4.89 us
    ppermute x3, waiting for transfers between devices, turn(): return lax.ppermute(x, axis, [(i, (i + step) % size) for i in range(size)])  3.62 us
    ppermute x3, starting transfers between devices, turn(): return lax.ppermute(x, axis, [(i, (i + step) % size) for i in range(size)])  2.85 us
  transfers between devices with their start and end apart: 27, of which 12 were waited for; matrix products, arithmetic and copies ran while one was open for 1% of the time, Pallas kernels for 18%

profile of v3, /device:TPU:1, one launch (start us, length us, event | category | flops | bytes accessed | tf_op | source)
XLA Modules:
  0.0 129.2 jit_solution(4765906007486641556)
XLA Ops:
  0.6 1.8 %shard_map.128 = (bf16[192,256]{1,0:T(8,128)(2,1)}, bf16[192,256]{1,0:T(8,128)(2,1)}, bf16[192,256]{1,0:T(8,128)(2,1)}, bf16[192,256]{1,0:T(8,128)(2,1)}) custom-call(s32[1]{0:T(128)} %bitcast.info, bf16[128,512]{1,0:T(8,128)(2,1)} %bitcast.17, bf16[128,512]{1,0:T(8,128)(2,1)} %bitcast.18, bf16[64,512]{1,0:T(8,128)(2,1)} %kp.1, bf16[64,512]{1,0:T(8,128)(2,1)} %vp.1), custom_call_target="tpu_custom_call" | custom-call | bytes 1000000 | tf_op jit(solution)/shard_map/pallas_call | solution.py:386
  2.5 3.7 %collective-permute-start.4 = (bf16[192,256]{1,0:T(8,128)(2,1)}, bf16[192,256]{1,0:T(8,128)(2,1)S(1)}, u32[]{:S(2)}, u32[]{:S(2)}) collective-permute-start(bf16[192,256]{1,0:T(8,128)(2,1)} %get-tuple-element.69), channel_id=1, source_target_pairs={{0,128},{1,129},{16,144},{17,145},{32,160},{33,161},{48,176},{49,1... | collective-permute-start | bytes 294920 | tf_op jit(solution)/shard_map/ppermute | solution.py:416
  6.1 5.5 %collective-permute-start.5 = (bf16[192,256]{1,0:T(8,128)(2,1)}, bf16[192,256]{1,0:T(8,128)(2,1)S(1)}, u32[]{:S(2)}, u32[]{:S(2)}) collective-permute-start(bf16[192,256]{1,0:T(8,128)(2,1)} %get-tuple-element.70), channel_id=1, source_target_pairs={{0,144},{1,241},{16,128},{17,161},{32,176},{33,145},{48,160},{49,1... | collective-permute-start | bytes 294920 | tf_op jit(solution)/shard_map/ppermute | solution.py:416
  11.7 2.2 %shard_map.127 = (bf16[128,1024]{1,0:T(8,128)(2,1)}, bf16[128,1024]{1,0:T(8,128)(2,1)}, bf16[128,1024]{1,0:T(8,128)(2,1)}, bf16[128,1024]{1,0:T(8,128)(2,1)}) custom-call(s32[1]{0:T(128)} %bitcast.info, bf16[128,2048]{1,0:T(8,128)(2,1)} %bitcast.15, bf16[128,2048]{1,0:T(8,128)(2,1)} %bitcast.16), custom_call_target="tpu_custom_call" | custom-call | bytes 1000000 | tf_op jit(solution)/shard_map/pallas_call | solution.py:386
  14.1 2.8 %collective-permute-start.1 = (bf16[128,1024]{1,0:T(8,128)(2,1)}, bf16[128,1024]{1,0:T(8,128)(2,1)S(1)}, u32[]{:S(2)}, u32[]{:S(2)}) collective-permute-start(bf16[128,1024]{1,0:T(8,128)(2,1)} %get-tuple-element.65), channel_id=1, source_target_pairs={{0,128},{1,129},{16,144},{17,145},{32,160},{33,161},{48,176},{49,1... | collective-permute-start | bytes 786440 | tf_op jit(solution)/shard_map/ppermute | solution.py:416
  16.8 2.6 %collective-permute-start.3 = (bf16[192,256]{1,0:T(8,128)(2,1)}, bf16[192,256]{1,0:T(8,128)(2,1)S(1)}, u32[]{:S(2)}, u32[]{:S(2)}) collective-permute-start(bf16[192,256]{1,0:T(8,128)(2,1)} %get-tuple-element.68), channel_id=1, source_target_pairs={{0,16},{1,113},{16,0},{17,33},{32,48},{33,17},{48,32},{49,65},{64,... | collective-permute-start | bytes 294920 | tf_op jit(solution)/shard_map/ppermute | solution.py:416
  20.2 1.9 %collective-permute-done.3 = bf16[192,256]{1,0:T(8,128)(2,1)S(1)} collective-permute-done((bf16[192,256]{1,0:T(8,128)(2,1)}, bf16[192,256]{1,0:T(8,128)(2,1)S(1)}, u32[]{:S(2)}, u32[]{:S(2)}) %collective-permute-start.3) | collective-permute-done | bytes 98336 | tf_op jit(solution)/shard_map/ppermute | solution.py:416
  23.0 4.2 %collective-permute-start.10 = (bf16[2,192,256]{2,1,0:T(8,128)(2,1)S(1)}, bf16[2,192,256]{2,1,0:T(8,128)(2,1)S(1)}, u32[]{:S(2)}, u32[]{:S(2)}) collective-permute-start(bf16[2,192,256]{2,1,0:T(8,128)(2,1)S(1)} %pad_maximum_fusion.1.own_b), channel_id=1, source_target_pairs={{0,32},{1,33},{16,48},{17,49},{32,64},{33,65},{48,80},{49,81},{64,... | collective-permute-start | bytes 589832 | tf_op jit(solution)/shard_map/ppermute | solution.py:416
  27.2 1.7 %collective-permute-done.1.qd2 = bf16[128,1024]{1,0:T(8,128)(2,1)S(1)} collective-permute-done((bf16[128,1024]{1,0:T(8,128)(2,1)}, bf16[128,1024]{1,0:T(8,128)(2,1)S(1)}, u32[]{:S(2)}, u32[]{:S(2)}) %collective-permute-start.1) | collective-permute-done | bytes 262176 | tf_op jit(solution)/shard_map/ppermute | solution.py:416
  31.4 3.4 %shard_map.129 = (bf16[2,128,1024]{2,1,0:T(8,128)(2,1)S(1)}, bf16[2,1024,128]{2,1,0:T(8,128)(2,1)S(1)}, bf16[2,128,1024]{2,1,0:T(8,128)(2,1)S(1)}, bf16[1,1280,1...) custom-call(s32[5]{0:T(128)S(1)} %stack.33.info, ...), custom_call_target="tpu_custom_call" | custom-call | flops 1342177280 | bytes 1000000 | tf_op jit(solution)/shard_map/pallas_call | solution.py:386
  34.8 3.5 %collective-permute-start.9 = (bf16[2,192,256]{2,1,0:T(8,128)(2,1)S(1)}, bf16[2,192,256]{2,1,0:T(8,128)(2,1)S(1)}, u32[]{:S(2)}, u32[]{:S(2)}) collective-permute-start(bf16[2,192,256]{2,1,0:T(8,128)(2,1)S(1)} %collective-permute-done.8.right_b), channel_id=1, source_target_pairs={{0,96},{1,97},{16,112},{17,113},{32,0},{33,1},{48,16},{49,17},{64,... | collective-permute-start | bytes 589832 | tf_op jit(solution)/shard_map/ppermute | solution.py:416
  38.3 7.9 %collective-permute-done.10.left_b = bf16[2,192,256]{2,1,0:T(8,128)(2,1)S(1)} collective-permute-done((bf16[2,192,256]{2,1,0:T(8,128)(2,1)S(1)}, bf16[2,192,256]{2,1,0:T(8,128)(2,1)S(1)}, u32[]{:S(2)}, u32[]{:S(2)}) %collective-permute-start.10) | collective-permute-done | bytes 196640 | tf_op jit(solution)/shard_map/ppermute | solution.py:416
  46.1 5.7 %shard_map.130 = (bf16[2,1280,1024]{2,1,0:T(8,128)(2,1)S(1)}, f32[2,1,1024]{2,1,0:T(1,128)S(1)}, f32[2,1,1024]{2,1,0:T(1,128)S(1)}, f32[2,128,1024]{2,1,0:T(8,128)S(1)}) custom-call(s32[5]{0:T(128)S(1)} %stack.33.info, bf16[2,128,1024]{2,1,0:T(8,128)(2,1)S(1)} %get-tuple-element.72.qt, bf16[2,192,256]{2,1,0:T(8,128)(2,1)S(1)} %collective-permute-done.6.left_a, ...), custom_call_target="tpu_custom_call" | custom-call | flops 2684354560 | bytes 1000000 | tf_op jit(solution)/shard_map/pallas_call | solution.py:386
  51.9 5.8 %shard_map.131 = (f32[2,1,1024]{2,1,0:T(1,128)S(1)}, bf16[2,128,1024]{2,1,0:T(8,128)(2,1)S(1)}, bf16[2,1024,128]{2,1,0:T(8,128)(2,1)S(1)}, f32[2,1,1024]{2,1,0:T...) custom-call(s32[5]{0:T(128)S(1)} %stack.33.info, ...), custom_call_target="tpu_custom_call" | custom-call | flops 4026531840 | bytes 1000000 | tf_op jit(solution)/shard_map/pallas_call | solution.py:386
  58.1 3.2 %collective-permute-start.13 = (bf16[2,192,256]{2,1,0:T(8,128)(2,1)S(1)}, bf16[2,192,256]{2,1,0:T(8,128)(2,1)S(1)}, u32[]{:S(2)}, u32[]{:S(2)}) collective-permute-start(bf16[2,192,256]{2,1,0:T(8,128)(2,1)S(1)} %get-tuple-element.94), channel_id=1, source_target_pairs={{0,96},{1,97},{16,112},{17,113},{32,0},{33,1},{48,16},{49,17},{64,... | collective-permute-start | bytes 589832 | tf_op jit(solution)/shard_map/ppermute | solution.py:416
  61.3 6.4 %shard_map.132 = (f32[2,128,1024]{2,1,0:T(8,128)S(1)}, bf16[4,192,256]{2,1,0:T(8,128)(2,1)S(1)}, bf16[4,192,256]{2,1,0:T(8,128)(2,1)S(1)}) custom-call(s32[5]{0:T(128)S(1)} %stack.33.info, bf16[2,1024,128]{2,1,0:T(8,128)(2,1)S(1)} %get-tuple-element.71.q, bf16[2,128,1024]{2,1,0:T(8,128)(2,1)S(1)} %get-tuple-element.80.uplt, ...), custom_call_target="tpu_custom_call" | custom-call | flops 5368709120 | bytes 1000000 | tf_op jit(solution)/shard_map/pallas_call | solution.py:386
  67.7 2.8 %collective-permute-done.12.far_a = bf16[2,192,256]{2,1,0:T(8,128)(2,1)S(1)} collective-permute-done((bf16[2,192,256]{2,1,0:T(8,128)(2,1)S(1)}, bf16[2,192,256]{2,1,0:T(8,128)(2,1)S(1)}, u32[]{:S(2)}, u32[]{:S(2)}) %collective-permute-start.12) | collective-permute-done | bytes 196640 | tf_op jit(solution)/shard_map/ppermute | solution.py:416
  70.5 1.5 %collective-permute-done.13.far_b = bf16[2,192,256]{2,1,0:T(8,128)(2,1)S(1)} collective-permute-done((bf16[2,192,256]{2,1,0:T(8,128)(2,1)S(1)}, bf16[2,192,256]{2,1,0:T(8,128)(2,1)S(1)}, u32[]{:S(2)}, u32[]{:S(2)}) %collective-permute-start.13) | collective-permute-done | bytes 196640 | tf_op jit(solution)/shard_map/ppermute | solution.py:416
  72.4 2.4 %collective-permute-start.15 = (bf16[4,192,256]{2,1,0:T(8,128)(2,1)S(1)}, bf16[4,192,256]{2,1,0:T(8,128)(2,1)S(1)}, u32[]{:S(2)}, u32[]{:S(2)}) collective-permute-start(bf16[4,192,256]{2,1,0:T(8,128)(2,1)S(1)} %get-tuple-element.96), channel_id=1, source_target_pairs={{0,32},{1,33},{16,48},{17,49},{32,64},{33,65},{48,80},{49,81},{64,... | collective-permute-start | bytes 1179656 | tf_op jit(solution)/shard_map/ppermute | solution.py:416
  74.8 4.4 %shard_map.133 = (bf16[4,192,256]{2,1,0:T(8,128)(2,1)S(1)}, bf16[128,1024]{1,0:T(8,128)(2,1)S(1)}, bf16[128,1024]{1,0:T(8,128)(2,1)S(1)}, bf16[128,1024]{1,0:T(8,128)(2,1)S(1)}, bf16[128,1024]{1,0:T(8,128)(2,1)S(1)}) custom-call(s32[5]{0:T(128)S(1)} %stack.33.info, bf16[2,1024,128]{2,1,0:T(8,128)(2,1)S(1)} %get-tuple-element.71.q, ...), custom_call_target="tpu_custom_call" | custom-call | flops 2684354560 | bytes 1000000 | tf_op jit(solution)/shard_map/pallas_call | solution.py:386
  79.3 4.3 %collective-permute-start.20 = (bf16[128,1024]{1,0:T(8,128)(2,1)S(1)}, bf16[128,1024]{1,0:T(8,128)(2,1)S(1)}, u32[]{:S(2)}, u32[]{:S(2)}) collective-permute-start(bf16[128,1024]{1,0:T(8,128)(2,1)S(1)} %get-tuple-element.105), channel_id=1, source_target_pairs={{0,128},{1,129},{16,144},{17,145},{32,160},{33,161},{48,176},{49,1... | collective-permute-start | bytes 786440 | tf_op jit(solution)/shard_map/ppermute | solution.py:416
  83.5 7.5 %collective-permute-done.14.left = bf16[4,192,256]{2,1,0:T(8,128)(2,1)S(1)} collective-permute-done((bf16[4,192,256]{2,1,0:T(8,128)(2,1)S(1)}, bf16[4,192,256]{2,1,0:T(8,128)(2,1)S(1)}, u32[]{:S(2)}, u32[]{:S(2)}) %collective-permute-start.14) | collective-permute-done | bytes 393248 | tf_op jit(solution)/shard_map/ppermute | solution.py:416
  91.3 3.5 %collective-permute-start.17 = (bf16[192,256]{1,0:T(8,128)(2,1)S(1)}, bf16[192,256]{1,0:T(8,128)(2,1)S(1)}, u32[]{:S(2)}, u32[]{:S(2)}) collective-permute-start(bf16[192,256]{1,0:T(8,128)(2,1)S(1)} %get-tuple-element.102), channel_id=1, source_target_pairs={{0,128},{1,129},{16,144},{17,145},{32,160},{33,161},{48,176},{49,1... | collective-permute-start | bytes 294920 | tf_op jit(solution)/shard_map/ppermute | solution.py:416
  94.8 1.8 %collective-permute-start.18 = (bf16[192,256]{1,0:T(8,128)(2,1)S(1)}, bf16[192,256]{1,0:T(8,128)(2,1)S(1)}, u32[]{:S(2)}, u32[]{:S(2)}) collective-permute-start(bf16[192,256]{1,0:T(8,128)(2,1)S(1)} %get-tuple-element.103), channel_id=1, source_target_pairs={{0,144},{1,241},{16,128},{17,161},{32,176},{33,145},{48,160},{49,1... | collective-permute-start | bytes 294920 | tf_op jit(solution)/shard_map/ppermute | solution.py:416
  97.3 4.6 %collective-permute-done.18.g3 = bf16[192,256]{1,0:T(8,128)(2,1)S(1)} collective-permute-done((bf16[192,256]{1,0:T(8,128)(2,1)S(1)}, bf16[192,256]{1,0:T(8,128)(2,1)S(1)}, u32[]{:S(2)}, u32[]{:S(2)}) %collective-permute-start.18) | collective-permute-done | bytes 98336 | tf_op jit(solution)/shard_map/ppermute | solution.py:416
  101.9 1.3 %shard_map.136 = (bf16[128,512]{1,0:T(8,128)(2,1)}, bf16[128,512]{1,0:T(8,128)(2,1)}, bf16[64,1024]{1,0:T(8,128)(2,1)S(1)}) custom-call(s32[5]{0:T(128)S(1)} %stack.33.info, bf16[192,256]{1,0:T(8,128)(2,1)S(1)} %get-tuple-element.108.g0, bf16[192,256]{1,0:T(8,128)(2,1)S(1)} %collective-permute-done.16.g1, bf16[192,256]{1,0:T(8,128)(2,1)S(1)} %collective-permute-done.17.g2, ...), custom_call_target="tpu_custom_call" | custom-call | bytes 1000000 | tf_op jit(solution)/shard_map/pallas_call | solution.py:386
  103.2 5.0 %collective-permute-start.21 = (bf16[64,1024]{1,0:T(8,128)(2,1)S(1)}, bf16[64,1024]{1,0:T(8,128)(2,1)S(1)}, u32[]{:S(2)}, u32[]{:S(2)}) collective-permute-start(bf16[64,1024]{1,0:T(8,128)(2,1)S(1)} %get-tuple-element.112), channel_id=1, source_target_pairs={{0,1},{1,0},{2,3},{3,2},{4,5},{5,4},{6,7},{7,6},{8,9},{9,8},{10,11... | collective-permute-start | bytes 393224 | tf_op jit(solution)/shard_map/ppermute | solution.py:402
  110.1 3.9 %collective-permute-done.22 = bf16[64,1024]{1,0:T(8,128)(2,1)S(1)} collective-permute-done((bf16[64,1024]{1,0:T(8,128)(2,1)S(1)}, bf16[64,1024]{1,0:T(8,128)(2,1)S(1)}, u32[]{:S(2)}, u32[]{:S(2)}) %collective-permute-start.22) | collective-permute-done | bytes 131104 | tf_op jit(solution)/shard_map/ppermute | solution.py:402
  114.0 6.3 %collective-permute-done.23.od3 = bf16[128,1024]{1,0:T(8,128)(2,1)S(1)} collective-permute-done((bf16[128,1024]{1,0:T(8,128)(2,1)S(1)}, bf16[128,1024]{1,0:T(8,128)(2,1)S(1)}, u32[]{:S(2)}, u32[]{:S(2)}) %collective-permute-start.23) | collective-permute-done | bytes 262176 | tf_op jit(solution)/shard_map/ppermute | solution.py:416
  121.9 1.4 %collective-permute-start.24 = (bf16[64,1024]{1,0:T(8,128)(2,1)S(1)}, bf16[64,1024]{1,0:T(8,128)(2,1)S(1)}, u32[]{:S(2)}, u32[]{:S(2)}) collective-permute-start(bf16[64,1024]{1,0:T(8,128)(2,1)S(1)} %add_convert_fusion.1), channel_id=1, source_target_pairs={{0,8},{4,12},{8,0},{12,4},{1,9},{5,13},{9,1},{13,5},{2,10},{6,14},... | collective-permute-start | bytes 393224 | tf_op jit(solution)/shard_map/ppermute | solution.py:407
  123.2 1.6 %shard_map.137 = (bf16[128,2048]{1,0:T(8,128)(2,1)}, bf16[128,2048]{1,0:T(8,128)(2,1)}) custom-call(s32[5]{0:T(128)S(1)} %stack.33.info, bf16[128,1024]{1,0:T(8,128)(2,1)S(1)} %get-tuple-element.89.od0, bf16[128,1024]{1,0:T(8,128)(2,1)S(1)} %collective-permute-done.19.od1, bf16[128,1024]{1,0:T(8,128)(2,1)S(1)} %collective-permute-done.20.od2, ...), custom_call_target="tpu_custom_call" | custom-call | bytes 1000000 | tf_op jit(solution)/shard_map/pallas_call | solution.py:386
  124.8 3.6 %collective-permute-done.25 = bf16[64,1024]{1,0:T(8,128)(2,1)S(1)} collective-permute-done((bf16[64,1024]{1,0:T(8,128)(2,1)S(1)}, bf16[64,1024]{1,0:T(8,128)(2,1)S(1)}, u32[]{:S(2)}, u32[]{:S(2)}) %collective-permute-start.25) | collective-permute-done | bytes 131104 | tf_op jit(solution)/shard_map/ppermute | solution.py:407
  (42 shorter events, 9.0 us)
Async XLA Ops:
  2.5 16.9 %collective-permute-start.4 = (bf16[192,256]{1,0:T(8,128)(2,1)}, bf16[192,256]{1,0:T(8,128)(2,1)S(1)}, u32[]{:S(2)}, u32[]{:S(2)}) collective-permute-start(bf16[192,256]{1,0:T(8,128)(2,1)} %get-tuple-element.69), channel_id=1, source_target_pairs={{0,128},{1,129},{16,144},{17,145},{32,160},{33,161},{48,176},{49,1... | collective-permute-start | bytes 294920 | tf_op jit(solution)/shard_map/ppermute | solution.py:416
  6.1 13.3 %collective-permute-start.5 = (bf16[192,256]{1,0:T(8,128)(2,1)}, bf16[192,256]{1,0:T(8,128)(2,1)S(1)}, u32[]{:S(2)}, u32[]{:S(2)}) collective-permute-start(bf16[192,256]{1,0:T(8,128)(2,1)} %get-tuple-element.70), channel_id=1, source_target_pairs={{0,144},{1,241},{16,128},{17,161},{32,176},{33,145},{48,160},{49,1... | collective-permute-start | bytes 294920 | tf_op jit(solution)/shard_map/ppermute | solution.py:416
  13.9 9.1 %collective-permute-start = (bf16[128,1024]{1,0:T(8,128)(2,1)}, bf16[128,1024]{1,0:T(8,128)(2,1)S(1)}, u32[]{:S(2)}, u32[]{:S(2)}) collective-permute-start(bf16[128,1024]{1,0:T(8,128)(2,1)} %get-tuple-element.64), channel_id=1, source_target_pairs={{0,16},{1,113},{16,0},{17,33},{32,48},{33,17},{48,32},{49,65},{64,... | collective-permute-start | bytes 786440 | tf_op jit(solution)/shard_map/ppermute | solution.py:416
  14.1 14.9 %collective-permute-start.1 = (bf16[128,1024]{1,0:T(8,128)(2,1)}, bf16[128,1024]{1,0:T(8,128)(2,1)S(1)}, u32[]{:S(2)}, u32[]{:S(2)}) collective-permute-start(bf16[128,1024]{1,0:T(8,128)(2,1)} %get-tuple-element.65), channel_id=1, source_target_pairs={{0,128},{1,129},{16,144},{17,145},{32,160},{33,161},{48,176},{49,1... | collective-permute-start | bytes 786440 | tf_op jit(solution)/shard_map/ppermute | solution.py:416
  16.8 5.2 %collective-permute-start.3 = (bf16[192,256]{1,0:T(8,128)(2,1)}, bf16[192,256]{1,0:T(8,128)(2,1)S(1)}, u32[]{:S(2)}, u32[]{:S(2)}) collective-permute-start(bf16[192,256]{1,0:T(8,128)(2,1)} %get-tuple-element.68), channel_id=1, source_target_pairs={{0,16},{1,113},{16,0},{17,33},{32,48},{33,17},{48,32},{49,65},{64,... | collective-permute-start | bytes 294920 | tf_op jit(solution)/shard_map/ppermute | solution.py:416
  19.4 11.0 %collective-permute-start.2 = (bf16[128,1024]{1,0:T(8,128)(2,1)}, bf16[128,1024]{1,0:T(8,128)(2,1)S(1)}, u32[]{:S(2)}, u32[]{:S(2)}) collective-permute-start(bf16[128,1024]{1,0:T(8,128)(2,1)} %get-tuple-element.66), channel_id=1, source_target_pairs={{0,144},{1,241},{16,128},{17,161},{32,176},{33,145},{48,160},{49,1... | collective-permute-start | bytes 786440 | tf_op jit(solution)/shard_map/ppermute | solution.py:416
  19.5 15.3 %collective-permute-start.8 = (bf16[2,192,256]{2,1,0:T(8,128)(2,1)S(1)}, bf16[2,192,256]{2,1,0:T(8,128)(2,1)S(1)}, u32[]{:S(2)}, u32[]{:S(2)}) collective-permute-start(bf16[2,192,256]{2,1,0:T(8,128)(2,1)S(1)} %pad_maximum_fusion.1.own_b), channel_id=1, source_target_pairs={{0,96},{1,97},{16,112},{17,113},{32,0},{33,1},{48,16},{49,17},{64,... | collective-permute-start | bytes 589832 | tf_op jit(solution)/shard_map/ppermute | solution.py:416
  22.9 15.3 %collective-permute-start.6 = (bf16[2,192,256]{2,1,0:T(8,128)(2,1)S(1)}, bf16[2,192,256]{2,1,0:T(8,128)(2,1)S(1)}, u32[]{:S(2)}, u32[]{:S(2)}) collective-permute-start(bf16[2,192,256]{2,1,0:T(8,128)(2,1)S(1)} %pad_maximum_fusion.own_a), channel_id=1, source_target_pairs={{0,32},{1,33},{16,48},{17,49},{32,64},{33,65},{48,80},{49,81},{64,... | collective-permute-start | bytes 589832 | tf_op jit(solution)/shard_map/ppermute | solution.py:416
  23.0 23.1 %collective-permute-start.10 = (bf16[2,192,256]{2,1,0:T(8,128)(2,1)S(1)}, bf16[2,192,256]{2,1,0:T(8,128)(2,1)S(1)}, u32[]{:S(2)}, u32[]{:S(2)}) collective-permute-start(bf16[2,192,256]{2,1,0:T(8,128)(2,1)S(1)} %pad_maximum_fusion.1.own_b), channel_id=1, source_target_pairs={{0,32},{1,33},{16,48},{17,49},{32,64},{33,65},{48,80},{49,81},{64,... | collective-permute-start | bytes 589832 | tf_op jit(solution)/shard_map/ppermute | solution.py:416
  29.0 17.2 %collective-permute-start.11 = (bf16[2,192,256]{2,1,0:T(8,128)(2,1)S(1)}, bf16[2,192,256]{2,1,0:T(8,128)(2,1)S(1)}, u32[]{:S(2)}, u32[]{:S(2)}) collective-permute-start(bf16[2,192,256]{2,1,0:T(8,128)(2,1)S(1)} %pad_maximum_fusion.own_a), channel_id=1, source_target_pairs={{0,96},{1,97},{16,112},{17,113},{32,0},{33,1},{48,16},{49,17},{64,... | collective-permute-start | bytes 589832 | tf_op jit(solution)/shard_map/ppermute | solution.py:416
  30.4 1.0 copy-start
  34.8 17.1 %collective-permute-start.9 = (bf16[2,192,256]{2,1,0:T(8,128)(2,1)S(1)}, bf16[2,192,256]{2,1,0:T(8,128)(2,1)S(1)}, u32[]{:S(2)}, u32[]{:S(2)}) collective-permute-start(bf16[2,192,256]{2,1,0:T(8,128)(2,1)S(1)} %collective-permute-done.8.right_b), channel_id=1, source_target_pairs={{0,96},{1,97},{16,112},{17,113},{32,0},{33,1},{48,16},{49,17},{64,... | collective-permute-start | bytes 589832 | tf_op jit(solution)/shard_map/ppermute | solution.py:416
  38.2 13.6 %collective-permute-start.7 = (bf16[2,192,256]{2,1,0:T(8,128)(2,1)S(1)}, bf16[2,192,256]{2,1,0:T(8,128)(2,1)S(1)}, u32[]{:S(2)}, u32[]{:S(2)}) collective-permute-start(bf16[2,192,256]{2,1,0:T(8,128)(2,1)S(1)} %collective-permute-done.6.left_a), channel_id=1, source_target_pairs={{0,32},{1,33},{16,48},{17,49},{32,64},{33,65},{48,80},{49,81},{64,... | collective-permute-start | bytes 589832 | tf_op jit(solution)/shard_map/ppermute | solution.py:416
  57.6 12.9 %collective-permute-start.12 = (bf16[2,192,256]{2,1,0:T(8,128)(2,1)S(1)}, bf16[2,192,256]{2,1,0:T(8,128)(2,1)S(1)}, u32[]{:S(2)}, u32[]{:S(2)}) collective-permute-start(bf16[2,192,256]{2,1,0:T(8,128)(2,1)S(1)} %get-tuple-element.93), channel_id=1, source_target_pairs={{0,32},{1,33},{16,48},{17,49},{32,64},{33,65},{48,80},{49,81},{64,... | collective-permute-start | bytes 589832 | tf_op jit(solution)/shard_map/ppermute | solution.py:416
  58.1 13.9 %collective-permute-start.13 = (bf16[2,192,256]{2,1,0:T(8,128)(2,1)S(1)}, bf16[2,192,256]{2,1,0:T(8,128)(2,1)S(1)}, u32[]{:S(2)}, u32[]{:S(2)}) collective-permute-start(bf16[2,192,256]{2,1,0:T(8,128)(2,1)S(1)} %get-tuple-element.94), channel_id=1, source_target_pairs={{0,96},{1,97},{16,112},{17,113},{32,0},{33,1},{48,16},{49,17},{64,... | collective-permute-start | bytes 589832 | tf_op jit(solution)/shard_map/ppermute | solution.py:416
  72.1 18.9 %collective-permute-start.14 = (bf16[4,192,256]{2,1,0:T(8,128)(2,1)S(1)}, bf16[4,192,256]{2,1,0:T(8,128)(2,1)S(1)}, u32[]{:S(2)}, u32[]{:S(2)}) collective-permute-start(bf16[4,192,256]{2,1,0:T(8,128)(2,1)S(1)} %get-tuple-element.95), channel_id=1, source_target_pairs={{0,96},{1,97},{16,112},{17,113},{32,0},{33,1},{48,16},{49,17},{64,... | collective-permute-start | bytes 1179656 | tf_op jit(solution)/shard_map/ppermute | solution.py:416
  72.4 18.6 %collective-permute-start.15 = (bf16[4,192,256]{2,1,0:T(8,128)(2,1)S(1)}, bf16[4,192,256]{2,1,0:T(8,128)(2,1)S(1)}, u32[]{:S(2)}, u32[]{:S(2)}) collective-permute-start(bf16[4,192,256]{2,1,0:T(8,128)(2,1)S(1)} %get-tuple-element.96), channel_id=1, source_target_pairs={{0,32},{1,33},{16,48},{17,49},{32,64},{33,65},{48,80},{49,81},{64,... | collective-permute-start | bytes 1179656 | tf_op jit(solution)/shard_map/ppermute | solution.py:416
  79.2 17.5 %collective-permute-start.19 = (bf16[128,1024]{1,0:T(8,128)(2,1)S(1)}, bf16[128,1024]{1,0:T(8,128)(2,1)S(1)}, u32[]{:S(2)}, u32[]{:S(2)}) collective-permute-start(bf16[128,1024]{1,0:T(8,128)(2,1)S(1)} %get-tuple-element.104), channel_id=1, source_target_pairs={{0,16},{1,113},{16,0},{17,33},{32,48},{33,17},{48,32},{49,65},{64,... | collective-permute-start | bytes 786440 | tf_op jit(solution)/shard_map/ppermute | solution.py:416
  79.3 17.4 %collective-permute-start.20 = (bf16[128,1024]{1,0:T(8,128)(2,1)S(1)}, bf16[128,1024]{1,0:T(8,128)(2,1)S(1)}, u32[]{:S(2)}, u32[]{:S(2)}) collective-permute-start(bf16[128,1024]{1,0:T(8,128)(2,1)S(1)} %get-tuple-element.105), channel_id=1, source_target_pairs={{0,128},{1,129},{16,144},{17,145},{32,160},{33,161},{48,176},{49,1... | collective-permute-start | bytes 786440 | tf_op jit(solution)/shard_map/ppermute | solution.py:416
  91.2 6.1 %collective-permute-start.16 = (bf16[192,256]{1,0:T(8,128)(2,1)S(1)}, bf16[192,256]{1,0:T(8,128)(2,1)S(1)}, u32[]{:S(2)}, u32[]{:S(2)}) collective-permute-start(bf16[192,256]{1,0:T(8,128)(2,1)S(1)} %get-tuple-element.101), channel_id=1, source_target_pairs={{0,16},{1,113},{16,0},{17,33},{32,48},{33,17},{48,32},{49,65},{64,... | collective-permute-start | bytes 294920 | tf_op jit(solution)/shard_map/ppermute | solution.py:416
  91.3 6.0 %collective-permute-start.17 = (bf16[192,256]{1,0:T(8,128)(2,1)S(1)}, bf16[192,256]{1,0:T(8,128)(2,1)S(1)}, u32[]{:S(2)}, u32[]{:S(2)}) collective-permute-start(bf16[192,256]{1,0:T(8,128)(2,1)S(1)} %get-tuple-element.102), channel_id=1, source_target_pairs={{0,128},{1,129},{16,144},{17,145},{32,160},{33,161},{48,176},{49,1... | collective-permute-start | bytes 294920 | tf_op jit(solution)/shard_map/ppermute | solution.py:416
  94.8 7.1 %collective-permute-start.18 = (bf16[192,256]{1,0:T(8,128)(2,1)S(1)}, bf16[192,256]{1,0:T(8,128)(2,1)S(1)}, u32[]{:S(2)}, u32[]{:S(2)}) collective-permute-start(bf16[192,256]{1,0:T(8,128)(2,1)S(1)} %get-tuple-element.103), channel_id=1, source_target_pairs={{0,144},{1,241},{16,128},{17,161},{32,176},{33,145},{48,160},{49,1... | collective-permute-start | bytes 294920 | tf_op jit(solution)/shard_map/ppermute | solution.py:416
  103.2 6.0 %collective-permute-start.21 = (bf16[64,1024]{1,0:T(8,128)(2,1)S(1)}, bf16[64,1024]{1,0:T(8,128)(2,1)S(1)}, u32[]{:S(2)}, u32[]{:S(2)}) collective-permute-start(bf16[64,1024]{1,0:T(8,128)(2,1)S(1)} %get-tuple-element.112), channel_id=1, source_target_pairs={{0,1},{1,0},{2,3},{3,2},{4,5},{5,4},{6,7},{7,6},{8,9},{9,8},{10,11... | collective-permute-start | bytes 393224 | tf_op jit(solution)/shard_map/ppermute | solution.py:402
  109.2 4.8 %collective-permute-start.22 = (bf16[64,1024]{1,0:T(8,128)(2,1)S(1)}, bf16[64,1024]{1,0:T(8,128)(2,1)S(1)}, u32[]{:S(2)}, u32[]{:S(2)}) collective-permute-start(bf16[64,1024]{1,0:T(8,128)(2,1)S(1)} %add_convert_fusion.2), channel_id=1, source_target_pairs={{0,2},{2,0},{1,3},{3,1},{4,6},{6,4},{5,7},{7,5},{8,10},{10,8},{9,1... | collective-permute-start | bytes 393224 | tf_op jit(solution)/shard_map/ppermute | solution.py:402
  109.3 11.1 %collective-permute-start.23 = (bf16[128,1024]{1,0:T(8,128)(2,1)S(1)}, bf16[128,1024]{1,0:T(8,128)(2,1)S(1)}, u32[]{:S(2)}, u32[]{:S(2)}) collective-permute-start(bf16[128,1024]{1,0:T(8,128)(2,1)S(1)} %get-tuple-element.113), channel_id=1, source_target_pairs={{0,144},{1,241},{16,128},{17,161},{32,176},{33,145},{48,160},{49,1... | collective-permute-start | bytes 786440 | tf_op jit(solution)/shard_map/ppermute | solution.py:416
  120.4 4.4 %collective-permute-start.26 = (bf16[64,1024]{1,0:T(8,128)(2,1)S(1)}, bf16[64,1024]{1,0:T(8,128)(2,1)S(1)}, u32[]{:S(2)}, u32[]{:S(2)}) collective-permute-start(bf16[64,1024]{1,0:T(8,128)(2,1)S(1)} %add_convert_fusion.1), channel_id=1, source_target_pairs={{0,12},{4,0},{8,4},{12,8},{1,13},{5,1},{9,5},{13,9},{2,14},{6,2},{... | collective-permute-start | bytes 393224 | tf_op jit(solution)/shard_map/ppermute | solution.py:407
  121.6 6.8 %collective-permute-start.25 = (bf16[64,1024]{1,0:T(8,128)(2,1)S(1)}, bf16[64,1024]{1,0:T(8,128)(2,1)S(1)}, u32[]{:S(2)}, u32[]{:S(2)}) collective-permute-start(bf16[64,1024]{1,0:T(8,128)(2,1)S(1)} %add_convert_fusion.1), channel_id=1, source_target_pairs={{0,4},{4,8},{8,12},{12,0},{1,5},{5,9},{9,13},{13,1},{2,6},{6,10},{... | collective-permute-start | bytes 393224 | tf_op jit(solution)/shard_map/ppermute | solution.py:407
  121.9 6.6 %collective-permute-start.24 = (bf16[64,1024]{1,0:T(8,128)(2,1)S(1)}, bf16[64,1024]{1,0:T(8,128)(2,1)S(1)}, u32[]{:S(2)}, u32[]{:S(2)}) collective-permute-start(bf16[64,1024]{1,0:T(8,128)(2,1)S(1)} %add_convert_fusion.1), channel_id=1, source_target_pairs={{0,8},{4,12},{8,0},{12,4},{1,9},{5,13},{9,1},{13,5},{2,10},{6,14},... | collective-permute-start | bytes 393224 | tf_op jit(solution)/shard_map/ppermute | solution.py:407

commit v4 on v3

--- a/solution.py
+++ b/solution.py
@@ -359,15 +359,21 @@
         out[...] = total.astype(BF16)
 
 
-def finish_kernel(info, g0, g1, g2, g3, key_grad, value_grad, share):
+def share_kernel(info, g0, g1, g2, g3, keep, send):
+    mine, first = info[0], info[2] == 0
+    for d, g in enumerate((g0, g1, g2, g3)):
+        at = pl.ds(pl.multiple_of((mine ^ d) * HEAD_DIM, HEAD_DIM), HEAD_DIM)
+        keys, values = g[ROWS:, :HEAD_DIM], g[ROWS:, HEAD_DIM:]
+        keep[:, at] = jnp.where(first, keys, values)
+        send[:, at] = jnp.where(first, values, keys)
+
+
+def finish_kernel(info, g0, g1, g2, g3, key_grad, value_grad):
     mine = info[0]
     for d, g in enumerate((g0, g1, g2, g3)):
         at = pl.ds(pl.multiple_of((mine ^ d) * HEAD_DIM, HEAD_DIM), HEAD_DIM)
         key_grad[:, at] = g[:ROWS, :HEAD_DIM]
         value_grad[:, at] = g[:ROWS, HEAD_DIM:]
-        share[:, at] = g[ROWS:, :HEAD_DIM]
-        at = pl.ds(pl.multiple_of(KV_HEADS * HEAD_DIM + (mine ^ d) * HEAD_DIM, HEAD_DIM), HEAD_DIM)
-        share[:, at] = g[ROWS:, HEAD_DIM:]
 
 
 def bf16(*shape):
@@ -522,36 +528,39 @@
         q, uplt, upl, delta, shift1, shift3, probs1, own_a, own_b, dqt, attn,
         products=4,
     )
-    od[1], od[2] = partner(od[1], 1), partner(od[2], 2)
-    left_g, right_g, od[3] = lax.optimization_barrier((left_g, right_g, od[3]))
-    od[3] = partner(od[3], 3)
+    od[3], od[2] = partner(od[3], 3), partner(od[2], 2)
+    left_g, right_g, od[1] = lax.optimization_barrier((left_g, right_g, od[1]))
+    od[1] = partner(od[1], 1)
     grads = list(call(sum_kernel, (bf16(BOTH, WIDE),) * 4, (), (), own_g, left_g, right_g))
     for d in (1, 2, 3):
         grads[d] = partner(grads[d], d)
-    tied = lax.optimization_barrier((*grads, od[1], od[2]))
-    grads, od[1:3] = tied[:4], tied[4:]
+    tied = lax.optimization_barrier((*grads, od[2], od[3]))
+    grads, od[2:] = tied[:4], tied[4:]
     rows = bf16(ROWS, HEADS * HEAD_DIM)
-    key_grad, value_grad, share = call(
-        finish_kernel,
-        (bf16(ROWS, width), bf16(ROWS, width), bf16(PROWS, 2 * width)),
-        (),
-        (info,),
-        *grads,
-    )
-    for axis in ("core", "xl"):
-        share = rounded(share.astype(F32) + swap(share, axis).astype(F32))
-    share, od[3] = lax.optimization_barrier((share, od[3]))
+    keep, send = call(share_kernel, (bf16(PROWS, width),) * 2, (), (info,), *grads)
+    share = rounded(keep.astype(F32) + swap(send, "core").astype(F32))
+    share = rounded(share.astype(F32) + swap(share, "xl").astype(F32))
+    share, od[1] = lax.optimization_barrier((share, od[1]))
     across = share.astype(F32) + turn(share, "y", 2).astype(F32)
     beside = turn(share, "y", 1).astype(F32) + turn(share, "y", 3).astype(F32)
     share = (across + beside).astype(BF16)
+    key_grad, value_grad = call(
+        finish_kernel, (bf16(ROWS, width),) * 2, (), (info,), *grads
+    )
     attended, query_grad = call(unpack_kernel, (rows, rows), (), (info,), *od)
+    share, key_grad, value_grad, attended, query_grad = lax.optimization_barrier(
+        (share, key_grad, value_grad, attended, query_grad)
+    )
+    other = swap(share, "core")
+    key_share = jnp.where(core == 0, share, other)
+    value_share = jnp.where(core == 0, other, share)
     return (
         attended[None],
         query_grad[None],
         key_grad[None],
         value_grad[None],
-        share[:, :width],
-        share[:, width:],
+        key_share,
+        value_share,
     )
 
 

time: 131 us -> 125 us (0.954); the launches traced: 129 us -> 125 us
  waiting for transfers between devices: 43.4 us -> 37.8 us
    ppermute x22, waiting for transfers between devices: 34.9 us -> 32.1 us  [local_permute(): return lax.ppermute(x, LOCAL, pairs)]
    ppermute x3, waiting for transfers between devices: 3.62 us -> 0.88 us  [turn(): return lax.ppermute(x, axis, [(i, (i + step) % size) for i in range(size)])]
    ppermute x2 -> x3, starting transfers between devices: 5.06 us -> 6.01 us  [swap(): return lax.ppermute(x, axis, [(0, 1), (1, 0)])]
    pallas_call x11 -> x12, Pallas kernels: 32.9 us -> 33.4 us  [call(): pl.pallas_call(kernel, out_shape=tuple(outs), in_specs=[SMEM] * len(scala...]
    ppermute x2 -> x3, waiting for transfers between devices: 4.89 us -> 4.81 us  [swap(): return lax.ppermute(x, axis, [(0, 1), (1, 0)])]
  transfers between devices with their start and end apart: 27 -> 28, of which waited for: 12 -> 15; matrix products, arithmetic and copies ran while one was open for 1% -> 1% of each run, Pallas kernels for 18% -> 20%
where the time goes in v4:
time: 125 us
  starting transfers between devices  49 us (39%)
  waiting for transfers between devices  37.8 us (30%)
  Pallas kernels  33.4 us (27%)
  between operations  2.18 us (2%)
  other arithmetic  1.67 us (1%)
    ppermute x22, starting transfers between devices, local_permute(): return lax.ppermute(x, LOCAL, pairs)  39.2 us
    pallas_call x12, Pallas kernels, call(): pl.pallas_call(kernel, out_shape=tuple(outs), in_specs=[SMEM] * len(scala...  33.4 us
    ppermute x22, waiting for transfers between devices, local_permute(): return lax.ppermute(x, LOCAL, pairs)  32.1 us
    ppermute x3, starting transfers between devices, swap(): return lax.ppermute(x, axis, [(0, 1), (1, 0)])  6.01 us
    ppermute x3, waiting for transfers between devices, swap(): return lax.ppermute(x, axis, [(0, 1), (1, 0)])  4.81 us
    ppermute x3, starting transfers between devices, turn(): return lax.ppermute(x, axis, [(i, (i + step) % size) for i in range(size)])  3.81 us
  transfers between devices with their start and end apart: 28, of which 15 were waited for; matrix products, arithmetic and copies ran while one was open for 1% of the time, Pallas kernels for 20%

profile of v4, /device:TPU:1, one launch (start us, length us, event | category | flops | bytes accessed | tf_op | source)
XLA Modules:
  0.0 125.1 jit_solution(3902303288723440301)
XLA Ops:
  0.6 1.8 %shard_map.128 = (bf16[192,256]{1,0:T(8,128)(2,1)}, bf16[192,256]{1,0:T(8,128)(2,1)}, bf16[192,256]{1,0:T(8,128)(2,1)}, bf16[192,256]{1,0:T(8,128)(2,1)}) custom-call(s32[1]{0:T(128)} %bitcast.info, bf16[128,512]{1,0:T(8,128)(2,1)} %bitcast.17, bf16[128,512]{1,0:T(8,128)(2,1)} %bitcast.18, bf16[64,512]{1,0:T(8,128)(2,1)} %kp.1, bf16[64,512]{1,0:T(8,128)(2,1)} %vp.1), custom_call_target="tpu_custom_call" | custom-call | bytes 1000000 | tf_op jit(solution)/shard_map/pallas_call | solution.py:392
  2.5 3.7 %collective-permute-start.4 = (bf16[192,256]{1,0:T(8,128)(2,1)}, bf16[192,256]{1,0:T(8,128)(2,1)S(1)}, u32[]{:S(2)}, u32[]{:S(2)}) collective-permute-start(bf16[192,256]{1,0:T(8,128)(2,1)} %get-tuple-element.75), channel_id=1, source_target_pairs={{0,128},{1,129},{16,144},{17,145},{32,160},{33,161},{48,176},{49,1... | collective-permute-start | bytes 294920 | tf_op jit(solution)/shard_map/ppermute | solution.py:422
  6.1 5.5 %collective-permute-start.5 = (bf16[192,256]{1,0:T(8,128)(2,1)}, bf16[192,256]{1,0:T(8,128)(2,1)S(1)}, u32[]{:S(2)}, u32[]{:S(2)}) collective-permute-start(bf16[192,256]{1,0:T(8,128)(2,1)} %get-tuple-element.76), channel_id=1, source_target_pairs={{0,144},{1,241},{16,128},{17,161},{32,176},{33,145},{48,160},{49,1... | collective-permute-start | bytes 294920 | tf_op jit(solution)/shard_map/ppermute | solution.py:422
  11.7 2.2 %shard_map.127 = (bf16[128,1024]{1,0:T(8,128)(2,1)}, bf16[128,1024]{1,0:T(8,128)(2,1)}, bf16[128,1024]{1,0:T(8,128)(2,1)}, bf16[128,1024]{1,0:T(8,128)(2,1)}) custom-call(s32[1]{0:T(128)} %bitcast.info, bf16[128,2048]{1,0:T(8,128)(2,1)} %bitcast.15, bf16[128,2048]{1,0:T(8,128)(2,1)} %bitcast.16), custom_call_target="tpu_custom_call" | custom-call | bytes 1000000 | tf_op jit(solution)/shard_map/pallas_call | solution.py:392
  14.1 2.8 %collective-permute-start.1 = (bf16[128,1024]{1,0:T(8,128)(2,1)}, bf16[128,1024]{1,0:T(8,128)(2,1)S(1)}, u32[]{:S(2)}, u32[]{:S(2)}) collective-permute-start(bf16[128,1024]{1,0:T(8,128)(2,1)} %get-tuple-element.71), channel_id=1, source_target_pairs={{0,128},{1,129},{16,144},{17,145},{32,160},{33,161},{48,176},{49,1... | collective-permute-start | bytes 786440 | tf_op jit(solution)/shard_map/ppermute | solution.py:422
  16.8 2.6 %collective-permute-start.3 = (bf16[192,256]{1,0:T(8,128)(2,1)}, bf16[192,256]{1,0:T(8,128)(2,1)S(1)}, u32[]{:S(2)}, u32[]{:S(2)}) collective-permute-start(bf16[192,256]{1,0:T(8,128)(2,1)} %get-tuple-element.74), channel_id=1, source_target_pairs={{0,16},{1,113},{16,0},{17,33},{32,48},{33,17},{48,32},{49,65},{64,... | collective-permute-start | bytes 294920 | tf_op jit(solution)/shard_map/ppermute | solution.py:422
  20.2 1.9 %collective-permute-done.3 = bf16[192,256]{1,0:T(8,128)(2,1)S(1)} collective-permute-done((bf16[192,256]{1,0:T(8,128)(2,1)}, bf16[192,256]{1,0:T(8,128)(2,1)S(1)}, u32[]{:S(2)}, u32[]{:S(2)}) %collective-permute-start.3) | collective-permute-done | bytes 98336 | tf_op jit(solution)/shard_map/ppermute | solution.py:422
  23.0 4.2 %collective-permute-start.10 = (bf16[2,192,256]{2,1,0:T(8,128)(2,1)S(1)}, bf16[2,192,256]{2,1,0:T(8,128)(2,1)S(1)}, u32[]{:S(2)}, u32[]{:S(2)}) collective-permute-start(bf16[2,192,256]{2,1,0:T(8,128)(2,1)S(1)} %pad_maximum_fusion.1.own_b), channel_id=1, source_target_pairs={{0,32},{1,33},{16,48},{17,49},{32,64},{33,65},{48,80},{49,81},{64,... | collective-permute-start | bytes 589832 | tf_op jit(solution)/shard_map/ppermute | solution.py:422
  27.2 1.7 %collective-permute-done.1.qd2 = bf16[128,1024]{1,0:T(8,128)(2,1)S(1)} collective-permute-done((bf16[128,1024]{1,0:T(8,128)(2,1)}, bf16[128,1024]{1,0:T(8,128)(2,1)S(1)}, u32[]{:S(2)}, u32[]{:S(2)}) %collective-permute-start.1) | collective-permute-done | bytes 262176 | tf_op jit(solution)/shard_map/ppermute | solution.py:422
  31.4 3.4 %shard_map.129 = (bf16[2,128,1024]{2,1,0:T(8,128)(2,1)S(1)}, bf16[2,1024,128]{2,1,0:T(8,128)(2,1)S(1)}, bf16[2,128,1024]{2,1,0:T(8,128)(2,1)S(1)}, bf16[1,1280,1...) custom-call(s32[5]{0:T(128)S(1)} %stack.33.info, ...), custom_call_target="tpu_custom_call" | custom-call | flops 1342177280 | bytes 1000000 | tf_op jit(solution)/shard_map/pallas_call | solution.py:392
  34.8 3.5 %collective-permute-start.9 = (bf16[2,192,256]{2,1,0:T(8,128)(2,1)S(1)}, bf16[2,192,256]{2,1,0:T(8,128)(2,1)S(1)}, u32[]{:S(2)}, u32[]{:S(2)}) collective-permute-start(bf16[2,192,256]{2,1,0:T(8,128)(2,1)S(1)} %collective-permute-done.8.right_b), channel_id=1, source_target_pairs={{0,96},{1,97},{16,112},{17,113},{32,0},{33,1},{48,16},{49,17},{64,... | collective-permute-start | bytes 589832 | tf_op jit(solution)/shard_map/ppermute | solution.py:422
  38.2 7.9 %collective-permute-done.10.left_b = bf16[2,192,256]{2,1,0:T(8,128)(2,1)S(1)} collective-permute-done((bf16[2,192,256]{2,1,0:T(8,128)(2,1)S(1)}, bf16[2,192,256]{2,1,0:T(8,128)(2,1)S(1)}, u32[]{:S(2)}, u32[]{:S(2)}) %collective-permute-start.10) | collective-permute-done | bytes 196640 | tf_op jit(solution)/shard_map/ppermute | solution.py:422
  46.1 5.7 %shard_map.130 = (bf16[2,1280,1024]{2,1,0:T(8,128)(2,1)S(1)}, f32[2,1,1024]{2,1,0:T(1,128)S(1)}, f32[2,1,1024]{2,1,0:T(1,128)S(1)}, f32[2,128,1024]{2,1,0:T(8,128)S(1)}) custom-call(s32[5]{0:T(128)S(1)} %stack.33.info, bf16[2,128,1024]{2,1,0:T(8,128)(2,1)S(1)} %get-tuple-element.78.qt, bf16[2,192,256]{2,1,0:T(8,128)(2,1)S(1)} %collective-permute-done.6.left_a, ...), custom_call_target="tpu_custom_call" | custom-call | flops 2684354560 | bytes 1000000 | tf_op jit(solution)/shard_map/pallas_call | solution.py:392
  51.9 5.8 %shard_map.131 = (f32[2,1,1024]{2,1,0:T(1,128)S(1)}, bf16[2,128,1024]{2,1,0:T(8,128)(2,1)S(1)}, bf16[2,1024,128]{2,1,0:T(8,128)(2,1)S(1)}, f32[2,1,1024]{2,1,0:T...) custom-call(s32[5]{0:T(128)S(1)} %stack.33.info, ...), custom_call_target="tpu_custom_call" | custom-call | flops 4026531840 | bytes 1000000 | tf_op jit(solution)/shard_map/pallas_call | solution.py:392
  58.1 3.2 %collective-permute-start.13 = (bf16[2,192,256]{2,1,0:T(8,128)(2,1)S(1)}, bf16[2,192,256]{2,1,0:T(8,128)(2,1)S(1)}, u32[]{:S(2)}, u32[]{:S(2)}) collective-permute-start(bf16[2,192,256]{2,1,0:T(8,128)(2,1)S(1)} %get-tuple-element.99), channel_id=1, source_target_pairs={{0,96},{1,97},{16,112},{17,113},{32,0},{33,1},{48,16},{49,17},{64,... | collective-permute-start | bytes 589832 | tf_op jit(solution)/shard_map/ppermute | solution.py:422
  61.3 6.4 %shard_map.132 = (f32[2,128,1024]{2,1,0:T(8,128)S(1)}, bf16[4,192,256]{2,1,0:T(8,128)(2,1)S(1)}, bf16[4,192,256]{2,1,0:T(8,128)(2,1)S(1)}) custom-call(s32[5]{0:T(128)S(1)} %stack.33.info, bf16[2,1024,128]{2,1,0:T(8,128)(2,1)S(1)} %get-tuple-element.77.q, bf16[2,128,1024]{2,1,0:T(8,128)(2,1)S(1)} %get-tuple-element.86.uplt, ...), custom_call_target="tpu_custom_call" | custom-call | flops 5368709120 | bytes 1000000 | tf_op jit(solution)/shard_map/pallas_call | solution.py:392
  67.7 2.8 %collective-permute-done.12.far_a = bf16[2,192,256]{2,1,0:T(8,128)(2,1)S(1)} collective-permute-done((bf16[2,192,256]{2,1,0:T(8,128)(2,1)S(1)}, bf16[2,192,256]{2,1,0:T(8,128)(2,1)S(1)}, u32[]{:S(2)}, u32[]{:S(2)}) %collective-permute-start.12) | collective-permute-done | bytes 196640 | tf_op jit(solution)/shard_map/ppermute | solution.py:422
  70.5 1.5 %collective-permute-done.13.far_b = bf16[2,192,256]{2,1,0:T(8,128)(2,1)S(1)} collective-permute-done((bf16[2,192,256]{2,1,0:T(8,128)(2,1)S(1)}, bf16[2,192,256]{2,1,0:T(8,128)(2,1)S(1)}, u32[]{:S(2)}, u32[]{:S(2)}) %collective-permute-start.13) | collective-permute-done | bytes 196640 | tf_op jit(solution)/shard_map/ppermute | solution.py:422
  72.4 2.4 %collective-permute-start.15 = (bf16[4,192,256]{2,1,0:T(8,128)(2,1)S(1)}, bf16[4,192,256]{2,1,0:T(8,128)(2,1)S(1)}, u32[]{:S(2)}, u32[]{:S(2)}) collective-permute-start(bf16[4,192,256]{2,1,0:T(8,128)(2,1)S(1)} %get-tuple-element.101), channel_id=1, source_target_pairs={{0,32},{1,33},{16,48},{17,49},{32,64},{33,65},{48,80},{49,81},{64,... | collective-permute-start | bytes 1179656 | tf_op jit(solution)/shard_map/ppermute | solution.py:422
  74.7 4.4 %shard_map.133 = (bf16[4,192,256]{2,1,0:T(8,128)(2,1)S(1)}, bf16[128,1024]{1,0:T(8,128)(2,1)S(1)}, bf16[128,1024]{1,0:T(8,128)(2,1)S(1)}, bf16[128,1024]{1,0:T(8,128)(2,1)S(1)}, bf16[128,1024]{1,0:T(8,128)(2,1)S(1)}) custom-call(s32[5]{0:T(128)S(1)} %stack.33.info, bf16[2,1024,128]{2,1,0:T(8,128)(2,1)S(1)} %get-tuple-element.77.q, ...), custom_call_target="tpu_custom_call" | custom-call | flops 2684354560 | bytes 1000000 | tf_op jit(solution)/shard_map/pallas_call | solution.py:392
  79.2 4.1 %collective-permute-start.20 = (bf16[128,1024]{1,0:T(8,128)(2,1)S(1)}, bf16[128,1024]{1,0:T(8,128)(2,1)S(1)}, u32[]{:S(2)}, u32[]{:S(2)}) collective-permute-start(bf16[128,1024]{1,0:T(8,128)(2,1)S(1)} %get-tuple-element.110), channel_id=1, source_target_pairs={{0,144},{1,241},{16,128},{17,161},{32,176},{33,145},{48,160},{49,1... | collective-permute-start | bytes 786440 | tf_op jit(solution)/shard_map/ppermute | solution.py:422
  83.4 7.6 %collective-permute-done.14.left = bf16[4,192,256]{2,1,0:T(8,128)(2,1)S(1)} collective-permute-done((bf16[4,192,256]{2,1,0:T(8,128)(2,1)S(1)}, bf16[4,192,256]{2,1,0:T(8,128)(2,1)S(1)}, u32[]{:S(2)}, u32[]{:S(2)}) %collective-permute-start.14) | collective-permute-done | bytes 393248 | tf_op jit(solution)/shard_map/ppermute | solution.py:422
  91.3 3.5 %collective-permute-start.17 = (bf16[192,256]{1,0:T(8,128)(2,1)S(1)}, bf16[192,256]{1,0:T(8,128)(2,1)S(1)}, u32[]{:S(2)}, u32[]{:S(2)}) collective-permute-start(bf16[192,256]{1,0:T(8,128)(2,1)S(1)} %get-tuple-element.107), channel_id=1, source_target_pairs={{0,128},{1,129},{16,144},{17,145},{32,160},{33,161},{48,176},{49,1... | collective-permute-start | bytes 294920 | tf_op jit(solution)/shard_map/ppermute | solution.py:422
  94.8 1.8 %collective-permute-start.18 = (bf16[192,256]{1,0:T(8,128)(2,1)S(1)}, bf16[192,256]{1,0:T(8,128)(2,1)S(1)}, u32[]{:S(2)}, u32[]{:S(2)}) collective-permute-start(bf16[192,256]{1,0:T(8,128)(2,1)S(1)} %get-tuple-element.108), channel_id=1, source_target_pairs={{0,144},{1,241},{16,128},{17,161},{32,176},{33,145},{48,160},{49,1... | collective-permute-start | bytes 294920 | tf_op jit(solution)/shard_map/ppermute | solution.py:422
  98.3 3.6 %collective-permute-done.18.g3 = bf16[192,256]{1,0:T(8,128)(2,1)S(1)} collective-permute-done((bf16[192,256]{1,0:T(8,128)(2,1)S(1)}, bf16[192,256]{1,0:T(8,128)(2,1)S(1)}, u32[]{:S(2)}, u32[]{:S(2)}) %collective-permute-start.18) | collective-permute-done | bytes 98336 | tf_op jit(solution)/shard_map/ppermute | solution.py:422
  102.5 4.1 %collective-permute-start.21 = (bf16[64,512]{1,0:T(8,128)(2,1)S(1)}, bf16[64,512]{1,0:T(8,128)(2,1)S(1)}, u32[]{:S(2)}, u32[]{:S(2)}) collective-permute-start(bf16[64,512]{1,0:T(8,128)(2,1)S(1)} %get-tuple-element.116), channel_id=1, source_target_pairs={{0,1},{1,0},{2,3},{3,2},{4,5},{5,4},{6,7},{7,6},{8,9},{9,8},{10,11... | collective-permute-start | bytes 196616 | tf_op jit(solution)/shard_map/ppermute | solution.py:408
  107.7 3.0 %collective-permute-done.22 = bf16[64,512]{1,0:T(8,128)(2,1)S(1)} collective-permute-done((bf16[64,512]{1,0:T(8,128)(2,1)S(1)}, bf16[64,512]{1,0:T(8,128)(2,1)S(1)}, u32[]{:S(2)}, u32[]{:S(2)}) %collective-permute-start.22) | collective-permute-done | bytes 65568 | tf_op jit(solution)/shard_map/ppermute | solution.py:408
  110.7 3.4 %collective-permute-done.23.od1 = bf16[128,1024]{1,0:T(8,128)(2,1)S(1)} collective-permute-done((bf16[128,1024]{1,0:T(8,128)(2,1)S(1)}, bf16[128,1024]{1,0:T(8,128)(2,1)S(1)}, u32[]{:S(2)}, u32[]{:S(2)}) %collective-permute-start.23) | collective-permute-done | bytes 262176 | tf_op jit(solution)/shard_map/ppermute | solution.py:422
  114.1 2.2 %collective-permute-start.26 = (bf16[64,512]{1,0:T(8,128)(2,1)S(1)}, bf16[64,512]{1,0:T(8,128)(2,1)S(1)}, u32[]{:S(2)}, u32[]{:S(2)}) collective-permute-start(bf16[64,512]{1,0:T(8,128)(2,1)S(1)} %add_convert_fusion.1), channel_id=1, source_target_pairs={{0,12},{4,0},{8,4},{12,8},{1,13},{5,1},{9,5},{13,9},{2,14},{6,2},{... | collective-permute-start | bytes 196616 | tf_op jit(solution)/shard_map/ppermute | solution.py:413
  116.3 1.6 %collective-permute-start.24 = (bf16[64,512]{1,0:T(8,128)(2,1)S(1)}, bf16[64,512]{1,0:T(8,128)(2,1)S(1)}, u32[]{:S(2)}, u32[]{:S(2)}) collective-permute-start(bf16[64,512]{1,0:T(8,128)(2,1)S(1)} %add_convert_fusion.1), channel_id=1, source_target_pairs={{0,8},{4,12},{8,0},{12,4},{1,9},{5,13},{9,1},{13,5},{2,10},{6,14},... | collective-permute-start | bytes 196616 | tf_op jit(solution)/shard_map/ppermute | solution.py:413
  119.2 1.6 %shard_map.138 = (bf16[128,2048]{1,0:T(8,128)(2,1)}, bf16[128,2048]{1,0:T(8,128)(2,1)}) custom-call(s32[5]{0:T(128)S(1)} %stack.33.info, bf16[128,1024]{1,0:T(8,128)(2,1)S(1)} %get-tuple-element.121.od0, bf16[128,1024]{1,0:T(8,128)(2,1)S(1)} %collective-permute-done.23.od1, bf16[128,1024]{1,0:T(8,128)(2,1)S(1)} %collective-permute-done.19.od2, ...), custom_call_target="tpu_custom_call" | custom-call | bytes 1000000 | tf_op jit(solution)/shard_map/pallas_call | solution.py:392
  121.7 1.8 %collective-permute-start.27 = (bf16[64,512]{1,0:T(8,128)(2,1)S(1)}, bf16[64,512]{1,0:T(8,128)(2,1)S(1)}, u32[]{:S(2)}, u32[]{:S(2)}) collective-permute-start(bf16[64,512]{1,0:T(8,128)(2,1)S(1)} %add_convert_fusion), channel_id=1, source_target_pairs={{0,1},{1,0},{2,3},{3,2},{4,5},{5,4},{6,7},{7,6},{8,9},{9,8},{10,11... | collective-permute-start | bytes 196616 | tf_op jit(solution)/shard_map/ppermute | solution.py:408
  (45 shorter events, 11.2 us)
Async XLA Ops:
  2.5 16.9 %collective-permute-start.4 = (bf16[192,256]{1,0:T(8,128)(2,1)}, bf16[192,256]{1,0:T(8,128)(2,1)S(1)}, u32[]{:S(2)}, u32[]{:S(2)}) collective-permute-start(bf16[192,256]{1,0:T(8,128)(2,1)} %get-tuple-element.75), channel_id=1, source_target_pairs={{0,128},{1,129},{16,144},{17,145},{32,160},{33,161},{48,176},{49,1... | collective-permute-start | bytes 294920 | tf_op jit(solution)/shard_map/ppermute | solution.py:422
  6.1 13.3 %collective-permute-start.5 = (bf16[192,256]{1,0:T(8,128)(2,1)}, bf16[192,256]{1,0:T(8,128)(2,1)S(1)}, u32[]{:S(2)}, u32[]{:S(2)}) collective-permute-start(bf16[192,256]{1,0:T(8,128)(2,1)} %get-tuple-element.76), channel_id=1, source_target_pairs={{0,144},{1,241},{16,128},{17,161},{32,176},{33,145},{48,160},{49,1... | collective-permute-start | bytes 294920 | tf_op jit(solution)/shard_map/ppermute | solution.py:422
  13.9 9.1 %collective-permute-start = (bf16[128,1024]{1,0:T(8,128)(2,1)}, bf16[128,1024]{1,0:T(8,128)(2,1)S(1)}, u32[]{:S(2)}, u32[]{:S(2)}) collective-permute-start(bf16[128,1024]{1,0:T(8,128)(2,1)} %get-tuple-element.70), channel_id=1, source_target_pairs={{0,16},{1,113},{16,0},{17,33},{32,48},{33,17},{48,32},{49,65},{64,... | collective-permute-start | bytes 786440 | tf_op jit(solution)/shard_map/ppermute | solution.py:422
  14.1 14.9 %collective-permute-start.1 = (bf16[128,1024]{1,0:T(8,128)(2,1)}, bf16[128,1024]{1,0:T(8,128)(2,1)S(1)}, u32[]{:S(2)}, u32[]{:S(2)}) collective-permute-start(bf16[128,1024]{1,0:T(8,128)(2,1)} %get-tuple-element.71), channel_id=1, source_target_pairs={{0,128},{1,129},{16,144},{17,145},{32,160},{33,161},{48,176},{49,1... | collective-permute-start | bytes 786440 | tf_op jit(solution)/shard_map/ppermute | solution.py:422
  16.8 5.2 %collective-permute-start.3 = (bf16[192,256]{1,0:T(8,128)(2,1)}, bf16[192,256]{1,0:T(8,128)(2,1)S(1)}, u32[]{:S(2)}, u32[]{:S(2)}) collective-permute-start(bf16[192,256]{1,0:T(8,128)(2,1)} %get-tuple-element.74), channel_id=1, source_target_pairs={{0,16},{1,113},{16,0},{17,33},{32,48},{33,17},{48,32},{49,65},{64,... | collective-permute-start | bytes 294920 | tf_op jit(solution)/shard_map/ppermute | solution.py:422
  19.4 11.0 %collective-permute-start.2 = (bf16[128,1024]{1,0:T(8,128)(2,1)}, bf16[128,1024]{1,0:T(8,128)(2,1)S(1)}, u32[]{:S(2)}, u32[]{:S(2)}) collective-permute-start(bf16[128,1024]{1,0:T(8,128)(2,1)} %get-tuple-element.72), channel_id=1, source_target_pairs={{0,144},{1,241},{16,128},{17,161},{32,176},{33,145},{48,160},{49,1... | collective-permute-start | bytes 786440 | tf_op jit(solution)/shard_map/ppermute | solution.py:422
  19.5 15.3 %collective-permute-start.8 = (bf16[2,192,256]{2,1,0:T(8,128)(2,1)S(1)}, bf16[2,192,256]{2,1,0:T(8,128)(2,1)S(1)}, u32[]{:S(2)}, u32[]{:S(2)}) collective-permute-start(bf16[2,192,256]{2,1,0:T(8,128)(2,1)S(1)} %pad_maximum_fusion.1.own_b), channel_id=1, source_target_pairs={{0,96},{1,97},{16,112},{17,113},{32,0},{33,1},{48,16},{49,17},{64,... | collective-permute-start | bytes 589832 | tf_op jit(solution)/shard_map/ppermute | solution.py:422
  22.9 15.3 %collective-permute-start.6 = (bf16[2,192,256]{2,1,0:T(8,128)(2,1)S(1)}, bf16[2,192,256]{2,1,0:T(8,128)(2,1)S(1)}, u32[]{:S(2)}, u32[]{:S(2)}) collective-permute-start(bf16[2,192,256]{2,1,0:T(8,128)(2,1)S(1)} %pad_maximum_fusion.own_a), channel_id=1, source_target_pairs={{0,32},{1,33},{16,48},{17,49},{32,64},{33,65},{48,80},{49,81},{64,... | collective-permute-start | bytes 589832 | tf_op jit(solution)/shard_map/ppermute | solution.py:422
  23.0 23.1 %collective-permute-start.10 = (bf16[2,192,256]{2,1,0:T(8,128)(2,1)S(1)}, bf16[2,192,256]{2,1,0:T(8,128)(2,1)S(1)}, u32[]{:S(2)}, u32[]{:S(2)}) collective-permute-start(bf16[2,192,256]{2,1,0:T(8,128)(2,1)S(1)} %pad_maximum_fusion.1.own_b), channel_id=1, source_target_pairs={{0,32},{1,33},{16,48},{17,49},{32,64},{33,65},{48,80},{49,81},{64,... | collective-permute-start | bytes 589832 | tf_op jit(solution)/shard_map/ppermute | solution.py:422
  29.0 17.2 %collective-permute-start.11 = (bf16[2,192,256]{2,1,0:T(8,128)(2,1)S(1)}, bf16[2,192,256]{2,1,0:T(8,128)(2,1)S(1)}, u32[]{:S(2)}, u32[]{:S(2)}) collective-permute-start(bf16[2,192,256]{2,1,0:T(8,128)(2,1)S(1)} %pad_maximum_fusion.own_a), channel_id=1, source_target_pairs={{0,96},{1,97},{16,112},{17,113},{32,0},{33,1},{48,16},{49,17},{64,... | collective-permute-start | bytes 589832 | tf_op jit(solution)/shard_map/ppermute | solution.py:422
  30.4 1.0 copy-start
  34.8 17.1 %collective-permute-start.9 = (bf16[2,192,256]{2,1,0:T(8,128)(2,1)S(1)}, bf16[2,192,256]{2,1,0:T(8,128)(2,1)S(1)}, u32[]{:S(2)}, u32[]{:S(2)}) collective-permute-start(bf16[2,192,256]{2,1,0:T(8,128)(2,1)S(1)} %collective-permute-done.8.right_b), channel_id=1, source_target_pairs={{0,96},{1,97},{16,112},{17,113},{32,0},{33,1},{48,16},{49,17},{64,... | collective-permute-start | bytes 589832 | tf_op jit(solution)/shard_map/ppermute | solution.py:422
  38.2 13.6 %collective-permute-start.7 = (bf16[2,192,256]{2,1,0:T(8,128)(2,1)S(1)}, bf16[2,192,256]{2,1,0:T(8,128)(2,1)S(1)}, u32[]{:S(2)}, u32[]{:S(2)}) collective-permute-start(bf16[2,192,256]{2,1,0:T(8,128)(2,1)S(1)} %collective-permute-done.6.left_a), channel_id=1, source_target_pairs={{0,32},{1,33},{16,48},{17,49},{32,64},{33,65},{48,80},{49,81},{64,... | collective-permute-start | bytes 589832 | tf_op jit(solution)/shard_map/ppermute | solution.py:422
  57.6 12.8 %collective-permute-start.12 = (bf16[2,192,256]{2,1,0:T(8,128)(2,1)S(1)}, bf16[2,192,256]{2,1,0:T(8,128)(2,1)S(1)}, u32[]{:S(2)}, u32[]{:S(2)}) collective-permute-start(bf16[2,192,256]{2,1,0:T(8,128)(2,1)S(1)} %get-tuple-element.98), channel_id=1, source_target_pairs={{0,32},{1,33},{16,48},{17,49},{32,64},{33,65},{48,80},{49,81},{64,... | collective-permute-start | bytes 589832 | tf_op jit(solution)/shard_map/ppermute | solution.py:422
  58.1 13.9 %collective-permute-start.13 = (bf16[2,192,256]{2,1,0:T(8,128)(2,1)S(1)}, bf16[2,192,256]{2,1,0:T(8,128)(2,1)S(1)}, u32[]{:S(2)}, u32[]{:S(2)}) collective-permute-start(bf16[2,192,256]{2,1,0:T(8,128)(2,1)S(1)} %get-tuple-element.99), channel_id=1, source_target_pairs={{0,96},{1,97},{16,112},{17,113},{32,0},{33,1},{48,16},{49,17},{64,... | collective-permute-start | bytes 589832 | tf_op jit(solution)/shard_map/ppermute | solution.py:422
  72.1 18.9 %collective-permute-start.14 = (bf16[4,192,256]{2,1,0:T(8,128)(2,1)S(1)}, bf16[4,192,256]{2,1,0:T(8,128)(2,1)S(1)}, u32[]{:S(2)}, u32[]{:S(2)}) collective-permute-start(bf16[4,192,256]{2,1,0:T(8,128)(2,1)S(1)} %get-tuple-element.100), channel_id=1, source_target_pairs={{0,96},{1,97},{16,112},{17,113},{32,0},{33,1},{48,16},{49,17},{64,... | collective-permute-start | bytes 1179656 | tf_op jit(solution)/shard_map/ppermute | solution.py:422
  72.4 18.6 %collective-permute-start.15 = (bf16[4,192,256]{2,1,0:T(8,128)(2,1)S(1)}, bf16[4,192,256]{2,1,0:T(8,128)(2,1)S(1)}, u32[]{:S(2)}, u32[]{:S(2)}) collective-permute-start(bf16[4,192,256]{2,1,0:T(8,128)(2,1)S(1)} %get-tuple-element.101), channel_id=1, source_target_pairs={{0,32},{1,33},{16,48},{17,49},{32,64},{33,65},{48,80},{49,81},{64,... | collective-permute-start | bytes 1179656 | tf_op jit(solution)/shard_map/ppermute | solution.py:422
  79.1 17.5 %collective-permute-start.19 = (bf16[128,1024]{1,0:T(8,128)(2,1)S(1)}, bf16[128,1024]{1,0:T(8,128)(2,1)S(1)}, u32[]{:S(2)}, u32[]{:S(2)}) collective-permute-start(bf16[128,1024]{1,0:T(8,128)(2,1)S(1)} %get-tuple-element.109), channel_id=1, source_target_pairs={{0,128},{1,129},{16,144},{17,145},{32,160},{33,161},{48,176},{49,1... | collective-permute-start | bytes 786440 | tf_op jit(solution)/shard_map/ppermute | solution.py:422
  79.2 18.1 %collective-permute-start.20 = (bf16[128,1024]{1,0:T(8,128)(2,1)S(1)}, bf16[128,1024]{1,0:T(8,128)(2,1)S(1)}, u32[]{:S(2)}, u32[]{:S(2)}) collective-permute-start(bf16[128,1024]{1,0:T(8,128)(2,1)S(1)} %get-tuple-element.110), channel_id=1, source_target_pairs={{0,144},{1,241},{16,128},{17,161},{32,176},{33,145},{48,160},{49,1... | collective-permute-start | bytes 786440 | tf_op jit(solution)/shard_map/ppermute | solution.py:422
  91.2 6.2 %collective-permute-start.16 = (bf16[192,256]{1,0:T(8,128)(2,1)S(1)}, bf16[192,256]{1,0:T(8,128)(2,1)S(1)}, u32[]{:S(2)}, u32[]{:S(2)}) collective-permute-start(bf16[192,256]{1,0:T(8,128)(2,1)S(1)} %get-tuple-element.106), channel_id=1, source_target_pairs={{0,16},{1,113},{16,0},{17,33},{32,48},{33,17},{48,32},{49,65},{64,... | collective-permute-start | bytes 294920 | tf_op jit(solution)/shard_map/ppermute | solution.py:422
  91.3 7.0 %collective-permute-start.17 = (bf16[192,256]{1,0:T(8,128)(2,1)S(1)}, bf16[192,256]{1,0:T(8,128)(2,1)S(1)}, u32[]{:S(2)}, u32[]{:S(2)}) collective-permute-start(bf16[192,256]{1,0:T(8,128)(2,1)S(1)} %get-tuple-element.107), channel_id=1, source_target_pairs={{0,128},{1,129},{16,144},{17,145},{32,160},{33,161},{48,176},{49,1... | collective-permute-start | bytes 294920 | tf_op jit(solution)/shard_map/ppermute | solution.py:422
  94.8 7.1 %collective-permute-start.18 = (bf16[192,256]{1,0:T(8,128)(2,1)S(1)}, bf16[192,256]{1,0:T(8,128)(2,1)S(1)}, u32[]{:S(2)}, u32[]{:S(2)}) collective-permute-start(bf16[192,256]{1,0:T(8,128)(2,1)S(1)} %get-tuple-element.108), channel_id=1, source_target_pairs={{0,144},{1,241},{16,128},{17,161},{32,176},{33,145},{48,160},{49,1... | collective-permute-start | bytes 294920 | tf_op jit(solution)/shard_map/ppermute | solution.py:422
  102.5 5.0 %collective-permute-start.21 = (bf16[64,512]{1,0:T(8,128)(2,1)S(1)}, bf16[64,512]{1,0:T(8,128)(2,1)S(1)}, u32[]{:S(2)}, u32[]{:S(2)}) collective-permute-start(bf16[64,512]{1,0:T(8,128)(2,1)S(1)} %get-tuple-element.116), channel_id=1, source_target_pairs={{0,1},{1,0},{2,3},{3,2},{4,5},{5,4},{6,7},{7,6},{8,9},{9,8},{10,11... | collective-permute-start | bytes 196616 | tf_op jit(solution)/shard_map/ppermute | solution.py:408
  107.5 3.2 %collective-permute-start.22 = (bf16[64,512]{1,0:T(8,128)(2,1)S(1)}, bf16[64,512]{1,0:T(8,128)(2,1)S(1)}, u32[]{:S(2)}, u32[]{:S(2)}) collective-permute-start(bf16[64,512]{1,0:T(8,128)(2,1)S(1)} %add_convert_fusion.2), channel_id=1, source_target_pairs={{0,2},{2,0},{1,3},{3,1},{4,6},{6,4},{5,7},{7,5},{8,10},{10,8},{9,1... | collective-permute-start | bytes 196616 | tf_op jit(solution)/shard_map/ppermute | solution.py:408
  107.6 6.5 %collective-permute-start.23 = (bf16[128,1024]{1,0:T(8,128)(2,1)S(1)}, bf16[128,1024]{1,0:T(8,128)(2,1)S(1)}, u32[]{:S(2)}, u32[]{:S(2)}) collective-permute-start(bf16[128,1024]{1,0:T(8,128)(2,1)S(1)} %get-tuple-element.117), channel_id=1, source_target_pairs={{0,16},{1,113},{16,0},{17,33},{32,48},{33,17},{48,32},{49,65},{64,... | collective-permute-start | bytes 786440 | tf_op jit(solution)/shard_map/ppermute | solution.py:422
  114.1 6.7 %collective-permute-start.26 = (bf16[64,512]{1,0:T(8,128)(2,1)S(1)}, bf16[64,512]{1,0:T(8,128)(2,1)S(1)}, u32[]{:S(2)}, u32[]{:S(2)}) collective-permute-start(bf16[64,512]{1,0:T(8,128)(2,1)S(1)} %add_convert_fusion.1), channel_id=1, source_target_pairs={{0,12},{4,0},{8,4},{12,8},{1,13},{5,1},{9,5},{13,9},{2,14},{6,2},{... | collective-permute-start | bytes 196616 | tf_op jit(solution)/shard_map/ppermute | solution.py:413
  116.3 5.1 %collective-permute-start.25 = (bf16[64,512]{1,0:T(8,128)(2,1)S(1)}, bf16[64,512]{1,0:T(8,128)(2,1)S(1)}, u32[]{:S(2)}, u32[]{:S(2)}) collective-permute-start(bf16[64,512]{1,0:T(8,128)(2,1)S(1)} %add_convert_fusion.1), channel_id=1, source_target_pairs={{0,4},{4,8},{8,12},{12,0},{1,5},{5,9},{9,13},{13,1},{2,6},{6,10},{... | collective-permute-start | bytes 196616 | tf_op jit(solution)/shard_map/ppermute | solution.py:413
  116.3 5.4 %collective-permute-start.24 = (bf16[64,512]{1,0:T(8,128)(2,1)S(1)}, bf16[64,512]{1,0:T(8,128)(2,1)S(1)}, u32[]{:S(2)}, u32[]{:S(2)}) collective-permute-start(bf16[64,512]{1,0:T(8,128)(2,1)S(1)} %add_convert_fusion.1), channel_id=1, source_target_pairs={{0,8},{4,12},{8,0},{12,4},{1,9},{5,13},{9,1},{13,5},{2,10},{6,14},... | collective-permute-start | bytes 196616 | tf_op jit(solution)/shard_map/ppermute | solution.py:413
  121.7 2.7 %collective-permute-start.27 = (bf16[64,512]{1,0:T(8,128)(2,1)S(1)}, bf16[64,512]{1,0:T(8,128)(2,1)S(1)}, u32[]{:S(2)}, u32[]{:S(2)}) collective-permute-start(bf16[64,512]{1,0:T(8,128)(2,1)S(1)} %add_convert_fusion), channel_id=1, source_target_pairs={{0,1},{1,0},{2,3},{3,2},{4,5},{5,4},{6,7},{7,6},{8,9},{9,8},{10,11... | collective-permute-start | bytes 196616 | tf_op jit(solution)/shard_map/ppermute | solution.py:408

commit v5 on v4

--- a/solution.py
+++ b/solution.py
@@ -534,16 +534,12 @@
     grads = list(call(sum_kernel, (bf16(BOTH, WIDE),) * 4, (), (), own_g, left_g, right_g))
     for d in (1, 2, 3):
         grads[d] = partner(grads[d], d)
-    tied = lax.optimization_barrier((*grads, od[2], od[3]))
-    grads, od[2:] = tied[:4], tied[4:]
+    tied = lax.optimization_barrier((*grads, *od[1:]))
+    grads, od[1:] = tied[:4], tied[4:]
     rows = bf16(ROWS, HEADS * HEAD_DIM)
     keep, send = call(share_kernel, (bf16(PROWS, width),) * 2, (), (info,), *grads)
     share = rounded(keep.astype(F32) + swap(send, "core").astype(F32))
     share = rounded(share.astype(F32) + swap(share, "xl").astype(F32))
-    share, od[1] = lax.optimization_barrier((share, od[1]))
-    across = share.astype(F32) + turn(share, "y", 2).astype(F32)
-    beside = turn(share, "y", 1).astype(F32) + turn(share, "y", 3).astype(F32)
-    share = (across + beside).astype(BF16)
     key_grad, value_grad = call(
         finish_kernel, (bf16(ROWS, width),) * 2, (), (info,), *grads
     )
@@ -551,6 +547,9 @@
     share, key_grad, value_grad, attended, query_grad = lax.optimization_barrier(
         (share, key_grad, value_grad, attended, query_grad)
     )
+    across = share.astype(F32) + turn(share, "y", 2).astype(F32)
+    beside = turn(share, "y", 1).astype(F32) + turn(share, "y", 3).astype(F32)
+    share = rounded(across + beside)
     other = swap(share, "core")
     key_share = jnp.where(core == 0, share, other)
     value_share = jnp.where(core == 0, other, share)

time: 125 us -> 123 us (0.984)
  waiting for transfers between devices: 37.8 us -> 34.7 us
    ppermute x22, waiting for transfers between devices: 32.1 us -> 29.3 us  [local_permute(): return lax.ppermute(x, LOCAL, pairs)]
    ppermute x3, waiting for transfers between devices: 4.81 us -> 2.03 us  [swap(): return lax.ppermute(x, axis, [(0, 1), (1, 0)])]
    ppermute x3, waiting for transfers between devices: 0.88 us -> 3.38 us  [turn(): return lax.ppermute(x, axis, [(i, (i + step) % size) for i in range(size)])]
  transfers between devices with their start and end apart: 28 -> 28, of which waited for: 15 -> 13; matrix products, arithmetic and copies ran while one was open for 1% -> 1% of each run, Pallas kernels for 20% -> 21%
where the time goes in v5:
time: 123 us
  starting transfers between devices  49.8 us (40%)
  waiting for transfers between devices  34.7 us (28%)
  Pallas kernels  33.4 us (27%)
  between operations  2.16 us (2%)
  other arithmetic  1.67 us (1%)
    ppermute x22, starting transfers between devices, local_permute(): return lax.ppermute(x, LOCAL, pairs)  39.2 us
    pallas_call x12, Pallas kernels, call(): pl.pallas_call(kernel, out_shape=tuple(outs), in_specs=[SMEM] * len(scala...  33.4 us
    ppermute x22, waiting for transfers between devices, local_permute(): return lax.ppermute(x, LOCAL, pairs)  29.3 us
    ppermute x3, starting transfers between devices, swap(): return lax.ppermute(x, axis, [(0, 1), (1, 0)])  5.93 us
    ppermute x3, starting transfers between devices, turn(): return lax.ppermute(x, axis, [(i, (i + step) % size) for i in range(size)])  4.62 us
    ppermute x3, waiting for transfers between devices, turn(): return lax.ppermute(x, axis, [(i, (i + step) % size) for i in range(size)])  3.38 us
  transfers between devices with their start and end apart: 28, of which 13 were waited for; matrix products, arithmetic and copies ran while one was open for 1% of the time, Pallas kernels for 21%

profile of v5, /device:TPU:1, one launch (start us, length us, event | category | flops | bytes accessed | tf_op | source)
XLA Modules:
  0.0 122.8 jit_solution(7949441382265437096)
XLA Ops:
  0.6 1.8 %shard_map.128 = (bf16[192,256]{1,0:T(8,128)(2,1)}, bf16[192,256]{1,0:T(8,128)(2,1)}, bf16[192,256]{1,0:T(8,128)(2,1)}, bf16[192,256]{1,0:T(8,128)(2,1)}) custom-call(s32[1]{0:T(128)} %bitcast.info, bf16[128,512]{1,0:T(8,128)(2,1)} %bitcast.17, bf16[128,512]{1,0:T(8,128)(2,1)} %bitcast.18, bf16[64,512]{1,0:T(8,128)(2,1)} %kp.1, bf16[64,512]{1,0:T(8,128)(2,1)} %vp.1), custom_call_target="tpu_custom_call" | custom-call | bytes 1000000 | tf_op jit(solution)/shard_map/pallas_call | solution.py:392
  2.5 3.7 %collective-permute-start.4 = (bf16[192,256]{1,0:T(8,128)(2,1)}, bf16[192,256]{1,0:T(8,128)(2,1)S(1)}, u32[]{:S(2)}, u32[]{:S(2)}) collective-permute-start(bf16[192,256]{1,0:T(8,128)(2,1)} %get-tuple-element.74), channel_id=1, source_target_pairs={{0,128},{1,129},{16,144},{17,145},{32,160},{33,161},{48,176},{49,1... | collective-permute-start | bytes 294920 | tf_op jit(solution)/shard_map/ppermute | solution.py:422
  6.1 5.5 %collective-permute-start.5 = (bf16[192,256]{1,0:T(8,128)(2,1)}, bf16[192,256]{1,0:T(8,128)(2,1)S(1)}, u32[]{:S(2)}, u32[]{:S(2)}) collective-permute-start(bf16[192,256]{1,0:T(8,128)(2,1)} %get-tuple-element.75), channel_id=1, source_target_pairs={{0,144},{1,241},{16,128},{17,161},{32,176},{33,145},{48,160},{49,1... | collective-permute-start | bytes 294920 | tf_op jit(solution)/shard_map/ppermute | solution.py:422
  11.7 2.2 %shard_map.127 = (bf16[128,1024]{1,0:T(8,128)(2,1)}, bf16[128,1024]{1,0:T(8,128)(2,1)}, bf16[128,1024]{1,0:T(8,128)(2,1)}, bf16[128,1024]{1,0:T(8,128)(2,1)}) custom-call(s32[1]{0:T(128)} %bitcast.info, bf16[128,2048]{1,0:T(8,128)(2,1)} %bitcast.15, bf16[128,2048]{1,0:T(8,128)(2,1)} %bitcast.16), custom_call_target="tpu_custom_call" | custom-call | bytes 1000000 | tf_op jit(solution)/shard_map/pallas_call | solution.py:392
  14.1 2.8 %collective-permute-start.1 = (bf16[128,1024]{1,0:T(8,128)(2,1)}, bf16[128,1024]{1,0:T(8,128)(2,1)S(1)}, u32[]{:S(2)}, u32[]{:S(2)}) collective-permute-start(bf16[128,1024]{1,0:T(8,128)(2,1)} %get-tuple-element.70), channel_id=1, source_target_pairs={{0,128},{1,129},{16,144},{17,145},{32,160},{33,161},{48,176},{49,1... | collective-permute-start | bytes 786440 | tf_op jit(solution)/shard_map/ppermute | solution.py:422
  16.8 2.6 %collective-permute-start.3 = (bf16[192,256]{1,0:T(8,128)(2,1)}, bf16[192,256]{1,0:T(8,128)(2,1)S(1)}, u32[]{:S(2)}, u32[]{:S(2)}) collective-permute-start(bf16[192,256]{1,0:T(8,128)(2,1)} %get-tuple-element.73), channel_id=1, source_target_pairs={{0,16},{1,113},{16,0},{17,33},{32,48},{33,17},{48,32},{49,65},{64,... | collective-permute-start | bytes 294920 | tf_op jit(solution)/shard_map/ppermute | solution.py:422
  20.2 1.9 %collective-permute-done.3 = bf16[192,256]{1,0:T(8,128)(2,1)S(1)} collective-permute-done((bf16[192,256]{1,0:T(8,128)(2,1)}, bf16[192,256]{1,0:T(8,128)(2,1)S(1)}, u32[]{:S(2)}, u32[]{:S(2)}) %collective-permute-start.3) | collective-permute-done | bytes 98336 | tf_op jit(solution)/shard_map/ppermute | solution.py:422
  23.0 4.2 %collective-permute-start.10 = (bf16[2,192,256]{2,1,0:T(8,128)(2,1)S(1)}, bf16[2,192,256]{2,1,0:T(8,128)(2,1)S(1)}, u32[]{:S(2)}, u32[]{:S(2)}) collective-permute-start(bf16[2,192,256]{2,1,0:T(8,128)(2,1)S(1)} %pad_maximum_fusion.1.own_b), channel_id=1, source_target_pairs={{0,32},{1,33},{16,48},{17,49},{32,64},{33,65},{48,80},{49,81},{64,... | collective-permute-start | bytes 589832 | tf_op jit(solution)/shard_map/ppermute | solution.py:422
  27.2 1.7 %collective-permute-done.1.qd2 = bf16[128,1024]{1,0:T(8,128)(2,1)S(1)} collective-permute-done((bf16[128,1024]{1,0:T(8,128)(2,1)}, bf16[128,1024]{1,0:T(8,128)(2,1)S(1)}, u32[]{:S(2)}, u32[]{:S(2)}) %collective-permute-start.1) | collective-permute-done | bytes 262176 | tf_op jit(solution)/shard_map/ppermute | solution.py:422
  31.4 3.4 %shard_map.129 = (bf16[2,128,1024]{2,1,0:T(8,128)(2,1)S(1)}, bf16[2,1024,128]{2,1,0:T(8,128)(2,1)S(1)}, bf16[2,128,1024]{2,1,0:T(8,128)(2,1)S(1)}, bf16[1,1280,1...) custom-call(s32[5]{0:T(128)S(1)} %stack.33.info, ...), custom_call_target="tpu_custom_call" | custom-call | flops 1342177280 | bytes 1000000 | tf_op jit(solution)/shard_map/pallas_call | solution.py:392
  34.8 3.5 %collective-permute-start.9 = (bf16[2,192,256]{2,1,0:T(8,128)(2,1)S(1)}, bf16[2,192,256]{2,1,0:T(8,128)(2,1)S(1)}, u32[]{:S(2)}, u32[]{:S(2)}) collective-permute-start(bf16[2,192,256]{2,1,0:T(8,128)(2,1)S(1)} %collective-permute-done.8.right_b), channel_id=1, source_target_pairs={{0,96},{1,97},{16,112},{17,113},{32,0},{33,1},{48,16},{49,17},{64,... | collective-permute-start | bytes 589832 | tf_op jit(solution)/shard_map/ppermute | solution.py:422
  38.2 7.9 %collective-permute-done.10.left_b = bf16[2,192,256]{2,1,0:T(8,128)(2,1)S(1)} collective-permute-done((bf16[2,192,256]{2,1,0:T(8,128)(2,1)S(1)}, bf16[2,192,256]{2,1,0:T(8,128)(2,1)S(1)}, u32[]{:S(2)}, u32[]{:S(2)}) %collective-permute-start.10) | collective-permute-done | bytes 196640 | tf_op jit(solution)/shard_map/ppermute | solution.py:422
  46.1 5.7 %shard_map.130 = (bf16[2,1280,1024]{2,1,0:T(8,128)(2,1)S(1)}, f32[2,1,1024]{2,1,0:T(1,128)S(1)}, f32[2,1,1024]{2,1,0:T(1,128)S(1)}, f32[2,128,1024]{2,1,0:T(8,128)S(1)}) custom-call(s32[5]{0:T(128)S(1)} %stack.33.info, bf16[2,128,1024]{2,1,0:T(8,128)(2,1)S(1)} %get-tuple-element.77.qt, bf16[2,192,256]{2,1,0:T(8,128)(2,1)S(1)} %collective-permute-done.6.left_a, ...), custom_call_target="tpu_custom_call" | custom-call | flops 2684354560 | bytes 1000000 | tf_op jit(solution)/shard_map/pallas_call | solution.py:392
  51.9 5.8 %shard_map.131 = (f32[2,1,1024]{2,1,0:T(1,128)S(1)}, bf16[2,128,1024]{2,1,0:T(8,128)(2,1)S(1)}, bf16[2,1024,128]{2,1,0:T(8,128)(2,1)S(1)}, f32[2,1,1024]{2,1,0:T...) custom-call(s32[5]{0:T(128)S(1)} %stack.33.info, ...), custom_call_target="tpu_custom_call" | custom-call | flops 4026531840 | bytes 1000000 | tf_op jit(solution)/shard_map/pallas_call | solution.py:392
  58.1 3.2 %collective-permute-start.13 = (bf16[2,192,256]{2,1,0:T(8,128)(2,1)S(1)}, bf16[2,192,256]{2,1,0:T(8,128)(2,1)S(1)}, u32[]{:S(2)}, u32[]{:S(2)}) collective-permute-start(bf16[2,192,256]{2,1,0:T(8,128)(2,1)S(1)} %get-tuple-element.98), channel_id=1, source_target_pairs={{0,96},{1,97},{16,112},{17,113},{32,0},{33,1},{48,16},{49,17},{64,... | collective-permute-start | bytes 589832 | tf_op jit(solution)/shard_map/ppermute | solution.py:422
  61.3 6.4 %shard_map.132 = (f32[2,128,1024]{2,1,0:T(8,128)S(1)}, bf16[4,192,256]{2,1,0:T(8,128)(2,1)S(1)}, bf16[4,192,256]{2,1,0:T(8,128)(2,1)S(1)}) custom-call(s32[5]{0:T(128)S(1)} %stack.33.info, bf16[2,1024,128]{2,1,0:T(8,128)(2,1)S(1)} %get-tuple-element.76.q, bf16[2,128,1024]{2,1,0:T(8,128)(2,1)S(1)} %get-tuple-element.85.uplt, ...), custom_call_target="tpu_custom_call" | custom-call | flops 5368709120 | bytes 1000000 | tf_op jit(solution)/shard_map/pallas_call | solution.py:392
  67.7 2.7 %collective-permute-done.12.far_a = bf16[2,192,256]{2,1,0:T(8,128)(2,1)S(1)} collective-permute-done((bf16[2,192,256]{2,1,0:T(8,128)(2,1)S(1)}, bf16[2,192,256]{2,1,0:T(8,128)(2,1)S(1)}, u32[]{:S(2)}, u32[]{:S(2)}) %collective-permute-start.12) | collective-permute-done | bytes 196640 | tf_op jit(solution)/shard_map/ppermute | solution.py:422
  70.5 1.5 %collective-permute-done.13.far_b = bf16[2,192,256]{2,1,0:T(8,128)(2,1)S(1)} collective-permute-done((bf16[2,192,256]{2,1,0:T(8,128)(2,1)S(1)}, bf16[2,192,256]{2,1,0:T(8,128)(2,1)S(1)}, u32[]{:S(2)}, u32[]{:S(2)}) %collective-permute-start.13) | collective-permute-done | bytes 196640 | tf_op jit(solution)/shard_map/ppermute | solution.py:422
  72.4 2.4 %collective-permute-start.15 = (bf16[4,192,256]{2,1,0:T(8,128)(2,1)S(1)}, bf16[4,192,256]{2,1,0:T(8,128)(2,1)S(1)}, u32[]{:S(2)}, u32[]{:S(2)}) collective-permute-start(bf16[4,192,256]{2,1,0:T(8,128)(2,1)S(1)} %get-tuple-element.100), channel_id=1, source_target_pairs={{0,32},{1,33},{16,48},{17,49},{32,64},{33,65},{48,80},{49,81},{64,... | collective-permute-start | bytes 1179656 | tf_op jit(solution)/shard_map/ppermute | solution.py:422
  74.7 4.4 %shard_map.133 = (bf16[4,192,256]{2,1,0:T(8,128)(2,1)S(1)}, bf16[128,1024]{1,0:T(8,128)(2,1)S(1)}, bf16[128,1024]{1,0:T(8,128)(2,1)S(1)}, bf16[128,1024]{1,0:T(8,128)(2,1)S(1)}, bf16[128,1024]{1,0:T(8,128)(2,1)S(1)}) custom-call(s32[5]{0:T(128)S(1)} %stack.33.info, bf16[2,1024,128]{2,1,0:T(8,128)(2,1)S(1)} %get-tuple-element.76.q, ...), custom_call_target="tpu_custom_call" | custom-call | flops 2684354560 | bytes 1000000 | tf_op jit(solution)/shard_map/pallas_call | solution.py:392
  79.2 4.1 %collective-permute-start.21 = (bf16[128,1024]{1,0:T(8,128)(2,1)S(1)}, bf16[128,1024]{1,0:T(8,128)(2,1)S(1)}, u32[]{:S(2)}, u32[]{:S(2)}) collective-permute-start(bf16[128,1024]{1,0:T(8,128)(2,1)S(1)} %get-tuple-element.110), channel_id=1, source_target_pairs={{0,144},{1,241},{16,128},{17,161},{32,176},{33,145},{48,160},{49,1... | collective-permute-start | bytes 786440 | tf_op jit(solution)/shard_map/ppermute | solution.py:422
  83.4 9.1 %collective-permute-done.14.left = bf16[4,192,256]{2,1,0:T(8,128)(2,1)S(1)} collective-permute-done((bf16[4,192,256]{2,1,0:T(8,128)(2,1)S(1)}, bf16[4,192,256]{2,1,0:T(8,128)(2,1)S(1)}, u32[]{:S(2)}, u32[]{:S(2)}) %collective-permute-start.14) | collective-permute-done | bytes 393248 | tf_op jit(solution)/shard_map/ppermute | solution.py:422
  92.7 2.8 %collective-permute-start.16 = (bf16[192,256]{1,0:T(8,128)(2,1)S(1)}, bf16[192,256]{1,0:T(8,128)(2,1)S(1)}, u32[]{:S(2)}, u32[]{:S(2)}) collective-permute-start(bf16[192,256]{1,0:T(8,128)(2,1)S(1)} %get-tuple-element.105), channel_id=1, source_target_pairs={{0,16},{1,113},{16,0},{17,33},{32,48},{33,17},{48,32},{49,65},{64,... | collective-permute-start | bytes 294920 | tf_op jit(solution)/shard_map/ppermute | solution.py:422
  95.4 2.8 %collective-permute-start.18 = (bf16[192,256]{1,0:T(8,128)(2,1)S(1)}, bf16[192,256]{1,0:T(8,128)(2,1)S(1)}, u32[]{:S(2)}, u32[]{:S(2)}) collective-permute-start(bf16[192,256]{1,0:T(8,128)(2,1)S(1)} %get-tuple-element.107), channel_id=1, source_target_pairs={{0,144},{1,241},{16,128},{17,161},{32,176},{33,145},{48,160},{49,1... | collective-permute-start | bytes 294920 | tf_op jit(solution)/shard_map/ppermute | solution.py:422
  98.2 1.9 %collective-permute-done.16.g1 = bf16[192,256]{1,0:T(8,128)(2,1)S(1)} collective-permute-done((bf16[192,256]{1,0:T(8,128)(2,1)S(1)}, bf16[192,256]{1,0:T(8,128)(2,1)S(1)}, u32[]{:S(2)}, u32[]{:S(2)}) %collective-permute-start.16) | collective-permute-done | bytes 98336 | tf_op jit(solution)/shard_map/ppermute | solution.py:422
  100.4 2.2 %collective-permute-done.18.g3 = bf16[192,256]{1,0:T(8,128)(2,1)S(1)} collective-permute-done((bf16[192,256]{1,0:T(8,128)(2,1)S(1)}, bf16[192,256]{1,0:T(8,128)(2,1)S(1)}, u32[]{:S(2)}, u32[]{:S(2)}) %collective-permute-start.18) | collective-permute-done | bytes 98336 | tf_op jit(solution)/shard_map/ppermute | solution.py:422
  103.2 2.8 %collective-permute-start.22 = (bf16[64,512]{1,0:T(8,128)(2,1)S(1)}, bf16[64,512]{1,0:T(8,128)(2,1)S(1)}, u32[]{:S(2)}, u32[]{:S(2)}) collective-permute-start(bf16[64,512]{1,0:T(8,128)(2,1)S(1)} %get-tuple-element.116), channel_id=1, source_target_pairs={{0,1},{1,0},{2,3},{3,2},{4,5},{5,4},{6,7},{7,6},{8,9},{9,8},{10,11... | collective-permute-start | bytes 196616 | tf_op jit(solution)/shard_map/ppermute | solution.py:408
  108.3 1.6 %shard_map.138 = (bf16[128,2048]{1,0:T(8,128)(2,1)}, bf16[128,2048]{1,0:T(8,128)(2,1)}) custom-call(s32[5]{0:T(128)S(1)} %stack.33.info, bf16[128,1024]{1,0:T(8,128)(2,1)S(1)} %get-tuple-element.119.od0, bf16[128,1024]{1,0:T(8,128)(2,1)S(1)} %collective-permute-done.19.od1, bf16[128,1024]{1,0:T(8,128)(2,1)S(1)} %collective-permute-done.20.od2, ...), custom_call_target="tpu_custom_call" | custom-call | bytes 1000000 | tf_op jit(solution)/shard_map/pallas_call | solution.py:392
  110.1 3.0 %collective-permute-start.26 = (bf16[64,512]{1,0:T(8,128)(2,1)S(1)}, bf16[64,512]{1,0:T(8,128)(2,1)S(1)}, u32[]{:S(2)}, u32[]{:S(2)}) collective-permute-start(bf16[64,512]{1,0:T(8,128)(2,1)S(1)} %add_convert_fusion.1), channel_id=1, source_target_pairs={{0,12},{4,0},{8,4},{12,8},{1,13},{5,1},{9,5},{13,9},{2,14},{6,2},{... | collective-permute-start | bytes 196616 | tf_op jit(solution)/shard_map/ppermute | solution.py:413
  113.1 1.6 %collective-permute-start.24 = (bf16[64,512]{1,0:T(8,128)(2,1)S(1)}, bf16[64,512]{1,0:T(8,128)(2,1)S(1)}, u32[]{:S(2)}, u32[]{:S(2)}) collective-permute-start(bf16[64,512]{1,0:T(8,128)(2,1)S(1)} %add_convert_fusion.1), channel_id=1, source_target_pairs={{0,8},{4,12},{8,0},{12,4},{1,9},{5,13},{9,1},{13,5},{2,10},{6,14},... | collective-permute-start | bytes 196616 | tf_op jit(solution)/shard_map/ppermute | solution.py:413
  114.7 3.4 %collective-permute-done.25 = bf16[64,512]{1,0:T(8,128)(2,1)S(1)} collective-permute-done((bf16[64,512]{1,0:T(8,128)(2,1)S(1)}, bf16[64,512]{1,0:T(8,128)(2,1)S(1)}, u32[]{:S(2)}, u32[]{:S(2)}) %collective-permute-start.25) | collective-permute-done | bytes 65568 | tf_op jit(solution)/shard_map/ppermute | solution.py:413
  118.2 3.0 %collective-permute-start.27 = (bf16[64,512]{1,0:T(8,128)(2,1)S(1)}, bf16[64,512]{1,0:T(8,128)(2,1)S(1)}, u32[]{:S(2)}, u32[]{:S(2)}) collective-permute-start(bf16[64,512]{1,0:T(8,128)(2,1)S(1)} %add_convert_fusion), channel_id=1, source_target_pairs={{0,1},{1,0},{2,3},{3,2},{4,5},{5,4},{6,7},{7,6},{8,9},{9,8},{10,11... | collective-permute-start | bytes 196616 | tf_op jit(solution)/shard_map/ppermute | solution.py:408
  (45 shorter events, 9.0 us)
Async XLA Ops:
  2.5 16.9 %collective-permute-start.4 = (bf16[192,256]{1,0:T(8,128)(2,1)}, bf16[192,256]{1,0:T(8,128)(2,1)S(1)}, u32[]{:S(2)}, u32[]{:S(2)}) collective-permute-start(bf16[192,256]{1,0:T(8,128)(2,1)} %get-tuple-element.74), channel_id=1, source_target_pairs={{0,128},{1,129},{16,144},{17,145},{32,160},{33,161},{48,176},{49,1... | collective-permute-start | bytes 294920 | tf_op jit(solution)/shard_map/ppermute | solution.py:422
  6.1 13.3 %collective-permute-start.5 = (bf16[192,256]{1,0:T(8,128)(2,1)}, bf16[192,256]{1,0:T(8,128)(2,1)S(1)}, u32[]{:S(2)}, u32[]{:S(2)}) collective-permute-start(bf16[192,256]{1,0:T(8,128)(2,1)} %get-tuple-element.75), channel_id=1, source_target_pairs={{0,144},{1,241},{16,128},{17,161},{32,176},{33,145},{48,160},{49,1... | collective-permute-start | bytes 294920 | tf_op jit(solution)/shard_map/ppermute | solution.py:422
  13.9 9.1 %collective-permute-start = (bf16[128,1024]{1,0:T(8,128)(2,1)}, bf16[128,1024]{1,0:T(8,128)(2,1)S(1)}, u32[]{:S(2)}, u32[]{:S(2)}) collective-permute-start(bf16[128,1024]{1,0:T(8,128)(2,1)} %get-tuple-element.69), channel_id=1, source_target_pairs={{0,16},{1,113},{16,0},{17,33},{32,48},{33,17},{48,32},{49,65},{64,... | collective-permute-start | bytes 786440 | tf_op jit(solution)/shard_map/ppermute | solution.py:422
  14.1 14.9 %collective-permute-start.1 = (bf16[128,1024]{1,0:T(8,128)(2,1)}, bf16[128,1024]{1,0:T(8,128)(2,1)S(1)}, u32[]{:S(2)}, u32[]{:S(2)}) collective-permute-start(bf16[128,1024]{1,0:T(8,128)(2,1)} %get-tuple-element.70), channel_id=1, source_target_pairs={{0,128},{1,129},{16,144},{17,145},{32,160},{33,161},{48,176},{49,1... | collective-permute-start | bytes 786440 | tf_op jit(solution)/shard_map/ppermute | solution.py:422
  16.8 5.2 %collective-permute-start.3 = (bf16[192,256]{1,0:T(8,128)(2,1)}, bf16[192,256]{1,0:T(8,128)(2,1)S(1)}, u32[]{:S(2)}, u32[]{:S(2)}) collective-permute-start(bf16[192,256]{1,0:T(8,128)(2,1)} %get-tuple-element.73), channel_id=1, source_target_pairs={{0,16},{1,113},{16,0},{17,33},{32,48},{33,17},{48,32},{49,65},{64,... | collective-permute-start | bytes 294920 | tf_op jit(solution)/shard_map/ppermute | solution.py:422
  19.4 11.0 %collective-permute-start.2 = (bf16[128,1024]{1,0:T(8,128)(2,1)}, bf16[128,1024]{1,0:T(8,128)(2,1)S(1)}, u32[]{:S(2)}, u32[]{:S(2)}) collective-permute-start(bf16[128,1024]{1,0:T(8,128)(2,1)} %get-tuple-element.71), channel_id=1, source_target_pairs={{0,144},{1,241},{16,128},{17,161},{32,176},{33,145},{48,160},{49,1... | collective-permute-start | bytes 786440 | tf_op jit(solution)/shard_map/ppermute | solution.py:422
  19.5 15.3 %collective-permute-start.8 = (bf16[2,192,256]{2,1,0:T(8,128)(2,1)S(1)}, bf16[2,192,256]{2,1,0:T(8,128)(2,1)S(1)}, u32[]{:S(2)}, u32[]{:S(2)}) collective-permute-start(bf16[2,192,256]{2,1,0:T(8,128)(2,1)S(1)} %pad_maximum_fusion.1.own_b), channel_id=1, source_target_pairs={{0,96},{1,97},{16,112},{17,113},{32,0},{33,1},{48,16},{49,17},{64,... | collective-permute-start | bytes 589832 | tf_op jit(solution)/shard_map/ppermute | solution.py:422
  22.9 15.3 %collective-permute-start.6 = (bf16[2,192,256]{2,1,0:T(8,128)(2,1)S(1)}, bf16[2,192,256]{2,1,0:T(8,128)(2,1)S(1)}, u32[]{:S(2)}, u32[]{:S(2)}) collective-permute-start(bf16[2,192,256]{2,1,0:T(8,128)(2,1)S(1)} %pad_maximum_fusion.own_a), channel_id=1, source_target_pairs={{0,32},{1,33},{16,48},{17,49},{32,64},{33,65},{48,80},{49,81},{64,... | collective-permute-start | bytes 589832 | tf_op jit(solution)/shard_map/ppermute | solution.py:422
  23.0 23.1 %collective-permute-start.10 = (bf16[2,192,256]{2,1,0:T(8,128)(2,1)S(1)}, bf16[2,192,256]{2,1,0:T(8,128)(2,1)S(1)}, u32[]{:S(2)}, u32[]{:S(2)}) collective-permute-start(bf16[2,192,256]{2,1,0:T(8,128)(2,1)S(1)} %pad_maximum_fusion.1.own_b), channel_id=1, source_target_pairs={{0,32},{1,33},{16,48},{17,49},{32,64},{33,65},{48,80},{49,81},{64,... | collective-permute-start | bytes 589832 | tf_op jit(solution)/shard_map/ppermute | solution.py:422
  29.0 17.2 %collective-permute-start.11 = (bf16[2,192,256]{2,1,0:T(8,128)(2,1)S(1)}, bf16[2,192,256]{2,1,0:T(8,128)(2,1)S(1)}, u32[]{:S(2)}, u32[]{:S(2)}) collective-permute-start(bf16[2,192,256]{2,1,0:T(8,128)(2,1)S(1)} %pad_maximum_fusion.own_a), channel_id=1, source_target_pairs={{0,96},{1,97},{16,112},{17,113},{32,0},{33,1},{48,16},{49,17},{64,... | collective-permute-start | bytes 589832 | tf_op jit(solution)/shard_map/ppermute | solution.py:422
  30.4 1.0 copy-start
  34.8 17.1 %collective-permute-start.9 = (bf16[2,192,256]{2,1,0:T(8,128)(2,1)S(1)}, bf16[2,192,256]{2,1,0:T(8,128)(2,1)S(1)}, u32[]{:S(2)}, u32[]{:S(2)}) collective-permute-start(bf16[2,192,256]{2,1,0:T(8,128)(2,1)S(1)} %collective-permute-done.8.right_b), channel_id=1, source_target_pairs={{0,96},{1,97},{16,112},{17,113},{32,0},{33,1},{48,16},{49,17},{64,... | collective-permute-start | bytes 589832 | tf_op jit(solution)/shard_map/ppermute | solution.py:422
  38.2 13.6 %collective-permute-start.7 = (bf16[2,192,256]{2,1,0:T(8,128)(2,1)S(1)}, bf16[2,192,256]{2,1,0:T(8,128)(2,1)S(1)}, u32[]{:S(2)}, u32[]{:S(2)}) collective-permute-start(bf16[2,192,256]{2,1,0:T(8,128)(2,1)S(1)} %collective-permute-done.6.left_a), channel_id=1, source_target_pairs={{0,32},{1,33},{16,48},{17,49},{32,64},{33,65},{48,80},{49,81},{64,... | collective-permute-start | bytes 589832 | tf_op jit(solution)/shard_map/ppermute | solution.py:422
  57.6 12.8 %collective-permute-start.12 = (bf16[2,192,256]{2,1,0:T(8,128)(2,1)S(1)}, bf16[2,192,256]{2,1,0:T(8,128)(2,1)S(1)}, u32[]{:S(2)}, u32[]{:S(2)}) collective-permute-start(bf16[2,192,256]{2,1,0:T(8,128)(2,1)S(1)} %get-tuple-element.97), channel_id=1, source_target_pairs={{0,32},{1,33},{16,48},{17,49},{32,64},{33,65},{48,80},{49,81},{64,... | collective-permute-start | bytes 589832 | tf_op jit(solution)/shard_map/ppermute | solution.py:422
  58.1 13.9 %collective-permute-start.13 = (bf16[2,192,256]{2,1,0:T(8,128)(2,1)S(1)}, bf16[2,192,256]{2,1,0:T(8,128)(2,1)S(1)}, u32[]{:S(2)}, u32[]{:S(2)}) collective-permute-start(bf16[2,192,256]{2,1,0:T(8,128)(2,1)S(1)} %get-tuple-element.98), channel_id=1, source_target_pairs={{0,96},{1,97},{16,112},{17,113},{32,0},{33,1},{48,16},{49,17},{64,... | collective-permute-start | bytes 589832 | tf_op jit(solution)/shard_map/ppermute | solution.py:422
  72.1 20.4 %collective-permute-start.14 = (bf16[4,192,256]{2,1,0:T(8,128)(2,1)S(1)}, bf16[4,192,256]{2,1,0:T(8,128)(2,1)S(1)}, u32[]{:S(2)}, u32[]{:S(2)}) collective-permute-start(bf16[4,192,256]{2,1,0:T(8,128)(2,1)S(1)} %get-tuple-element.99), channel_id=1, source_target_pairs={{0,96},{1,97},{16,112},{17,113},{32,0},{33,1},{48,16},{49,17},{64,... | collective-permute-start | bytes 1179656 | tf_op jit(solution)/shard_map/ppermute | solution.py:422
  72.4 20.1 %collective-permute-start.15 = (bf16[4,192,256]{2,1,0:T(8,128)(2,1)S(1)}, bf16[4,192,256]{2,1,0:T(8,128)(2,1)S(1)}, u32[]{:S(2)}, u32[]{:S(2)}) collective-permute-start(bf16[4,192,256]{2,1,0:T(8,128)(2,1)S(1)} %get-tuple-element.100), channel_id=1, source_target_pairs={{0,32},{1,33},{16,48},{17,49},{32,64},{33,65},{48,80},{49,81},{64,... | collective-permute-start | bytes 1179656 | tf_op jit(solution)/shard_map/ppermute | solution.py:422
  79.1 16.3 %collective-permute-start.20 = (bf16[128,1024]{1,0:T(8,128)(2,1)S(1)}, bf16[128,1024]{1,0:T(8,128)(2,1)S(1)}, u32[]{:S(2)}, u32[]{:S(2)}) collective-permute-start(bf16[128,1024]{1,0:T(8,128)(2,1)S(1)} %get-tuple-element.109), channel_id=1, source_target_pairs={{0,128},{1,129},{16,144},{17,145},{32,160},{33,161},{48,176},{49,1... | collective-permute-start | bytes 786440 | tf_op jit(solution)/shard_map/ppermute | solution.py:422
  79.2 19.0 %collective-permute-start.21 = (bf16[128,1024]{1,0:T(8,128)(2,1)S(1)}, bf16[128,1024]{1,0:T(8,128)(2,1)S(1)}, u32[]{:S(2)}, u32[]{:S(2)}) collective-permute-start(bf16[128,1024]{1,0:T(8,128)(2,1)S(1)} %get-tuple-element.110), channel_id=1, source_target_pairs={{0,144},{1,241},{16,128},{17,161},{32,176},{33,145},{48,160},{49,1... | collective-permute-start | bytes 786440 | tf_op jit(solution)/shard_map/ppermute | solution.py:422
  92.5 10.1 %collective-permute-start.19 = (bf16[128,1024]{1,0:T(8,128)(2,1)S(1)}, bf16[128,1024]{1,0:T(8,128)(2,1)S(1)}, u32[]{:S(2)}, u32[]{:S(2)}) collective-permute-start(bf16[128,1024]{1,0:T(8,128)(2,1)S(1)} %get-tuple-element.108), channel_id=1, source_target_pairs={{0,16},{1,113},{16,0},{17,33},{32,48},{33,17},{48,32},{49,65},{64,... | collective-permute-start | bytes 786440 | tf_op jit(solution)/shard_map/ppermute | solution.py:422
  92.7 7.5 %collective-permute-start.16 = (bf16[192,256]{1,0:T(8,128)(2,1)S(1)}, bf16[192,256]{1,0:T(8,128)(2,1)S(1)}, u32[]{:S(2)}, u32[]{:S(2)}) collective-permute-start(bf16[192,256]{1,0:T(8,128)(2,1)S(1)} %get-tuple-element.105), channel_id=1, source_target_pairs={{0,16},{1,113},{16,0},{17,33},{32,48},{33,17},{48,32},{49,65},{64,... | collective-permute-start | bytes 294920 | tf_op jit(solution)/shard_map/ppermute | solution.py:422
  95.4 5.0 %collective-permute-start.17 = (bf16[192,256]{1,0:T(8,128)(2,1)S(1)}, bf16[192,256]{1,0:T(8,128)(2,1)S(1)}, u32[]{:S(2)}, u32[]{:S(2)}) collective-permute-start(bf16[192,256]{1,0:T(8,128)(2,1)S(1)} %get-tuple-element.106), channel_id=1, source_target_pairs={{0,128},{1,129},{16,144},{17,145},{32,160},{33,161},{48,176},{49,1... | collective-permute-start | bytes 294920 | tf_op jit(solution)/shard_map/ppermute | solution.py:422
  95.4 7.2 %collective-permute-start.18 = (bf16[192,256]{1,0:T(8,128)(2,1)S(1)}, bf16[192,256]{1,0:T(8,128)(2,1)S(1)}, u32[]{:S(2)}, u32[]{:S(2)}) collective-permute-start(bf16[192,256]{1,0:T(8,128)(2,1)S(1)} %get-tuple-element.107), channel_id=1, source_target_pairs={{0,144},{1,241},{16,128},{17,161},{32,176},{33,145},{48,160},{49,1... | collective-permute-start | bytes 294920 | tf_op jit(solution)/shard_map/ppermute | solution.py:422
  103.2 3.7 %collective-permute-start.22 = (bf16[64,512]{1,0:T(8,128)(2,1)S(1)}, bf16[64,512]{1,0:T(8,128)(2,1)S(1)}, u32[]{:S(2)}, u32[]{:S(2)}) collective-permute-start(bf16[64,512]{1,0:T(8,128)(2,1)S(1)} %get-tuple-element.116), channel_id=1, source_target_pairs={{0,1},{1,0},{2,3},{3,2},{4,5},{5,4},{6,7},{7,6},{8,9},{9,8},{10,11... | collective-permute-start | bytes 196616 | tf_op jit(solution)/shard_map/ppermute | solution.py:408
  106.9 3.2 %collective-permute-start.23 = (bf16[64,512]{1,0:T(8,128)(2,1)S(1)}, bf16[64,512]{1,0:T(8,128)(2,1)S(1)}, u32[]{:S(2)}, u32[]{:S(2)}) collective-permute-start(bf16[64,512]{1,0:T(8,128)(2,1)S(1)} %add_convert_fusion.2), channel_id=1, source_target_pairs={{0,2},{2,0},{1,3},{3,1},{4,6},{6,4},{5,7},{7,5},{8,10},{10,8},{9,1... | collective-permute-start | bytes 196616 | tf_op jit(solution)/shard_map/ppermute | solution.py:408
  110.1 4.6 %collective-permute-start.26 = (bf16[64,512]{1,0:T(8,128)(2,1)S(1)}, bf16[64,512]{1,0:T(8,128)(2,1)S(1)}, u32[]{:S(2)}, u32[]{:S(2)}) collective-permute-start(bf16[64,512]{1,0:T(8,128)(2,1)S(1)} %add_convert_fusion.1), channel_id=1, source_target_pairs={{0,12},{4,0},{8,4},{12,8},{1,13},{5,1},{9,5},{13,9},{2,14},{6,2},{... | collective-permute-start | bytes 196616 | tf_op jit(solution)/shard_map/ppermute | solution.py:413
  113.1 5.0 %collective-permute-start.25 = (bf16[64,512]{1,0:T(8,128)(2,1)S(1)}, bf16[64,512]{1,0:T(8,128)(2,1)S(1)}, u32[]{:S(2)}, u32[]{:S(2)}) collective-permute-start(bf16[64,512]{1,0:T(8,128)(2,1)S(1)} %add_convert_fusion.1), channel_id=1, source_target_pairs={{0,4},{4,8},{8,12},{12,0},{1,5},{5,9},{9,13},{13,1},{2,6},{6,10},{... | collective-permute-start | bytes 196616 | tf_op jit(solution)/shard_map/ppermute | solution.py:413
  113.1 5.0 %collective-permute-start.24 = (bf16[64,512]{1,0:T(8,128)(2,1)S(1)}, bf16[64,512]{1,0:T(8,128)(2,1)S(1)}, u32[]{:S(2)}, u32[]{:S(2)}) collective-permute-start(bf16[64,512]{1,0:T(8,128)(2,1)S(1)} %add_convert_fusion.1), channel_id=1, source_target_pairs={{0,8},{4,12},{8,0},{12,4},{1,9},{5,13},{9,1},{13,5},{2,10},{6,14},... | collective-permute-start | bytes 196616 | tf_op jit(solution)/shard_map/ppermute | solution.py:413
  118.2 3.9 %collective-permute-start.27 = (bf16[64,512]{1,0:T(8,128)(2,1)S(1)}, bf16[64,512]{1,0:T(8,128)(2,1)S(1)}, u32[]{:S(2)}, u32[]{:S(2)}) collective-permute-start(bf16[64,512]{1,0:T(8,128)(2,1)S(1)} %add_convert_fusion), channel_id=1, source_target_pairs={{0,1},{1,0},{2,3},{3,2},{4,5},{5,4},{6,7},{7,6},{8,9},{9,8},{10,11... | collective-permute-start | bytes 196616 | tf_op jit(solution)/shard_map/ppermute | solution.py:408

commit v6 on v5

--- a/solution.py
+++ b/solution.py
@@ -136,7 +136,7 @@
                 at = slice(c * CHUNK, (c + 1) * CHUNK)
                 score = dot(k_s[g, at, :], qt[x])
                 if c > 0:
-                    score = jnp.where(key_rows(info, c - 1, quads(g)) <= place, score, NEG)
+                    score = jnp.where(key_rows(info, c - 1, quads(g, c - 1)) <= place, score, NEG)
                 score_s[g, at, :] = score
                 running = jnp.maximum(running, fold(score, jnp.max))
             return running
@@ -248,7 +248,7 @@
             grad = qd[:, HALF + h * HEAD_DIM : HALF + (h + 1) * HEAD_DIM]
             upt[x, :, cols] = (grad.T.astype(F32) * row_weight).astype(BF16)
     forward(
-        info, lambda g: quad, 1, k_s, v_s, qt, None, score_s, probs, vt_s, shift, total, acc
+        info, lambda g, x: quad, 1, k_s, v_s, qt, None, score_s, probs, vt_s, shift, total, acc
     )
 
 
@@ -258,10 +258,10 @@
     k_s, v_s, vt_s, score_s,
 ):
     mine, quad = info[0], info[1]
-    load_keys(mine, 0, pieces(left_a, left_b), k_s, v_s)
-    load_keys(mine, 1, pieces(right_a, right_b), k_s, v_s)
+    load_keys(mine, 0, pieces(left_a, right_b), k_s, v_s)
+    load_keys(mine, 1, pieces(right_a, left_b), k_s, v_s)
     forward(
-        info, lambda g: (quad + 3 + 2 * g) & 3, 2, k_s, v_s, qt, (shift0, total0, acc0),
+        info, lambda g, x: (quad + 3 - 2 * (g ^ x ^ (mine // 2))) & 3, 2, k_s, v_s, qt, (shift0, total0, acc0),
         score_s, probs, vt_s, shift, total, acc,
     )
 
@@ -274,7 +274,7 @@
     mine, quad, length = info[0], info[1], info[3]
     load_keys(mine, 0, pieces(far_a, far_b), k_s, v_s)
     forward(
-        info, lambda g: (quad + 2) & 3, 1, k_s, v_s, qt, (shift0, total0, acc0),
+        info, lambda g, x: (quad + 2) & 3, 1, k_s, v_s, qt, (shift0, total0, acc0),
         score_s, probs, vt_s, shift, total, acc,
     )
     for x in range(2):
@@ -289,40 +289,35 @@
             for h in range(GROUP):
                 upl[x, lanes_at(j, h), :] = up_low[:, lanes_at(j, h)].T
     backward(
-        1, False, k_s, v_s, kt_s, q, uplt, upl, delta, probs, None, grad_s, None, dqt
+        1, True, k_s, v_s, kt_s, q, uplt, upl, delta, probs, None, grad_s, None, dqt
     )
     store_grads(mine, 0, k_s, v_s, pieces(out_a, out_b))
 
 
-def back_side_kernel(
-    info, q, uplt, upl, delta, shift_then, shift_last, probs,
-    left_a, left_b, right_a, right_b, dqt0,
-    dqt, out_l, out_r,
+def back_kernel(
+    info, q, uplt, upl, delta, shift_then, shift_last, probs, kv_a, kv_b, dqt0,
+    dqt, out_a, out_b,
     k_s, v_s, kt_s, grad_s,
 ):
     mine = info[0]
     factors = [jnp.exp2(shift_then[x] - shift_last[x]) for x in range(2)]
-    load_keys(mine, 0, pieces(left_a, left_b), k_s, v_s)
-    load_keys(mine, 1, pieces(right_a, right_b), k_s, v_s)
+    load_keys(mine, 0, pieces(kv_a, kv_b), k_s, v_s)
     backward(
-        2, False, k_s, v_s, kt_s, q, uplt, upl, delta, probs, factors, grad_s, dqt0, dqt
-    )
-    store_grads(mine, 0, k_s, v_s, pieces(out_l))
-    store_grads(mine, 1, k_s, v_s, pieces(out_r))
-
-
-def back_own_kernel(
-    info, q, uplt, upl, delta, shift_then, shift_last, probs, own_a, own_b, dqt0, attn,
-    out, od0, od1, od2, od3,
+        1, True, k_s, v_s, kt_s, q, uplt, upl, delta, probs, factors, grad_s, dqt0, dqt
+    )
+    store_grads(mine, 0, k_s, v_s, pieces(out_a, out_b))
+
+
+def back_last_kernel(
+    info, q, uplt, upl, delta, shift_then, shift_last, probs, kv_a, kv_b, dqt0, attn,
+    out_a, out_b, od0, od1, od2, od3,
     k_s, v_s, kt_s, grad_s, dqt, dq_s,
 ):
     mine = info[0]
-    factors = [jnp.exp2(shift_then[x] - shift_last[x]) for x in range(2)]
-    load_keys(mine, 0, pieces(own_a, own_b), k_s, v_s)
-    backward(
-        1, True, k_s, v_s, kt_s, q, uplt, upl, delta, probs, factors, grad_s, dqt0, dqt
-    )
-    store_grads(mine, 0, k_s, v_s, pieces(out))
+    back_kernel(
+        info, q, uplt, upl, delta, shift_then, shift_last, probs.at[pl.ds(1, 1)], kv_a, kv_b,
+        dqt0, dqt, out_a, out_b, k_s, v_s, kt_s, grad_s,
+    )
     for x in range(2):
         dq_s[x] = (dqt[x] * SCALE).astype(BF16)
     for d, od in enumerate((od0, od1, od2, od3)):
@@ -346,16 +341,15 @@
     return (a.astype(F32) + b.astype(F32)).astype(BF16)
 
 
-def add_kernel(side_l, side_r, far_a, far_b, out_l, out_r):
-    out_r[:2] = both(side_r[:2], far_a[...])
-    out_r[2:] = side_r[2:]
-    out_l[:2] = side_l[:2]
-    out_l[2:] = both(side_l[2:], far_b[...])
-
-
-def sum_kernel(own, left, right, *outs):
-    for d, out in enumerate(outs):
-        total = own[d].astype(F32) + left[d].astype(F32) + right[d].astype(F32)
+def add_kernel(side_a, side_b, far_a, far_b, out_a, out_b):
+    out_a[...] = both(side_a[...], far_a[...])
+    out_b[...] = both(side_b[...], far_b[...])
+
+
+def sum_kernel(own_a, own_b, left_a, left_b, right_a, right_b, *outs):
+    owns, lefts, rights = pieces(own_a, own_b), pieces(left_a, left_b), pieces(right_a, right_b)
+    for own, left, right, out in zip(owns, lefts, rights, outs, strict=True):
+        total = own[...].astype(F32) + left[...].astype(F32) + right[...].astype(F32)
         out[...] = total.astype(BF16)
 
 
@@ -397,8 +391,8 @@
         scratch_shapes=scratch,
         compiler_params=pltpu.CompilerParams(vmem_limit_bytes=(56 if copies else 32) * 2**20),
         cost_estimate=pl.CostEstimate(
-            flops=products * PROBS * LANES * HEAD_DIM * 4,
-            bytes_accessed=1_000_000,
+            flops=products * PROBS * LANES * HEAD_DIM * 4 + 1,
+            bytes_accessed=1_000_000 * products + 1,
             transcendentals=0,
         ),
     )(*scalars, *operands)
@@ -406,11 +400,6 @@
 
 def swap(x, axis):
     return lax.ppermute(x, axis, [(0, 1), (1, 0)])
-
-
-def turn(x, axis, step):
-    size = lax.axis_size(axis)
-    return lax.ppermute(x, axis, [(i, (i + step) % size) for i in range(size)])
 
 
 def local_permute(x, place):
@@ -509,29 +498,39 @@
         products=6,
     )
     far_ga, far_gb = quad_turn(far_ga, 1), quad_turn(far_gb, -1)
-    dqt, left_g, right_g = call(
-        back_side_kernel,
-        (f32(*tiles), whole, whole),
-        keys(2) + [turned, grad_s],
-        (info,),
-        q, uplt, upl, delta, shift2, shift3, probs2,
-        left_a, left_b, right_a, right_b, dqt,
-        products=8,
-    )
-    left_g, right_g = call(add_kernel, (whole, whole), (), (), left_g, right_g, far_ga, far_gb)
-    left_g, right_g = quad_turn(left_g, -1), quad_turn(right_g, 1)
-    own_g, *od = call(
-        back_own_kernel,
-        (whole,) + (bf16(ROWS, LANES),) * 4,
+
+    def back(shift, probs, kv_a, kv_b, dqt, products):
+        return call(
+            back_kernel,
+            (f32(*tiles), pair, pair),
+            keys(1) + [turned, grad_s],
+            (info,),
+            q, uplt, upl, delta, shift, shift3, probs, kv_a, kv_b, dqt,
+            products=products,
+        )
+
+    dqt, left_ga, right_gb = back(shift2, probs2, left_a, right_b, dqt, 4)
+    left_ga, right_gb = quad_turn(left_ga, -1), quad_turn(right_gb, 1)
+    dqt, own_ga, own_gb = back(shift1, probs1, own_a, own_b, dqt, 0)
+    dqt, far_ga, far_gb = lax.optimization_barrier((dqt, far_ga, far_gb))
+    right_ga, left_gb, *od = call(
+        back_last_kernel,
+        (pair, pair) + (bf16(ROWS, LANES),) * 4,
         keys(1) + [turned, grad_s, (tiles, F32), (tiles, BF16)],
         (info,),
-        q, uplt, upl, delta, shift1, shift3, probs1, own_a, own_b, dqt, attn,
-        products=4,
-    )
-    od[3], od[2] = partner(od[3], 3), partner(od[2], 2)
-    left_g, right_g, od[1] = lax.optimization_barrier((left_g, right_g, od[1]))
-    od[1] = partner(od[1], 1)
-    grads = list(call(sum_kernel, (bf16(BOTH, WIDE),) * 4, (), (), own_g, left_g, right_g))
+        q, uplt, upl, delta, shift2, shift3, probs2, right_a, left_b, dqt, attn,
+    )
+    far_ga, far_gb, left_ga, right_gb = lax.optimization_barrier(
+        (far_ga, far_gb, left_ga, right_gb)
+    )
+    right_ga, left_gb = call(
+        add_kernel, (pair, pair), (), (), right_ga, left_gb, far_ga, far_gb
+    )
+    left_gb, right_ga, od[1] = lax.optimization_barrier((left_gb, right_ga, od[1]))
+    left_gb, right_ga = quad_turn(left_gb, -1), quad_turn(right_ga, 1)
+    for d in (3, 2, 1):
+        od[d] = partner(od[d], d)
+    grads = list(call(sum_kernel, (bf16(BOTH, WIDE),) * 4, (), (), own_ga, own_gb, left_ga, left_gb, right_ga, right_gb))
     for d in (1, 2, 3):
         grads[d] = partner(grads[d], d)
     tied = lax.optimization_barrier((*grads, *od[1:]))
@@ -547,9 +546,8 @@
     share, key_grad, value_grad, attended, query_grad = lax.optimization_barrier(
         (share, key_grad, value_grad, attended, query_grad)
     )
-    across = share.astype(F32) + turn(share, "y", 2).astype(F32)
-    beside = turn(share, "y", 1).astype(F32) + turn(share, "y", 3).astype(F32)
-    share = rounded(across + beside)
+    for pairs in ([(0, 1), (1, 0), (2, 3), (3, 2)], [(0, 3), (3, 0), (1, 2), (2, 1)]):
+        share = rounded(share.astype(F32) + lax.ppermute(share, "y", pairs).astype(F32))
     other = swap(share, "core")
     key_share = jnp.where(core == 0, share, other)
     value_share = jnp.where(core == 0, other, share)

time: 123 us -> 130 us (1.057)
  starting transfers between devices: 49.8 us -> 55.4 us
  Pallas kernels: 33.4 us -> 35.8 us
    ppermute x22 -> x24, starting transfers between devices: 39.2 us -> 44.3 us  [local_permute(): return lax.ppermute(x, LOCAL, pairs)]
    pallas_call x12 -> x13, Pallas kernels: 33.4 us -> 35.8 us  [call(): pl.pallas_call(kernel, out_shape=tuple(outs), in_specs=[SMEM] * len(scala...]
    ppermute x22 -> x24, waiting for transfers between devices: 29.3 us -> 28.8 us  [local_permute(): return lax.ppermute(x, LOCAL, pairs)]
    ppermute x3 -> x2, starting transfers between devices: 4.62 us -> 4.16 us  [body(): lax.ppermute(share, 'y', pairs).astype(F32)]
    ppermute x3 -> x2, waiting for transfers between devices: 3.38 us -> 3.49 us  [body(): lax.ppermute(share, 'y', pairs).astype(F32)]
  transfers between devices with their start and end apart: 28 -> 29, of which waited for: 13 -> 13; matrix products, arithmetic and copies ran while one was open for 1% -> 1% of each run, Pallas kernels for 21% -> 17%
where the time goes in v6:
time: 130 us
  starting transfers between devices  55.4 us (43%)
  Pallas kernels  35.8 us (28%)
  waiting for transfers between devices  34.1 us (26%)
  between operations  2.16 us (2%)
  other arithmetic  1.67 us (1%)
    ppermute x24, starting transfers between devices, local_permute(): return lax.ppermute(x, LOCAL, pairs)  44.3 us
    pallas_call x13, Pallas kernels, call(): pl.pallas_call(kernel, out_shape=tuple(outs), in_specs=[SMEM] * len(scala...  35.8 us
    ppermute x24, waiting for transfers between devices, local_permute(): return lax.ppermute(x, LOCAL, pairs)  28.8 us
    ppermute x3, starting transfers between devices, swap(): return lax.ppermute(x, axis, [(0, 1), (1, 0)])  7 us
    ppermute x2, starting transfers between devices, body(): lax.ppermute(share, 'y', pairs).astype(F32)  4.16 us
    ppermute x2, waiting for transfers between devices, body(): lax.ppermute(share, 'y', pairs).astype(F32)  3.49 us
  transfers between devices with their start and end apart: 29, of which 13 were waited for; matrix products, arithmetic and copies ran while one was open for 1% of the time, Pallas kernels for 17%

profile of v6, /device:TPU:1, one launch (start us, length us, event | category | flops | bytes accessed | tf_op | source)
XLA Modules:
  0.0 130.1 jit_solution(3644349933559022367)
XLA Ops:
  0.6 1.8 %shard_map.128 = (bf16[192,256]{1,0:T(8,128)(2,1)}, bf16[192,256]{1,0:T(8,128)(2,1)}, bf16[192,256]{1,0:T(8,128)(2,1)}, bf16[192,256]{1,0:T(8,128)(2,1)}) custom-call(s32[1]{0:T(128)} %bitcast.info, bf16[128,512]{1,0:T(8,128)(2,1)} %bitcast.17, bf16[128,512]{1,0:T(8,128)(2,1)} %bitcast.18, bf16[64,512]{1,0:T(8,128)(2,1)} %kp.1, bf16[64,512]{1,0:T(8,128)(2,1)} %vp.1), custom_call_target="tpu_custom_call" | custom-call | flops 1 | bytes 1 | tf_op jit(solution)/shard_map/pallas_call | solution.py:386
  2.5 3.7 %collective-permute-start.4 = (bf16[192,256]{1,0:T(8,128)(2,1)}, bf16[192,256]{1,0:T(8,128)(2,1)S(1)}, u32[]{:S(2)}, u32[]{:S(2)}) collective-permute-start(bf16[192,256]{1,0:T(8,128)(2,1)} %get-tuple-element.85), channel_id=1, source_target_pairs={{0,128},{1,129},{16,144},{17,145},{32,160},{33,161},{48,176},{49,1... | collective-permute-start | bytes 294920 | tf_op jit(solution)/shard_map/ppermute | solution.py:411
  6.1 5.5 %collective-permute-start.5 = (bf16[192,256]{1,0:T(8,128)(2,1)}, bf16[192,256]{1,0:T(8,128)(2,1)S(1)}, u32[]{:S(2)}, u32[]{:S(2)}) collective-permute-start(bf16[192,256]{1,0:T(8,128)(2,1)} %get-tuple-element.86), channel_id=1, source_target_pairs={{0,144},{1,241},{16,128},{17,161},{32,176},{33,145},{48,160},{49,1... | collective-permute-start | bytes 294920 | tf_op jit(solution)/shard_map/ppermute | solution.py:411
  11.7 2.3 %shard_map.127 = (bf16[128,1024]{1,0:T(8,128)(2,1)}, bf16[128,1024]{1,0:T(8,128)(2,1)}, bf16[128,1024]{1,0:T(8,128)(2,1)}, bf16[128,1024]{1,0:T(8,128)(2,1)}) custom-call(s32[1]{0:T(128)} %bitcast.info, bf16[128,2048]{1,0:T(8,128)(2,1)} %bitcast.15, bf16[128,2048]{1,0:T(8,128)(2,1)} %bitcast.16), custom_call_target="tpu_custom_call" | custom-call | flops 1 | bytes 1 | tf_op jit(solution)/shard_map/pallas_call | solution.py:386
  14.1 2.8 %collective-permute-start.1 = (bf16[128,1024]{1,0:T(8,128)(2,1)}, bf16[128,1024]{1,0:T(8,128)(2,1)S(1)}, u32[]{:S(2)}, u32[]{:S(2)}) collective-permute-start(bf16[128,1024]{1,0:T(8,128)(2,1)} %get-tuple-element.81), channel_id=1, source_target_pairs={{0,128},{1,129},{16,144},{17,145},{32,160},{33,161},{48,176},{49,1... | collective-permute-start | bytes 786440 | tf_op jit(solution)/shard_map/ppermute | solution.py:411
  16.9 2.6 %collective-permute-start.3 = (bf16[192,256]{1,0:T(8,128)(2,1)}, bf16[192,256]{1,0:T(8,128)(2,1)S(1)}, u32[]{:S(2)}, u32[]{:S(2)}) collective-permute-start(bf16[192,256]{1,0:T(8,128)(2,1)} %get-tuple-element.84), channel_id=1, source_target_pairs={{0,16},{1,113},{16,0},{17,33},{32,48},{33,17},{48,32},{49,65},{64,... | collective-permute-start | bytes 294920 | tf_op jit(solution)/shard_map/ppermute | solution.py:411
  20.2 1.9 %collective-permute-done.3 = bf16[192,256]{1,0:T(8,128)(2,1)S(1)} collective-permute-done((bf16[192,256]{1,0:T(8,128)(2,1)}, bf16[192,256]{1,0:T(8,128)(2,1)S(1)}, u32[]{:S(2)}, u32[]{:S(2)}) %collective-permute-start.3) | collective-permute-done | bytes 98336 | tf_op jit(solution)/shard_map/ppermute | solution.py:411
  23.1 4.2 %collective-permute-start.10 = (bf16[2,192,256]{2,1,0:T(8,128)(2,1)S(1)}, bf16[2,192,256]{2,1,0:T(8,128)(2,1)S(1)}, u32[]{:S(2)}, u32[]{:S(2)}) collective-permute-start(bf16[2,192,256]{2,1,0:T(8,128)(2,1)S(1)} %pad_maximum_fusion.1.own_b.kv_b), channel_id=1, source_target_pairs={{0,32},{1,33},{16,48},{17,49},{32,64},{33,65},{48,80},{49,81},{64,... | collective-permute-start | bytes 589832 | tf_op jit(solution)/shard_map/ppermute | solution.py:411
  27.2 1.7 %collective-permute-done.1.qd2 = bf16[128,1024]{1,0:T(8,128)(2,1)S(1)} collective-permute-done((bf16[128,1024]{1,0:T(8,128)(2,1)}, bf16[128,1024]{1,0:T(8,128)(2,1)S(1)}, u32[]{:S(2)}, u32[]{:S(2)}) %collective-permute-start.1) | collective-permute-done | bytes 262176 | tf_op jit(solution)/shard_map/ppermute | solution.py:411
  31.4 3.4 %shard_map.129 = (bf16[2,128,1024]{2,1,0:T(8,128)(2,1)S(1)}, bf16[2,1024,128]{2,1,0:T(8,128)(2,1)S(1)}, bf16[2,128,1024]{2,1,0:T(8,128)(2,1)S(1)}, bf16[1,1280,1...) custom-call(s32[5]{0:T(128)S(1)} %stack.33.info, ...), custom_call_target="tpu_custom_call" | custom-call | flops 1342177280 | bytes 2000001 | tf_op jit(solution)/shard_map/pallas_call | solution.py:386
  34.8 3.5 %collective-permute-start.9 = (bf16[2,192,256]{2,1,0:T(8,128)(2,1)S(1)}, bf16[2,192,256]{2,1,0:T(8,128)(2,1)S(1)}, u32[]{:S(2)}, u32[]{:S(2)}) collective-permute-start(bf16[2,192,256]{2,1,0:T(8,128)(2,1)S(1)} %collective-permute-done.8.right_b.kv_b), channel_id=1, source_target_pairs={{0,96},{1,97},{16,112},{17,113},{32,0},{33,1},{48,16},{49,17},{64,... | collective-permute-start | bytes 589832 | tf_op jit(solution)/shard_map/ppermute | solution.py:411
  38.3 7.9 %collective-permute-done.10.left_b.kv_b = bf16[2,192,256]{2,1,0:T(8,128)(2,1)S(1)} collective-permute-done((bf16[2,192,256]{2,1,0:T(8,128)(2,1)S(1)}, bf16[2,192,256]{2,1,0:T(8,128)(2,1)S(1)}, u32[]{:S(2)}, u32[]{:S(2)}) %collective-permute-start.10) | collective-permute-done | bytes 196640 | tf_op jit(solution)/shard_map/ppermute | solution.py:411
  46.2 5.7 %shard_map.130 = (bf16[2,1280,1024]{2,1,0:T(8,128)(2,1)S(1)}, f32[2,1,1024]{2,1,0:T(1,128)S(1)}, f32[2,1,1024]{2,1,0:T(1,128)S(1)}, f32[2,128,1024]{2,1,0:T(8,128)S(1)}) custom-call(s32[5]{0:T(128)S(1)} %stack.33.info, bf16[2,128,1024]{2,1,0:T(8,128)(2,1)S(1)} %get-tuple-element.88.qt, bf16[2,192,256]{2,1,0:T(8,128)(2,1)S(1)} %collective-permute-done.6.left_a.kv_a, ...), custom_call_target="tpu_custom_call" | custom-call | flops 2684354560 | bytes 4000001 | tf_op jit(solution)/shard_map/pallas_call | solution.py:386
  51.9 6.4 %shard_map.131 = (f32[2,1,1024]{2,1,0:T(1,128)S(1)}, bf16[2,128,1024]{2,1,0:T(8,128)(2,1)S(1)}, bf16[2,1024,128]{2,1,0:T(8,128)(2,1)S(1)}, f32[2,1,1024]{2,1,0:T...) custom-call(s32[5]{0:T(128)S(1)} %stack.33.info, ...), custom_call_target="tpu_custom_call" | custom-call | flops 4026531840 | bytes 6000001 | tf_op jit(solution)/shard_map/pallas_call | solution.py:386
  58.7 3.2 %collective-permute-start.13 = (bf16[2,192,256]{2,1,0:T(8,128)(2,1)S(1)}, bf16[2,192,256]{2,1,0:T(8,128)(2,1)S(1)}, u32[]{:S(2)}, u32[]{:S(2)}) collective-permute-start(bf16[2,192,256]{2,1,0:T(8,128)(2,1)S(1)} %get-tuple-element.108), channel_id=1, source_target_pairs={{0,96},{1,97},{16,112},{17,113},{32,0},{33,1},{48,16},{49,17},{64,... | collective-permute-start | bytes 589832 | tf_op jit(solution)/shard_map/ppermute | solution.py:411
  61.9 4.1 %shard_map.132 = (f32[2,128,1024]{2,1,0:T(8,128)S(1)}, bf16[2,192,256]{2,1,0:T(8,128)(2,1)S(1)}, bf16[2,192,256]{2,1,0:T(8,128)(2,1)S(1)}) custom-call(s32[5]{0:T(128)S(1)} %stack.33.info, bf16[2,1024,128]{2,1,0:T(8,128)(2,1)S(1)} %get-tuple-element.87.q, bf16[2,128,1024]{2,1,0:T(8,128)(2,1)S(1)} %get-tuple-element.96.uplt, ...), custom_call_target="tpu_custom_call" | custom-call | flops 2684354560 | bytes 4000001 | tf_op jit(solution)/shard_map/pallas_call | solution.py:386
  68.4 4.1 %shard_map.133 = (f32[2,128,1024]{2,1,0:T(8,128)S(1)}, bf16[2,192,256]{2,1,0:T(8,128)(2,1)S(1)}, bf16[2,192,256]{2,1,0:T(8,128)(2,1)S(1)}) custom-call(s32[5]{0:T(128)S(1)} %stack.33.info, bf16[2,1024,128]{2,1,0:T(8,128)(2,1)S(1)} %get-tuple-element.87.q, bf16[2,128,1024]{2,1,0:T(8,128)(2,1)S(1)} %get-tuple-element.96.uplt, ...), custom_call_target="tpu_custom_call" | custom-call | flops 1 | bytes 1 | tf_op jit(solution)/shard_map/pallas_call | solution.py:386
  72.5 1.9 %collective-permute-done.13.far_b = bf16[2,192,256]{2,1,0:T(8,128)(2,1)S(1)} collective-permute-done((bf16[2,192,256]{2,1,0:T(8,128)(2,1)S(1)}, bf16[2,192,256]{2,1,0:T(8,128)(2,1)S(1)}, u32[]{:S(2)}, u32[]{:S(2)}) %collective-permute-start.13) | collective-permute-done | bytes 196640 | tf_op jit(solution)/shard_map/ppermute | solution.py:411
  74.4 6.1 %collective-permute-done.14.left_a = bf16[2,192,256]{2,1,0:T(8,128)(2,1)S(1)} collective-permute-done((bf16[2,192,256]{2,1,0:T(8,128)(2,1)S(1)}, bf16[2,192,256]{2,1,0:T(8,128)(2,1)S(1)}, u32[]{:S(2)}, u32[]{:S(2)}) %collective-permute-start.14) | collective-permute-done | bytes 196640 | tf_op jit(solution)/shard_map/ppermute | solution.py:411
  80.6 4.4 %shard_map.134 = (bf16[2,192,256]{2,1,0:T(8,128)(2,1)S(1)}, bf16[2,192,256]{2,1,0:T(8,128)(2,1)S(1)}, bf16[128,1024]{1,0:T(8,128)(2,1)S(1)}, bf16[128,1024]{1,0:...) custom-call(s32[5]{0:T(128)S(1)} %stack.33.info, ...), custom_call_target="tpu_custom_call" | custom-call | flops 1 | bytes 1 | tf_op jit(solution)/shard_map/pallas_call | solution.py:386
  85.1 3.2 %collective-permute-start.21 = (bf16[128,1024]{1,0:T(8,128)(2,1)S(1)}, bf16[128,1024]{1,0:T(8,128)(2,1)S(1)}, u32[]{:S(2)}, u32[]{:S(2)}) collective-permute-start(bf16[128,1024]{1,0:T(8,128)(2,1)S(1)} %get-tuple-element.130), channel_id=1, source_target_pairs={{0,16},{1,113},{16,0},{17,33},{32,48},{33,17},{48,32},{49,65},{64,... | collective-permute-start | bytes 786440 | tf_op jit(solution)/shard_map/ppermute | solution.py:411
  88.3 2.4 %collective-permute-start.17 = (bf16[2,192,256]{2,1,0:T(8,128)(2,1)S(1)}, bf16[2,192,256]{2,1,0:T(8,128)(2,1)S(1)}, u32[]{:S(2)}, u32[]{:S(2)}) collective-permute-start(bf16[2,192,256]{2,1,0:T(8,128)(2,1)S(1)} %get-tuple-element.124), channel_id=1, source_target_pairs={{0,32},{1,33},{16,48},{17,49},{32,64},{33,65},{48,80},{49,81},{64,... | collective-permute-start | bytes 589832 | tf_op jit(solution)/shard_map/ppermute | solution.py:411
  91.1 3.5 %collective-permute-start.23 = (bf16[128,1024]{1,0:T(8,128)(2,1)S(1)}, bf16[128,1024]{1,0:T(8,128)(2,1)S(1)}, u32[]{:S(2)}, u32[]{:S(2)}) collective-permute-start(bf16[128,1024]{1,0:T(8,128)(2,1)S(1)} %get-tuple-element.132), channel_id=1, source_target_pairs={{0,144},{1,241},{16,128},{17,161},{32,176},{33,145},{48,160},{49,1... | collective-permute-start | bytes 786440 | tf_op jit(solution)/shard_map/ppermute | solution.py:411
  94.7 5.4 %collective-permute-done.16.left_b = bf16[2,192,256]{2,1,0:T(8,128)(2,1)S(1)} collective-permute-done((bf16[2,192,256]{2,1,0:T(8,128)(2,1)S(1)}, bf16[2,192,256]{2,1,0:T(8,128)(2,1)S(1)}, u32[]{:S(2)}, u32[]{:S(2)}) %collective-permute-start.16) | collective-permute-done | bytes 196640 | tf_op jit(solution)/shard_map/ppermute | solution.py:411
  102.3 4.2 %collective-permute-start.20 = (bf16[192,256]{1,0:T(8,128)(2,1)S(1)}, bf16[192,256]{1,0:T(8,128)(2,1)S(1)}, u32[]{:S(2)}, u32[]{:S(2)}) collective-permute-start(bf16[192,256]{1,0:T(8,128)(2,1)S(1)} %get-tuple-element.129), channel_id=1, source_target_pairs={{0,144},{1,241},{16,128},{17,161},{32,176},{33,145},{48,160},{49,1... | collective-permute-start | bytes 294920 | tf_op jit(solution)/shard_map/ppermute | solution.py:411
  106.9 2.6 %collective-permute-done.20.g3 = bf16[192,256]{1,0:T(8,128)(2,1)S(1)} collective-permute-done((bf16[192,256]{1,0:T(8,128)(2,1)S(1)}, bf16[192,256]{1,0:T(8,128)(2,1)S(1)}, u32[]{:S(2)}, u32[]{:S(2)}) %collective-permute-start.20) | collective-permute-done | bytes 98336 | tf_op jit(solution)/shard_map/ppermute | solution.py:411
  110.0 2.8 %collective-permute-start.24 = (bf16[64,512]{1,0:T(8,128)(2,1)S(1)}, bf16[64,512]{1,0:T(8,128)(2,1)S(1)}, u32[]{:S(2)}, u32[]{:S(2)}) collective-permute-start(bf16[64,512]{1,0:T(8,128)(2,1)S(1)} %get-tuple-element.138), channel_id=1, source_target_pairs={{0,1},{1,0},{2,3},{3,2},{4,5},{5,4},{6,7},{7,6},{8,9},{9,8},{10,11... | collective-permute-start | bytes 196616 | tf_op jit(solution)/shard_map/ppermute | solution.py:402
  115.7 1.6 %shard_map.139 = (bf16[128,2048]{1,0:T(8,128)(2,1)}, bf16[128,2048]{1,0:T(8,128)(2,1)}) custom-call(s32[5]{0:T(128)S(1)} %stack.33.info, bf16[128,1024]{1,0:T(8,128)(2,1)S(1)} %get-tuple-element.141.od0, bf16[128,1024]{1,0:T(8,128)(2,1)S(1)} %collective-permute-done.21.od1, bf16[128,1024]{1,0:T(8,128)(2,1)S(1)} %collective-permute-done.22.od2, ...), custom_call_target="tpu_custom_call" | custom-call | flops 1 | bytes 1 | tf_op jit(solution)/shard_map/pallas_call | solution.py:386
  118.7 1.8 %collective-permute-done.26 = bf16[64,512]{1,0:T(8,128)(2,1)S(1)} collective-permute-done((bf16[64,512]{1,0:T(8,128)(2,1)S(1)}, bf16[64,512]{1,0:T(8,128)(2,1)S(1)}, u32[]{:S(2)}, u32[]{:S(2)}) %collective-permute-start.26) | collective-permute-done | bytes 65568 | tf_op jit(solution)/shard_map/ppermute | solution.py:550
  120.6 2.8 %collective-permute-start.27 = (bf16[64,512]{1,0:T(8,128)(2,1)S(1)}, bf16[64,512]{1,0:T(8,128)(2,1)S(1)}, u32[]{:S(2)}, u32[]{:S(2)}) collective-permute-start(bf16[64,512]{1,0:T(8,128)(2,1)S(1)} %add_convert_fusion.1), channel_id=1, source_target_pairs={{0,12},{12,0},{4,8},{8,4},{1,13},{13,1},{5,9},{9,5},{2,14},{14,2},... | collective-permute-start | bytes 196616 | tf_op jit(solution)/shard_map/ppermute | solution.py:550
  123.4 1.7 %collective-permute-done.27 = bf16[64,512]{1,0:T(8,128)(2,1)S(1)} collective-permute-done((bf16[64,512]{1,0:T(8,128)(2,1)S(1)}, bf16[64,512]{1,0:T(8,128)(2,1)S(1)}, u32[]{:S(2)}, u32[]{:S(2)}) %collective-permute-start.27) | collective-permute-done | bytes 65568 | tf_op jit(solution)/shard_map/ppermute | solution.py:550
  125.1 3.5 %collective-permute-start.28 = (bf16[64,512]{1,0:T(8,128)(2,1)S(1)}, bf16[64,512]{1,0:T(8,128)(2,1)S(1)}, u32[]{:S(2)}, u32[]{:S(2)}) collective-permute-start(bf16[64,512]{1,0:T(8,128)(2,1)S(1)} %add_convert_fusion), channel_id=1, source_target_pairs={{0,1},{1,0},{2,3},{3,2},{4,5},{5,4},{6,7},{7,6},{8,9},{9,8},{10,11... | collective-permute-start | bytes 196616 | tf_op jit(solution)/shard_map/ppermute | solution.py:402
  (49 shorter events, 15.4 us)
Async XLA Ops:
  2.5 17.0 %collective-permute-start.4 = (bf16[192,256]{1,0:T(8,128)(2,1)}, bf16[192,256]{1,0:T(8,128)(2,1)S(1)}, u32[]{:S(2)}, u32[]{:S(2)}) collective-permute-start(bf16[192,256]{1,0:T(8,128)(2,1)} %get-tuple-element.85), channel_id=1, source_target_pairs={{0,128},{1,129},{16,144},{17,145},{32,160},{33,161},{48,176},{49,1... | collective-permute-start | bytes 294920 | tf_op jit(solution)/shard_map/ppermute | solution.py:411
  6.1 13.3 %collective-permute-start.5 = (bf16[192,256]{1,0:T(8,128)(2,1)}, bf16[192,256]{1,0:T(8,128)(2,1)S(1)}, u32[]{:S(2)}, u32[]{:S(2)}) collective-permute-start(bf16[192,256]{1,0:T(8,128)(2,1)} %get-tuple-element.86), channel_id=1, source_target_pairs={{0,144},{1,241},{16,128},{17,161},{32,176},{33,145},{48,160},{49,1... | collective-permute-start | bytes 294920 | tf_op jit(solution)/shard_map/ppermute | solution.py:411
  13.9 9.1 %collective-permute-start = (bf16[128,1024]{1,0:T(8,128)(2,1)}, bf16[128,1024]{1,0:T(8,128)(2,1)S(1)}, u32[]{:S(2)}, u32[]{:S(2)}) collective-permute-start(bf16[128,1024]{1,0:T(8,128)(2,1)} %get-tuple-element.80), channel_id=1, source_target_pairs={{0,16},{1,113},{16,0},{17,33},{32,48},{33,17},{48,32},{49,65},{64,... | collective-permute-start | bytes 786440 | tf_op jit(solution)/shard_map/ppermute | solution.py:411
  14.1 14.9 %collective-permute-start.1 = (bf16[128,1024]{1,0:T(8,128)(2,1)}, bf16[128,1024]{1,0:T(8,128)(2,1)S(1)}, u32[]{:S(2)}, u32[]{:S(2)}) collective-permute-start(bf16[128,1024]{1,0:T(8,128)(2,1)} %get-tuple-element.81), channel_id=1, source_target_pairs={{0,128},{1,129},{16,144},{17,145},{32,160},{33,161},{48,176},{49,1... | collective-permute-start | bytes 786440 | tf_op jit(solution)/shard_map/ppermute | solution.py:411
  16.9 5.2 %collective-permute-start.3 = (bf16[192,256]{1,0:T(8,128)(2,1)}, bf16[192,256]{1,0:T(8,128)(2,1)S(1)}, u32[]{:S(2)}, u32[]{:S(2)}) collective-permute-start(bf16[192,256]{1,0:T(8,128)(2,1)} %get-tuple-element.84), channel_id=1, source_target_pairs={{0,16},{1,113},{16,0},{17,33},{32,48},{33,17},{48,32},{49,65},{64,... | collective-permute-start | bytes 294920 | tf_op jit(solution)/shard_map/ppermute | solution.py:411
  19.4 11.0 %collective-permute-start.2 = (bf16[128,1024]{1,0:T(8,128)(2,1)}, bf16[128,1024]{1,0:T(8,128)(2,1)S(1)}, u32[]{:S(2)}, u32[]{:S(2)}) collective-permute-start(bf16[128,1024]{1,0:T(8,128)(2,1)} %get-tuple-element.82), channel_id=1, source_target_pairs={{0,144},{1,241},{16,128},{17,161},{32,176},{33,145},{48,160},{49,1... | collective-permute-start | bytes 786440 | tf_op jit(solution)/shard_map/ppermute | solution.py:411
  19.5 15.3 %collective-permute-start.8 = (bf16[2,192,256]{2,1,0:T(8,128)(2,1)S(1)}, bf16[2,192,256]{2,1,0:T(8,128)(2,1)S(1)}, u32[]{:S(2)}, u32[]{:S(2)}) collective-permute-start(bf16[2,192,256]{2,1,0:T(8,128)(2,1)S(1)} %pad_maximum_fusion.1.own_b.kv_b), channel_id=1, source_target_pairs={{0,96},{1,97},{16,112},{17,113},{32,0},{33,1},{48,16},{49,17},{64,... | collective-permute-start | bytes 589832 | tf_op jit(solution)/shard_map/ppermute | solution.py:411
  23.0 15.3 %collective-permute-start.6 = (bf16[2,192,256]{2,1,0:T(8,128)(2,1)S(1)}, bf16[2,192,256]{2,1,0:T(8,128)(2,1)S(1)}, u32[]{:S(2)}, u32[]{:S(2)}) collective-permute-start(bf16[2,192,256]{2,1,0:T(8,128)(2,1)S(1)} %pad_maximum_fusion.own_a.kv_a), channel_id=1, source_target_pairs={{0,32},{1,33},{16,48},{17,49},{32,64},{33,65},{48,80},{49,81},{64,... | collective-permute-start | bytes 589832 | tf_op jit(solution)/shard_map/ppermute | solution.py:411
  23.1 23.1 %collective-permute-start.10 = (bf16[2,192,256]{2,1,0:T(8,128)(2,1)S(1)}, bf16[2,192,256]{2,1,0:T(8,128)(2,1)S(1)}, u32[]{:S(2)}, u32[]{:S(2)}) collective-permute-start(bf16[2,192,256]{2,1,0:T(8,128)(2,1)S(1)} %pad_maximum_fusion.1.own_b.kv_b), channel_id=1, source_target_pairs={{0,32},{1,33},{16,48},{17,49},{32,64},{33,65},{48,80},{49,81},{64,... | collective-permute-start | bytes 589832 | tf_op jit(solution)/shard_map/ppermute | solution.py:411
  29.0 17.2 %collective-permute-start.11 = (bf16[2,192,256]{2,1,0:T(8,128)(2,1)S(1)}, bf16[2,192,256]{2,1,0:T(8,128)(2,1)S(1)}, u32[]{:S(2)}, u32[]{:S(2)}) collective-permute-start(bf16[2,192,256]{2,1,0:T(8,128)(2,1)S(1)} %pad_maximum_fusion.own_a.kv_a), channel_id=1, source_target_pairs={{0,96},{1,97},{16,112},{17,113},{32,0},{33,1},{48,16},{49,17},{64,... | collective-permute-start | bytes 589832 | tf_op jit(solution)/shard_map/ppermute | solution.py:411
  30.4 1.0 copy-start
  34.8 17.1 %collective-permute-start.9 = (bf16[2,192,256]{2,1,0:T(8,128)(2,1)S(1)}, bf16[2,192,256]{2,1,0:T(8,128)(2,1)S(1)}, u32[]{:S(2)}, u32[]{:S(2)}) collective-permute-start(bf16[2,192,256]{2,1,0:T(8,128)(2,1)S(1)} %collective-permute-done.8.right_b.kv_b), channel_id=1, source_target_pairs={{0,96},{1,97},{16,112},{17,113},{32,0},{33,1},{48,16},{49,17},{64,... | collective-permute-start | bytes 589832 | tf_op jit(solution)/shard_map/ppermute | solution.py:411
  38.3 13.6 %collective-permute-start.7 = (bf16[2,192,256]{2,1,0:T(8,128)(2,1)S(1)}, bf16[2,192,256]{2,1,0:T(8,128)(2,1)S(1)}, u32[]{:S(2)}, u32[]{:S(2)}) collective-permute-start(bf16[2,192,256]{2,1,0:T(8,128)(2,1)S(1)} %collective-permute-done.6.left_a.kv_a), channel_id=1, source_target_pairs={{0,32},{1,33},{16,48},{17,49},{32,64},{33,65},{48,80},{49,81},{64,... | collective-permute-start | bytes 589832 | tf_op jit(solution)/shard_map/ppermute | solution.py:411
  58.3 14.2 %collective-permute-start.12 = (bf16[2,192,256]{2,1,0:T(8,128)(2,1)S(1)}, bf16[2,192,256]{2,1,0:T(8,128)(2,1)S(1)}, u32[]{:S(2)}, u32[]{:S(2)}) collective-permute-start(bf16[2,192,256]{2,1,0:T(8,128)(2,1)S(1)} %get-tuple-element.107), channel_id=1, source_target_pairs={{0,32},{1,33},{16,48},{17,49},{32,64},{33,65},{48,80},{49,81},{64,... | collective-permute-start | bytes 589832 | tf_op jit(solution)/shard_map/ppermute | solution.py:411
  58.7 15.7 %collective-permute-start.13 = (bf16[2,192,256]{2,1,0:T(8,128)(2,1)S(1)}, bf16[2,192,256]{2,1,0:T(8,128)(2,1)S(1)}, u32[]{:S(2)}, u32[]{:S(2)}) collective-permute-start(bf16[2,192,256]{2,1,0:T(8,128)(2,1)S(1)} %get-tuple-element.108), channel_id=1, source_target_pairs={{0,96},{1,97},{16,112},{17,113},{32,0},{33,1},{48,16},{49,17},{64,... | collective-permute-start | bytes 589832 | tf_op jit(solution)/shard_map/ppermute | solution.py:411
  66.0 14.6 %collective-permute-start.14 = (bf16[2,192,256]{2,1,0:T(8,128)(2,1)S(1)}, bf16[2,192,256]{2,1,0:T(8,128)(2,1)S(1)}, u32[]{:S(2)}, u32[]{:S(2)}) collective-permute-start(bf16[2,192,256]{2,1,0:T(8,128)(2,1)S(1)} %get-tuple-element.111), channel_id=1, source_target_pairs={{0,96},{1,97},{16,112},{17,113},{32,0},{33,1},{48,16},{49,17},{64,... | collective-permute-start | bytes 589832 | tf_op jit(solution)/shard_map/ppermute | solution.py:411
  67.3 13.3 %collective-permute-start.15 = (bf16[2,192,256]{2,1,0:T(8,128)(2,1)S(1)}, bf16[2,192,256]{2,1,0:T(8,128)(2,1)S(1)}, u32[]{:S(2)}, u32[]{:S(2)}) collective-permute-start(bf16[2,192,256]{2,1,0:T(8,128)(2,1)S(1)} %get-tuple-element.112), channel_id=1, source_target_pairs={{0,32},{1,33},{16,48},{17,49},{32,64},{33,65},{48,80},{49,81},{64,... | collective-permute-start | bytes 589832 | tf_op jit(solution)/shard_map/ppermute | solution.py:411
  85.1 17.2 %collective-permute-start.21 = (bf16[128,1024]{1,0:T(8,128)(2,1)S(1)}, bf16[128,1024]{1,0:T(8,128)(2,1)S(1)}, u32[]{:S(2)}, u32[]{:S(2)}) collective-permute-start(bf16[128,1024]{1,0:T(8,128)(2,1)S(1)} %get-tuple-element.130), channel_id=1, source_target_pairs={{0,16},{1,113},{16,0},{17,33},{32,48},{33,17},{48,32},{49,65},{64,... | collective-permute-start | bytes 786440 | tf_op jit(solution)/shard_map/ppermute | solution.py:411
  88.3 11.7 %collective-permute-start.16 = (bf16[2,192,256]{2,1,0:T(8,128)(2,1)S(1)}, bf16[2,192,256]{2,1,0:T(8,128)(2,1)S(1)}, u32[]{:S(2)}, u32[]{:S(2)}) collective-permute-start(bf16[2,192,256]{2,1,0:T(8,128)(2,1)S(1)} %get-tuple-element.123), channel_id=1, source_target_pairs={{0,96},{1,97},{16,112},{17,113},{32,0},{33,1},{48,16},{49,17},{64,... | collective-permute-start | bytes 589832 | tf_op jit(solution)/shard_map/ppermute | solution.py:411
  88.3 12.6 %collective-permute-start.17 = (bf16[2,192,256]{2,1,0:T(8,128)(2,1)S(1)}, bf16[2,192,256]{2,1,0:T(8,128)(2,1)S(1)}, u32[]{:S(2)}, u32[]{:S(2)}) collective-permute-start(bf16[2,192,256]{2,1,0:T(8,128)(2,1)S(1)} %get-tuple-element.124), channel_id=1, source_target_pairs={{0,32},{1,33},{16,48},{17,49},{32,64},{33,65},{48,80},{49,81},{64,... | collective-permute-start | bytes 589832 | tf_op jit(solution)/shard_map/ppermute | solution.py:411
  90.7 15.9 %collective-permute-start.22 = (bf16[128,1024]{1,0:T(8,128)(2,1)S(1)}, bf16[128,1024]{1,0:T(8,128)(2,1)S(1)}, u32[]{:S(2)}, u32[]{:S(2)}) collective-permute-start(bf16[128,1024]{1,0:T(8,128)(2,1)S(1)} %get-tuple-element.131), channel_id=1, source_target_pairs={{0,128},{1,129},{16,144},{17,145},{32,160},{33,161},{48,176},{49,1... | collective-permute-start | bytes 786440 | tf_op jit(solution)/shard_map/ppermute | solution.py:411
  91.1 15.4 %collective-permute-start.23 = (bf16[128,1024]{1,0:T(8,128)(2,1)S(1)}, bf16[128,1024]{1,0:T(8,128)(2,1)S(1)}, u32[]{:S(2)}, u32[]{:S(2)}) collective-permute-start(bf16[128,1024]{1,0:T(8,128)(2,1)S(1)} %get-tuple-element.132), channel_id=1, source_target_pairs={{0,144},{1,241},{16,128},{17,161},{32,176},{33,145},{48,160},{49,1... | collective-permute-start | bytes 786440 | tf_op jit(solution)/shard_map/ppermute | solution.py:411
  101.1 5.5 %collective-permute-start.18 = (bf16[192,256]{1,0:T(8,128)(2,1)S(1)}, bf16[192,256]{1,0:T(8,128)(2,1)S(1)}, u32[]{:S(2)}, u32[]{:S(2)}) collective-permute-start(bf16[192,256]{1,0:T(8,128)(2,1)S(1)} %get-tuple-element.127), channel_id=1, source_target_pairs={{0,16},{1,113},{16,0},{17,33},{32,48},{33,17},{48,32},{49,65},{64,... | collective-permute-start | bytes 294920 | tf_op jit(solution)/shard_map/ppermute | solution.py:411
  101.8 5.0 %collective-permute-start.19 = (bf16[192,256]{1,0:T(8,128)(2,1)S(1)}, bf16[192,256]{1,0:T(8,128)(2,1)S(1)}, u32[]{:S(2)}, u32[]{:S(2)}) collective-permute-start(bf16[192,256]{1,0:T(8,128)(2,1)S(1)} %get-tuple-element.128), channel_id=1, source_target_pairs={{0,128},{1,129},{16,144},{17,145},{32,160},{33,161},{48,176},{49,1... | collective-permute-start | bytes 294920 | tf_op jit(solution)/shard_map/ppermute | solution.py:411
  102.3 7.1 %collective-permute-start.20 = (bf16[192,256]{1,0:T(8,128)(2,1)S(1)}, bf16[192,256]{1,0:T(8,128)(2,1)S(1)}, u32[]{:S(2)}, u32[]{:S(2)}) collective-permute-start(bf16[192,256]{1,0:T(8,128)(2,1)S(1)} %get-tuple-element.129), channel_id=1, source_target_pairs={{0,144},{1,241},{16,128},{17,161},{32,176},{33,145},{48,160},{49,1... | collective-permute-start | bytes 294920 | tf_op jit(solution)/shard_map/ppermute | solution.py:411
  110.0 3.7 %collective-permute-start.24 = (bf16[64,512]{1,0:T(8,128)(2,1)S(1)}, bf16[64,512]{1,0:T(8,128)(2,1)S(1)}, u32[]{:S(2)}, u32[]{:S(2)}) collective-permute-start(bf16[64,512]{1,0:T(8,128)(2,1)S(1)} %get-tuple-element.138), channel_id=1, source_target_pairs={{0,1},{1,0},{2,3},{3,2},{4,5},{5,4},{6,7},{7,6},{8,9},{9,8},{10,11... | collective-permute-start | bytes 196616 | tf_op jit(solution)/shard_map/ppermute | solution.py:402
  113.8 3.5 %collective-permute-start.25 = (bf16[64,512]{1,0:T(8,128)(2,1)S(1)}, bf16[64,512]{1,0:T(8,128)(2,1)S(1)}, u32[]{:S(2)}, u32[]{:S(2)}) collective-permute-start(bf16[64,512]{1,0:T(8,128)(2,1)S(1)} %add_convert_fusion.3), channel_id=1, source_target_pairs={{0,2},{2,0},{1,3},{3,1},{4,6},{6,4},{5,7},{7,5},{8,10},{10,8},{9,1... | collective-permute-start | bytes 196616 | tf_op jit(solution)/shard_map/ppermute | solution.py:402
  117.4 3.2 %collective-permute-start.26 = (bf16[64,512]{1,0:T(8,128)(2,1)S(1)}, bf16[64,512]{1,0:T(8,128)(2,1)S(1)}, u32[]{:S(2)}, u32[]{:S(2)}) collective-permute-start(bf16[64,512]{1,0:T(8,128)(2,1)S(1)} %add_convert_fusion.2), channel_id=1, source_target_pairs={{0,4},{4,0},{8,12},{12,8},{1,5},{5,1},{9,13},{13,9},{2,6},{6,2},{1... | collective-permute-start | bytes 196616 | tf_op jit(solution)/shard_map/ppermute | solution.py:550
  120.6 4.4 %collective-permute-start.27 = (bf16[64,512]{1,0:T(8,128)(2,1)S(1)}, bf16[64,512]{1,0:T(8,128)(2,1)S(1)}, u32[]{:S(2)}, u32[]{:S(2)}) collective-permute-start(bf16[64,512]{1,0:T(8,128)(2,1)S(1)} %add_convert_fusion.1), channel_id=1, source_target_pairs={{0,12},{12,0},{4,8},{8,4},{1,13},{13,1},{5,9},{9,5},{2,14},{14,2},... | collective-permute-start | bytes 196616 | tf_op jit(solution)/shard_map/ppermute | solution.py:550
  125.1 4.4 %collective-permute-start.28 = (bf16[64,512]{1,0:T(8,128)(2,1)S(1)}, bf16[64,512]{1,0:T(8,128)(2,1)S(1)}, u32[]{:S(2)}, u32[]{:S(2)}) collective-permute-start(bf16[64,512]{1,0:T(8,128)(2,1)S(1)} %add_convert_fusion), channel_id=1, source_target_pairs={{0,1},{1,0},{2,3},{3,2},{4,5},{5,4},{6,7},{7,6},{8,9},{9,8},{10,11... | collective-permute-start | bytes 196616 | tf_op jit(solution)/shard_map/ppermute | solution.py:402

commit v7 on v5

--- a/solution.py
+++ b/solution.py
@@ -528,9 +528,8 @@
         q, uplt, upl, delta, shift1, shift3, probs1, own_a, own_b, dqt, attn,
         products=4,
     )
-    od[3], od[2] = partner(od[3], 3), partner(od[2], 2)
-    left_g, right_g, od[1] = lax.optimization_barrier((left_g, right_g, od[1]))
-    od[1] = partner(od[1], 1)
+    for d in (3, 2, 1):
+        od[d] = partner(od[d], d)
     grads = list(call(sum_kernel, (bf16(BOTH, WIDE),) * 4, (), (), own_g, left_g, right_g))
     for d in (1, 2, 3):
         grads[d] = partner(grads[d], d)

time: 123 us -> 123 us (level)
  transfers between devices with their start and end apart: 28 -> 28, of which waited for: 13 -> 15; matrix products, arithmetic and copies ran while one was open for 1% -> 1% of each run, Pallas kernels for 21% -> 20%
where the time goes in v7:
time: 123 us
  starting transfers between devices  49.4 us (40%)
  waiting for transfers between devices  35.5 us (29%)
  Pallas kernels  33.4 us (27%)
  between operations  2.16 us (2%)
  other arithmetic  1.67 us (1%)
    ppermute x22, starting transfers between devices, local_permute(): return lax.ppermute(x, LOCAL, pairs)  39 us
    pallas_call x12, Pallas kernels, call(): pl.pallas_call(kernel, out_shape=tuple(outs), in_specs=[SMEM] * len(scala...  33.4 us
    ppermute x22, waiting for transfers between devices, local_permute(): return lax.ppermute(x, LOCAL, pairs)  30.1 us
    ppermute x3, starting transfers between devices, swap(): return lax.ppermute(x, axis, [(0, 1), (1, 0)])  6.18 us
    ppermute x3, starting transfers between devices, turn(): return lax.ppermute(x, axis, [(i, (i + step) % size) for i in range(size)])  4.19 us
    ppermute x3, waiting for transfers between devices, turn(): return lax.ppermute(x, axis, [(i, (i + step) % size) for i in range(size)])  3.38 us
  transfers between devices with their start and end apart: 28, of which 15 were waited for; matrix products, arithmetic and copies ran while one was open for 1% of the time, Pallas kernels for 20%

profile of v7, /device:TPU:1, one launch (start us, length us, event | category | flops | bytes accessed | tf_op | source)
XLA Modules:
  0.0 123.2 jit_solution(9637575144646843601)
XLA Ops:
  0.6 1.8 %shard_map.128 = (bf16[192,256]{1,0:T(8,128)(2,1)}, bf16[192,256]{1,0:T(8,128)(2,1)}, bf16[192,256]{1,0:T(8,128)(2,1)}, bf16[192,256]{1,0:T(8,128)(2,1)}) custom-call(s32[1]{0:T(128)} %bitcast.info, bf16[128,512]{1,0:T(8,128)(2,1)} %bitcast.17, bf16[128,512]{1,0:T(8,128)(2,1)} %bitcast.18, bf16[64,512]{1,0:T(8,128)(2,1)} %kp.1, bf16[64,512]{1,0:T(8,128)(2,1)} %vp.1), custom_call_target="tpu_custom_call" | custom-call | bytes 1000000 | tf_op jit(solution)/shard_map/pallas_call | solution.py:392
  2.5 3.7 %collective-permute-start.4 = (bf16[192,256]{1,0:T(8,128)(2,1)}, bf16[192,256]{1,0:T(8,128)(2,1)S(1)}, u32[]{:S(2)}, u32[]{:S(2)}) collective-permute-start(bf16[192,256]{1,0:T(8,128)(2,1)} %get-tuple-element.71), channel_id=1, source_target_pairs={{0,128},{1,129},{16,144},{17,145},{32,160},{33,161},{48,176},{49,1... | collective-permute-start | bytes 294920 | tf_op jit(solution)/shard_map/ppermute | solution.py:422
  6.1 5.5 %collective-permute-start.5 = (bf16[192,256]{1,0:T(8,128)(2,1)}, bf16[192,256]{1,0:T(8,128)(2,1)S(1)}, u32[]{:S(2)}, u32[]{:S(2)}) collective-permute-start(bf16[192,256]{1,0:T(8,128)(2,1)} %get-tuple-element.72), channel_id=1, source_target_pairs={{0,144},{1,241},{16,128},{17,161},{32,176},{33,145},{48,160},{49,1... | collective-permute-start | bytes 294920 | tf_op jit(solution)/shard_map/ppermute | solution.py:422
  11.7 2.2 %shard_map.127 = (bf16[128,1024]{1,0:T(8,128)(2,1)}, bf16[128,1024]{1,0:T(8,128)(2,1)}, bf16[128,1024]{1,0:T(8,128)(2,1)}, bf16[128,1024]{1,0:T(8,128)(2,1)}) custom-call(s32[1]{0:T(128)} %bitcast.info, bf16[128,2048]{1,0:T(8,128)(2,1)} %bitcast.15, bf16[128,2048]{1,0:T(8,128)(2,1)} %bitcast.16), custom_call_target="tpu_custom_call" | custom-call | bytes 1000000 | tf_op jit(solution)/shard_map/pallas_call | solution.py:392
  14.1 2.8 %collective-permute-start.1 = (bf16[128,1024]{1,0:T(8,128)(2,1)}, bf16[128,1024]{1,0:T(8,128)(2,1)S(1)}, u32[]{:S(2)}, u32[]{:S(2)}) collective-permute-start(bf16[128,1024]{1,0:T(8,128)(2,1)} %get-tuple-element.67), channel_id=1, source_target_pairs={{0,128},{1,129},{16,144},{17,145},{32,160},{33,161},{48,176},{49,1... | collective-permute-start | bytes 786440 | tf_op jit(solution)/shard_map/ppermute | solution.py:422
  16.8 2.6 %collective-permute-start.3 = (bf16[192,256]{1,0:T(8,128)(2,1)}, bf16[192,256]{1,0:T(8,128)(2,1)S(1)}, u32[]{:S(2)}, u32[]{:S(2)}) collective-permute-start(bf16[192,256]{1,0:T(8,128)(2,1)} %get-tuple-element.70), channel_id=1, source_target_pairs={{0,16},{1,113},{16,0},{17,33},{32,48},{33,17},{48,32},{49,65},{64,... | collective-permute-start | bytes 294920 | tf_op jit(solution)/shard_map/ppermute | solution.py:422
  20.2 1.9 %collective-permute-done.3 = bf16[192,256]{1,0:T(8,128)(2,1)S(1)} collective-permute-done((bf16[192,256]{1,0:T(8,128)(2,1)}, bf16[192,256]{1,0:T(8,128)(2,1)S(1)}, u32[]{:S(2)}, u32[]{:S(2)}) %collective-permute-start.3) | collective-permute-done | bytes 98336 | tf_op jit(solution)/shard_map/ppermute | solution.py:422
  23.0 4.2 %collective-permute-start.10 = (bf16[2,192,256]{2,1,0:T(8,128)(2,1)S(1)}, bf16[2,192,256]{2,1,0:T(8,128)(2,1)S(1)}, u32[]{:S(2)}, u32[]{:S(2)}) collective-permute-start(bf16[2,192,256]{2,1,0:T(8,128)(2,1)S(1)} %pad_maximum_fusion.1.own_b), channel_id=1, source_target_pairs={{0,32},{1,33},{16,48},{17,49},{32,64},{33,65},{48,80},{49,81},{64,... | collective-permute-start | bytes 589832 | tf_op jit(solution)/shard_map/ppermute | solution.py:422
  27.2 1.7 %collective-permute-done.1.qd2 = bf16[128,1024]{1,0:T(8,128)(2,1)S(1)} collective-permute-done((bf16[128,1024]{1,0:T(8,128)(2,1)}, bf16[128,1024]{1,0:T(8,128)(2,1)S(1)}, u32[]{:S(2)}, u32[]{:S(2)}) %collective-permute-start.1) | collective-permute-done | bytes 262176 | tf_op jit(solution)/shard_map/ppermute | solution.py:422
  31.4 3.4 %shard_map.129 = (bf16[2,128,1024]{2,1,0:T(8,128)(2,1)S(1)}, bf16[2,1024,128]{2,1,0:T(8,128)(2,1)S(1)}, bf16[2,128,1024]{2,1,0:T(8,128)(2,1)S(1)}, bf16[1,1280,1...) custom-call(s32[5]{0:T(128)S(1)} %stack.33.info, ...), custom_call_target="tpu_custom_call" | custom-call | flops 1342177280 | bytes 1000000 | tf_op jit(solution)/shard_map/pallas_call | solution.py:392
  34.8 3.5 %collective-permute-start.9 = (bf16[2,192,256]{2,1,0:T(8,128)(2,1)S(1)}, bf16[2,192,256]{2,1,0:T(8,128)(2,1)S(1)}, u32[]{:S(2)}, u32[]{:S(2)}) collective-permute-start(bf16[2,192,256]{2,1,0:T(8,128)(2,1)S(1)} %collective-permute-done.8.right_b), channel_id=1, source_target_pairs={{0,96},{1,97},{16,112},{17,113},{32,0},{33,1},{48,16},{49,17},{64,... | collective-permute-start | bytes 589832 | tf_op jit(solution)/shard_map/ppermute | solution.py:422
  38.2 7.9 %collective-permute-done.10.left_b = bf16[2,192,256]{2,1,0:T(8,128)(2,1)S(1)} collective-permute-done((bf16[2,192,256]{2,1,0:T(8,128)(2,1)S(1)}, bf16[2,192,256]{2,1,0:T(8,128)(2,1)S(1)}, u32[]{:S(2)}, u32[]{:S(2)}) %collective-permute-start.10) | collective-permute-done | bytes 196640 | tf_op jit(solution)/shard_map/ppermute | solution.py:422
  46.1 5.7 %shard_map.130 = (bf16[2,1280,1024]{2,1,0:T(8,128)(2,1)S(1)}, f32[2,1,1024]{2,1,0:T(1,128)S(1)}, f32[2,1,1024]{2,1,0:T(1,128)S(1)}, f32[2,128,1024]{2,1,0:T(8,128)S(1)}) custom-call(s32[5]{0:T(128)S(1)} %stack.33.info, bf16[2,128,1024]{2,1,0:T(8,128)(2,1)S(1)} %get-tuple-element.74.qt, bf16[2,192,256]{2,1,0:T(8,128)(2,1)S(1)} %collective-permute-done.6.left_a, ...), custom_call_target="tpu_custom_call" | custom-call | flops 2684354560 | bytes 1000000 | tf_op jit(solution)/shard_map/pallas_call | solution.py:392
  51.9 5.8 %shard_map.131 = (f32[2,1,1024]{2,1,0:T(1,128)S(1)}, bf16[2,128,1024]{2,1,0:T(8,128)(2,1)S(1)}, bf16[2,1024,128]{2,1,0:T(8,128)(2,1)S(1)}, f32[2,1,1024]{2,1,0:T...) custom-call(s32[5]{0:T(128)S(1)} %stack.33.info, ...), custom_call_target="tpu_custom_call" | custom-call | flops 4026531840 | bytes 1000000 | tf_op jit(solution)/shard_map/pallas_call | solution.py:392
  58.1 3.2 %collective-permute-start.13 = (bf16[2,192,256]{2,1,0:T(8,128)(2,1)S(1)}, bf16[2,192,256]{2,1,0:T(8,128)(2,1)S(1)}, u32[]{:S(2)}, u32[]{:S(2)}) collective-permute-start(bf16[2,192,256]{2,1,0:T(8,128)(2,1)S(1)} %get-tuple-element.95), channel_id=1, source_target_pairs={{0,96},{1,97},{16,112},{17,113},{32,0},{33,1},{48,16},{49,17},{64,... | collective-permute-start | bytes 589832 | tf_op jit(solution)/shard_map/ppermute | solution.py:422
  61.3 6.4 %shard_map.132 = (f32[2,128,1024]{2,1,0:T(8,128)S(1)}, bf16[4,192,256]{2,1,0:T(8,128)(2,1)S(1)}, bf16[4,192,256]{2,1,0:T(8,128)(2,1)S(1)}) custom-call(s32[5]{0:T(128)S(1)} %stack.33.info, bf16[2,1024,128]{2,1,0:T(8,128)(2,1)S(1)} %get-tuple-element.73.q, bf16[2,128,1024]{2,1,0:T(8,128)(2,1)S(1)} %get-tuple-element.82.uplt, ...), custom_call_target="tpu_custom_call" | custom-call | flops 5368709120 | bytes 1000000 | tf_op jit(solution)/shard_map/pallas_call | solution.py:392
  67.7 2.7 %collective-permute-done.12.far_a = bf16[2,192,256]{2,1,0:T(8,128)(2,1)S(1)} collective-permute-done((bf16[2,192,256]{2,1,0:T(8,128)(2,1)S(1)}, bf16[2,192,256]{2,1,0:T(8,128)(2,1)S(1)}, u32[]{:S(2)}, u32[]{:S(2)}) %collective-permute-start.12) | collective-permute-done | bytes 196640 | tf_op jit(solution)/shard_map/ppermute | solution.py:422
  70.5 1.5 %collective-permute-done.13.far_b = bf16[2,192,256]{2,1,0:T(8,128)(2,1)S(1)} collective-permute-done((bf16[2,192,256]{2,1,0:T(8,128)(2,1)S(1)}, bf16[2,192,256]{2,1,0:T(8,128)(2,1)S(1)}, u32[]{:S(2)}, u32[]{:S(2)}) %collective-permute-start.13) | collective-permute-done | bytes 196640 | tf_op jit(solution)/shard_map/ppermute | solution.py:422
  72.4 2.4 %collective-permute-start.15 = (bf16[4,192,256]{2,1,0:T(8,128)(2,1)S(1)}, bf16[4,192,256]{2,1,0:T(8,128)(2,1)S(1)}, u32[]{:S(2)}, u32[]{:S(2)}) collective-permute-start(bf16[4,192,256]{2,1,0:T(8,128)(2,1)S(1)} %get-tuple-element.97), channel_id=1, source_target_pairs={{0,32},{1,33},{16,48},{17,49},{32,64},{33,65},{48,80},{49,81},{64,... | collective-permute-start | bytes 1179656 | tf_op jit(solution)/shard_map/ppermute | solution.py:422
  74.7 4.4 %shard_map.133 = (bf16[4,192,256]{2,1,0:T(8,128)(2,1)S(1)}, bf16[128,1024]{1,0:T(8,128)(2,1)S(1)}, bf16[128,1024]{1,0:T(8,128)(2,1)S(1)}, bf16[128,1024]{1,0:T(8,128)(2,1)S(1)}, bf16[128,1024]{1,0:T(8,128)(2,1)S(1)}) custom-call(s32[5]{0:T(128)S(1)} %stack.33.info, bf16[2,1024,128]{2,1,0:T(8,128)(2,1)S(1)} %get-tuple-element.73.q, ...), custom_call_target="tpu_custom_call" | custom-call | flops 2684354560 | bytes 1000000 | tf_op jit(solution)/shard_map/pallas_call | solution.py:392
  79.4 4.2 %collective-permute-start.20 = (bf16[128,1024]{1,0:T(8,128)(2,1)S(1)}, bf16[128,1024]{1,0:T(8,128)(2,1)S(1)}, u32[]{:S(2)}, u32[]{:S(2)}) collective-permute-start(bf16[128,1024]{1,0:T(8,128)(2,1)S(1)} %get-tuple-element.103), channel_id=1, source_target_pairs={{0,128},{1,129},{16,144},{17,145},{32,160},{33,161},{48,176},{49,1... | collective-permute-start | bytes 786440 | tf_op jit(solution)/shard_map/ppermute | solution.py:422
  84.6 7.9 %collective-permute-done.14.left = bf16[4,192,256]{2,1,0:T(8,128)(2,1)S(1)} collective-permute-done((bf16[4,192,256]{2,1,0:T(8,128)(2,1)S(1)}, bf16[4,192,256]{2,1,0:T(8,128)(2,1)S(1)}, u32[]{:S(2)}, u32[]{:S(2)}) %collective-permute-start.14) | collective-permute-done | bytes 393248 | tf_op jit(solution)/shard_map/ppermute | solution.py:422
  92.8 2.1 %collective-permute-start.17 = (bf16[192,256]{1,0:T(8,128)(2,1)S(1)}, bf16[192,256]{1,0:T(8,128)(2,1)S(1)}, u32[]{:S(2)}, u32[]{:S(2)}) collective-permute-start(bf16[192,256]{1,0:T(8,128)(2,1)S(1)} %get-tuple-element.100), channel_id=1, source_target_pairs={{0,128},{1,129},{16,144},{17,145},{32,160},{33,161},{48,176},{49,1... | collective-permute-start | bytes 294920 | tf_op jit(solution)/shard_map/ppermute | solution.py:422
  94.8 1.3 %collective-permute-done.19.od1 = bf16[128,1024]{1,0:T(8,128)(2,1)S(1)} collective-permute-done((bf16[128,1024]{1,0:T(8,128)(2,1)S(1)}, bf16[128,1024]{1,0:T(8,128)(2,1)S(1)}, u32[]{:S(2)}, u32[]{:S(2)}) %collective-permute-start.19) | collective-permute-done | bytes 262176 | tf_op jit(solution)/shard_map/ppermute | solution.py:422
  96.1 2.0 %collective-permute-start.18 = (bf16[192,256]{1,0:T(8,128)(2,1)S(1)}, bf16[192,256]{1,0:T(8,128)(2,1)S(1)}, u32[]{:S(2)}, u32[]{:S(2)}) collective-permute-start(bf16[192,256]{1,0:T(8,128)(2,1)S(1)} %get-tuple-element.101), channel_id=1, source_target_pairs={{0,144},{1,241},{16,128},{17,161},{32,176},{33,145},{48,160},{49,1... | collective-permute-start | bytes 294920 | tf_op jit(solution)/shard_map/ppermute | solution.py:422
  98.1 2.1 %collective-permute-done.21.od3 = bf16[128,1024]{1,0:T(8,128)(2,1)S(1)} collective-permute-done((bf16[128,1024]{1,0:T(8,128)(2,1)S(1)}, bf16[128,1024]{1,0:T(8,128)(2,1)S(1)}, u32[]{:S(2)}, u32[]{:S(2)}) %collective-permute-start.21) | collective-permute-done | bytes 262176 | tf_op jit(solution)/shard_map/ppermute | solution.py:422
  103.8 3.1 %collective-permute-start.22 = (bf16[64,512]{1,0:T(8,128)(2,1)S(1)}, bf16[64,512]{1,0:T(8,128)(2,1)S(1)}, u32[]{:S(2)}, u32[]{:S(2)}) collective-permute-start(bf16[64,512]{1,0:T(8,128)(2,1)S(1)} %get-tuple-element.110), channel_id=1, source_target_pairs={{0,1},{1,0},{2,3},{3,2},{4,5},{5,4},{6,7},{7,6},{8,9},{9,8},{10,11... | collective-permute-start | bytes 196616 | tf_op jit(solution)/shard_map/ppermute | solution.py:408
  109.2 1.6 %shard_map.138 = (bf16[128,2048]{1,0:T(8,128)(2,1)}, bf16[128,2048]{1,0:T(8,128)(2,1)}) custom-call(s32[5]{0:T(128)S(1)} %stack.33.info, bf16[128,1024]{1,0:T(8,128)(2,1)S(1)} %get-tuple-element.113.od0, bf16[128,1024]{1,0:T(8,128)(2,1)S(1)} %collective-permute-done.19.od1, bf16[128,1024]{1,0:T(8,128)(2,1)S(1)} %collective-permute-done.20.od2, ...), custom_call_target="tpu_custom_call" | custom-call | bytes 1000000 | tf_op jit(solution)/shard_map/pallas_call | solution.py:392
  111.0 2.5 %collective-permute-start.26 = (bf16[64,512]{1,0:T(8,128)(2,1)S(1)}, bf16[64,512]{1,0:T(8,128)(2,1)S(1)}, u32[]{:S(2)}, u32[]{:S(2)}) collective-permute-start(bf16[64,512]{1,0:T(8,128)(2,1)S(1)} %add_convert_fusion.1), channel_id=1, source_target_pairs={{0,12},{4,0},{8,4},{12,8},{1,13},{5,1},{9,5},{13,9},{2,14},{6,2},{... | collective-permute-start | bytes 196616 | tf_op jit(solution)/shard_map/ppermute | solution.py:413
  113.6 1.6 %collective-permute-start.24 = (bf16[64,512]{1,0:T(8,128)(2,1)S(1)}, bf16[64,512]{1,0:T(8,128)(2,1)S(1)}, u32[]{:S(2)}, u32[]{:S(2)}) collective-permute-start(bf16[64,512]{1,0:T(8,128)(2,1)S(1)} %add_convert_fusion.1), channel_id=1, source_target_pairs={{0,8},{4,12},{8,0},{12,4},{1,9},{5,13},{9,1},{13,5},{2,10},{6,14},... | collective-permute-start | bytes 196616 | tf_op jit(solution)/shard_map/ppermute | solution.py:413
  115.2 3.4 %collective-permute-done.25 = bf16[64,512]{1,0:T(8,128)(2,1)S(1)} collective-permute-done((bf16[64,512]{1,0:T(8,128)(2,1)S(1)}, bf16[64,512]{1,0:T(8,128)(2,1)S(1)}, u32[]{:S(2)}, u32[]{:S(2)}) %collective-permute-start.25) | collective-permute-done | bytes 65568 | tf_op jit(solution)/shard_map/ppermute | solution.py:413
  118.6 3.0 %collective-permute-start.27 = (bf16[64,512]{1,0:T(8,128)(2,1)S(1)}, bf16[64,512]{1,0:T(8,128)(2,1)S(1)}, u32[]{:S(2)}, u32[]{:S(2)}) collective-permute-start(bf16[64,512]{1,0:T(8,128)(2,1)S(1)} %add_convert_fusion), channel_id=1, source_target_pairs={{0,1},{1,0},{2,3},{3,2},{4,5},{5,4},{6,7},{7,6},{8,9},{9,8},{10,11... | collective-permute-start | bytes 196616 | tf_op jit(solution)/shard_map/ppermute | solution.py:408
  (45 shorter events, 13.0 us)
Async XLA Ops:
  2.5 16.9 %collective-permute-start.4 = (bf16[192,256]{1,0:T(8,128)(2,1)}, bf16[192,256]{1,0:T(8,128)(2,1)S(1)}, u32[]{:S(2)}, u32[]{:S(2)}) collective-permute-start(bf16[192,256]{1,0:T(8,128)(2,1)} %get-tuple-element.71), channel_id=1, source_target_pairs={{0,128},{1,129},{16,144},{17,145},{32,160},{33,161},{48,176},{49,1... | collective-permute-start | bytes 294920 | tf_op jit(solution)/shard_map/ppermute | solution.py:422
  6.1 13.3 %collective-permute-start.5 = (bf16[192,256]{1,0:T(8,128)(2,1)}, bf16[192,256]{1,0:T(8,128)(2,1)S(1)}, u32[]{:S(2)}, u32[]{:S(2)}) collective-permute-start(bf16[192,256]{1,0:T(8,128)(2,1)} %get-tuple-element.72), channel_id=1, source_target_pairs={{0,144},{1,241},{16,128},{17,161},{32,176},{33,145},{48,160},{49,1... | collective-permute-start | bytes 294920 | tf_op jit(solution)/shard_map/ppermute | solution.py:422
  13.9 9.1 %collective-permute-start = (bf16[128,1024]{1,0:T(8,128)(2,1)}, bf16[128,1024]{1,0:T(8,128)(2,1)S(1)}, u32[]{:S(2)}, u32[]{:S(2)}) collective-permute-start(bf16[128,1024]{1,0:T(8,128)(2,1)} %get-tuple-element.66), channel_id=1, source_target_pairs={{0,16},{1,113},{16,0},{17,33},{32,48},{33,17},{48,32},{49,65},{64,... | collective-permute-start | bytes 786440 | tf_op jit(solution)/shard_map/ppermute | solution.py:422
  14.1 14.9 %collective-permute-start.1 = (bf16[128,1024]{1,0:T(8,128)(2,1)}, bf16[128,1024]{1,0:T(8,128)(2,1)S(1)}, u32[]{:S(2)}, u32[]{:S(2)}) collective-permute-start(bf16[128,1024]{1,0:T(8,128)(2,1)} %get-tuple-element.67), channel_id=1, source_target_pairs={{0,128},{1,129},{16,144},{17,145},{32,160},{33,161},{48,176},{49,1... | collective-permute-start | bytes 786440 | tf_op jit(solution)/shard_map/ppermute | solution.py:422
  16.8 5.2 %collective-permute-start.3 = (bf16[192,256]{1,0:T(8,128)(2,1)}, bf16[192,256]{1,0:T(8,128)(2,1)S(1)}, u32[]{:S(2)}, u32[]{:S(2)}) collective-permute-start(bf16[192,256]{1,0:T(8,128)(2,1)} %get-tuple-element.70), channel_id=1, source_target_pairs={{0,16},{1,113},{16,0},{17,33},{32,48},{33,17},{48,32},{49,65},{64,... | collective-permute-start | bytes 294920 | tf_op jit(solution)/shard_map/ppermute | solution.py:422
  19.4 11.0 %collective-permute-start.2 = (bf16[128,1024]{1,0:T(8,128)(2,1)}, bf16[128,1024]{1,0:T(8,128)(2,1)S(1)}, u32[]{:S(2)}, u32[]{:S(2)}) collective-permute-start(bf16[128,1024]{1,0:T(8,128)(2,1)} %get-tuple-element.68), channel_id=1, source_target_pairs={{0,144},{1,241},{16,128},{17,161},{32,176},{33,145},{48,160},{49,1... | collective-permute-start | bytes 786440 | tf_op jit(solution)/shard_map/ppermute | solution.py:422
  19.5 15.3 %collective-permute-start.8 = (bf16[2,192,256]{2,1,0:T(8,128)(2,1)S(1)}, bf16[2,192,256]{2,1,0:T(8,128)(2,1)S(1)}, u32[]{:S(2)}, u32[]{:S(2)}) collective-permute-start(bf16[2,192,256]{2,1,0:T(8,128)(2,1)S(1)} %pad_maximum_fusion.1.own_b), channel_id=1, source_target_pairs={{0,96},{1,97},{16,112},{17,113},{32,0},{33,1},{48,16},{49,17},{64,... | collective-permute-start | bytes 589832 | tf_op jit(solution)/shard_map/ppermute | solution.py:422
  22.9 15.3 %collective-permute-start.6 = (bf16[2,192,256]{2,1,0:T(8,128)(2,1)S(1)}, bf16[2,192,256]{2,1,0:T(8,128)(2,1)S(1)}, u32[]{:S(2)}, u32[]{:S(2)}) collective-permute-start(bf16[2,192,256]{2,1,0:T(8,128)(2,1)S(1)} %pad_maximum_fusion.own_a), channel_id=1, source_target_pairs={{0,32},{1,33},{16,48},{17,49},{32,64},{33,65},{48,80},{49,81},{64,... | collective-permute-start | bytes 589832 | tf_op jit(solution)/shard_map/ppermute | solution.py:422
  23.0 23.1 %collective-permute-start.10 = (bf16[2,192,256]{2,1,0:T(8,128)(2,1)S(1)}, bf16[2,192,256]{2,1,0:T(8,128)(2,1)S(1)}, u32[]{:S(2)}, u32[]{:S(2)}) collective-permute-start(bf16[2,192,256]{2,1,0:T(8,128)(2,1)S(1)} %pad_maximum_fusion.1.own_b), channel_id=1, source_target_pairs={{0,32},{1,33},{16,48},{17,49},{32,64},{33,65},{48,80},{49,81},{64,... | collective-permute-start | bytes 589832 | tf_op jit(solution)/shard_map/ppermute | solution.py:422
  29.0 17.2 %collective-permute-start.11 = (bf16[2,192,256]{2,1,0:T(8,128)(2,1)S(1)}, bf16[2,192,256]{2,1,0:T(8,128)(2,1)S(1)}, u32[]{:S(2)}, u32[]{:S(2)}) collective-permute-start(bf16[2,192,256]{2,1,0:T(8,128)(2,1)S(1)} %pad_maximum_fusion.own_a), channel_id=1, source_target_pairs={{0,96},{1,97},{16,112},{17,113},{32,0},{33,1},{48,16},{49,17},{64,... | collective-permute-start | bytes 589832 | tf_op jit(solution)/shard_map/ppermute | solution.py:422
  30.4 1.0 copy-start
  34.8 17.1 %collective-permute-start.9 = (bf16[2,192,256]{2,1,0:T(8,128)(2,1)S(1)}, bf16[2,192,256]{2,1,0:T(8,128)(2,1)S(1)}, u32[]{:S(2)}, u32[]{:S(2)}) collective-permute-start(bf16[2,192,256]{2,1,0:T(8,128)(2,1)S(1)} %collective-permute-done.8.right_b), channel_id=1, source_target_pairs={{0,96},{1,97},{16,112},{17,113},{32,0},{33,1},{48,16},{49,17},{64,... | collective-permute-start | bytes 589832 | tf_op jit(solution)/shard_map/ppermute | solution.py:422
  38.2 13.6 %collective-permute-start.7 = (bf16[2,192,256]{2,1,0:T(8,128)(2,1)S(1)}, bf16[2,192,256]{2,1,0:T(8,128)(2,1)S(1)}, u32[]{:S(2)}, u32[]{:S(2)}) collective-permute-start(bf16[2,192,256]{2,1,0:T(8,128)(2,1)S(1)} %collective-permute-done.6.left_a), channel_id=1, source_target_pairs={{0,32},{1,33},{16,48},{17,49},{32,64},{33,65},{48,80},{49,81},{64,... | collective-permute-start | bytes 589832 | tf_op jit(solution)/shard_map/ppermute | solution.py:422
  57.6 12.8 %collective-permute-start.12 = (bf16[2,192,256]{2,1,0:T(8,128)(2,1)S(1)}, bf16[2,192,256]{2,1,0:T(8,128)(2,1)S(1)}, u32[]{:S(2)}, u32[]{:S(2)}) collective-permute-start(bf16[2,192,256]{2,1,0:T(8,128)(2,1)S(1)} %get-tuple-element.94), channel_id=1, source_target_pairs={{0,32},{1,33},{16,48},{17,49},{32,64},{33,65},{48,80},{49,81},{64,... | collective-permute-start | bytes 589832 | tf_op jit(solution)/shard_map/ppermute | solution.py:422
  58.1 13.9 %collective-permute-start.13 = (bf16[2,192,256]{2,1,0:T(8,128)(2,1)S(1)}, bf16[2,192,256]{2,1,0:T(8,128)(2,1)S(1)}, u32[]{:S(2)}, u32[]{:S(2)}) collective-permute-start(bf16[2,192,256]{2,1,0:T(8,128)(2,1)S(1)} %get-tuple-element.95), channel_id=1, source_target_pairs={{0,96},{1,97},{16,112},{17,113},{32,0},{33,1},{48,16},{49,17},{64,... | collective-permute-start | bytes 589832 | tf_op jit(solution)/shard_map/ppermute | solution.py:422
  72.1 20.4 %collective-permute-start.14 = (bf16[4,192,256]{2,1,0:T(8,128)(2,1)S(1)}, bf16[4,192,256]{2,1,0:T(8,128)(2,1)S(1)}, u32[]{:S(2)}, u32[]{:S(2)}) collective-permute-start(bf16[4,192,256]{2,1,0:T(8,128)(2,1)S(1)} %get-tuple-element.96), channel_id=1, source_target_pairs={{0,96},{1,97},{16,112},{17,113},{32,0},{33,1},{48,16},{49,17},{64,... | collective-permute-start | bytes 1179656 | tf_op jit(solution)/shard_map/ppermute | solution.py:422
  72.4 20.1 %collective-permute-start.15 = (bf16[4,192,256]{2,1,0:T(8,128)(2,1)S(1)}, bf16[4,192,256]{2,1,0:T(8,128)(2,1)S(1)}, u32[]{:S(2)}, u32[]{:S(2)}) collective-permute-start(bf16[4,192,256]{2,1,0:T(8,128)(2,1)S(1)} %get-tuple-element.97), channel_id=1, source_target_pairs={{0,32},{1,33},{16,48},{17,49},{32,64},{33,65},{48,80},{49,81},{64,... | collective-permute-start | bytes 1179656 | tf_op jit(solution)/shard_map/ppermute | solution.py:422
  79.1 17.0 %collective-permute-start.19 = (bf16[128,1024]{1,0:T(8,128)(2,1)S(1)}, bf16[128,1024]{1,0:T(8,128)(2,1)S(1)}, u32[]{:S(2)}, u32[]{:S(2)}) collective-permute-start(bf16[128,1024]{1,0:T(8,128)(2,1)S(1)} %get-tuple-element.102), channel_id=1, source_target_pairs={{0,16},{1,113},{16,0},{17,33},{32,48},{33,17},{48,32},{49,65},{64,... | collective-permute-start | bytes 786440 | tf_op jit(solution)/shard_map/ppermute | solution.py:422
  79.4 18.7 %collective-permute-start.20 = (bf16[128,1024]{1,0:T(8,128)(2,1)S(1)}, bf16[128,1024]{1,0:T(8,128)(2,1)S(1)}, u32[]{:S(2)}, u32[]{:S(2)}) collective-permute-start(bf16[128,1024]{1,0:T(8,128)(2,1)S(1)} %get-tuple-element.103), channel_id=1, source_target_pairs={{0,128},{1,129},{16,144},{17,145},{32,160},{33,161},{48,176},{49,1... | collective-permute-start | bytes 786440 | tf_op jit(solution)/shard_map/ppermute | solution.py:422
  83.6 16.6 %collective-permute-start.21 = (bf16[128,1024]{1,0:T(8,128)(2,1)S(1)}, bf16[128,1024]{1,0:T(8,128)(2,1)S(1)}, u32[]{:S(2)}, u32[]{:S(2)}) collective-permute-start(bf16[128,1024]{1,0:T(8,128)(2,1)S(1)} %get-tuple-element.104), channel_id=1, source_target_pairs={{0,144},{1,241},{16,128},{17,161},{32,176},{33,145},{48,160},{49,1... | collective-permute-start | bytes 786440 | tf_op jit(solution)/shard_map/ppermute | solution.py:422
  92.7 8.1 %collective-permute-start.16 = (bf16[192,256]{1,0:T(8,128)(2,1)S(1)}, bf16[192,256]{1,0:T(8,128)(2,1)S(1)}, u32[]{:S(2)}, u32[]{:S(2)}) collective-permute-start(bf16[192,256]{1,0:T(8,128)(2,1)S(1)} %get-tuple-element.99), channel_id=1, source_target_pairs={{0,16},{1,113},{16,0},{17,33},{32,48},{33,17},{48,32},{49,65},{64,... | collective-permute-start | bytes 294920 | tf_op jit(solution)/shard_map/ppermute | solution.py:422
  92.8 9.3 %collective-permute-start.17 = (bf16[192,256]{1,0:T(8,128)(2,1)S(1)}, bf16[192,256]{1,0:T(8,128)(2,1)S(1)}, u32[]{:S(2)}, u32[]{:S(2)}) collective-permute-start(bf16[192,256]{1,0:T(8,128)(2,1)S(1)} %get-tuple-element.100), channel_id=1, source_target_pairs={{0,128},{1,129},{16,144},{17,145},{32,160},{33,161},{48,176},{49,1... | collective-permute-start | bytes 294920 | tf_op jit(solution)/shard_map/ppermute | solution.py:422
  96.1 7.1 %collective-permute-start.18 = (bf16[192,256]{1,0:T(8,128)(2,1)S(1)}, bf16[192,256]{1,0:T(8,128)(2,1)S(1)}, u32[]{:S(2)}, u32[]{:S(2)}) collective-permute-start(bf16[192,256]{1,0:T(8,128)(2,1)S(1)} %get-tuple-element.101), channel_id=1, source_target_pairs={{0,144},{1,241},{16,128},{17,161},{32,176},{33,145},{48,160},{49,1... | collective-permute-start | bytes 294920 | tf_op jit(solution)/shard_map/ppermute | solution.py:422
  103.8 4.0 %collective-permute-start.22 = (bf16[64,512]{1,0:T(8,128)(2,1)S(1)}, bf16[64,512]{1,0:T(8,128)(2,1)S(1)}, u32[]{:S(2)}, u32[]{:S(2)}) collective-permute-start(bf16[64,512]{1,0:T(8,128)(2,1)S(1)} %get-tuple-element.110), channel_id=1, source_target_pairs={{0,1},{1,0},{2,3},{3,2},{4,5},{5,4},{6,7},{7,6},{8,9},{9,8},{10,11... | collective-permute-start | bytes 196616 | tf_op jit(solution)/shard_map/ppermute | solution.py:408
  107.8 3.2 %collective-permute-start.23 = (bf16[64,512]{1,0:T(8,128)(2,1)S(1)}, bf16[64,512]{1,0:T(8,128)(2,1)S(1)}, u32[]{:S(2)}, u32[]{:S(2)}) collective-permute-start(bf16[64,512]{1,0:T(8,128)(2,1)S(1)} %add_convert_fusion.2), channel_id=1, source_target_pairs={{0,2},{2,0},{1,3},{3,1},{4,6},{6,4},{5,7},{7,5},{8,10},{10,8},{9,1... | collective-permute-start | bytes 196616 | tf_op jit(solution)/shard_map/ppermute | solution.py:408
  111.0 4.2 %collective-permute-start.26 = (bf16[64,512]{1,0:T(8,128)(2,1)S(1)}, bf16[64,512]{1,0:T(8,128)(2,1)S(1)}, u32[]{:S(2)}, u32[]{:S(2)}) collective-permute-start(bf16[64,512]{1,0:T(8,128)(2,1)S(1)} %add_convert_fusion.1), channel_id=1, source_target_pairs={{0,12},{4,0},{8,4},{12,8},{1,13},{5,1},{9,5},{13,9},{2,14},{6,2},{... | collective-permute-start | bytes 196616 | tf_op jit(solution)/shard_map/ppermute | solution.py:413
  113.6 5.0 %collective-permute-start.25 = (bf16[64,512]{1,0:T(8,128)(2,1)S(1)}, bf16[64,512]{1,0:T(8,128)(2,1)S(1)}, u32[]{:S(2)}, u32[]{:S(2)}) collective-permute-start(bf16[64,512]{1,0:T(8,128)(2,1)S(1)} %add_convert_fusion.1), channel_id=1, source_target_pairs={{0,4},{4,8},{8,12},{12,0},{1,5},{5,9},{9,13},{13,1},{2,6},{6,10},{... | collective-permute-start | bytes 196616 | tf_op jit(solution)/shard_map/ppermute | solution.py:413
  113.6 5.0 %collective-permute-start.24 = (bf16[64,512]{1,0:T(8,128)(2,1)S(1)}, bf16[64,512]{1,0:T(8,128)(2,1)S(1)}, u32[]{:S(2)}, u32[]{:S(2)}) collective-permute-start(bf16[64,512]{1,0:T(8,128)(2,1)S(1)} %add_convert_fusion.1), channel_id=1, source_target_pairs={{0,8},{4,12},{8,0},{12,4},{1,9},{5,13},{9,1},{13,5},{2,10},{6,14},... | collective-permute-start | bytes 196616 | tf_op jit(solution)/shard_map/ppermute | solution.py:413
  118.6 3.9 %collective-permute-start.27 = (bf16[64,512]{1,0:T(8,128)(2,1)S(1)}, bf16[64,512]{1,0:T(8,128)(2,1)S(1)}, u32[]{:S(2)}, u32[]{:S(2)}) collective-permute-start(bf16[64,512]{1,0:T(8,128)(2,1)S(1)} %add_convert_fusion), channel_id=1, source_target_pairs={{0,1},{1,0},{2,3},{3,2},{4,5},{5,4},{6,7},{7,6},{8,9},{9,8},{10,11... | collective-permute-start | bytes 196616 | tf_op jit(solution)/shard_map/ppermute | solution.py:408

commit v8 on v5

--- a/solution.py
+++ b/solution.py
@@ -464,9 +464,10 @@
     )
     for d in (1, 2, 3):
         kv[d] = partner(kv[d], d)
-    for d in (1, 2, 3):
-        qd[d] = partner(qd[d], d)
+    qd[1], qd[2] = partner(qd[1], 1), partner(qd[2], 2)
     own_a, own_b = jnp.stack(kv[:2]), jnp.stack(kv[2:])
+    own_a, own_b, qd[3] = lax.optimization_barrier((own_a, own_b, qd[3]))
+    qd[3] = partner(qd[3], 3)
     left_a, right_b = quad_turn(own_a, 1), quad_turn(own_b, -1)
     left_b, right_a = quad_turn(own_b, 1), quad_turn(own_a, -1)
     far_a, far_b = quad_turn(left_a, 1), quad_turn(right_b, -1)

time: 123 us -> 128 us (1.041)
  starting transfers between devices: 49.8 us -> 54.6 us
    ppermute x3, starting transfers between devices: 5.93 us -> 12.6 us  [swap(): return lax.ppermute(x, axis, [(0, 1), (1, 0)])]
    ppermute x22, starting transfers between devices: 39.2 us -> 37.5 us  [local_permute(): return lax.ppermute(x, LOCAL, pairs)]
  transfers between devices with their start and end apart: 28 -> 28, of which waited for: 13 -> 12; matrix products, arithmetic and copies ran while one was open for 1% -> 1% of each run, Pallas kernels for 21% -> 20%
where the time goes in v8:
time: 128 us
  starting transfers between devices  54.6 us (43%)
  waiting for transfers between devices  35.3 us (28%)
  Pallas kernels  33.4 us (26%)
  between operations  2.18 us (2%)
  other arithmetic  1.67 us (1%)
    ppermute x22, starting transfers between devices, local_permute(): return lax.ppermute(x, LOCAL, pairs)  37.5 us
    pallas_call x12, Pallas kernels, call(): pl.pallas_call(kernel, out_shape=tuple(outs), in_specs=[SMEM] * len(scala...  33.4 us
    ppermute x22, waiting for transfers between devices, local_permute(): return lax.ppermute(x, LOCAL, pairs)  29.8 us
    ppermute x3, starting transfers between devices, swap(): return lax.ppermute(x, axis, [(0, 1), (1, 0)])  12.6 us
    ppermute x3, starting transfers between devices, turn(): return lax.ppermute(x, axis, [(i, (i + step) % size) for i in range(size)])  4.47 us
    ppermute x3, waiting for transfers between devices, turn(): return lax.ppermute(x, axis, [(i, (i + step) % size) for i in range(size)])  3.63 us
  transfers between devices with their start and end apart: 28, of which 12 were waited for; matrix products, arithmetic and copies ran while one was open for 1% of the time, Pallas kernels for 20%

profile of v8, /device:TPU:1, one launch (start us, length us, event | category | flops | bytes accessed | tf_op | source)
XLA Modules:
  0.0 128.1 jit_solution(5567606902120538769)
XLA Ops:
  0.6 1.8 %shard_map.128 = (bf16[192,256]{1,0:T(8,128)(2,1)}, bf16[192,256]{1,0:T(8,128)(2,1)}, bf16[192,256]{1,0:T(8,128)(2,1)}, bf16[192,256]{1,0:T(8,128)(2,1)}) custom-call(s32[1]{0:T(128)} %bitcast.info, bf16[128,512]{1,0:T(8,128)(2,1)} %bitcast.17, bf16[128,512]{1,0:T(8,128)(2,1)} %bitcast.18, bf16[64,512]{1,0:T(8,128)(2,1)} %kp.1, bf16[64,512]{1,0:T(8,128)(2,1)} %vp.1), custom_call_target="tpu_custom_call" | custom-call | bytes 1000000 | tf_op jit(solution)/shard_map/pallas_call | solution.py:392
  2.5 6.5 %collective-permute-start.2 = (bf16[192,256]{1,0:T(8,128)(2,1)}, bf16[192,256]{1,0:T(8,128)(2,1)S(1)}, u32[]{:S(2)}, u32[]{:S(2)}) collective-permute-start(bf16[192,256]{1,0:T(8,128)(2,1)} %get-tuple-element.75), channel_id=1, source_target_pairs={{0,16},{1,113},{16,0},{17,33},{32,48},{33,17},{48,32},{49,65},{64,... | collective-permute-start | bytes 294920 | tf_op jit(solution)/shard_map/ppermute | solution.py:422
  9.0 2.7 %collective-permute-start.3 = (bf16[192,256]{1,0:T(8,128)(2,1)}, bf16[192,256]{1,0:T(8,128)(2,1)S(1)}, u32[]{:S(2)}, u32[]{:S(2)}) collective-permute-start(bf16[192,256]{1,0:T(8,128)(2,1)} %get-tuple-element.76), channel_id=1, source_target_pairs={{0,128},{1,129},{16,144},{17,145},{32,160},{33,161},{48,176},{49,1... | collective-permute-start | bytes 294920 | tf_op jit(solution)/shard_map/ppermute | solution.py:422
  11.8 2.2 %shard_map.127 = (bf16[128,1024]{1,0:T(8,128)(2,1)}, bf16[128,1024]{1,0:T(8,128)(2,1)}, bf16[128,1024]{1,0:T(8,128)(2,1)}, bf16[128,1024]{1,0:T(8,128)(2,1)}) custom-call(s32[1]{0:T(128)} %bitcast.info, bf16[128,2048]{1,0:T(8,128)(2,1)} %bitcast.15, bf16[128,2048]{1,0:T(8,128)(2,1)} %bitcast.16), custom_call_target="tpu_custom_call" | custom-call | bytes 1000000 | tf_op jit(solution)/shard_map/pallas_call | solution.py:392
  14.0 2.7 %collective-permute-start = (bf16[128,1024]{1,0:T(8,128)(2,1)}, bf16[128,1024]{1,0:T(8,128)(2,1)S(1)}, u32[]{:S(2)}, u32[]{:S(2)}) collective-permute-start(bf16[128,1024]{1,0:T(8,128)(2,1)} %get-tuple-element.72), channel_id=1, source_target_pairs={{0,16},{1,113},{16,0},{17,33},{32,48},{33,17},{48,32},{49,65},{64,... | collective-permute-start | bytes 786440 | tf_op jit(solution)/shard_map/ppermute | solution.py:422
  16.7 2.7 %collective-permute-start.1 = (bf16[128,1024]{1,0:T(8,128)(2,1)}, bf16[128,1024]{1,0:T(8,128)(2,1)S(1)}, u32[]{:S(2)}, u32[]{:S(2)}) collective-permute-start(bf16[128,1024]{1,0:T(8,128)(2,1)} %get-tuple-element.73), channel_id=1, source_target_pairs={{0,128},{1,129},{16,144},{17,145},{32,160},{33,161},{48,176},{49,1... | collective-permute-start | bytes 786440 | tf_op jit(solution)/shard_map/ppermute | solution.py:422
  20.6 3.6 %collective-permute-start.8 = (bf16[2,192,256]{2,1,0:T(8,128)(2,1)S(1)}, bf16[2,192,256]{2,1,0:T(8,128)(2,1)S(1)}, u32[]{:S(2)}, u32[]{:S(2)}) collective-permute-start(bf16[2,192,256]{2,1,0:T(8,128)(2,1)S(1)} %pad_maximum_fusion.1.own_b), channel_id=1, source_target_pairs={{0,96},{1,97},{16,112},{17,113},{32,0},{33,1},{48,16},{49,17},{64,... | collective-permute-start | bytes 589832 | tf_op jit(solution)/shard_map/ppermute | solution.py:422
  24.7 3.2 %collective-permute-done.1.qd2 = bf16[128,1024]{1,0:T(8,128)(2,1)S(1)} collective-permute-done((bf16[128,1024]{1,0:T(8,128)(2,1)}, bf16[128,1024]{1,0:T(8,128)(2,1)S(1)}, u32[]{:S(2)}, u32[]{:S(2)}) %collective-permute-start.1) | collective-permute-done | bytes 262176 | tf_op jit(solution)/shard_map/ppermute | solution.py:422
  29.3 6.0 %collective-permute-done.6.left_a = bf16[2,192,256]{2,1,0:T(8,128)(2,1)S(1)} collective-permute-done((bf16[2,192,256]{2,1,0:T(8,128)(2,1)S(1)}, bf16[2,192,256]{2,1,0:T(8,128)(2,1)S(1)}, u32[]{:S(2)}, u32[]{:S(2)}) %collective-permute-start.6) | collective-permute-done | bytes 196640 | tf_op jit(solution)/shard_map/ppermute | solution.py:422
  35.3 3.6 %collective-permute-start.9 = (bf16[2,192,256]{2,1,0:T(8,128)(2,1)S(1)}, bf16[2,192,256]{2,1,0:T(8,128)(2,1)S(1)}, u32[]{:S(2)}, u32[]{:S(2)}) collective-permute-start(bf16[2,192,256]{2,1,0:T(8,128)(2,1)S(1)} %collective-permute-done.8.right_b), channel_id=1, source_target_pairs={{0,96},{1,97},{16,112},{17,113},{32,0},{33,1},{48,16},{49,17},{64,... | collective-permute-start | bytes 589832 | tf_op jit(solution)/shard_map/ppermute | solution.py:422
  39.9 3.4 %shard_map.129 = (bf16[2,128,1024]{2,1,0:T(8,128)(2,1)S(1)}, bf16[2,1024,128]{2,1,0:T(8,128)(2,1)S(1)}, bf16[2,128,1024]{2,1,0:T(8,128)(2,1)S(1)}, bf16[1,1280,1...) custom-call(s32[5]{0:T(128)S(1)} %stack.33.info, ...), custom_call_target="tpu_custom_call" | custom-call | flops 1342177280 | bytes 1000000 | tf_op jit(solution)/shard_map/pallas_call | solution.py:392
  43.3 3.2 %collective-permute-done.10.left_b = bf16[2,192,256]{2,1,0:T(8,128)(2,1)S(1)} collective-permute-done((bf16[2,192,256]{2,1,0:T(8,128)(2,1)S(1)}, bf16[2,192,256]{2,1,0:T(8,128)(2,1)S(1)}, u32[]{:S(2)}, u32[]{:S(2)}) %collective-permute-start.10) | collective-permute-done | bytes 196640 | tf_op jit(solution)/shard_map/ppermute | solution.py:422
  46.4 5.7 %shard_map.130 = (bf16[2,1280,1024]{2,1,0:T(8,128)(2,1)S(1)}, f32[2,1,1024]{2,1,0:T(1,128)S(1)}, f32[2,1,1024]{2,1,0:T(1,128)S(1)}, f32[2,128,1024]{2,1,0:T(8,128)S(1)}) custom-call(s32[5]{0:T(128)S(1)} %stack.33.info, bf16[2,128,1024]{2,1,0:T(8,128)(2,1)S(1)} %get-tuple-element.83.qt, bf16[2,192,256]{2,1,0:T(8,128)(2,1)S(1)} %collective-permute-done.6.left_a, ...), custom_call_target="tpu_custom_call" | custom-call | flops 2684354560 | bytes 1000000 | tf_op jit(solution)/shard_map/pallas_call | solution.py:392
  52.2 5.7 %shard_map.131 = (f32[2,1,1024]{2,1,0:T(1,128)S(1)}, bf16[2,128,1024]{2,1,0:T(8,128)(2,1)S(1)}, bf16[2,1024,128]{2,1,0:T(8,128)(2,1)S(1)}, f32[2,1,1024]{2,1,0:T...) custom-call(s32[5]{0:T(128)S(1)} %stack.33.info, ...), custom_call_target="tpu_custom_call" | custom-call | flops 4026531840 | bytes 1000000 | tf_op jit(solution)/shard_map/pallas_call | solution.py:392
  58.0 3.6 %collective-permute-start.13 = (bf16[2,192,256]{2,1,0:T(8,128)(2,1)S(1)}, bf16[2,192,256]{2,1,0:T(8,128)(2,1)S(1)}, u32[]{:S(2)}, u32[]{:S(2)}) collective-permute-start(bf16[2,192,256]{2,1,0:T(8,128)(2,1)S(1)} %get-tuple-element.104), channel_id=1, source_target_pairs={{0,96},{1,97},{16,112},{17,113},{32,0},{33,1},{48,16},{49,17},{64,... | collective-permute-start | bytes 589832 | tf_op jit(solution)/shard_map/ppermute | solution.py:422
  61.6 6.4 %shard_map.132 = (f32[2,128,1024]{2,1,0:T(8,128)S(1)}, bf16[4,192,256]{2,1,0:T(8,128)(2,1)S(1)}, bf16[4,192,256]{2,1,0:T(8,128)(2,1)S(1)}) custom-call(s32[5]{0:T(128)S(1)} %stack.33.info, bf16[2,1024,128]{2,1,0:T(8,128)(2,1)S(1)} %get-tuple-element.82.q, bf16[2,128,1024]{2,1,0:T(8,128)(2,1)S(1)} %get-tuple-element.91.uplt, ...), custom_call_target="tpu_custom_call" | custom-call | flops 5368709120 | bytes 1000000 | tf_op jit(solution)/shard_map/pallas_call | solution.py:392
  68.5 2.1 %collective-permute-start.15 = (bf16[4,192,256]{2,1,0:T(8,128)(2,1)S(1)}, bf16[4,192,256]{2,1,0:T(8,128)(2,1)S(1)}, u32[]{:S(2)}, u32[]{:S(2)}) collective-permute-start(bf16[4,192,256]{2,1,0:T(8,128)(2,1)S(1)} %get-tuple-element.106), channel_id=1, source_target_pairs={{0,32},{1,33},{16,48},{17,49},{32,64},{33,65},{48,80},{49,81},{64,... | collective-permute-start | bytes 1179656 | tf_op jit(solution)/shard_map/ppermute | solution.py:422
  70.6 4.4 %shard_map.133 = (bf16[4,192,256]{2,1,0:T(8,128)(2,1)S(1)}, bf16[128,1024]{1,0:T(8,128)(2,1)S(1)}, bf16[128,1024]{1,0:T(8,128)(2,1)S(1)}, bf16[128,1024]{1,0:T(8,128)(2,1)S(1)}, bf16[128,1024]{1,0:T(8,128)(2,1)S(1)}) custom-call(s32[5]{0:T(128)S(1)} %stack.33.info, bf16[2,1024,128]{2,1,0:T(8,128)(2,1)S(1)} %get-tuple-element.82.q, ...), custom_call_target="tpu_custom_call" | custom-call | flops 2684354560 | bytes 1000000 | tf_op jit(solution)/shard_map/pallas_call | solution.py:392
  75.0 2.8 %collective-permute-start.20 = (bf16[128,1024]{1,0:T(8,128)(2,1)S(1)}, bf16[128,1024]{1,0:T(8,128)(2,1)S(1)}, u32[]{:S(2)}, u32[]{:S(2)}) collective-permute-start(bf16[128,1024]{1,0:T(8,128)(2,1)S(1)} %get-tuple-element.115), channel_id=1, source_target_pairs={{0,128},{1,129},{16,144},{17,145},{32,160},{33,161},{48,176},{49,1... | collective-permute-start | bytes 786440 | tf_op jit(solution)/shard_map/ppermute | solution.py:422
  77.8 3.4 %collective-permute-done.14.left = bf16[4,192,256]{2,1,0:T(8,128)(2,1)S(1)} collective-permute-done((bf16[4,192,256]{2,1,0:T(8,128)(2,1)S(1)}, bf16[4,192,256]{2,1,0:T(8,128)(2,1)S(1)}, u32[]{:S(2)}, u32[]{:S(2)}) %collective-permute-start.14) | collective-permute-done | bytes 393248 | tf_op jit(solution)/shard_map/ppermute | solution.py:422
  81.2 3.7 %collective-permute-done.15.right = bf16[4,192,256]{2,1,0:T(8,128)(2,1)S(1)} collective-permute-done((bf16[4,192,256]{2,1,0:T(8,128)(2,1)S(1)}, bf16[4,192,256]{2,1,0:T(8,128)(2,1)S(1)}, u32[]{:S(2)}, u32[]{:S(2)}) %collective-permute-start.15) | collective-permute-done | bytes 393248 | tf_op jit(solution)/shard_map/ppermute | solution.py:422
  85.1 2.8 %collective-permute-start.16 = (bf16[192,256]{1,0:T(8,128)(2,1)S(1)}, bf16[192,256]{1,0:T(8,128)(2,1)S(1)}, u32[]{:S(2)}, u32[]{:S(2)}) collective-permute-start(bf16[192,256]{1,0:T(8,128)(2,1)S(1)} %get-tuple-element.111), channel_id=1, source_target_pairs={{0,16},{1,113},{16,0},{17,33},{32,48},{33,17},{48,32},{49,65},{64,... | collective-permute-start | bytes 294920 | tf_op jit(solution)/shard_map/ppermute | solution.py:422
  87.8 3.3 %collective-permute-start.17 = (bf16[192,256]{1,0:T(8,128)(2,1)S(1)}, bf16[192,256]{1,0:T(8,128)(2,1)S(1)}, u32[]{:S(2)}, u32[]{:S(2)}) collective-permute-start(bf16[192,256]{1,0:T(8,128)(2,1)S(1)} %get-tuple-element.112), channel_id=1, source_target_pairs={{0,128},{1,129},{16,144},{17,145},{32,160},{33,161},{48,176},{49,1... | collective-permute-start | bytes 294920 | tf_op jit(solution)/shard_map/ppermute | solution.py:422
  91.4 6.0 %collective-permute-done.16.g1 = bf16[192,256]{1,0:T(8,128)(2,1)S(1)} collective-permute-done((bf16[192,256]{1,0:T(8,128)(2,1)S(1)}, bf16[192,256]{1,0:T(8,128)(2,1)S(1)}, u32[]{:S(2)}, u32[]{:S(2)}) %collective-permute-start.16) | collective-permute-done | bytes 98336 | tf_op jit(solution)/shard_map/ppermute | solution.py:422
  97.4 4.1 %collective-permute-done.18.g3 = bf16[192,256]{1,0:T(8,128)(2,1)S(1)} collective-permute-done((bf16[192,256]{1,0:T(8,128)(2,1)S(1)}, bf16[192,256]{1,0:T(8,128)(2,1)S(1)}, u32[]{:S(2)}, u32[]{:S(2)}) %collective-permute-start.18) | collective-permute-done | bytes 98336 | tf_op jit(solution)/shard_map/ppermute | solution.py:422
  102.0 8.3 %collective-permute-start.22 = (bf16[64,512]{1,0:T(8,128)(2,1)S(1)}, bf16[64,512]{1,0:T(8,128)(2,1)S(1)}, u32[]{:S(2)}, u32[]{:S(2)}) collective-permute-start(bf16[64,512]{1,0:T(8,128)(2,1)S(1)} %get-tuple-element.122), channel_id=1, source_target_pairs={{0,1},{1,0},{2,3},{3,2},{4,5},{5,4},{6,7},{7,6},{8,9},{9,8},{10,11... | collective-permute-start | bytes 196616 | tf_op jit(solution)/shard_map/ppermute | solution.py:408
  111.3 2.2 %collective-permute-start.23 = (bf16[64,512]{1,0:T(8,128)(2,1)S(1)}, bf16[64,512]{1,0:T(8,128)(2,1)S(1)}, u32[]{:S(2)}, u32[]{:S(2)}) collective-permute-start(bf16[64,512]{1,0:T(8,128)(2,1)S(1)} %add_convert_fusion.2), channel_id=1, source_target_pairs={{0,2},{2,0},{1,3},{3,1},{4,6},{6,4},{5,7},{7,5},{8,10},{10,8},{9,1... | collective-permute-start | bytes 196616 | tf_op jit(solution)/shard_map/ppermute | solution.py:408
  114.8 1.6 %shard_map.138 = (bf16[128,2048]{1,0:T(8,128)(2,1)}, bf16[128,2048]{1,0:T(8,128)(2,1)}) custom-call(s32[5]{0:T(128)S(1)} %stack.33.info, bf16[128,1024]{1,0:T(8,128)(2,1)S(1)} %get-tuple-element.125.od0, bf16[128,1024]{1,0:T(8,128)(2,1)S(1)} %collective-permute-done.19.od1, bf16[128,1024]{1,0:T(8,128)(2,1)S(1)} %collective-permute-done.20.od2, ...), custom_call_target="tpu_custom_call" | custom-call | bytes 1000000 | tf_op jit(solution)/shard_map/pallas_call | solution.py:392
  116.4 2.8 %collective-permute-start.26 = (bf16[64,512]{1,0:T(8,128)(2,1)S(1)}, bf16[64,512]{1,0:T(8,128)(2,1)S(1)}, u32[]{:S(2)}, u32[]{:S(2)}) collective-permute-start(bf16[64,512]{1,0:T(8,128)(2,1)S(1)} %add_convert_fusion.1), channel_id=1, source_target_pairs={{0,12},{4,0},{8,4},{12,8},{1,13},{5,1},{9,5},{13,9},{2,14},{6,2},{... | collective-permute-start | bytes 196616 | tf_op jit(solution)/shard_map/ppermute | solution.py:413
  119.2 1.6 %collective-permute-start.24 = (bf16[64,512]{1,0:T(8,128)(2,1)S(1)}, bf16[64,512]{1,0:T(8,128)(2,1)S(1)}, u32[]{:S(2)}, u32[]{:S(2)}) collective-permute-start(bf16[64,512]{1,0:T(8,128)(2,1)S(1)} %add_convert_fusion.1), channel_id=1, source_target_pairs={{0,8},{4,12},{8,0},{12,4},{1,9},{5,13},{9,1},{13,5},{2,10},{6,14},... | collective-permute-start | bytes 196616 | tf_op jit(solution)/shard_map/ppermute | solution.py:413
  120.9 3.1 %collective-permute-done.25 = bf16[64,512]{1,0:T(8,128)(2,1)S(1)} collective-permute-done((bf16[64,512]{1,0:T(8,128)(2,1)S(1)}, bf16[64,512]{1,0:T(8,128)(2,1)S(1)}, u32[]{:S(2)}, u32[]{:S(2)}) %collective-permute-start.25) | collective-permute-done | bytes 65568 | tf_op jit(solution)/shard_map/ppermute | solution.py:413
  124.5 2.0 %collective-permute-start.27 = (bf16[64,512]{1,0:T(8,128)(2,1)S(1)}, bf16[64,512]{1,0:T(8,128)(2,1)S(1)}, u32[]{:S(2)}, u32[]{:S(2)}) collective-permute-start(bf16[64,512]{1,0:T(8,128)(2,1)S(1)} %add_convert_fusion), channel_id=1, source_target_pairs={{0,1},{1,0},{2,3},{3,2},{4,5},{5,4},{6,7},{7,6},{8,9},{9,8},{10,11... | collective-permute-start | bytes 196616 | tf_op jit(solution)/shard_map/ppermute | solution.py:408
  (45 shorter events, 8.7 us)
Async XLA Ops:
  2.5 16.9 %collective-permute-start.2 = (bf16[192,256]{1,0:T(8,128)(2,1)}, bf16[192,256]{1,0:T(8,128)(2,1)S(1)}, u32[]{:S(2)}, u32[]{:S(2)}) collective-permute-start(bf16[192,256]{1,0:T(8,128)(2,1)} %get-tuple-element.75), channel_id=1, source_target_pairs={{0,16},{1,113},{16,0},{17,33},{32,48},{33,17},{48,32},{49,65},{64,... | collective-permute-start | bytes 294920 | tf_op jit(solution)/shard_map/ppermute | solution.py:422
  9.0 11.4 %collective-permute-start.3 = (bf16[192,256]{1,0:T(8,128)(2,1)}, bf16[192,256]{1,0:T(8,128)(2,1)S(1)}, u32[]{:S(2)}, u32[]{:S(2)}) collective-permute-start(bf16[192,256]{1,0:T(8,128)(2,1)} %get-tuple-element.76), channel_id=1, source_target_pairs={{0,128},{1,129},{16,144},{17,145},{32,160},{33,161},{48,176},{49,1... | collective-permute-start | bytes 294920 | tf_op jit(solution)/shard_map/ppermute | solution.py:422
  11.7 8.6 %collective-permute-start.4 = (bf16[192,256]{1,0:T(8,128)(2,1)}, bf16[192,256]{1,0:T(8,128)(2,1)S(1)}, u32[]{:S(2)}, u32[]{:S(2)}) collective-permute-start(bf16[192,256]{1,0:T(8,128)(2,1)} %get-tuple-element.77), channel_id=1, source_target_pairs={{0,144},{1,241},{16,128},{17,161},{32,176},{33,145},{48,160},{49,1... | collective-permute-start | bytes 294920 | tf_op jit(solution)/shard_map/ppermute | solution.py:422
  14.0 10.1 %collective-permute-start = (bf16[128,1024]{1,0:T(8,128)(2,1)}, bf16[128,1024]{1,0:T(8,128)(2,1)S(1)}, u32[]{:S(2)}, u32[]{:S(2)}) collective-permute-start(bf16[128,1024]{1,0:T(8,128)(2,1)} %get-tuple-element.72), channel_id=1, source_target_pairs={{0,16},{1,113},{16,0},{17,33},{32,48},{33,17},{48,32},{49,65},{64,... | collective-permute-start | bytes 786440 | tf_op jit(solution)/shard_map/ppermute | solution.py:422
  16.7 11.2 %collective-permute-start.1 = (bf16[128,1024]{1,0:T(8,128)(2,1)}, bf16[128,1024]{1,0:T(8,128)(2,1)S(1)}, u32[]{:S(2)}, u32[]{:S(2)}) collective-permute-start(bf16[128,1024]{1,0:T(8,128)(2,1)} %get-tuple-element.73), channel_id=1, source_target_pairs={{0,128},{1,129},{16,144},{17,145},{32,160},{33,161},{48,176},{49,1... | collective-permute-start | bytes 786440 | tf_op jit(solution)/shard_map/ppermute | solution.py:422
  20.4 18.5 %collective-permute-start.5 = (bf16[128,1024]{1,0:T(8,128)(2,1)}, bf16[128,1024]{1,0:T(8,128)(2,1)S(1)}, u32[]{:S(2)}, u32[]{:S(2)}) collective-permute-start(bf16[128,1024]{1,0:T(8,128)(2,1)} %get-tuple-element.79), channel_id=1, source_target_pairs={{0,144},{1,241},{16,128},{17,161},{32,176},{33,145},{48,160},{49,1... | collective-permute-start | bytes 786440 | tf_op jit(solution)/shard_map/ppermute | solution.py:422
  20.5 14.8 %collective-permute-start.6 = (bf16[2,192,256]{2,1,0:T(8,128)(2,1)S(1)}, bf16[2,192,256]{2,1,0:T(8,128)(2,1)S(1)}, u32[]{:S(2)}, u32[]{:S(2)}) collective-permute-start(bf16[2,192,256]{2,1,0:T(8,128)(2,1)S(1)} %pad_maximum_fusion.own_a), channel_id=1, source_target_pairs={{0,32},{1,33},{16,48},{17,49},{32,64},{33,65},{48,80},{49,81},{64,... | collective-permute-start | bytes 589832 | tf_op jit(solution)/shard_map/ppermute | solution.py:422
  20.6 14.8 %collective-permute-start.8 = (bf16[2,192,256]{2,1,0:T(8,128)(2,1)S(1)}, bf16[2,192,256]{2,1,0:T(8,128)(2,1)S(1)}, u32[]{:S(2)}, u32[]{:S(2)}) collective-permute-start(bf16[2,192,256]{2,1,0:T(8,128)(2,1)S(1)} %pad_maximum_fusion.1.own_b), channel_id=1, source_target_pairs={{0,96},{1,97},{16,112},{17,113},{32,0},{33,1},{48,16},{49,17},{64,... | collective-permute-start | bytes 589832 | tf_op jit(solution)/shard_map/ppermute | solution.py:422
  24.1 19.1 %collective-permute-start.11 = (bf16[2,192,256]{2,1,0:T(8,128)(2,1)S(1)}, bf16[2,192,256]{2,1,0:T(8,128)(2,1)S(1)}, u32[]{:S(2)}, u32[]{:S(2)}) collective-permute-start(bf16[2,192,256]{2,1,0:T(8,128)(2,1)S(1)} %pad_maximum_fusion.own_a), channel_id=1, source_target_pairs={{0,96},{1,97},{16,112},{17,113},{32,0},{33,1},{48,16},{49,17},{64,... | collective-permute-start | bytes 589832 | tf_op jit(solution)/shard_map/ppermute | solution.py:422
  27.9 18.6 %collective-permute-start.10 = (bf16[2,192,256]{2,1,0:T(8,128)(2,1)S(1)}, bf16[2,192,256]{2,1,0:T(8,128)(2,1)S(1)}, u32[]{:S(2)}, u32[]{:S(2)}) collective-permute-start(bf16[2,192,256]{2,1,0:T(8,128)(2,1)S(1)} %pad_maximum_fusion.1.own_b), channel_id=1, source_target_pairs={{0,32},{1,33},{16,48},{17,49},{32,64},{33,65},{48,80},{49,81},{64,... | collective-permute-start | bytes 589832 | tf_op jit(solution)/shard_map/ppermute | solution.py:422
  35.3 16.8 %collective-permute-start.7 = (bf16[2,192,256]{2,1,0:T(8,128)(2,1)S(1)}, bf16[2,192,256]{2,1,0:T(8,128)(2,1)S(1)}, u32[]{:S(2)}, u32[]{:S(2)}) collective-permute-start(bf16[2,192,256]{2,1,0:T(8,128)(2,1)S(1)} %collective-permute-done.6.left_a), channel_id=1, source_target_pairs={{0,32},{1,33},{16,48},{17,49},{32,64},{33,65},{48,80},{49,81},{64,... | collective-permute-start | bytes 589832 | tf_op jit(solution)/shard_map/ppermute | solution.py:422
  35.3 16.8 %collective-permute-start.9 = (bf16[2,192,256]{2,1,0:T(8,128)(2,1)S(1)}, bf16[2,192,256]{2,1,0:T(8,128)(2,1)S(1)}, u32[]{:S(2)}, u32[]{:S(2)}) collective-permute-start(bf16[2,192,256]{2,1,0:T(8,128)(2,1)S(1)} %collective-permute-done.8.right_b), channel_id=1, source_target_pairs={{0,96},{1,97},{16,112},{17,113},{32,0},{33,1},{48,16},{49,17},{64,... | collective-permute-start | bytes 589832 | tf_op jit(solution)/shard_map/ppermute | solution.py:422
  38.9 1.0 copy-start
  57.9 10.1 %collective-permute-start.12 = (bf16[2,192,256]{2,1,0:T(8,128)(2,1)S(1)}, bf16[2,192,256]{2,1,0:T(8,128)(2,1)S(1)}, u32[]{:S(2)}, u32[]{:S(2)}) collective-permute-start(bf16[2,192,256]{2,1,0:T(8,128)(2,1)S(1)} %get-tuple-element.103), channel_id=1, source_target_pairs={{0,32},{1,33},{16,48},{17,49},{32,64},{33,65},{48,80},{49,81},{64,... | collective-permute-start | bytes 589832 | tf_op jit(solution)/shard_map/ppermute | solution.py:422
  58.0 10.0 %collective-permute-start.13 = (bf16[2,192,256]{2,1,0:T(8,128)(2,1)S(1)}, bf16[2,192,256]{2,1,0:T(8,128)(2,1)S(1)}, u32[]{:S(2)}, u32[]{:S(2)}) collective-permute-start(bf16[2,192,256]{2,1,0:T(8,128)(2,1)S(1)} %get-tuple-element.104), channel_id=1, source_target_pairs={{0,96},{1,97},{16,112},{17,113},{32,0},{33,1},{48,16},{49,17},{64,... | collective-permute-start | bytes 589832 | tf_op jit(solution)/shard_map/ppermute | solution.py:422
  68.1 13.0 %collective-permute-start.14 = (bf16[4,192,256]{2,1,0:T(8,128)(2,1)S(1)}, bf16[4,192,256]{2,1,0:T(8,128)(2,1)S(1)}, u32[]{:S(2)}, u32[]{:S(2)}) collective-permute-start(bf16[4,192,256]{2,1,0:T(8,128)(2,1)S(1)} %get-tuple-element.105), channel_id=1, source_target_pairs={{0,96},{1,97},{16,112},{17,113},{32,0},{33,1},{48,16},{49,17},{64,... | collective-permute-start | bytes 1179656 | tf_op jit(solution)/shard_map/ppermute | solution.py:422
  68.5 16.4 %collective-permute-start.15 = (bf16[4,192,256]{2,1,0:T(8,128)(2,1)S(1)}, bf16[4,192,256]{2,1,0:T(8,128)(2,1)S(1)}, u32[]{:S(2)}, u32[]{:S(2)}) collective-permute-start(bf16[4,192,256]{2,1,0:T(8,128)(2,1)S(1)} %get-tuple-element.106), channel_id=1, source_target_pairs={{0,32},{1,33},{16,48},{17,49},{32,64},{33,65},{48,80},{49,81},{64,... | collective-permute-start | bytes 1179656 | tf_op jit(solution)/shard_map/ppermute | solution.py:422
  75.0 16.1 %collective-permute-start.20 = (bf16[128,1024]{1,0:T(8,128)(2,1)S(1)}, bf16[128,1024]{1,0:T(8,128)(2,1)S(1)}, u32[]{:S(2)}, u32[]{:S(2)}) collective-permute-start(bf16[128,1024]{1,0:T(8,128)(2,1)S(1)} %get-tuple-element.115), channel_id=1, source_target_pairs={{0,128},{1,129},{16,144},{17,145},{32,160},{33,161},{48,176},{49,1... | collective-permute-start | bytes 786440 | tf_op jit(solution)/shard_map/ppermute | solution.py:422
  77.8 13.6 %collective-permute-start.21 = (bf16[128,1024]{1,0:T(8,128)(2,1)S(1)}, bf16[128,1024]{1,0:T(8,128)(2,1)S(1)}, u32[]{:S(2)}, u32[]{:S(2)}) collective-permute-start(bf16[128,1024]{1,0:T(8,128)(2,1)S(1)} %get-tuple-element.116), channel_id=1, source_target_pairs={{0,144},{1,241},{16,128},{17,161},{32,176},{33,145},{48,160},{49,1... | collective-permute-start | bytes 786440 | tf_op jit(solution)/shard_map/ppermute | solution.py:422
  84.9 16.5 %collective-permute-start.19 = (bf16[128,1024]{1,0:T(8,128)(2,1)S(1)}, bf16[128,1024]{1,0:T(8,128)(2,1)S(1)}, u32[]{:S(2)}, u32[]{:S(2)}) collective-permute-start(bf16[128,1024]{1,0:T(8,128)(2,1)S(1)} %get-tuple-element.114), channel_id=1, source_target_pairs={{0,16},{1,113},{16,0},{17,33},{32,48},{33,17},{48,32},{49,65},{64,... | collective-permute-start | bytes 786440 | tf_op jit(solution)/shard_map/ppermute | solution.py:422
  85.1 12.3 %collective-permute-start.16 = (bf16[192,256]{1,0:T(8,128)(2,1)S(1)}, bf16[192,256]{1,0:T(8,128)(2,1)S(1)}, u32[]{:S(2)}, u32[]{:S(2)}) collective-permute-start(bf16[192,256]{1,0:T(8,128)(2,1)S(1)} %get-tuple-element.111), channel_id=1, source_target_pairs={{0,16},{1,113},{16,0},{17,33},{32,48},{33,17},{48,32},{49,65},{64,... | collective-permute-start | bytes 294920 | tf_op jit(solution)/shard_map/ppermute | solution.py:422
  87.8 9.6 %collective-permute-start.17 = (bf16[192,256]{1,0:T(8,128)(2,1)S(1)}, bf16[192,256]{1,0:T(8,128)(2,1)S(1)}, u32[]{:S(2)}, u32[]{:S(2)}) collective-permute-start(bf16[192,256]{1,0:T(8,128)(2,1)S(1)} %get-tuple-element.112), channel_id=1, source_target_pairs={{0,128},{1,129},{16,144},{17,145},{32,160},{33,161},{48,176},{49,1... | collective-permute-start | bytes 294920 | tf_op jit(solution)/shard_map/ppermute | solution.py:422
  91.1 10.3 %collective-permute-start.18 = (bf16[192,256]{1,0:T(8,128)(2,1)S(1)}, bf16[192,256]{1,0:T(8,128)(2,1)S(1)}, u32[]{:S(2)}, u32[]{:S(2)}) collective-permute-start(bf16[192,256]{1,0:T(8,128)(2,1)S(1)} %get-tuple-element.113), channel_id=1, source_target_pairs={{0,144},{1,241},{16,128},{17,161},{32,176},{33,145},{48,160},{49,1... | collective-permute-start | bytes 294920 | tf_op jit(solution)/shard_map/ppermute | solution.py:422
  102.0 9.2 %collective-permute-start.22 = (bf16[64,512]{1,0:T(8,128)(2,1)S(1)}, bf16[64,512]{1,0:T(8,128)(2,1)S(1)}, u32[]{:S(2)}, u32[]{:S(2)}) collective-permute-start(bf16[64,512]{1,0:T(8,128)(2,1)S(1)} %get-tuple-element.122), channel_id=1, source_target_pairs={{0,1},{1,0},{2,3},{3,2},{4,5},{5,4},{6,7},{7,6},{8,9},{9,8},{10,11... | collective-permute-start | bytes 196616 | tf_op jit(solution)/shard_map/ppermute | solution.py:408
  111.3 5.1 %collective-permute-start.23 = (bf16[64,512]{1,0:T(8,128)(2,1)S(1)}, bf16[64,512]{1,0:T(8,128)(2,1)S(1)}, u32[]{:S(2)}, u32[]{:S(2)}) collective-permute-start(bf16[64,512]{1,0:T(8,128)(2,1)S(1)} %add_convert_fusion.2), channel_id=1, source_target_pairs={{0,2},{2,0},{1,3},{3,1},{4,6},{6,4},{5,7},{7,5},{8,10},{10,8},{9,1... | collective-permute-start | bytes 196616 | tf_op jit(solution)/shard_map/ppermute | solution.py:408
  116.4 4.5 %collective-permute-start.26 = (bf16[64,512]{1,0:T(8,128)(2,1)S(1)}, bf16[64,512]{1,0:T(8,128)(2,1)S(1)}, u32[]{:S(2)}, u32[]{:S(2)}) collective-permute-start(bf16[64,512]{1,0:T(8,128)(2,1)S(1)} %add_convert_fusion.1), channel_id=1, source_target_pairs={{0,12},{4,0},{8,4},{12,8},{1,13},{5,1},{9,5},{13,9},{2,14},{6,2},{... | collective-permute-start | bytes 196616 | tf_op jit(solution)/shard_map/ppermute | solution.py:413
  119.2 4.8 %collective-permute-start.25 = (bf16[64,512]{1,0:T(8,128)(2,1)S(1)}, bf16[64,512]{1,0:T(8,128)(2,1)S(1)}, u32[]{:S(2)}, u32[]{:S(2)}) collective-permute-start(bf16[64,512]{1,0:T(8,128)(2,1)S(1)} %add_convert_fusion.1), channel_id=1, source_target_pairs={{0,4},{4,8},{8,12},{12,0},{1,5},{5,9},{9,13},{13,1},{2,6},{6,10},{... | collective-permute-start | bytes 196616 | tf_op jit(solution)/shard_map/ppermute | solution.py:413
  119.2 5.3 %collective-permute-start.24 = (bf16[64,512]{1,0:T(8,128)(2,1)S(1)}, bf16[64,512]{1,0:T(8,128)(2,1)S(1)}, u32[]{:S(2)}, u32[]{:S(2)}) collective-permute-start(bf16[64,512]{1,0:T(8,128)(2,1)S(1)} %add_convert_fusion.1), channel_id=1, source_target_pairs={{0,8},{4,12},{8,0},{12,4},{1,9},{5,13},{9,1},{13,5},{2,10},{6,14},... | collective-permute-start | bytes 196616 | tf_op jit(solution)/shard_map/ppermute | solution.py:413
  124.5 3.0 %collective-permute-start.27 = (bf16[64,512]{1,0:T(8,128)(2,1)S(1)}, bf16[64,512]{1,0:T(8,128)(2,1)S(1)}, u32[]{:S(2)}, u32[]{:S(2)}) collective-permute-start(bf16[64,512]{1,0:T(8,128)(2,1)S(1)} %add_convert_fusion), channel_id=1, source_target_pairs={{0,1},{1,0},{2,3},{3,2},{4,5},{5,4},{6,7},{7,6},{8,9},{9,8},{10,11... | collective-permute-start | bytes 196616 | tf_op jit(solution)/shard_map/ppermute | solution.py:408

commit v9 on v5

--- a/solution.py
+++ b/solution.py
@@ -532,10 +532,10 @@
     left_g, right_g, od[1] = lax.optimization_barrier((left_g, right_g, od[1]))
     od[1] = partner(od[1], 1)
     grads = list(call(sum_kernel, (bf16(BOTH, WIDE),) * 4, (), (), own_g, left_g, right_g))
-    for d in (1, 2, 3):
+    for d in (3, 2, 1):
         grads[d] = partner(grads[d], d)
-    tied = lax.optimization_barrier((*grads, *od[1:]))
-    grads, od[1:] = tied[:4], tied[4:]
+    tied = lax.optimization_barrier((*grads[::-1], *od[:0:-1]))
+    grads, od[1:] = tied[3::-1], tied[:3:-1]
     rows = bf16(ROWS, HEADS * HEAD_DIM)
     keep, send = call(share_kernel, (bf16(PROWS, width),) * 2, (), (info,), *grads)
     share = rounded(keep.astype(F32) + swap(send, "core").astype(F32))

time: 123 us -> 123 us (level)
    ppermute x3, starting transfers between devices: 4.62 us -> 2.6 us  [turn(): return lax.ppermute(x, axis, [(i, (i + step) % size) for i in range(size)])]
    ppermute x3, starting transfers between devices: 5.93 us -> 7.93 us  [swap(): return lax.ppermute(x, axis, [(0, 1), (1, 0)])]
  transfers between devices with their start and end apart: 28 -> 28, of which waited for: 13 -> 17; matrix products, arithmetic and copies ran while one was open for 1% -> 1% of each run, Pallas kernels for 21% -> 21%
where the time goes in v9:
time: 123 us
  starting transfers between devices  49.6 us (40%)
  waiting for transfers between devices  34.8 us (28%)
  Pallas kernels  33.4 us (27%)
  between operations  2.16 us (2%)
  other arithmetic  1.67 us (1%)
    ppermute x22, starting transfers between devices, local_permute(): return lax.ppermute(x, LOCAL, pairs)  39 us
    pallas_call x12, Pallas kernels, call(): pl.pallas_call(kernel, out_shape=tuple(outs), in_specs=[SMEM] * len(scala...  33.4 us
    ppermute x22, waiting for transfers between devices, local_permute(): return lax.ppermute(x, LOCAL, pairs)  28.9 us
    ppermute x3, starting transfers between devices, swap(): return lax.ppermute(x, axis, [(0, 1), (1, 0)])  7.93 us
    ppermute x3, waiting for transfers between devices, turn(): return lax.ppermute(x, axis, [(i, (i + step) % size) for i in range(size)])  3.94 us
    ppermute x3, starting transfers between devices, turn(): return lax.ppermute(x, axis, [(i, (i + step) % size) for i in range(size)])  2.6 us
  transfers between devices with their start and end apart: 28, of which 17 were waited for; matrix products, arithmetic and copies ran while one was open for 1% of the time, Pallas kernels for 21%

profile of v9, /device:TPU:1, one launch (start us, length us, event | category | flops | bytes accessed | tf_op | source)
XLA Modules:
  0.0 122.7 jit_solution(18327059190171254167)
XLA Ops:
  0.6 1.8 %shard_map.128 = (bf16[192,256]{1,0:T(8,128)(2,1)}, bf16[192,256]{1,0:T(8,128)(2,1)}, bf16[192,256]{1,0:T(8,128)(2,1)}, bf16[192,256]{1,0:T(8,128)(2,1)}) custom-call(s32[1]{0:T(128)} %bitcast.info, bf16[128,512]{1,0:T(8,128)(2,1)} %bitcast.17, bf16[128,512]{1,0:T(8,128)(2,1)} %bitcast.18, bf16[64,512]{1,0:T(8,128)(2,1)} %kp.1, bf16[64,512]{1,0:T(8,128)(2,1)} %vp.1), custom_call_target="tpu_custom_call" | custom-call | bytes 1000000 | tf_op jit(solution)/shard_map/pallas_call | solution.py:392
  2.5 3.7 %collective-permute-start.4 = (bf16[192,256]{1,0:T(8,128)(2,1)}, bf16[192,256]{1,0:T(8,128)(2,1)S(1)}, u32[]{:S(2)}, u32[]{:S(2)}) collective-permute-start(bf16[192,256]{1,0:T(8,128)(2,1)} %get-tuple-element.74), channel_id=1, source_target_pairs={{0,128},{1,129},{16,144},{17,145},{32,160},{33,161},{48,176},{49,1... | collective-permute-start | bytes 294920 | tf_op jit(solution)/shard_map/ppermute | solution.py:422
  6.1 5.5 %collective-permute-start.5 = (bf16[192,256]{1,0:T(8,128)(2,1)}, bf16[192,256]{1,0:T(8,128)(2,1)S(1)}, u32[]{:S(2)}, u32[]{:S(2)}) collective-permute-start(bf16[192,256]{1,0:T(8,128)(2,1)} %get-tuple-element.75), channel_id=1, source_target_pairs={{0,144},{1,241},{16,128},{17,161},{32,176},{33,145},{48,160},{49,1... | collective-permute-start | bytes 294920 | tf_op jit(solution)/shard_map/ppermute | solution.py:422
  11.7 2.2 %shard_map.127 = (bf16[128,1024]{1,0:T(8,128)(2,1)}, bf16[128,1024]{1,0:T(8,128)(2,1)}, bf16[128,1024]{1,0:T(8,128)(2,1)}, bf16[128,1024]{1,0:T(8,128)(2,1)}) custom-call(s32[1]{0:T(128)} %bitcast.info, bf16[128,2048]{1,0:T(8,128)(2,1)} %bitcast.15, bf16[128,2048]{1,0:T(8,128)(2,1)} %bitcast.16), custom_call_target="tpu_custom_call" | custom-call | bytes 1000000 | tf_op jit(solution)/shard_map/pallas_call | solution.py:392
  14.1 2.8 %collective-permute-start.1 = (bf16[128,1024]{1,0:T(8,128)(2,1)}, bf16[128,1024]{1,0:T(8,128)(2,1)S(1)}, u32[]{:S(2)}, u32[]{:S(2)}) collective-permute-start(bf16[128,1024]{1,0:T(8,128)(2,1)} %get-tuple-element.70), channel_id=1, source_target_pairs={{0,128},{1,129},{16,144},{17,145},{32,160},{33,161},{48,176},{49,1... | collective-permute-start | bytes 786440 | tf_op jit(solution)/shard_map/ppermute | solution.py:422
  16.8 2.6 %collective-permute-start.3 = (bf16[192,256]{1,0:T(8,128)(2,1)}, bf16[192,256]{1,0:T(8,128)(2,1)S(1)}, u32[]{:S(2)}, u32[]{:S(2)}) collective-permute-start(bf16[192,256]{1,0:T(8,128)(2,1)} %get-tuple-element.73), channel_id=1, source_target_pairs={{0,16},{1,113},{16,0},{17,33},{32,48},{33,17},{48,32},{49,65},{64,... | collective-permute-start | bytes 294920 | tf_op jit(solution)/shard_map/ppermute | solution.py:422
  20.2 1.9 %collective-permute-done.3 = bf16[192,256]{1,0:T(8,128)(2,1)S(1)} collective-permute-done((bf16[192,256]{1,0:T(8,128)(2,1)}, bf16[192,256]{1,0:T(8,128)(2,1)S(1)}, u32[]{:S(2)}, u32[]{:S(2)}) %collective-permute-start.3) | collective-permute-done | bytes 98336 | tf_op jit(solution)/shard_map/ppermute | solution.py:422
  23.0 4.2 %collective-permute-start.10 = (bf16[2,192,256]{2,1,0:T(8,128)(2,1)S(1)}, bf16[2,192,256]{2,1,0:T(8,128)(2,1)S(1)}, u32[]{:S(2)}, u32[]{:S(2)}) collective-permute-start(bf16[2,192,256]{2,1,0:T(8,128)(2,1)S(1)} %pad_maximum_fusion.1.own_b), channel_id=1, source_target_pairs={{0,32},{1,33},{16,48},{17,49},{32,64},{33,65},{48,80},{49,81},{64,... | collective-permute-start | bytes 589832 | tf_op jit(solution)/shard_map/ppermute | solution.py:422
  27.2 1.7 %collective-permute-done.1.qd2 = bf16[128,1024]{1,0:T(8,128)(2,1)S(1)} collective-permute-done((bf16[128,1024]{1,0:T(8,128)(2,1)}, bf16[128,1024]{1,0:T(8,128)(2,1)S(1)}, u32[]{:S(2)}, u32[]{:S(2)}) %collective-permute-start.1) | collective-permute-done | bytes 262176 | tf_op jit(solution)/shard_map/ppermute | solution.py:422
  31.4 3.4 %shard_map.129 = (bf16[2,128,1024]{2,1,0:T(8,128)(2,1)S(1)}, bf16[2,1024,128]{2,1,0:T(8,128)(2,1)S(1)}, bf16[2,128,1024]{2,1,0:T(8,128)(2,1)S(1)}, bf16[1,1280,1...) custom-call(s32[5]{0:T(128)S(1)} %stack.33.info, ...), custom_call_target="tpu_custom_call" | custom-call | flops 1342177280 | bytes 1000000 | tf_op jit(solution)/shard_map/pallas_call | solution.py:392
  34.8 3.5 %collective-permute-start.9 = (bf16[2,192,256]{2,1,0:T(8,128)(2,1)S(1)}, bf16[2,192,256]{2,1,0:T(8,128)(2,1)S(1)}, u32[]{:S(2)}, u32[]{:S(2)}) collective-permute-start(bf16[2,192,256]{2,1,0:T(8,128)(2,1)S(1)} %collective-permute-done.8.right_b), channel_id=1, source_target_pairs={{0,96},{1,97},{16,112},{17,113},{32,0},{33,1},{48,16},{49,17},{64,... | collective-permute-start | bytes 589832 | tf_op jit(solution)/shard_map/ppermute | solution.py:422
  38.2 7.9 %collective-permute-done.10.left_b = bf16[2,192,256]{2,1,0:T(8,128)(2,1)S(1)} collective-permute-done((bf16[2,192,256]{2,1,0:T(8,128)(2,1)S(1)}, bf16[2,192,256]{2,1,0:T(8,128)(2,1)S(1)}, u32[]{:S(2)}, u32[]{:S(2)}) %collective-permute-start.10) | collective-permute-done | bytes 196640 | tf_op jit(solution)/shard_map/ppermute | solution.py:422
  46.1 5.7 %shard_map.130 = (bf16[2,1280,1024]{2,1,0:T(8,128)(2,1)S(1)}, f32[2,1,1024]{2,1,0:T(1,128)S(1)}, f32[2,1,1024]{2,1,0:T(1,128)S(1)}, f32[2,128,1024]{2,1,0:T(8,128)S(1)}) custom-call(s32[5]{0:T(128)S(1)} %stack.33.info, bf16[2,128,1024]{2,1,0:T(8,128)(2,1)S(1)} %get-tuple-element.77.qt, bf16[2,192,256]{2,1,0:T(8,128)(2,1)S(1)} %collective-permute-done.6.left_a, ...), custom_call_target="tpu_custom_call" | custom-call | flops 2684354560 | bytes 1000000 | tf_op jit(solution)/shard_map/pallas_call | solution.py:392
  51.9 5.8 %shard_map.131 = (f32[2,1,1024]{2,1,0:T(1,128)S(1)}, bf16[2,128,1024]{2,1,0:T(8,128)(2,1)S(1)}, bf16[2,1024,128]{2,1,0:T(8,128)(2,1)S(1)}, f32[2,1,1024]{2,1,0:T...) custom-call(s32[5]{0:T(128)S(1)} %stack.33.info, ...), custom_call_target="tpu_custom_call" | custom-call | flops 4026531840 | bytes 1000000 | tf_op jit(solution)/shard_map/pallas_call | solution.py:392
  58.1 3.2 %collective-permute-start.13 = (bf16[2,192,256]{2,1,0:T(8,128)(2,1)S(1)}, bf16[2,192,256]{2,1,0:T(8,128)(2,1)S(1)}, u32[]{:S(2)}, u32[]{:S(2)}) collective-permute-start(bf16[2,192,256]{2,1,0:T(8,128)(2,1)S(1)} %get-tuple-element.98), channel_id=1, source_target_pairs={{0,96},{1,97},{16,112},{17,113},{32,0},{33,1},{48,16},{49,17},{64,... | collective-permute-start | bytes 589832 | tf_op jit(solution)/shard_map/ppermute | solution.py:422
  61.3 6.4 %shard_map.132 = (f32[2,128,1024]{2,1,0:T(8,128)S(1)}, bf16[4,192,256]{2,1,0:T(8,128)(2,1)S(1)}, bf16[4,192,256]{2,1,0:T(8,128)(2,1)S(1)}) custom-call(s32[5]{0:T(128)S(1)} %stack.33.info, bf16[2,1024,128]{2,1,0:T(8,128)(2,1)S(1)} %get-tuple-element.76.q, bf16[2,128,1024]{2,1,0:T(8,128)(2,1)S(1)} %get-tuple-element.85.uplt, ...), custom_call_target="tpu_custom_call" | custom-call | flops 5368709120 | bytes 1000000 | tf_op jit(solution)/shard_map/pallas_call | solution.py:392
  67.7 2.8 %collective-permute-done.12.far_a = bf16[2,192,256]{2,1,0:T(8,128)(2,1)S(1)} collective-permute-done((bf16[2,192,256]{2,1,0:T(8,128)(2,1)S(1)}, bf16[2,192,256]{2,1,0:T(8,128)(2,1)S(1)}, u32[]{:S(2)}, u32[]{:S(2)}) %collective-permute-start.12) | collective-permute-done | bytes 196640 | tf_op jit(solution)/shard_map/ppermute | solution.py:422
  70.5 1.5 %collective-permute-done.13.far_b = bf16[2,192,256]{2,1,0:T(8,128)(2,1)S(1)} collective-permute-done((bf16[2,192,256]{2,1,0:T(8,128)(2,1)S(1)}, bf16[2,192,256]{2,1,0:T(8,128)(2,1)S(1)}, u32[]{:S(2)}, u32[]{:S(2)}) %collective-permute-start.13) | collective-permute-done | bytes 196640 | tf_op jit(solution)/shard_map/ppermute | solution.py:422
  72.4 2.4 %collective-permute-start.15 = (bf16[4,192,256]{2,1,0:T(8,128)(2,1)S(1)}, bf16[4,192,256]{2,1,0:T(8,128)(2,1)S(1)}, u32[]{:S(2)}, u32[]{:S(2)}) collective-permute-start(bf16[4,192,256]{2,1,0:T(8,128)(2,1)S(1)} %get-tuple-element.100), channel_id=1, source_target_pairs={{0,32},{1,33},{16,48},{17,49},{32,64},{33,65},{48,80},{49,81},{64,... | collective-permute-start | bytes 1179656 | tf_op jit(solution)/shard_map/ppermute | solution.py:422
  74.7 4.4 %shard_map.133 = (bf16[4,192,256]{2,1,0:T(8,128)(2,1)S(1)}, bf16[128,1024]{1,0:T(8,128)(2,1)S(1)}, bf16[128,1024]{1,0:T(8,128)(2,1)S(1)}, bf16[128,1024]{1,0:T(8,128)(2,1)S(1)}, bf16[128,1024]{1,0:T(8,128)(2,1)S(1)}) custom-call(s32[5]{0:T(128)S(1)} %stack.33.info, bf16[2,1024,128]{2,1,0:T(8,128)(2,1)S(1)} %get-tuple-element.76.q, ...), custom_call_target="tpu_custom_call" | custom-call | flops 2684354560 | bytes 1000000 | tf_op jit(solution)/shard_map/pallas_call | solution.py:392
  79.1 4.1 %collective-permute-start.19 = (bf16[128,1024]{1,0:T(8,128)(2,1)S(1)}, bf16[128,1024]{1,0:T(8,128)(2,1)S(1)}, u32[]{:S(2)}, u32[]{:S(2)}) collective-permute-start(bf16[128,1024]{1,0:T(8,128)(2,1)S(1)} %get-tuple-element.108), channel_id=1, source_target_pairs={{0,144},{1,241},{16,128},{17,161},{32,176},{33,145},{48,160},{49,1... | collective-permute-start | bytes 786440 | tf_op jit(solution)/shard_map/ppermute | solution.py:422
  83.3 7.7 %collective-permute-done.14.left = bf16[4,192,256]{2,1,0:T(8,128)(2,1)S(1)} collective-permute-done((bf16[4,192,256]{2,1,0:T(8,128)(2,1)S(1)}, bf16[4,192,256]{2,1,0:T(8,128)(2,1)S(1)}, u32[]{:S(2)}, u32[]{:S(2)}) %collective-permute-start.14) | collective-permute-done | bytes 393248 | tf_op jit(solution)/shard_map/ppermute | solution.py:422
  91.2 3.4 %collective-permute-start.16 = (bf16[192,256]{1,0:T(8,128)(2,1)S(1)}, bf16[192,256]{1,0:T(8,128)(2,1)S(1)}, u32[]{:S(2)}, u32[]{:S(2)}) collective-permute-start(bf16[192,256]{1,0:T(8,128)(2,1)S(1)} %get-tuple-element.104), channel_id=1, source_target_pairs={{0,144},{1,241},{16,128},{17,161},{32,176},{33,145},{48,160},{49,1... | collective-permute-start | bytes 294920 | tf_op jit(solution)/shard_map/ppermute | solution.py:422
  94.5 2.1 %collective-permute-start.17 = (bf16[192,256]{1,0:T(8,128)(2,1)S(1)}, bf16[192,256]{1,0:T(8,128)(2,1)S(1)}, u32[]{:S(2)}, u32[]{:S(2)}) collective-permute-start(bf16[192,256]{1,0:T(8,128)(2,1)S(1)} %get-tuple-element.105), channel_id=1, source_target_pairs={{0,128},{1,129},{16,144},{17,145},{32,160},{33,161},{48,176},{49,1... | collective-permute-start | bytes 294920 | tf_op jit(solution)/shard_map/ppermute | solution.py:422
  98.4 1.6 %collective-permute-done.16.g3 = bf16[192,256]{1,0:T(8,128)(2,1)S(1)} collective-permute-done((bf16[192,256]{1,0:T(8,128)(2,1)S(1)}, bf16[192,256]{1,0:T(8,128)(2,1)S(1)}, u32[]{:S(2)}, u32[]{:S(2)}) %collective-permute-start.16) | collective-permute-done | bytes 98336 | tf_op jit(solution)/shard_map/ppermute | solution.py:422
  100.6 1.4 %collective-permute-done.18.g1 = bf16[192,256]{1,0:T(8,128)(2,1)S(1)} collective-permute-done((bf16[192,256]{1,0:T(8,128)(2,1)S(1)}, bf16[192,256]{1,0:T(8,128)(2,1)S(1)}, u32[]{:S(2)}, u32[]{:S(2)}) %collective-permute-start.18) | collective-permute-done | bytes 98336 | tf_op jit(solution)/shard_map/ppermute | solution.py:422
  102.6 4.9 %collective-permute-start.22 = (bf16[64,512]{1,0:T(8,128)(2,1)S(1)}, bf16[64,512]{1,0:T(8,128)(2,1)S(1)}, u32[]{:S(2)}, u32[]{:S(2)}) collective-permute-start(bf16[64,512]{1,0:T(8,128)(2,1)S(1)} %get-tuple-element.116), channel_id=1, source_target_pairs={{0,1},{1,0},{2,3},{3,2},{4,5},{5,4},{6,7},{7,6},{8,9},{9,8},{10,11... | collective-permute-start | bytes 196616 | tf_op jit(solution)/shard_map/ppermute | solution.py:408
  108.5 1.3 %shard_map.137 = (bf16[128,512]{1,0:T(8,128)(2,1)}, bf16[128,512]{1,0:T(8,128)(2,1)}) custom-call(s32[5]{0:T(128)S(1)} %stack.33.info, bf16[192,256]{1,0:T(8,128)(2,1)S(1)} %get-tuple-element.111.g0, bf16[192,256]{1,0:T(8,128)(2,1)S(1)} %collective-permute-done.18.g1, bf16[192,256]{1,0:T(8,128)(2,1)S(1)} %collective-permute-done.17.g2, ...), custom_call_target="tpu_custom_call" | custom-call | bytes 1000000 | tf_op jit(solution)/shard_map/pallas_call | solution.py:392
  109.8 1.6 %shard_map.138 = (bf16[128,2048]{1,0:T(8,128)(2,1)}, bf16[128,2048]{1,0:T(8,128)(2,1)}) custom-call(s32[5]{0:T(128)S(1)} %stack.33.info, bf16[128,1024]{1,0:T(8,128)(2,1)S(1)} %get-tuple-element.119.od0, bf16[128,1024]{1,0:T(8,128)(2,1)S(1)} %collective-permute-done.21.od1, bf16[128,1024]{1,0:T(8,128)(2,1)S(1)} %collective-permute-done.20.od2, ...), custom_call_target="tpu_custom_call" | custom-call | bytes 1000000 | tf_op jit(solution)/shard_map/pallas_call | solution.py:392
  114.8 2.1 %collective-permute-done.25 = bf16[64,512]{1,0:T(8,128)(2,1)S(1)} collective-permute-done((bf16[64,512]{1,0:T(8,128)(2,1)S(1)}, bf16[64,512]{1,0:T(8,128)(2,1)S(1)}, u32[]{:S(2)}, u32[]{:S(2)}) %collective-permute-start.25) | collective-permute-done | bytes 65568 | tf_op jit(solution)/shard_map/ppermute | solution.py:413
  116.9 1.3 %collective-permute-done.24 = bf16[64,512]{1,0:T(8,128)(2,1)S(1)} collective-permute-done((bf16[64,512]{1,0:T(8,128)(2,1)S(1)}, bf16[64,512]{1,0:T(8,128)(2,1)S(1)}, u32[]{:S(2)}, u32[]{:S(2)}) %collective-permute-start.24) | collective-permute-done | bytes 65568 | tf_op jit(solution)/shard_map/ppermute | solution.py:413
  118.2 2.9 %collective-permute-start.27 = (bf16[64,512]{1,0:T(8,128)(2,1)S(1)}, bf16[64,512]{1,0:T(8,128)(2,1)S(1)}, u32[]{:S(2)}, u32[]{:S(2)}) collective-permute-start(bf16[64,512]{1,0:T(8,128)(2,1)S(1)} %add_convert_fusion), channel_id=1, source_target_pairs={{0,1},{1,0},{2,3},{3,2},{4,5},{5,4},{6,7},{7,6},{8,9},{9,8},{10,11... | collective-permute-start | bytes 196616 | tf_op jit(solution)/shard_map/ppermute | solution.py:408
  (45 shorter events, 12.9 us)
Async XLA Ops:
  2.5 16.9 %collective-permute-start.4 = (bf16[192,256]{1,0:T(8,128)(2,1)}, bf16[192,256]{1,0:T(8,128)(2,1)S(1)}, u32[]{:S(2)}, u32[]{:S(2)}) collective-permute-start(bf16[192,256]{1,0:T(8,128)(2,1)} %get-tuple-element.74), channel_id=1, source_target_pairs={{0,128},{1,129},{16,144},{17,145},{32,160},{33,161},{48,176},{49,1... | collective-permute-start | bytes 294920 | tf_op jit(solution)/shard_map/ppermute | solution.py:422
  6.1 13.3 %collective-permute-start.5 = (bf16[192,256]{1,0:T(8,128)(2,1)}, bf16[192,256]{1,0:T(8,128)(2,1)S(1)}, u32[]{:S(2)}, u32[]{:S(2)}) collective-permute-start(bf16[192,256]{1,0:T(8,128)(2,1)} %get-tuple-element.75), channel_id=1, source_target_pairs={{0,144},{1,241},{16,128},{17,161},{32,176},{33,145},{48,160},{49,1... | collective-permute-start | bytes 294920 | tf_op jit(solution)/shard_map/ppermute | solution.py:422
  13.9 9.1 %collective-permute-start = (bf16[128,1024]{1,0:T(8,128)(2,1)}, bf16[128,1024]{1,0:T(8,128)(2,1)S(1)}, u32[]{:S(2)}, u32[]{:S(2)}) collective-permute-start(bf16[128,1024]{1,0:T(8,128)(2,1)} %get-tuple-element.69), channel_id=1, source_target_pairs={{0,16},{1,113},{16,0},{17,33},{32,48},{33,17},{48,32},{49,65},{64,... | collective-permute-start | bytes 786440 | tf_op jit(solution)/shard_map/ppermute | solution.py:422
  14.1 14.9 %collective-permute-start.1 = (bf16[128,1024]{1,0:T(8,128)(2,1)}, bf16[128,1024]{1,0:T(8,128)(2,1)S(1)}, u32[]{:S(2)}, u32[]{:S(2)}) collective-permute-start(bf16[128,1024]{1,0:T(8,128)(2,1)} %get-tuple-element.70), channel_id=1, source_target_pairs={{0,128},{1,129},{16,144},{17,145},{32,160},{33,161},{48,176},{49,1... | collective-permute-start | bytes 786440 | tf_op jit(solution)/shard_map/ppermute | solution.py:422
  16.8 5.2 %collective-permute-start.3 = (bf16[192,256]{1,0:T(8,128)(2,1)}, bf16[192,256]{1,0:T(8,128)(2,1)S(1)}, u32[]{:S(2)}, u32[]{:S(2)}) collective-permute-start(bf16[192,256]{1,0:T(8,128)(2,1)} %get-tuple-element.73), channel_id=1, source_target_pairs={{0,16},{1,113},{16,0},{17,33},{32,48},{33,17},{48,32},{49,65},{64,... | collective-permute-start | bytes 294920 | tf_op jit(solution)/shard_map/ppermute | solution.py:422
  19.4 11.0 %collective-permute-start.2 = (bf16[128,1024]{1,0:T(8,128)(2,1)}, bf16[128,1024]{1,0:T(8,128)(2,1)S(1)}, u32[]{:S(2)}, u32[]{:S(2)}) collective-permute-start(bf16[128,1024]{1,0:T(8,128)(2,1)} %get-tuple-element.71), channel_id=1, source_target_pairs={{0,144},{1,241},{16,128},{17,161},{32,176},{33,145},{48,160},{49,1... | collective-permute-start | bytes 786440 | tf_op jit(solution)/shard_map/ppermute | solution.py:422
  19.5 15.3 %collective-permute-start.8 = (bf16[2,192,256]{2,1,0:T(8,128)(2,1)S(1)}, bf16[2,192,256]{2,1,0:T(8,128)(2,1)S(1)}, u32[]{:S(2)}, u32[]{:S(2)}) collective-permute-start(bf16[2,192,256]{2,1,0:T(8,128)(2,1)S(1)} %pad_maximum_fusion.1.own_b), channel_id=1, source_target_pairs={{0,96},{1,97},{16,112},{17,113},{32,0},{33,1},{48,16},{49,17},{64,... | collective-permute-start | bytes 589832 | tf_op jit(solution)/shard_map/ppermute | solution.py:422
  22.9 15.3 %collective-permute-start.6 = (bf16[2,192,256]{2,1,0:T(8,128)(2,1)S(1)}, bf16[2,192,256]{2,1,0:T(8,128)(2,1)S(1)}, u32[]{:S(2)}, u32[]{:S(2)}) collective-permute-start(bf16[2,192,256]{2,1,0:T(8,128)(2,1)S(1)} %pad_maximum_fusion.own_a), channel_id=1, source_target_pairs={{0,32},{1,33},{16,48},{17,49},{32,64},{33,65},{48,80},{49,81},{64,... | collective-permute-start | bytes 589832 | tf_op jit(solution)/shard_map/ppermute | solution.py:422
  23.0 23.1 %collective-permute-start.10 = (bf16[2,192,256]{2,1,0:T(8,128)(2,1)S(1)}, bf16[2,192,256]{2,1,0:T(8,128)(2,1)S(1)}, u32[]{:S(2)}, u32[]{:S(2)}) collective-permute-start(bf16[2,192,256]{2,1,0:T(8,128)(2,1)S(1)} %pad_maximum_fusion.1.own_b), channel_id=1, source_target_pairs={{0,32},{1,33},{16,48},{17,49},{32,64},{33,65},{48,80},{49,81},{64,... | collective-permute-start | bytes 589832 | tf_op jit(solution)/shard_map/ppermute | solution.py:422
  29.0 17.2 %collective-permute-start.11 = (bf16[2,192,256]{2,1,0:T(8,128)(2,1)S(1)}, bf16[2,192,256]{2,1,0:T(8,128)(2,1)S(1)}, u32[]{:S(2)}, u32[]{:S(2)}) collective-permute-start(bf16[2,192,256]{2,1,0:T(8,128)(2,1)S(1)} %pad_maximum_fusion.own_a), channel_id=1, source_target_pairs={{0,96},{1,97},{16,112},{17,113},{32,0},{33,1},{48,16},{49,17},{64,... | collective-permute-start | bytes 589832 | tf_op jit(solution)/shard_map/ppermute | solution.py:422
  30.4 1.0 copy-start
  34.8 17.1 %collective-permute-start.9 = (bf16[2,192,256]{2,1,0:T(8,128)(2,1)S(1)}, bf16[2,192,256]{2,1,0:T(8,128)(2,1)S(1)}, u32[]{:S(2)}, u32[]{:S(2)}) collective-permute-start(bf16[2,192,256]{2,1,0:T(8,128)(2,1)S(1)} %collective-permute-done.8.right_b), channel_id=1, source_target_pairs={{0,96},{1,97},{16,112},{17,113},{32,0},{33,1},{48,16},{49,17},{64,... | collective-permute-start | bytes 589832 | tf_op jit(solution)/shard_map/ppermute | solution.py:422
  38.2 13.6 %collective-permute-start.7 = (bf16[2,192,256]{2,1,0:T(8,128)(2,1)S(1)}, bf16[2,192,256]{2,1,0:T(8,128)(2,1)S(1)}, u32[]{:S(2)}, u32[]{:S(2)}) collective-permute-start(bf16[2,192,256]{2,1,0:T(8,128)(2,1)S(1)} %collective-permute-done.6.left_a), channel_id=1, source_target_pairs={{0,32},{1,33},{16,48},{17,49},{32,64},{33,65},{48,80},{49,81},{64,... | collective-permute-start | bytes 589832 | tf_op jit(solution)/shard_map/ppermute | solution.py:422
  57.6 12.8 %collective-permute-start.12 = (bf16[2,192,256]{2,1,0:T(8,128)(2,1)S(1)}, bf16[2,192,256]{2,1,0:T(8,128)(2,1)S(1)}, u32[]{:S(2)}, u32[]{:S(2)}) collective-permute-start(bf16[2,192,256]{2,1,0:T(8,128)(2,1)S(1)} %get-tuple-element.97), channel_id=1, source_target_pairs={{0,32},{1,33},{16,48},{17,49},{32,64},{33,65},{48,80},{49,81},{64,... | collective-permute-start | bytes 589832 | tf_op jit(solution)/shard_map/ppermute | solution.py:422
  58.1 13.9 %collective-permute-start.13 = (bf16[2,192,256]{2,1,0:T(8,128)(2,1)S(1)}, bf16[2,192,256]{2,1,0:T(8,128)(2,1)S(1)}, u32[]{:S(2)}, u32[]{:S(2)}) collective-permute-start(bf16[2,192,256]{2,1,0:T(8,128)(2,1)S(1)} %get-tuple-element.98), channel_id=1, source_target_pairs={{0,96},{1,97},{16,112},{17,113},{32,0},{33,1},{48,16},{49,17},{64,... | collective-permute-start | bytes 589832 | tf_op jit(solution)/shard_map/ppermute | solution.py:422
  72.1 18.9 %collective-permute-start.14 = (bf16[4,192,256]{2,1,0:T(8,128)(2,1)S(1)}, bf16[4,192,256]{2,1,0:T(8,128)(2,1)S(1)}, u32[]{:S(2)}, u32[]{:S(2)}) collective-permute-start(bf16[4,192,256]{2,1,0:T(8,128)(2,1)S(1)} %get-tuple-element.99), channel_id=1, source_target_pairs={{0,96},{1,97},{16,112},{17,113},{32,0},{33,1},{48,16},{49,17},{64,... | collective-permute-start | bytes 1179656 | tf_op jit(solution)/shard_map/ppermute | solution.py:422
  72.4 18.6 %collective-permute-start.15 = (bf16[4,192,256]{2,1,0:T(8,128)(2,1)S(1)}, bf16[4,192,256]{2,1,0:T(8,128)(2,1)S(1)}, u32[]{:S(2)}, u32[]{:S(2)}) collective-permute-start(bf16[4,192,256]{2,1,0:T(8,128)(2,1)S(1)} %get-tuple-element.100), channel_id=1, source_target_pairs={{0,32},{1,33},{16,48},{17,49},{32,64},{33,65},{48,80},{49,81},{64,... | collective-permute-start | bytes 1179656 | tf_op jit(solution)/shard_map/ppermute | solution.py:422
  79.1 18.2 %collective-permute-start.19 = (bf16[128,1024]{1,0:T(8,128)(2,1)S(1)}, bf16[128,1024]{1,0:T(8,128)(2,1)S(1)}, u32[]{:S(2)}, u32[]{:S(2)}) collective-permute-start(bf16[128,1024]{1,0:T(8,128)(2,1)S(1)} %get-tuple-element.108), channel_id=1, source_target_pairs={{0,144},{1,241},{16,128},{17,161},{32,176},{33,145},{48,160},{49,1... | collective-permute-start | bytes 786440 | tf_op jit(solution)/shard_map/ppermute | solution.py:422
  83.3 15.1 %collective-permute-start.20 = (bf16[128,1024]{1,0:T(8,128)(2,1)S(1)}, bf16[128,1024]{1,0:T(8,128)(2,1)S(1)}, u32[]{:S(2)}, u32[]{:S(2)}) collective-permute-start(bf16[128,1024]{1,0:T(8,128)(2,1)S(1)} %get-tuple-element.109), channel_id=1, source_target_pairs={{0,128},{1,129},{16,144},{17,145},{32,160},{33,161},{48,176},{49,1... | collective-permute-start | bytes 786440 | tf_op jit(solution)/shard_map/ppermute | solution.py:422
  91.0 11.0 %collective-permute-start.21 = (bf16[128,1024]{1,0:T(8,128)(2,1)S(1)}, bf16[128,1024]{1,0:T(8,128)(2,1)S(1)}, u32[]{:S(2)}, u32[]{:S(2)}) collective-permute-start(bf16[128,1024]{1,0:T(8,128)(2,1)S(1)} %get-tuple-element.110), channel_id=1, source_target_pairs={{0,16},{1,113},{16,0},{17,33},{32,48},{33,17},{48,32},{49,65},{64,... | collective-permute-start | bytes 786440 | tf_op jit(solution)/shard_map/ppermute | solution.py:422
  91.2 8.9 %collective-permute-start.16 = (bf16[192,256]{1,0:T(8,128)(2,1)S(1)}, bf16[192,256]{1,0:T(8,128)(2,1)S(1)}, u32[]{:S(2)}, u32[]{:S(2)}) collective-permute-start(bf16[192,256]{1,0:T(8,128)(2,1)S(1)} %get-tuple-element.104), channel_id=1, source_target_pairs={{0,144},{1,241},{16,128},{17,161},{32,176},{33,145},{48,160},{49,1... | collective-permute-start | bytes 294920 | tf_op jit(solution)/shard_map/ppermute | solution.py:422
  94.5 6.0 %collective-permute-start.17 = (bf16[192,256]{1,0:T(8,128)(2,1)S(1)}, bf16[192,256]{1,0:T(8,128)(2,1)S(1)}, u32[]{:S(2)}, u32[]{:S(2)}) collective-permute-start(bf16[192,256]{1,0:T(8,128)(2,1)S(1)} %get-tuple-element.105), channel_id=1, source_target_pairs={{0,128},{1,129},{16,144},{17,145},{32,160},{33,161},{48,176},{49,1... | collective-permute-start | bytes 294920 | tf_op jit(solution)/shard_map/ppermute | solution.py:422
  97.3 4.7 %collective-permute-start.18 = (bf16[192,256]{1,0:T(8,128)(2,1)S(1)}, bf16[192,256]{1,0:T(8,128)(2,1)S(1)}, u32[]{:S(2)}, u32[]{:S(2)}) collective-permute-start(bf16[192,256]{1,0:T(8,128)(2,1)S(1)} %get-tuple-element.106), channel_id=1, source_target_pairs={{0,16},{1,113},{16,0},{17,33},{32,48},{33,17},{48,32},{49,65},{64,... | collective-permute-start | bytes 294920 | tf_op jit(solution)/shard_map/ppermute | solution.py:422
  102.6 5.8 %collective-permute-start.22 = (bf16[64,512]{1,0:T(8,128)(2,1)S(1)}, bf16[64,512]{1,0:T(8,128)(2,1)S(1)}, u32[]{:S(2)}, u32[]{:S(2)}) collective-permute-start(bf16[64,512]{1,0:T(8,128)(2,1)S(1)} %get-tuple-element.116), channel_id=1, source_target_pairs={{0,1},{1,0},{2,3},{3,2},{4,5},{5,4},{6,7},{7,6},{8,9},{9,8},{10,11... | collective-permute-start | bytes 196616 | tf_op jit(solution)/shard_map/ppermute | solution.py:408
  108.4 3.2 %collective-permute-start.23 = (bf16[64,512]{1,0:T(8,128)(2,1)S(1)}, bf16[64,512]{1,0:T(8,128)(2,1)S(1)}, u32[]{:S(2)}, u32[]{:S(2)}) collective-permute-start(bf16[64,512]{1,0:T(8,128)(2,1)S(1)} %add_convert_fusion.2), channel_id=1, source_target_pairs={{0,2},{2,0},{1,3},{3,1},{4,6},{6,4},{5,7},{7,5},{8,10},{10,8},{9,1... | collective-permute-start | bytes 196616 | tf_op jit(solution)/shard_map/ppermute | solution.py:408
  111.6 3.2 %collective-permute-start.26 = (bf16[64,512]{1,0:T(8,128)(2,1)S(1)}, bf16[64,512]{1,0:T(8,128)(2,1)S(1)}, u32[]{:S(2)}, u32[]{:S(2)}) collective-permute-start(bf16[64,512]{1,0:T(8,128)(2,1)S(1)} %add_convert_fusion.1), channel_id=1, source_target_pairs={{0,12},{4,0},{8,4},{12,8},{1,13},{5,1},{9,5},{13,9},{2,14},{6,2},{... | collective-permute-start | bytes 196616 | tf_op jit(solution)/shard_map/ppermute | solution.py:413
  112.6 4.3 %collective-permute-start.25 = (bf16[64,512]{1,0:T(8,128)(2,1)S(1)}, bf16[64,512]{1,0:T(8,128)(2,1)S(1)}, u32[]{:S(2)}, u32[]{:S(2)}) collective-permute-start(bf16[64,512]{1,0:T(8,128)(2,1)S(1)} %add_convert_fusion.1), channel_id=1, source_target_pairs={{0,4},{4,8},{8,12},{12,0},{1,5},{5,9},{9,13},{13,1},{2,6},{6,10},{... | collective-permute-start | bytes 196616 | tf_op jit(solution)/shard_map/ppermute | solution.py:413
  113.2 5.0 %collective-permute-start.24 = (bf16[64,512]{1,0:T(8,128)(2,1)S(1)}, bf16[64,512]{1,0:T(8,128)(2,1)S(1)}, u32[]{:S(2)}, u32[]{:S(2)}) collective-permute-start(bf16[64,512]{1,0:T(8,128)(2,1)S(1)} %add_convert_fusion.1), channel_id=1, source_target_pairs={{0,8},{4,12},{8,0},{12,4},{1,9},{5,13},{9,1},{13,5},{2,10},{6,14},... | collective-permute-start | bytes 196616 | tf_op jit(solution)/shard_map/ppermute | solution.py:413
  118.2 3.8 %collective-permute-start.27 = (bf16[64,512]{1,0:T(8,128)(2,1)S(1)}, bf16[64,512]{1,0:T(8,128)(2,1)S(1)}, u32[]{:S(2)}, u32[]{:S(2)}) collective-permute-start(bf16[64,512]{1,0:T(8,128)(2,1)S(1)} %add_convert_fusion), channel_id=1, source_target_pairs={{0,1},{1,0},{2,3},{3,2},{4,5},{5,4},{6,7},{7,6},{8,9},{9,8},{10,11... | collective-permute-start | bytes 196616 | tf_op jit(solution)/shard_map/ppermute | solution.py:408

commit v10 on v9

--- a/solution.py
+++ b/solution.py
@@ -452,6 +452,10 @@
             copies=4,
         )
     )
+    for d in (1, 2, 3):
+        kv[d] = partner(kv[d], d)
+    own_a = jnp.stack(kv[:2])
+    own_a, spot = lax.optimization_barrier((own_a, spot))
     qd = list(
         call(
             pack_qd_kernel,
@@ -462,13 +466,12 @@
             copies=2,
         )
     )
-    for d in (1, 2, 3):
-        kv[d] = partner(kv[d], d)
+    left_a, right_a = quad_turn(own_a, 1), quad_turn(own_a, -1)
     for d in (1, 2, 3):
         qd[d] = partner(qd[d], d)
-    own_a, own_b = jnp.stack(kv[:2]), jnp.stack(kv[2:])
-    left_a, right_b = quad_turn(own_a, 1), quad_turn(own_b, -1)
-    left_b, right_a = quad_turn(own_b, 1), quad_turn(own_a, -1)
+    own_b = jnp.stack(kv[2:])
+    own_b, left_a, right_a = lax.optimization_barrier((own_b, left_a, right_a))
+    left_b, right_b = quad_turn(own_b, 1), quad_turn(own_b, -1)
     far_a, far_b = quad_turn(left_a, 1), quad_turn(right_b, -1)
 
     tiles = (2, HEAD_DIM, LANES)

time: 123 us -> 125 us (1.016)
  starting transfers between devices: 49.6 us -> 56.1 us
  waiting for transfers between devices: 34.8 us -> 30.1 us
    ppermute x22, starting transfers between devices: 39 us -> 44.9 us  [local_permute(): return lax.ppermute(x, LOCAL, pairs)]
    ppermute x22, waiting for transfers between devices: 28.9 us -> 24.9 us  [local_permute(): return lax.ppermute(x, LOCAL, pairs)]
    ppermute x3, starting transfers between devices: 2.6 us -> 4.44 us  [turn(): return lax.ppermute(x, axis, [(i, (i + step) % size) for i in range(size)])]
  transfers between devices with their start and end apart: 28 -> 28, of which waited for: 17 -> 12; matrix products, arithmetic and copies ran while one was open for 1% -> 1% of each run, Pallas kernels for 21% -> 20%
where the time goes in v10:
time: 125 us
  starting transfers between devices  56.1 us (45%)
  Pallas kernels  33.4 us (27%)
  waiting for transfers between devices  30.1 us (24%)
  between operations  2.13 us (2%)
  other arithmetic  1.67 us (1%)
    ppermute x22, starting transfers between devices, local_permute(): return lax.ppermute(x, LOCAL, pairs)  44.9 us
    pallas_call x12, Pallas kernels, call(): pl.pallas_call(kernel, out_shape=tuple(outs), in_specs=[SMEM] * len(scala...  33.4 us
    ppermute x22, waiting for transfers between devices, local_permute(): return lax.ppermute(x, LOCAL, pairs)  24.9 us
    ppermute x3, starting transfers between devices, swap(): return lax.ppermute(x, axis, [(0, 1), (1, 0)])  6.82 us
    ppermute x3, starting transfers between devices, turn(): return lax.ppermute(x, axis, [(i, (i + step) % size) for i in range(size)])  4.44 us
    ppermute x3, waiting for transfers between devices, turn(): return lax.ppermute(x, axis, [(i, (i + step) % size) for i in range(size)])  3.38 us
  transfers between devices with their start and end apart: 28, of which 12 were waited for; matrix products, arithmetic and copies ran while one was open for 1% of the time, Pallas kernels for 20%

profile of v10, /device:TPU:1, one launch (start us, length us, event | category | flops | bytes accessed | tf_op | source)
XLA Modules:
  0.0 124.5 jit_solution(4574585035082794845)
XLA Ops:
  0.6 1.8 %shard_map.127 = (bf16[192,256]{1,0:T(8,128)(2,1)}, bf16[192,256]{1,0:T(8,128)(2,1)}, bf16[192,256]{1,0:T(8,128)(2,1)}, bf16[192,256]{1,0:T(8,128)(2,1)}) custom-call(s32[1]{0:T(128)} %bitcast.info, bf16[128,512]{1,0:T(8,128)(2,1)} %bitcast.17, bf16[128,512]{1,0:T(8,128)(2,1)} %bitcast.18, bf16[64,512]{1,0:T(8,128)(2,1)} %kp.1, bf16[64,512]{1,0:T(8,128)(2,1)} %vp.1), custom_call_target="tpu_custom_call" | custom-call | bytes 1000000 | tf_op jit(solution)/shard_map/pallas_call | solution.py:392
  2.5 6.5 %collective-permute-start = (bf16[192,256]{1,0:T(8,128)(2,1)}, bf16[192,256]{1,0:T(8,128)(2,1)S(1)}, u32[]{:S(2)}, u32[]{:S(2)}) collective-permute-start(bf16[192,256]{1,0:T(8,128)(2,1)} %get-tuple-element.74), channel_id=1, source_target_pairs={{0,16},{1,113},{16,0},{17,33},{32,48},{33,17},{48,32},{49,65},{64,... | collective-permute-start | bytes 294920 | tf_op jit(solution)/shard_map/ppermute | solution.py:422
  9.0 2.7 %collective-permute-start.4 = (bf16[192,256]{1,0:T(8,128)(2,1)}, bf16[192,256]{1,0:T(8,128)(2,1)S(1)}, u32[]{:S(2)}, u32[]{:S(2)}) collective-permute-start(bf16[192,256]{1,0:T(8,128)(2,1)} %get-tuple-element.81), channel_id=1, source_target_pairs={{0,128},{1,129},{16,144},{17,145},{32,160},{33,161},{48,176},{49,1... | collective-permute-start | bytes 294920 | tf_op jit(solution)/shard_map/ppermute | solution.py:422
  12.7 1.9 %collective-permute-start.7 = (bf16[2,192,256]{2,1,0:T(8,128)(2,1)S(1)}, bf16[2,192,256]{2,1,0:T(8,128)(2,1)S(1)}, u32[]{:S(2)}, u32[]{:S(2)}) collective-permute-start(bf16[2,192,256]{2,1,0:T(8,128)(2,1)S(1)} %pad_maximum_fusion.own_a), channel_id=1, source_target_pairs={{0,96},{1,97},{16,112},{17,113},{32,0},{33,1},{48,16},{49,17},{64,... | collective-permute-start | bytes 589832 | tf_op jit(solution)/shard_map/ppermute | solution.py:422
  15.1 2.2 %shard_map.128 = (bf16[128,1024]{1,0:T(8,128)(2,1)}, bf16[128,1024]{1,0:T(8,128)(2,1)}, bf16[128,1024]{1,0:T(8,128)(2,1)}, bf16[128,1024]{1,0:T(8,128)(2,1)}) custom-call(s32[1]{0:T(128)} %bitcast.info, bf16[128,2048]{1,0:T(8,128)(2,1)} %bitcast.15, bf16[128,2048]{1,0:T(8,128)(2,1)} %bitcast.16), custom_call_target="tpu_custom_call" | custom-call | bytes 1000000 | tf_op jit(solution)/shard_map/pallas_call | solution.py:392
  17.4 3.9 %collective-permute-start.1 = (bf16[128,1024]{1,0:T(8,128)(2,1)}, bf16[128,1024]{1,0:T(8,128)(2,1)S(1)}, u32[]{:S(2)}, u32[]{:S(2)}) collective-permute-start(bf16[128,1024]{1,0:T(8,128)(2,1)} %get-tuple-element.77), channel_id=1, source_target_pairs={{0,16},{1,113},{16,0},{17,33},{32,48},{33,17},{48,32},{49,65},{64,... | collective-permute-start | bytes 786440 | tf_op jit(solution)/shard_map/ppermute | solution.py:422
  21.2 2.7 %collective-permute-start.2 = (bf16[128,1024]{1,0:T(8,128)(2,1)}, bf16[128,1024]{1,0:T(8,128)(2,1)S(1)}, u32[]{:S(2)}, u32[]{:S(2)}) collective-permute-start(bf16[128,1024]{1,0:T(8,128)(2,1)} %get-tuple-element.78), channel_id=1, source_target_pairs={{0,128},{1,129},{16,144},{17,145},{32,160},{33,161},{48,176},{49,1... | collective-permute-start | bytes 786440 | tf_op jit(solution)/shard_map/ppermute | solution.py:422
  24.8 1.8 %collective-permute-start.11 = (bf16[2,192,256]{2,1,0:T(8,128)(2,1)S(1)}, bf16[2,192,256]{2,1,0:T(8,128)(2,1)S(1)}, u32[]{:S(2)}, u32[]{:S(2)}) collective-permute-start(bf16[2,192,256]{2,1,0:T(8,128)(2,1)S(1)} %pad_maximum_fusion.1.own_b), channel_id=1, source_target_pairs={{0,32},{1,33},{16,48},{17,49},{32,64},{33,65},{48,80},{49,81},{64,... | collective-permute-start | bytes 589832 | tf_op jit(solution)/shard_map/ppermute | solution.py:422
  28.0 5.0 %collective-permute-done.1.qd1 = bf16[128,1024]{1,0:T(8,128)(2,1)S(1)} collective-permute-done((bf16[128,1024]{1,0:T(8,128)(2,1)}, bf16[128,1024]{1,0:T(8,128)(2,1)S(1)}, u32[]{:S(2)}, u32[]{:S(2)}) %collective-permute-start.1) | collective-permute-done | bytes 262176 | tf_op jit(solution)/shard_map/ppermute | solution.py:422
  33.0 7.9 %collective-permute-done.3.qd3 = bf16[128,1024]{1,0:T(8,128)(2,1)S(1)} collective-permute-done((bf16[128,1024]{1,0:T(8,128)(2,1)}, bf16[128,1024]{1,0:T(8,128)(2,1)S(1)}, u32[]{:S(2)}, u32[]{:S(2)}) %collective-permute-start.3) | collective-permute-done | bytes 262176 | tf_op jit(solution)/shard_map/ppermute | solution.py:422
  41.8 3.4 %shard_map.129 = (bf16[2,128,1024]{2,1,0:T(8,128)(2,1)S(1)}, bf16[2,1024,128]{2,1,0:T(8,128)(2,1)S(1)}, bf16[2,128,1024]{2,1,0:T(8,128)(2,1)S(1)}, bf16[1,1280,1...) custom-call(s32[5]{0:T(128)S(1)} %stack.33.info, ...), custom_call_target="tpu_custom_call" | custom-call | flops 1342177280 | bytes 1000000 | tf_op jit(solution)/shard_map/pallas_call | solution.py:392
  45.5 5.7 %shard_map.130 = (bf16[2,1280,1024]{2,1,0:T(8,128)(2,1)S(1)}, f32[2,1,1024]{2,1,0:T(1,128)S(1)}, f32[2,1,1024]{2,1,0:T(1,128)S(1)}, f32[2,128,1024]{2,1,0:T(8,128)S(1)}) custom-call(s32[5]{0:T(128)S(1)} %stack.33.info, bf16[2,128,1024]{2,1,0:T(8,128)(2,1)S(1)} %get-tuple-element.85.qt, bf16[2,192,256]{2,1,0:T(8,128)(2,1)S(1)} %collective-permute-done.6.left_a, ...), custom_call_target="tpu_custom_call" | custom-call | flops 2684354560 | bytes 1000000 | tf_op jit(solution)/shard_map/pallas_call | solution.py:392
  52.1 5.7 %shard_map.131 = (f32[2,1,1024]{2,1,0:T(1,128)S(1)}, bf16[2,128,1024]{2,1,0:T(8,128)(2,1)S(1)}, bf16[2,1024,128]{2,1,0:T(8,128)(2,1)S(1)}, f32[2,1,1024]{2,1,0:T...) custom-call(s32[5]{0:T(128)S(1)} %stack.33.info, ...), custom_call_target="tpu_custom_call" | custom-call | flops 4026531840 | bytes 1000000 | tf_op jit(solution)/shard_map/pallas_call | solution.py:392
  57.9 1.5 %collective-permute-start.12 = (bf16[2,192,256]{2,1,0:T(8,128)(2,1)S(1)}, bf16[2,192,256]{2,1,0:T(8,128)(2,1)S(1)}, u32[]{:S(2)}, u32[]{:S(2)}) collective-permute-start(bf16[2,192,256]{2,1,0:T(8,128)(2,1)S(1)} %get-tuple-element.107), channel_id=1, source_target_pairs={{0,32},{1,33},{16,48},{17,49},{32,64},{33,65},{48,80},{49,81},{64,... | collective-permute-start | bytes 589832 | tf_op jit(solution)/shard_map/ppermute | solution.py:422
  59.4 2.5 %collective-permute-start.13 = (bf16[2,192,256]{2,1,0:T(8,128)(2,1)S(1)}, bf16[2,192,256]{2,1,0:T(8,128)(2,1)S(1)}, u32[]{:S(2)}, u32[]{:S(2)}) collective-permute-start(bf16[2,192,256]{2,1,0:T(8,128)(2,1)S(1)} %get-tuple-element.108), channel_id=1, source_target_pairs={{0,96},{1,97},{16,112},{17,113},{32,0},{33,1},{48,16},{49,17},{64,... | collective-permute-start | bytes 589832 | tf_op jit(solution)/shard_map/ppermute | solution.py:422
  61.9 6.4 %shard_map.132 = (f32[2,128,1024]{2,1,0:T(8,128)S(1)}, bf16[4,192,256]{2,1,0:T(8,128)(2,1)S(1)}, bf16[4,192,256]{2,1,0:T(8,128)(2,1)S(1)}) custom-call(s32[5]{0:T(128)S(1)} %stack.33.info, bf16[2,1024,128]{2,1,0:T(8,128)(2,1)S(1)} %get-tuple-element.84.q, bf16[2,128,1024]{2,1,0:T(8,128)(2,1)S(1)} %get-tuple-element.95.uplt, ...), custom_call_target="tpu_custom_call" | custom-call | flops 5368709120 | bytes 1000000 | tf_op jit(solution)/shard_map/pallas_call | solution.py:392
  68.3 2.0 %collective-permute-done.12.far_a = bf16[2,192,256]{2,1,0:T(8,128)(2,1)S(1)} collective-permute-done((bf16[2,192,256]{2,1,0:T(8,128)(2,1)S(1)}, bf16[2,192,256]{2,1,0:T(8,128)(2,1)S(1)}, u32[]{:S(2)}, u32[]{:S(2)}) %collective-permute-start.12) | collective-permute-done | bytes 196640 | tf_op jit(solution)/shard_map/ppermute | solution.py:422
  70.4 3.1 %collective-permute-start.14 = (bf16[4,192,256]{2,1,0:T(8,128)(2,1)S(1)}, bf16[4,192,256]{2,1,0:T(8,128)(2,1)S(1)}, u32[]{:S(2)}, u32[]{:S(2)}) collective-permute-start(bf16[4,192,256]{2,1,0:T(8,128)(2,1)S(1)} %get-tuple-element.109), channel_id=1, source_target_pairs={{0,96},{1,97},{16,112},{17,113},{32,0},{33,1},{48,16},{49,17},{64,... | collective-permute-start | bytes 1179656 | tf_op jit(solution)/shard_map/ppermute | solution.py:422
  73.5 4.4 %shard_map.133 = (bf16[4,192,256]{2,1,0:T(8,128)(2,1)S(1)}, bf16[128,1024]{1,0:T(8,128)(2,1)S(1)}, bf16[128,1024]{1,0:T(8,128)(2,1)S(1)}, bf16[128,1024]{1,0:T(8,128)(2,1)S(1)}, bf16[128,1024]{1,0:T(8,128)(2,1)S(1)}) custom-call(s32[5]{0:T(128)S(1)} %stack.33.info, bf16[2,1024,128]{2,1,0:T(8,128)(2,1)S(1)} %get-tuple-element.84.q, ...), custom_call_target="tpu_custom_call" | custom-call | flops 2684354560 | bytes 1000000 | tf_op jit(solution)/shard_map/pallas_call | solution.py:392
  77.9 7.7 %collective-permute-start.19 = (bf16[128,1024]{1,0:T(8,128)(2,1)S(1)}, bf16[128,1024]{1,0:T(8,128)(2,1)S(1)}, u32[]{:S(2)}, u32[]{:S(2)}) collective-permute-start(bf16[128,1024]{1,0:T(8,128)(2,1)S(1)} %get-tuple-element.118), channel_id=1, source_target_pairs={{0,144},{1,241},{16,128},{17,161},{32,176},{33,145},{48,160},{49,1... | collective-permute-start | bytes 786440 | tf_op jit(solution)/shard_map/ppermute | solution.py:422
  85.7 4.1 %collective-permute-done.14.left = bf16[4,192,256]{2,1,0:T(8,128)(2,1)S(1)} collective-permute-done((bf16[4,192,256]{2,1,0:T(8,128)(2,1)S(1)}, bf16[4,192,256]{2,1,0:T(8,128)(2,1)S(1)}, u32[]{:S(2)}, u32[]{:S(2)}) %collective-permute-start.14) | collective-permute-done | bytes 393248 | tf_op jit(solution)/shard_map/ppermute | solution.py:422
  89.8 4.5 %collective-permute-start.21 = (bf16[128,1024]{1,0:T(8,128)(2,1)S(1)}, bf16[128,1024]{1,0:T(8,128)(2,1)S(1)}, u32[]{:S(2)}, u32[]{:S(2)}) collective-permute-start(bf16[128,1024]{1,0:T(8,128)(2,1)S(1)} %get-tuple-element.120), channel_id=1, source_target_pairs={{0,16},{1,113},{16,0},{17,33},{32,48},{33,17},{48,32},{49,65},{64,... | collective-permute-start | bytes 786440 | tf_op jit(solution)/shard_map/ppermute | solution.py:422
  94.4 2.9 %collective-permute-start.16 = (bf16[192,256]{1,0:T(8,128)(2,1)S(1)}, bf16[192,256]{1,0:T(8,128)(2,1)S(1)}, u32[]{:S(2)}, u32[]{:S(2)}) collective-permute-start(bf16[192,256]{1,0:T(8,128)(2,1)S(1)} %get-tuple-element.114), channel_id=1, source_target_pairs={{0,144},{1,241},{16,128},{17,161},{32,176},{33,145},{48,160},{49,1... | collective-permute-start | bytes 294920 | tf_op jit(solution)/shard_map/ppermute | solution.py:422
  98.6 1.6 %collective-permute-start.18 = (bf16[192,256]{1,0:T(8,128)(2,1)S(1)}, bf16[192,256]{1,0:T(8,128)(2,1)S(1)}, u32[]{:S(2)}, u32[]{:S(2)}) collective-permute-start(bf16[192,256]{1,0:T(8,128)(2,1)S(1)} %get-tuple-element.116), channel_id=1, source_target_pairs={{0,16},{1,113},{16,0},{17,33},{32,48},{33,17},{48,32},{49,65},{64,... | collective-permute-start | bytes 294920 | tf_op jit(solution)/shard_map/ppermute | solution.py:422
  100.2 2.3 %collective-permute-done.16.g3 = bf16[192,256]{1,0:T(8,128)(2,1)S(1)} collective-permute-done((bf16[192,256]{1,0:T(8,128)(2,1)S(1)}, bf16[192,256]{1,0:T(8,128)(2,1)S(1)}, u32[]{:S(2)}, u32[]{:S(2)}) %collective-permute-start.16) | collective-permute-done | bytes 98336 | tf_op jit(solution)/shard_map/ppermute | solution.py:422
  104.4 2.4 %collective-permute-start.22 = (bf16[64,512]{1,0:T(8,128)(2,1)S(1)}, bf16[64,512]{1,0:T(8,128)(2,1)S(1)}, u32[]{:S(2)}, u32[]{:S(2)}) collective-permute-start(bf16[64,512]{1,0:T(8,128)(2,1)S(1)} %get-tuple-element.126), channel_id=1, source_target_pairs={{0,1},{1,0},{2,3},{3,2},{4,5},{5,4},{6,7},{7,6},{8,9},{9,8},{10,11... | collective-permute-start | bytes 196616 | tf_op jit(solution)/shard_map/ppermute | solution.py:408
  107.8 1.4 %collective-permute-start.23 = (bf16[64,512]{1,0:T(8,128)(2,1)S(1)}, bf16[64,512]{1,0:T(8,128)(2,1)S(1)}, u32[]{:S(2)}, u32[]{:S(2)}) collective-permute-start(bf16[64,512]{1,0:T(8,128)(2,1)S(1)} %add_convert_fusion.2), channel_id=1, source_target_pairs={{0,2},{2,0},{1,3},{3,1},{4,6},{6,4},{5,7},{7,5},{8,10},{10,8},{9,1... | collective-permute-start | bytes 196616 | tf_op jit(solution)/shard_map/ppermute | solution.py:408
  110.5 1.6 %shard_map.138 = (bf16[128,2048]{1,0:T(8,128)(2,1)}, bf16[128,2048]{1,0:T(8,128)(2,1)}) custom-call(s32[5]{0:T(128)S(1)} %stack.33.info, bf16[128,1024]{1,0:T(8,128)(2,1)S(1)} %get-tuple-element.129.od0, bf16[128,1024]{1,0:T(8,128)(2,1)S(1)} %collective-permute-done.21.od1, bf16[128,1024]{1,0:T(8,128)(2,1)S(1)} %collective-permute-done.20.od2, ...), custom_call_target="tpu_custom_call" | custom-call | bytes 1000000 | tf_op jit(solution)/shard_map/pallas_call | solution.py:392
  112.1 2.8 %collective-permute-start.26 = (bf16[64,512]{1,0:T(8,128)(2,1)S(1)}, bf16[64,512]{1,0:T(8,128)(2,1)S(1)}, u32[]{:S(2)}, u32[]{:S(2)}) collective-permute-start(bf16[64,512]{1,0:T(8,128)(2,1)S(1)} %add_convert_fusion.1), channel_id=1, source_target_pairs={{0,12},{4,0},{8,4},{12,8},{1,13},{5,1},{9,5},{13,9},{2,14},{6,2},{... | collective-permute-start | bytes 196616 | tf_op jit(solution)/shard_map/ppermute | solution.py:413
  114.9 1.6 %collective-permute-start.24 = (bf16[64,512]{1,0:T(8,128)(2,1)S(1)}, bf16[64,512]{1,0:T(8,128)(2,1)S(1)}, u32[]{:S(2)}, u32[]{:S(2)}) collective-permute-start(bf16[64,512]{1,0:T(8,128)(2,1)S(1)} %add_convert_fusion.1), channel_id=1, source_target_pairs={{0,8},{4,12},{8,0},{12,4},{1,9},{5,13},{9,1},{13,5},{2,10},{6,14},... | collective-permute-start | bytes 196616 | tf_op jit(solution)/shard_map/ppermute | solution.py:413
  116.5 3.4 %collective-permute-done.25 = bf16[64,512]{1,0:T(8,128)(2,1)S(1)} collective-permute-done((bf16[64,512]{1,0:T(8,128)(2,1)S(1)}, bf16[64,512]{1,0:T(8,128)(2,1)S(1)}, u32[]{:S(2)}, u32[]{:S(2)}) %collective-permute-start.25) | collective-permute-done | bytes 65568 | tf_op jit(solution)/shard_map/ppermute | solution.py:413
  120.0 3.0 %collective-permute-start.27 = (bf16[64,512]{1,0:T(8,128)(2,1)S(1)}, bf16[64,512]{1,0:T(8,128)(2,1)S(1)}, u32[]{:S(2)}, u32[]{:S(2)}) collective-permute-start(bf16[64,512]{1,0:T(8,128)(2,1)S(1)} %add_convert_fusion), channel_id=1, source_target_pairs={{0,1},{1,0},{2,3},{3,2},{4,5},{5,4},{6,7},{7,6},{8,9},{9,8},{10,11... | collective-permute-start | bytes 196616 | tf_op jit(solution)/shard_map/ppermute | solution.py:408
  (45 shorter events, 11.8 us)
Async XLA Ops:
  2.5 9.3 %collective-permute-start = (bf16[192,256]{1,0:T(8,128)(2,1)}, bf16[192,256]{1,0:T(8,128)(2,1)S(1)}, u32[]{:S(2)}, u32[]{:S(2)}) collective-permute-start(bf16[192,256]{1,0:T(8,128)(2,1)} %get-tuple-element.74), channel_id=1, source_target_pairs={{0,16},{1,113},{16,0},{17,33},{32,48},{33,17},{48,32},{49,65},{64,... | collective-permute-start | bytes 294920 | tf_op jit(solution)/shard_map/ppermute | solution.py:422
  9.0 12.3 %collective-permute-start.4 = (bf16[192,256]{1,0:T(8,128)(2,1)}, bf16[192,256]{1,0:T(8,128)(2,1)S(1)}, u32[]{:S(2)}, u32[]{:S(2)}) collective-permute-start(bf16[192,256]{1,0:T(8,128)(2,1)} %get-tuple-element.81), channel_id=1, source_target_pairs={{0,128},{1,129},{16,144},{17,145},{32,160},{33,161},{48,176},{49,1... | collective-permute-start | bytes 294920 | tf_op jit(solution)/shard_map/ppermute | solution.py:422
  11.7 12.3 %collective-permute-start.5 = (bf16[192,256]{1,0:T(8,128)(2,1)}, bf16[192,256]{1,0:T(8,128)(2,1)S(1)}, u32[]{:S(2)}, u32[]{:S(2)}) collective-permute-start(bf16[192,256]{1,0:T(8,128)(2,1)} %get-tuple-element.82), channel_id=1, source_target_pairs={{0,144},{1,241},{16,128},{17,161},{32,176},{33,145},{48,160},{49,1... | collective-permute-start | bytes 294920 | tf_op jit(solution)/shard_map/ppermute | solution.py:422
  12.7 11.5 %collective-permute-start.7 = (bf16[2,192,256]{2,1,0:T(8,128)(2,1)S(1)}, bf16[2,192,256]{2,1,0:T(8,128)(2,1)S(1)}, u32[]{:S(2)}, u32[]{:S(2)}) collective-permute-start(bf16[2,192,256]{2,1,0:T(8,128)(2,1)S(1)} %pad_maximum_fusion.own_a), channel_id=1, source_target_pairs={{0,96},{1,97},{16,112},{17,113},{32,0},{33,1},{48,16},{49,17},{64,... | collective-permute-start | bytes 589832 | tf_op jit(solution)/shard_map/ppermute | solution.py:422
  14.6 9.6 %collective-permute-start.6 = (bf16[2,192,256]{2,1,0:T(8,128)(2,1)S(1)}, bf16[2,192,256]{2,1,0:T(8,128)(2,1)S(1)}, u32[]{:S(2)}, u32[]{:S(2)}) collective-permute-start(bf16[2,192,256]{2,1,0:T(8,128)(2,1)S(1)} %pad_maximum_fusion.own_a), channel_id=1, source_target_pairs={{0,32},{1,33},{16,48},{17,49},{32,64},{33,65},{48,80},{49,81},{64,... | collective-permute-start | bytes 589832 | tf_op jit(solution)/shard_map/ppermute | solution.py:422
  17.4 15.6 %collective-permute-start.1 = (bf16[128,1024]{1,0:T(8,128)(2,1)}, bf16[128,1024]{1,0:T(8,128)(2,1)S(1)}, u32[]{:S(2)}, u32[]{:S(2)}) collective-permute-start(bf16[128,1024]{1,0:T(8,128)(2,1)} %get-tuple-element.77), channel_id=1, source_target_pairs={{0,16},{1,113},{16,0},{17,33},{32,48},{33,17},{48,32},{49,65},{64,... | collective-permute-start | bytes 786440 | tf_op jit(solution)/shard_map/ppermute | solution.py:422
  21.2 11.7 %collective-permute-start.2 = (bf16[128,1024]{1,0:T(8,128)(2,1)}, bf16[128,1024]{1,0:T(8,128)(2,1)S(1)}, u32[]{:S(2)}, u32[]{:S(2)}) collective-permute-start(bf16[128,1024]{1,0:T(8,128)(2,1)} %get-tuple-element.78), channel_id=1, source_target_pairs={{0,128},{1,129},{16,144},{17,145},{32,160},{33,161},{48,176},{49,1... | collective-permute-start | bytes 786440 | tf_op jit(solution)/shard_map/ppermute | solution.py:422
  24.0 16.9 %collective-permute-start.3 = (bf16[128,1024]{1,0:T(8,128)(2,1)}, bf16[128,1024]{1,0:T(8,128)(2,1)S(1)}, u32[]{:S(2)}, u32[]{:S(2)}) collective-permute-start(bf16[128,1024]{1,0:T(8,128)(2,1)} %get-tuple-element.79), channel_id=1, source_target_pairs={{0,144},{1,241},{16,128},{17,161},{32,176},{33,145},{48,160},{49,1... | collective-permute-start | bytes 786440 | tf_op jit(solution)/shard_map/ppermute | solution.py:422
  24.1 21.1 %collective-permute-start.9 = (bf16[2,192,256]{2,1,0:T(8,128)(2,1)S(1)}, bf16[2,192,256]{2,1,0:T(8,128)(2,1)S(1)}, u32[]{:S(2)}, u32[]{:S(2)}) collective-permute-start(bf16[2,192,256]{2,1,0:T(8,128)(2,1)S(1)} %pad_maximum_fusion.1.own_b), channel_id=1, source_target_pairs={{0,96},{1,97},{16,112},{17,113},{32,0},{33,1},{48,16},{49,17},{64,... | collective-permute-start | bytes 589832 | tf_op jit(solution)/shard_map/ppermute | solution.py:422
  24.8 20.7 %collective-permute-start.11 = (bf16[2,192,256]{2,1,0:T(8,128)(2,1)S(1)}, bf16[2,192,256]{2,1,0:T(8,128)(2,1)S(1)}, u32[]{:S(2)}, u32[]{:S(2)}) collective-permute-start(bf16[2,192,256]{2,1,0:T(8,128)(2,1)S(1)} %pad_maximum_fusion.1.own_b), channel_id=1, source_target_pairs={{0,32},{1,33},{16,48},{17,49},{32,64},{33,65},{48,80},{49,81},{64,... | collective-permute-start | bytes 589832 | tf_op jit(solution)/shard_map/ppermute | solution.py:422
  33.0 18.2 %collective-permute-start.8 = (bf16[2,192,256]{2,1,0:T(8,128)(2,1)S(1)}, bf16[2,192,256]{2,1,0:T(8,128)(2,1)S(1)}, u32[]{:S(2)}, u32[]{:S(2)}) collective-permute-start(bf16[2,192,256]{2,1,0:T(8,128)(2,1)S(1)} %collective-permute-done.6.left_a), channel_id=1, source_target_pairs={{0,32},{1,33},{16,48},{17,49},{32,64},{33,65},{48,80},{49,81},{64,... | collective-permute-start | bytes 589832 | tf_op jit(solution)/shard_map/ppermute | solution.py:422
  40.9 1.0 copy-start
  45.2 6.9 %collective-permute-start.10 = (bf16[2,192,256]{2,1,0:T(8,128)(2,1)S(1)}, bf16[2,192,256]{2,1,0:T(8,128)(2,1)S(1)}, u32[]{:S(2)}, u32[]{:S(2)}) collective-permute-start(bf16[2,192,256]{2,1,0:T(8,128)(2,1)S(1)} %collective-permute-done.9.right_b), channel_id=1, source_target_pairs={{0,96},{1,97},{16,112},{17,113},{32,0},{33,1},{48,16},{49,17},{64,... | collective-permute-start | bytes 589832 | tf_op jit(solution)/shard_map/ppermute | solution.py:422
  57.9 12.4 %collective-permute-start.12 = (bf16[2,192,256]{2,1,0:T(8,128)(2,1)S(1)}, bf16[2,192,256]{2,1,0:T(8,128)(2,1)S(1)}, u32[]{:S(2)}, u32[]{:S(2)}) collective-permute-start(bf16[2,192,256]{2,1,0:T(8,128)(2,1)S(1)} %get-tuple-element.107), channel_id=1, source_target_pairs={{0,32},{1,33},{16,48},{17,49},{32,64},{33,65},{48,80},{49,81},{64,... | collective-permute-start | bytes 589832 | tf_op jit(solution)/shard_map/ppermute | solution.py:422
  59.4 10.9 %collective-permute-start.13 = (bf16[2,192,256]{2,1,0:T(8,128)(2,1)S(1)}, bf16[2,192,256]{2,1,0:T(8,128)(2,1)S(1)}, u32[]{:S(2)}, u32[]{:S(2)}) collective-permute-start(bf16[2,192,256]{2,1,0:T(8,128)(2,1)S(1)} %get-tuple-element.108), channel_id=1, source_target_pairs={{0,96},{1,97},{16,112},{17,113},{32,0},{33,1},{48,16},{49,17},{64,... | collective-permute-start | bytes 589832 | tf_op jit(solution)/shard_map/ppermute | solution.py:422
  70.4 19.3 %collective-permute-start.14 = (bf16[4,192,256]{2,1,0:T(8,128)(2,1)S(1)}, bf16[4,192,256]{2,1,0:T(8,128)(2,1)S(1)}, u32[]{:S(2)}, u32[]{:S(2)}) collective-permute-start(bf16[4,192,256]{2,1,0:T(8,128)(2,1)S(1)} %get-tuple-element.109), channel_id=1, source_target_pairs={{0,96},{1,97},{16,112},{17,113},{32,0},{33,1},{48,16},{49,17},{64,... | collective-permute-start | bytes 1179656 | tf_op jit(solution)/shard_map/ppermute | solution.py:422
  73.5 16.2 %collective-permute-start.15 = (bf16[4,192,256]{2,1,0:T(8,128)(2,1)S(1)}, bf16[4,192,256]{2,1,0:T(8,128)(2,1)S(1)}, u32[]{:S(2)}, u32[]{:S(2)}) collective-permute-start(bf16[4,192,256]{2,1,0:T(8,128)(2,1)S(1)} %get-tuple-element.110), channel_id=1, source_target_pairs={{0,32},{1,33},{16,48},{17,49},{32,64},{33,65},{48,80},{49,81},{64,... | collective-permute-start | bytes 1179656 | tf_op jit(solution)/shard_map/ppermute | solution.py:422
  77.9 20.7 %collective-permute-start.19 = (bf16[128,1024]{1,0:T(8,128)(2,1)S(1)}, bf16[128,1024]{1,0:T(8,128)(2,1)S(1)}, u32[]{:S(2)}, u32[]{:S(2)}) collective-permute-start(bf16[128,1024]{1,0:T(8,128)(2,1)S(1)} %get-tuple-element.118), channel_id=1, source_target_pairs={{0,144},{1,241},{16,128},{17,161},{32,176},{33,145},{48,160},{49,1... | collective-permute-start | bytes 786440 | tf_op jit(solution)/shard_map/ppermute | solution.py:422
  85.7 14.6 %collective-permute-start.20 = (bf16[128,1024]{1,0:T(8,128)(2,1)S(1)}, bf16[128,1024]{1,0:T(8,128)(2,1)S(1)}, u32[]{:S(2)}, u32[]{:S(2)}) collective-permute-start(bf16[128,1024]{1,0:T(8,128)(2,1)S(1)} %get-tuple-element.119), channel_id=1, source_target_pairs={{0,128},{1,129},{16,144},{17,145},{32,160},{33,161},{48,176},{49,1... | collective-permute-start | bytes 786440 | tf_op jit(solution)/shard_map/ppermute | solution.py:422
  89.8 14.1 %collective-permute-start.21 = (bf16[128,1024]{1,0:T(8,128)(2,1)S(1)}, bf16[128,1024]{1,0:T(8,128)(2,1)S(1)}, u32[]{:S(2)}, u32[]{:S(2)}) collective-permute-start(bf16[128,1024]{1,0:T(8,128)(2,1)S(1)} %get-tuple-element.120), channel_id=1, source_target_pairs={{0,16},{1,113},{16,0},{17,33},{32,48},{33,17},{48,32},{49,65},{64,... | collective-permute-start | bytes 786440 | tf_op jit(solution)/shard_map/ppermute | solution.py:422
  94.4 8.1 %collective-permute-start.16 = (bf16[192,256]{1,0:T(8,128)(2,1)S(1)}, bf16[192,256]{1,0:T(8,128)(2,1)S(1)}, u32[]{:S(2)}, u32[]{:S(2)}) collective-permute-start(bf16[192,256]{1,0:T(8,128)(2,1)S(1)} %get-tuple-element.114), channel_id=1, source_target_pairs={{0,144},{1,241},{16,128},{17,161},{32,176},{33,145},{48,160},{49,1... | collective-permute-start | bytes 294920 | tf_op jit(solution)/shard_map/ppermute | solution.py:422
  97.3 6.5 %collective-permute-start.17 = (bf16[192,256]{1,0:T(8,128)(2,1)S(1)}, bf16[192,256]{1,0:T(8,128)(2,1)S(1)}, u32[]{:S(2)}, u32[]{:S(2)}) collective-permute-start(bf16[192,256]{1,0:T(8,128)(2,1)S(1)} %get-tuple-element.115), channel_id=1, source_target_pairs={{0,128},{1,129},{16,144},{17,145},{32,160},{33,161},{48,176},{49,1... | collective-permute-start | bytes 294920 | tf_op jit(solution)/shard_map/ppermute | solution.py:422
  98.6 5.2 %collective-permute-start.18 = (bf16[192,256]{1,0:T(8,128)(2,1)S(1)}, bf16[192,256]{1,0:T(8,128)(2,1)S(1)}, u32[]{:S(2)}, u32[]{:S(2)}) collective-permute-start(bf16[192,256]{1,0:T(8,128)(2,1)S(1)} %get-tuple-element.116), channel_id=1, source_target_pairs={{0,16},{1,113},{16,0},{17,33},{32,48},{33,17},{48,32},{49,65},{64,... | collective-permute-start | bytes 294920 | tf_op jit(solution)/shard_map/ppermute | solution.py:422
  104.4 3.3 %collective-permute-start.22 = (bf16[64,512]{1,0:T(8,128)(2,1)S(1)}, bf16[64,512]{1,0:T(8,128)(2,1)S(1)}, u32[]{:S(2)}, u32[]{:S(2)}) collective-permute-start(bf16[64,512]{1,0:T(8,128)(2,1)S(1)} %get-tuple-element.126), channel_id=1, source_target_pairs={{0,1},{1,0},{2,3},{3,2},{4,5},{5,4},{6,7},{7,6},{8,9},{9,8},{10,11... | collective-permute-start | bytes 196616 | tf_op jit(solution)/shard_map/ppermute | solution.py:408
  107.8 4.3 %collective-permute-start.23 = (bf16[64,512]{1,0:T(8,128)(2,1)S(1)}, bf16[64,512]{1,0:T(8,128)(2,1)S(1)}, u32[]{:S(2)}, u32[]{:S(2)}) collective-permute-start(bf16[64,512]{1,0:T(8,128)(2,1)S(1)} %add_convert_fusion.2), channel_id=1, source_target_pairs={{0,2},{2,0},{1,3},{3,1},{4,6},{6,4},{5,7},{7,5},{8,10},{10,8},{9,1... | collective-permute-start | bytes 196616 | tf_op jit(solution)/shard_map/ppermute | solution.py:408
  112.1 4.4 %collective-permute-start.26 = (bf16[64,512]{1,0:T(8,128)(2,1)S(1)}, bf16[64,512]{1,0:T(8,128)(2,1)S(1)}, u32[]{:S(2)}, u32[]{:S(2)}) collective-permute-start(bf16[64,512]{1,0:T(8,128)(2,1)S(1)} %add_convert_fusion.1), channel_id=1, source_target_pairs={{0,12},{4,0},{8,4},{12,8},{1,13},{5,1},{9,5},{13,9},{2,14},{6,2},{... | collective-permute-start | bytes 196616 | tf_op jit(solution)/shard_map/ppermute | solution.py:413
  114.9 5.0 %collective-permute-start.25 = (bf16[64,512]{1,0:T(8,128)(2,1)S(1)}, bf16[64,512]{1,0:T(8,128)(2,1)S(1)}, u32[]{:S(2)}, u32[]{:S(2)}) collective-permute-start(bf16[64,512]{1,0:T(8,128)(2,1)S(1)} %add_convert_fusion.1), channel_id=1, source_target_pairs={{0,4},{4,8},{8,12},{12,0},{1,5},{5,9},{9,13},{13,1},{2,6},{6,10},{... | collective-permute-start | bytes 196616 | tf_op jit(solution)/shard_map/ppermute | solution.py:413
  114.9 5.0 %collective-permute-start.24 = (bf16[64,512]{1,0:T(8,128)(2,1)S(1)}, bf16[64,512]{1,0:T(8,128)(2,1)S(1)}, u32[]{:S(2)}, u32[]{:S(2)}) collective-permute-start(bf16[64,512]{1,0:T(8,128)(2,1)S(1)} %add_convert_fusion.1), channel_id=1, source_target_pairs={{0,8},{4,12},{8,0},{12,4},{1,9},{5,13},{9,1},{13,5},{2,10},{6,14},... | collective-permute-start | bytes 196616 | tf_op jit(solution)/shard_map/ppermute | solution.py:413
  120.0 3.9 %collective-permute-start.27 = (bf16[64,512]{1,0:T(8,128)(2,1)S(1)}, bf16[64,512]{1,0:T(8,128)(2,1)S(1)}, u32[]{:S(2)}, u32[]{:S(2)}) collective-permute-start(bf16[64,512]{1,0:T(8,128)(2,1)S(1)} %add_convert_fusion), channel_id=1, source_target_pairs={{0,1},{1,0},{2,3},{3,2},{4,5},{5,4},{6,7},{7,6},{8,9},{9,8},{10,11... | collective-permute-start | bytes 196616 | tf_op jit(solution)/shard_map/ppermute | solution.py:408

commit v11 on v10

--- a/solution.py
+++ b/solution.py
@@ -472,6 +472,7 @@
     own_b = jnp.stack(kv[2:])
     own_b, left_a, right_a = lax.optimization_barrier((own_b, left_a, right_a))
     left_b, right_b = quad_turn(own_b, 1), quad_turn(own_b, -1)
+    right_b, qd[3] = lax.optimization_barrier((right_b, qd[3]))
     far_a, far_b = quad_turn(left_a, 1), quad_turn(right_b, -1)
 
     tiles = (2, HEAD_DIM, LANES)

time: 125 us -> 123 us (0.984)
  starting transfers between devices: 56.1 us -> 51.5 us
  waiting for transfers between devices: 30.1 us -> 33.1 us
    ppermute x22, starting transfers between devices: 44.9 us -> 40.4 us  [local_permute(): return lax.ppermute(x, LOCAL, pairs)]
    ppermute x22, waiting for transfers between devices: 24.9 us -> 27.9 us  [local_permute(): return lax.ppermute(x, LOCAL, pairs)]
  transfers between devices with their start and end apart: 28 -> 28, of which waited for: 12 -> 11; matrix products, arithmetic and copies ran while one was open for 1% -> 1% of each run, Pallas kernels for 20% -> 21%
where the time goes in v11:
time: 123 us
  starting transfers between devices  51.5 us (42%)
  Pallas kernels  33.4 us (27%)
  waiting for transfers between devices  33.1 us (27%)
  between operations  2.13 us (2%)
  other arithmetic  1.67 us (1%)
    ppermute x22, starting transfers between devices, local_permute(): return lax.ppermute(x, LOCAL, pairs)  40.4 us
    pallas_call x12, Pallas kernels, call(): pl.pallas_call(kernel, out_shape=tuple(outs), in_specs=[SMEM] * len(scala...  33.4 us
    ppermute x22, waiting for transfers between devices, local_permute(): return lax.ppermute(x, LOCAL, pairs)  27.9 us
    ppermute x3, starting transfers between devices, swap(): return lax.ppermute(x, axis, [(0, 1), (1, 0)])  6.55 us
    ppermute x3, starting transfers between devices, turn(): return lax.ppermute(x, axis, [(i, (i + step) % size) for i in range(size)])  4.47 us
    ppermute x3, waiting for transfers between devices, turn(): return lax.ppermute(x, axis, [(i, (i + step) % size) for i in range(size)])  3.38 us
  transfers between devices with their start and end apart: 28, of which 11 were waited for; matrix products, arithmetic and copies ran while one was open for 1% of the time, Pallas kernels for 21%

profile of v11, /device:TPU:1, one launch (start us, length us, event | category | flops | bytes accessed | tf_op | source)
XLA Modules:
  0.0 122.8 jit_solution(10422802997488822568)
XLA Ops:
  0.6 1.8 %shard_map.127 = (bf16[192,256]{1,0:T(8,128)(2,1)}, bf16[192,256]{1,0:T(8,128)(2,1)}, bf16[192,256]{1,0:T(8,128)(2,1)}, bf16[192,256]{1,0:T(8,128)(2,1)}) custom-call(s32[1]{0:T(128)} %bitcast.info, bf16[128,512]{1,0:T(8,128)(2,1)} %bitcast.17, bf16[128,512]{1,0:T(8,128)(2,1)} %bitcast.18, bf16[64,512]{1,0:T(8,128)(2,1)} %kp.1, bf16[64,512]{1,0:T(8,128)(2,1)} %vp.1), custom_call_target="tpu_custom_call" | custom-call | bytes 1000000 | tf_op jit(solution)/shard_map/pallas_call | solution.py:392
  2.5 6.5 %collective-permute-start = (bf16[192,256]{1,0:T(8,128)(2,1)}, bf16[192,256]{1,0:T(8,128)(2,1)S(1)}, u32[]{:S(2)}, u32[]{:S(2)}) collective-permute-start(bf16[192,256]{1,0:T(8,128)(2,1)} %get-tuple-element.76), channel_id=1, source_target_pairs={{0,16},{1,113},{16,0},{17,33},{32,48},{33,17},{48,32},{49,65},{64,... | collective-permute-start | bytes 294920 | tf_op jit(solution)/shard_map/ppermute | solution.py:422
  9.0 2.7 %collective-permute-start.3 = (bf16[192,256]{1,0:T(8,128)(2,1)}, bf16[192,256]{1,0:T(8,128)(2,1)S(1)}, u32[]{:S(2)}, u32[]{:S(2)}) collective-permute-start(bf16[192,256]{1,0:T(8,128)(2,1)} %get-tuple-element.81), channel_id=1, source_target_pairs={{0,128},{1,129},{16,144},{17,145},{32,160},{33,161},{48,176},{49,1... | collective-permute-start | bytes 294920 | tf_op jit(solution)/shard_map/ppermute | solution.py:422
  12.7 1.9 %collective-permute-start.6 = (bf16[2,192,256]{2,1,0:T(8,128)(2,1)S(1)}, bf16[2,192,256]{2,1,0:T(8,128)(2,1)S(1)}, u32[]{:S(2)}, u32[]{:S(2)}) collective-permute-start(bf16[2,192,256]{2,1,0:T(8,128)(2,1)S(1)} %pad_maximum_fusion.own_a), channel_id=1, source_target_pairs={{0,96},{1,97},{16,112},{17,113},{32,0},{33,1},{48,16},{49,17},{64,... | collective-permute-start | bytes 589832 | tf_op jit(solution)/shard_map/ppermute | solution.py:422
  15.1 2.2 %shard_map.128 = (bf16[128,1024]{1,0:T(8,128)(2,1)}, bf16[128,1024]{1,0:T(8,128)(2,1)}, bf16[128,1024]{1,0:T(8,128)(2,1)}, bf16[128,1024]{1,0:T(8,128)(2,1)}) custom-call(s32[1]{0:T(128)} %bitcast.info, bf16[128,2048]{1,0:T(8,128)(2,1)} %bitcast.15, bf16[128,2048]{1,0:T(8,128)(2,1)} %bitcast.16), custom_call_target="tpu_custom_call" | custom-call | bytes 1000000 | tf_op jit(solution)/shard_map/pallas_call | solution.py:392
  17.4 3.9 %collective-permute-start.1 = (bf16[128,1024]{1,0:T(8,128)(2,1)}, bf16[128,1024]{1,0:T(8,128)(2,1)S(1)}, u32[]{:S(2)}, u32[]{:S(2)}) collective-permute-start(bf16[128,1024]{1,0:T(8,128)(2,1)} %get-tuple-element.79), channel_id=1, source_target_pairs={{0,16},{1,113},{16,0},{17,33},{32,48},{33,17},{48,32},{49,65},{64,... | collective-permute-start | bytes 786440 | tf_op jit(solution)/shard_map/ppermute | solution.py:422
  21.2 2.7 %collective-permute-start.2 = (bf16[128,1024]{1,0:T(8,128)(2,1)}, bf16[128,1024]{1,0:T(8,128)(2,1)S(1)}, u32[]{:S(2)}, u32[]{:S(2)}) collective-permute-start(bf16[128,1024]{1,0:T(8,128)(2,1)} %get-tuple-element.80), channel_id=1, source_target_pairs={{0,128},{1,129},{16,144},{17,145},{32,160},{33,161},{48,176},{49,1... | collective-permute-start | bytes 786440 | tf_op jit(solution)/shard_map/ppermute | solution.py:422
  24.8 1.8 %collective-permute-start.11 = (bf16[2,192,256]{2,1,0:T(8,128)(2,1)S(1)}, bf16[2,192,256]{2,1,0:T(8,128)(2,1)S(1)}, u32[]{:S(2)}, u32[]{:S(2)}) collective-permute-start(bf16[2,192,256]{2,1,0:T(8,128)(2,1)S(1)} %pad_maximum_fusion.1.own_b), channel_id=1, source_target_pairs={{0,32},{1,33},{16,48},{17,49},{32,64},{33,65},{48,80},{49,81},{64,... | collective-permute-start | bytes 589832 | tf_op jit(solution)/shard_map/ppermute | solution.py:422
  28.0 11.5 %collective-permute-done.8.qd3 = bf16[128,1024]{1,0:T(8,128)(2,1)S(1)} collective-permute-done((bf16[128,1024]{1,0:T(8,128)(2,1)}, bf16[128,1024]{1,0:T(8,128)(2,1)S(1)}, u32[]{:S(2)}, u32[]{:S(2)}) %collective-permute-start.8) | collective-permute-done | bytes 262176 | tf_op jit(solution)/shard_map/ppermute | solution.py:422
  39.5 3.6 %collective-permute-start.10 = (bf16[2,192,256]{2,1,0:T(8,128)(2,1)S(1)}, bf16[2,192,256]{2,1,0:T(8,128)(2,1)S(1)}, u32[]{:S(2)}, u32[]{:S(2)}) collective-permute-start(bf16[2,192,256]{2,1,0:T(8,128)(2,1)S(1)} %collective-permute-done.7.right_b), channel_id=1, source_target_pairs={{0,96},{1,97},{16,112},{17,113},{32,0},{33,1},{48,16},{49,17},{64,... | collective-permute-start | bytes 589832 | tf_op jit(solution)/shard_map/ppermute | solution.py:422
  44.0 3.4 %shard_map.129 = (bf16[2,128,1024]{2,1,0:T(8,128)(2,1)S(1)}, bf16[2,1024,128]{2,1,0:T(8,128)(2,1)S(1)}, bf16[2,128,1024]{2,1,0:T(8,128)(2,1)S(1)}, bf16[1,1280,1...) custom-call(s32[5]{0:T(128)S(1)} %stack.33.info, ...), custom_call_target="tpu_custom_call" | custom-call | flops 1342177280 | bytes 1000000 | tf_op jit(solution)/shard_map/pallas_call | solution.py:392
  47.4 5.7 %shard_map.130 = (bf16[2,1280,1024]{2,1,0:T(8,128)(2,1)S(1)}, f32[2,1,1024]{2,1,0:T(1,128)S(1)}, f32[2,1,1024]{2,1,0:T(1,128)S(1)}, f32[2,128,1024]{2,1,0:T(8,128)S(1)}) custom-call(s32[5]{0:T(128)S(1)} %stack.33.info, bf16[2,128,1024]{2,1,0:T(8,128)(2,1)S(1)} %get-tuple-element.88.qt, bf16[2,192,256]{2,1,0:T(8,128)(2,1)S(1)} %collective-permute-done.5.left_a, ...), custom_call_target="tpu_custom_call" | custom-call | flops 2684354560 | bytes 1000000 | tf_op jit(solution)/shard_map/pallas_call | solution.py:392
  53.1 5.7 %shard_map.131 = (f32[2,1,1024]{2,1,0:T(1,128)S(1)}, bf16[2,128,1024]{2,1,0:T(8,128)(2,1)S(1)}, bf16[2,1024,128]{2,1,0:T(8,128)(2,1)S(1)}, f32[2,1,1024]{2,1,0:T...) custom-call(s32[5]{0:T(128)S(1)} %stack.33.info, ...), custom_call_target="tpu_custom_call" | custom-call | flops 4026531840 | bytes 1000000 | tf_op jit(solution)/shard_map/pallas_call | solution.py:392
  59.2 3.3 %collective-permute-start.13 = (bf16[2,192,256]{2,1,0:T(8,128)(2,1)S(1)}, bf16[2,192,256]{2,1,0:T(8,128)(2,1)S(1)}, u32[]{:S(2)}, u32[]{:S(2)}) collective-permute-start(bf16[2,192,256]{2,1,0:T(8,128)(2,1)S(1)} %get-tuple-element.112), channel_id=1, source_target_pairs={{0,96},{1,97},{16,112},{17,113},{32,0},{33,1},{48,16},{49,17},{64,... | collective-permute-start | bytes 589832 | tf_op jit(solution)/shard_map/ppermute | solution.py:422
  62.5 6.4 %shard_map.132 = (f32[2,128,1024]{2,1,0:T(8,128)S(1)}, bf16[4,192,256]{2,1,0:T(8,128)(2,1)S(1)}, bf16[4,192,256]{2,1,0:T(8,128)(2,1)S(1)}) custom-call(s32[5]{0:T(128)S(1)} %stack.33.info, bf16[2,1024,128]{2,1,0:T(8,128)(2,1)S(1)} %get-tuple-element.87.q, bf16[2,128,1024]{2,1,0:T(8,128)(2,1)S(1)} %get-tuple-element.99.uplt, ...), custom_call_target="tpu_custom_call" | custom-call | flops 5368709120 | bytes 1000000 | tf_op jit(solution)/shard_map/pallas_call | solution.py:392
  69.0 1.0 collective-permute-done.12.far_a
  70.5 2.7 %collective-permute-start.14 = (bf16[4,192,256]{2,1,0:T(8,128)(2,1)S(1)}, bf16[4,192,256]{2,1,0:T(8,128)(2,1)S(1)}, u32[]{:S(2)}, u32[]{:S(2)}) collective-permute-start(bf16[4,192,256]{2,1,0:T(8,128)(2,1)S(1)} %get-tuple-element.113), channel_id=1, source_target_pairs={{0,96},{1,97},{16,112},{17,113},{32,0},{33,1},{48,16},{49,17},{64,... | collective-permute-start | bytes 1179656 | tf_op jit(solution)/shard_map/ppermute | solution.py:422
  73.3 4.4 %shard_map.133 = (bf16[4,192,256]{2,1,0:T(8,128)(2,1)S(1)}, bf16[128,1024]{1,0:T(8,128)(2,1)S(1)}, bf16[128,1024]{1,0:T(8,128)(2,1)S(1)}, bf16[128,1024]{1,0:T(8,128)(2,1)S(1)}, bf16[128,1024]{1,0:T(8,128)(2,1)S(1)}) custom-call(s32[5]{0:T(128)S(1)} %stack.33.info, bf16[2,1024,128]{2,1,0:T(8,128)(2,1)S(1)} %get-tuple-element.87.q, ...), custom_call_target="tpu_custom_call" | custom-call | flops 2684354560 | bytes 1000000 | tf_op jit(solution)/shard_map/pallas_call | solution.py:392
  77.7 3.6 %collective-permute-start.19 = (bf16[128,1024]{1,0:T(8,128)(2,1)S(1)}, bf16[128,1024]{1,0:T(8,128)(2,1)S(1)}, u32[]{:S(2)}, u32[]{:S(2)}) collective-permute-start(bf16[128,1024]{1,0:T(8,128)(2,1)S(1)} %get-tuple-element.122), channel_id=1, source_target_pairs={{0,144},{1,241},{16,128},{17,161},{32,176},{33,145},{48,160},{49,1... | collective-permute-start | bytes 786440 | tf_op jit(solution)/shard_map/ppermute | solution.py:422
  81.3 7.8 %collective-permute-done.14.left = bf16[4,192,256]{2,1,0:T(8,128)(2,1)S(1)} collective-permute-done((bf16[4,192,256]{2,1,0:T(8,128)(2,1)S(1)}, bf16[4,192,256]{2,1,0:T(8,128)(2,1)S(1)}, u32[]{:S(2)}, u32[]{:S(2)}) %collective-permute-start.14) | collective-permute-done | bytes 393248 | tf_op jit(solution)/shard_map/ppermute | solution.py:422
  89.3 4.7 %collective-permute-start.16 = (bf16[192,256]{1,0:T(8,128)(2,1)S(1)}, bf16[192,256]{1,0:T(8,128)(2,1)S(1)}, u32[]{:S(2)}, u32[]{:S(2)}) collective-permute-start(bf16[192,256]{1,0:T(8,128)(2,1)S(1)} %get-tuple-element.118), channel_id=1, source_target_pairs={{0,144},{1,241},{16,128},{17,161},{32,176},{33,145},{48,160},{49,1... | collective-permute-start | bytes 294920 | tf_op jit(solution)/shard_map/ppermute | solution.py:422
  94.8 2.7 %collective-permute-done.19.od3 = bf16[128,1024]{1,0:T(8,128)(2,1)S(1)} collective-permute-done((bf16[128,1024]{1,0:T(8,128)(2,1)S(1)}, bf16[128,1024]{1,0:T(8,128)(2,1)S(1)}, u32[]{:S(2)}, u32[]{:S(2)}) %collective-permute-start.19) | collective-permute-done | bytes 262176 | tf_op jit(solution)/shard_map/ppermute | solution.py:422
  98.0 3.3 %collective-permute-done.16.g3 = bf16[192,256]{1,0:T(8,128)(2,1)S(1)} collective-permute-done((bf16[192,256]{1,0:T(8,128)(2,1)S(1)}, bf16[192,256]{1,0:T(8,128)(2,1)S(1)}, u32[]{:S(2)}, u32[]{:S(2)}) %collective-permute-start.16) | collective-permute-done | bytes 98336 | tf_op jit(solution)/shard_map/ppermute | solution.py:422
  101.3 1.1 collective-permute-done.18.g1
  103.0 2.5 %collective-permute-start.22 = (bf16[64,512]{1,0:T(8,128)(2,1)S(1)}, bf16[64,512]{1,0:T(8,128)(2,1)S(1)}, u32[]{:S(2)}, u32[]{:S(2)}) collective-permute-start(bf16[64,512]{1,0:T(8,128)(2,1)S(1)} %get-tuple-element.130), channel_id=1, source_target_pairs={{0,1},{1,0},{2,3},{3,2},{4,5},{5,4},{6,7},{7,6},{8,9},{9,8},{10,11... | collective-permute-start | bytes 196616 | tf_op jit(solution)/shard_map/ppermute | solution.py:408
  106.4 1.2 collective-permute-start.23
  107.6 1.3 %shard_map.137 = (bf16[128,512]{1,0:T(8,128)(2,1)}, bf16[128,512]{1,0:T(8,128)(2,1)}) custom-call(s32[5]{0:T(128)S(1)} %stack.33.info, bf16[192,256]{1,0:T(8,128)(2,1)S(1)} %get-tuple-element.125.g0, bf16[192,256]{1,0:T(8,128)(2,1)S(1)} %collective-permute-done.18.g1, bf16[192,256]{1,0:T(8,128)(2,1)S(1)} %collective-permute-done.17.g2, ...), custom_call_target="tpu_custom_call" | custom-call | bytes 1000000 | tf_op jit(solution)/shard_map/pallas_call | solution.py:392
  108.9 1.6 %shard_map.138 = (bf16[128,2048]{1,0:T(8,128)(2,1)}, bf16[128,2048]{1,0:T(8,128)(2,1)}) custom-call(s32[5]{0:T(128)S(1)} %stack.33.info, bf16[128,1024]{1,0:T(8,128)(2,1)S(1)} %get-tuple-element.133.od0, bf16[128,1024]{1,0:T(8,128)(2,1)S(1)} %collective-permute-done.21.od1, bf16[128,1024]{1,0:T(8,128)(2,1)S(1)} %collective-permute-done.20.od2, ...), custom_call_target="tpu_custom_call" | custom-call | bytes 1000000 | tf_op jit(solution)/shard_map/pallas_call | solution.py:392
  110.5 2.8 %collective-permute-start.26 = (bf16[64,512]{1,0:T(8,128)(2,1)S(1)}, bf16[64,512]{1,0:T(8,128)(2,1)S(1)}, u32[]{:S(2)}, u32[]{:S(2)}) collective-permute-start(bf16[64,512]{1,0:T(8,128)(2,1)S(1)} %add_convert_fusion.1), channel_id=1, source_target_pairs={{0,12},{4,0},{8,4},{12,8},{1,13},{5,1},{9,5},{13,9},{2,14},{6,2},{... | collective-permute-start | bytes 196616 | tf_op jit(solution)/shard_map/ppermute | solution.py:413
  113.3 1.6 %collective-permute-start.24 = (bf16[64,512]{1,0:T(8,128)(2,1)S(1)}, bf16[64,512]{1,0:T(8,128)(2,1)S(1)}, u32[]{:S(2)}, u32[]{:S(2)}) collective-permute-start(bf16[64,512]{1,0:T(8,128)(2,1)S(1)} %add_convert_fusion.1), channel_id=1, source_target_pairs={{0,8},{4,12},{8,0},{12,4},{1,9},{5,13},{9,1},{13,5},{2,10},{6,14},... | collective-permute-start | bytes 196616 | tf_op jit(solution)/shard_map/ppermute | solution.py:413
  115.0 3.4 %collective-permute-done.25 = bf16[64,512]{1,0:T(8,128)(2,1)S(1)} collective-permute-done((bf16[64,512]{1,0:T(8,128)(2,1)S(1)}, bf16[64,512]{1,0:T(8,128)(2,1)S(1)}, u32[]{:S(2)}, u32[]{:S(2)}) %collective-permute-start.25) | collective-permute-done | bytes 65568 | tf_op jit(solution)/shard_map/ppermute | solution.py:413
  118.4 2.9 %collective-permute-start.27 = (bf16[64,512]{1,0:T(8,128)(2,1)S(1)}, bf16[64,512]{1,0:T(8,128)(2,1)S(1)}, u32[]{:S(2)}, u32[]{:S(2)}) collective-permute-start(bf16[64,512]{1,0:T(8,128)(2,1)S(1)} %add_convert_fusion), channel_id=1, source_target_pairs={{0,1},{1,0},{2,3},{3,2},{4,5},{5,4},{6,7},{7,6},{8,9},{9,8},{10,11... | collective-permute-start | bytes 196616 | tf_op jit(solution)/shard_map/ppermute | solution.py:408
  (45 shorter events, 9.0 us)
Async XLA Ops:
  2.5 9.3 %collective-permute-start = (bf16[192,256]{1,0:T(8,128)(2,1)}, bf16[192,256]{1,0:T(8,128)(2,1)S(1)}, u32[]{:S(2)}, u32[]{:S(2)}) collective-permute-start(bf16[192,256]{1,0:T(8,128)(2,1)} %get-tuple-element.76), channel_id=1, source_target_pairs={{0,16},{1,113},{16,0},{17,33},{32,48},{33,17},{48,32},{49,65},{64,... | collective-permute-start | bytes 294920 | tf_op jit(solution)/shard_map/ppermute | solution.py:422
  9.0 12.3 %collective-permute-start.3 = (bf16[192,256]{1,0:T(8,128)(2,1)}, bf16[192,256]{1,0:T(8,128)(2,1)S(1)}, u32[]{:S(2)}, u32[]{:S(2)}) collective-permute-start(bf16[192,256]{1,0:T(8,128)(2,1)} %get-tuple-element.81), channel_id=1, source_target_pairs={{0,128},{1,129},{16,144},{17,145},{32,160},{33,161},{48,176},{49,1... | collective-permute-start | bytes 294920 | tf_op jit(solution)/shard_map/ppermute | solution.py:422
  11.7 12.3 %collective-permute-start.4 = (bf16[192,256]{1,0:T(8,128)(2,1)}, bf16[192,256]{1,0:T(8,128)(2,1)S(1)}, u32[]{:S(2)}, u32[]{:S(2)}) collective-permute-start(bf16[192,256]{1,0:T(8,128)(2,1)} %get-tuple-element.82), channel_id=1, source_target_pairs={{0,144},{1,241},{16,128},{17,161},{32,176},{33,145},{48,160},{49,1... | collective-permute-start | bytes 294920 | tf_op jit(solution)/shard_map/ppermute | solution.py:422
  12.7 11.5 %collective-permute-start.6 = (bf16[2,192,256]{2,1,0:T(8,128)(2,1)S(1)}, bf16[2,192,256]{2,1,0:T(8,128)(2,1)S(1)}, u32[]{:S(2)}, u32[]{:S(2)}) collective-permute-start(bf16[2,192,256]{2,1,0:T(8,128)(2,1)S(1)} %pad_maximum_fusion.own_a), channel_id=1, source_target_pairs={{0,96},{1,97},{16,112},{17,113},{32,0},{33,1},{48,16},{49,17},{64,... | collective-permute-start | bytes 589832 | tf_op jit(solution)/shard_map/ppermute | solution.py:422
  14.6 9.6 %collective-permute-start.5 = (bf16[2,192,256]{2,1,0:T(8,128)(2,1)S(1)}, bf16[2,192,256]{2,1,0:T(8,128)(2,1)S(1)}, u32[]{:S(2)}, u32[]{:S(2)}) collective-permute-start(bf16[2,192,256]{2,1,0:T(8,128)(2,1)S(1)} %pad_maximum_fusion.own_a), channel_id=1, source_target_pairs={{0,32},{1,33},{16,48},{17,49},{32,64},{33,65},{48,80},{49,81},{64,... | collective-permute-start | bytes 589832 | tf_op jit(solution)/shard_map/ppermute | solution.py:422
  17.4 25.7 %collective-permute-start.1 = (bf16[128,1024]{1,0:T(8,128)(2,1)}, bf16[128,1024]{1,0:T(8,128)(2,1)S(1)}, u32[]{:S(2)}, u32[]{:S(2)}) collective-permute-start(bf16[128,1024]{1,0:T(8,128)(2,1)} %get-tuple-element.79), channel_id=1, source_target_pairs={{0,16},{1,113},{16,0},{17,33},{32,48},{33,17},{48,32},{49,65},{64,... | collective-permute-start | bytes 786440 | tf_op jit(solution)/shard_map/ppermute | solution.py:422
  21.2 21.8 %collective-permute-start.2 = (bf16[128,1024]{1,0:T(8,128)(2,1)}, bf16[128,1024]{1,0:T(8,128)(2,1)S(1)}, u32[]{:S(2)}, u32[]{:S(2)}) collective-permute-start(bf16[128,1024]{1,0:T(8,128)(2,1)} %get-tuple-element.80), channel_id=1, source_target_pairs={{0,128},{1,129},{16,144},{17,145},{32,160},{33,161},{48,176},{49,1... | collective-permute-start | bytes 786440 | tf_op jit(solution)/shard_map/ppermute | solution.py:422
  24.0 15.5 %collective-permute-start.8 = (bf16[128,1024]{1,0:T(8,128)(2,1)}, bf16[128,1024]{1,0:T(8,128)(2,1)S(1)}, u32[]{:S(2)}, u32[]{:S(2)}) collective-permute-start(bf16[128,1024]{1,0:T(8,128)(2,1)} %get-tuple-element.85), channel_id=1, source_target_pairs={{0,144},{1,241},{16,128},{17,161},{32,176},{33,145},{48,160},{49,1... | collective-permute-start | bytes 786440 | tf_op jit(solution)/shard_map/ppermute | solution.py:422
  24.1 15.3 %collective-permute-start.7 = (bf16[2,192,256]{2,1,0:T(8,128)(2,1)S(1)}, bf16[2,192,256]{2,1,0:T(8,128)(2,1)S(1)}, u32[]{:S(2)}, u32[]{:S(2)}) collective-permute-start(bf16[2,192,256]{2,1,0:T(8,128)(2,1)S(1)} %pad_maximum_fusion.1.own_b), channel_id=1, source_target_pairs={{0,96},{1,97},{16,112},{17,113},{32,0},{33,1},{48,16},{49,17},{64,... | collective-permute-start | bytes 589832 | tf_op jit(solution)/shard_map/ppermute | solution.py:422
  24.8 22.6 %collective-permute-start.11 = (bf16[2,192,256]{2,1,0:T(8,128)(2,1)S(1)}, bf16[2,192,256]{2,1,0:T(8,128)(2,1)S(1)}, u32[]{:S(2)}, u32[]{:S(2)}) collective-permute-start(bf16[2,192,256]{2,1,0:T(8,128)(2,1)S(1)} %pad_maximum_fusion.1.own_b), channel_id=1, source_target_pairs={{0,32},{1,33},{16,48},{17,49},{32,64},{33,65},{48,80},{49,81},{64,... | collective-permute-start | bytes 589832 | tf_op jit(solution)/shard_map/ppermute | solution.py:422
  39.5 13.6 %collective-permute-start.9 = (bf16[2,192,256]{2,1,0:T(8,128)(2,1)S(1)}, bf16[2,192,256]{2,1,0:T(8,128)(2,1)S(1)}, u32[]{:S(2)}, u32[]{:S(2)}) collective-permute-start(bf16[2,192,256]{2,1,0:T(8,128)(2,1)S(1)} %collective-permute-done.5.left_a), channel_id=1, source_target_pairs={{0,32},{1,33},{16,48},{17,49},{32,64},{33,65},{48,80},{49,81},{64,... | collective-permute-start | bytes 589832 | tf_op jit(solution)/shard_map/ppermute | solution.py:422
  39.5 13.7 %collective-permute-start.10 = (bf16[2,192,256]{2,1,0:T(8,128)(2,1)S(1)}, bf16[2,192,256]{2,1,0:T(8,128)(2,1)S(1)}, u32[]{:S(2)}, u32[]{:S(2)}) collective-permute-start(bf16[2,192,256]{2,1,0:T(8,128)(2,1)S(1)} %collective-permute-done.7.right_b), channel_id=1, source_target_pairs={{0,96},{1,97},{16,112},{17,113},{32,0},{33,1},{48,16},{49,17},{64,... | collective-permute-start | bytes 589832 | tf_op jit(solution)/shard_map/ppermute | solution.py:422
  43.0 1.0 copy-start
  58.9 11.1 %collective-permute-start.12 = (bf16[2,192,256]{2,1,0:T(8,128)(2,1)S(1)}, bf16[2,192,256]{2,1,0:T(8,128)(2,1)S(1)}, u32[]{:S(2)}, u32[]{:S(2)}) collective-permute-start(bf16[2,192,256]{2,1,0:T(8,128)(2,1)S(1)} %get-tuple-element.111), channel_id=1, source_target_pairs={{0,32},{1,33},{16,48},{17,49},{32,64},{33,65},{48,80},{49,81},{64,... | collective-permute-start | bytes 589832 | tf_op jit(solution)/shard_map/ppermute | solution.py:422
  59.2 11.2 %collective-permute-start.13 = (bf16[2,192,256]{2,1,0:T(8,128)(2,1)S(1)}, bf16[2,192,256]{2,1,0:T(8,128)(2,1)S(1)}, u32[]{:S(2)}, u32[]{:S(2)}) collective-permute-start(bf16[2,192,256]{2,1,0:T(8,128)(2,1)S(1)} %get-tuple-element.112), channel_id=1, source_target_pairs={{0,96},{1,97},{16,112},{17,113},{32,0},{33,1},{48,16},{49,17},{64,... | collective-permute-start | bytes 589832 | tf_op jit(solution)/shard_map/ppermute | solution.py:422
  70.5 18.6 %collective-permute-start.14 = (bf16[4,192,256]{2,1,0:T(8,128)(2,1)S(1)}, bf16[4,192,256]{2,1,0:T(8,128)(2,1)S(1)}, u32[]{:S(2)}, u32[]{:S(2)}) collective-permute-start(bf16[4,192,256]{2,1,0:T(8,128)(2,1)S(1)} %get-tuple-element.113), channel_id=1, source_target_pairs={{0,96},{1,97},{16,112},{17,113},{32,0},{33,1},{48,16},{49,17},{64,... | collective-permute-start | bytes 1179656 | tf_op jit(solution)/shard_map/ppermute | solution.py:422
  73.2 16.0 %collective-permute-start.15 = (bf16[4,192,256]{2,1,0:T(8,128)(2,1)S(1)}, bf16[4,192,256]{2,1,0:T(8,128)(2,1)S(1)}, u32[]{:S(2)}, u32[]{:S(2)}) collective-permute-start(bf16[4,192,256]{2,1,0:T(8,128)(2,1)S(1)} %get-tuple-element.114), channel_id=1, source_target_pairs={{0,32},{1,33},{16,48},{17,49},{32,64},{33,65},{48,80},{49,81},{64,... | collective-permute-start | bytes 1179656 | tf_op jit(solution)/shard_map/ppermute | solution.py:422
  77.7 19.7 %collective-permute-start.19 = (bf16[128,1024]{1,0:T(8,128)(2,1)S(1)}, bf16[128,1024]{1,0:T(8,128)(2,1)S(1)}, u32[]{:S(2)}, u32[]{:S(2)}) collective-permute-start(bf16[128,1024]{1,0:T(8,128)(2,1)S(1)} %get-tuple-element.122), channel_id=1, source_target_pairs={{0,144},{1,241},{16,128},{17,161},{32,176},{33,145},{48,160},{49,1... | collective-permute-start | bytes 786440 | tf_op jit(solution)/shard_map/ppermute | solution.py:422
  81.3 16.7 %collective-permute-start.20 = (bf16[128,1024]{1,0:T(8,128)(2,1)S(1)}, bf16[128,1024]{1,0:T(8,128)(2,1)S(1)}, u32[]{:S(2)}, u32[]{:S(2)}) collective-permute-start(bf16[128,1024]{1,0:T(8,128)(2,1)S(1)} %get-tuple-element.123), channel_id=1, source_target_pairs={{0,128},{1,129},{16,144},{17,145},{32,160},{33,161},{48,176},{49,1... | collective-permute-start | bytes 786440 | tf_op jit(solution)/shard_map/ppermute | solution.py:422
  89.2 13.3 %collective-permute-start.21 = (bf16[128,1024]{1,0:T(8,128)(2,1)S(1)}, bf16[128,1024]{1,0:T(8,128)(2,1)S(1)}, u32[]{:S(2)}, u32[]{:S(2)}) collective-permute-start(bf16[128,1024]{1,0:T(8,128)(2,1)S(1)} %get-tuple-element.124), channel_id=1, source_target_pairs={{0,16},{1,113},{16,0},{17,33},{32,48},{33,17},{48,32},{49,65},{64,... | collective-permute-start | bytes 786440 | tf_op jit(solution)/shard_map/ppermute | solution.py:422
  89.3 12.0 %collective-permute-start.16 = (bf16[192,256]{1,0:T(8,128)(2,1)S(1)}, bf16[192,256]{1,0:T(8,128)(2,1)S(1)}, u32[]{:S(2)}, u32[]{:S(2)}) collective-permute-start(bf16[192,256]{1,0:T(8,128)(2,1)S(1)} %get-tuple-element.118), channel_id=1, source_target_pairs={{0,144},{1,241},{16,128},{17,161},{32,176},{33,145},{48,160},{49,1... | collective-permute-start | bytes 294920 | tf_op jit(solution)/shard_map/ppermute | solution.py:422
  94.0 7.3 %collective-permute-start.17 = (bf16[192,256]{1,0:T(8,128)(2,1)S(1)}, bf16[192,256]{1,0:T(8,128)(2,1)S(1)}, u32[]{:S(2)}, u32[]{:S(2)}) collective-permute-start(bf16[192,256]{1,0:T(8,128)(2,1)S(1)} %get-tuple-element.119), channel_id=1, source_target_pairs={{0,128},{1,129},{16,144},{17,145},{32,160},{33,161},{48,176},{49,1... | collective-permute-start | bytes 294920 | tf_op jit(solution)/shard_map/ppermute | solution.py:422
  97.5 5.0 %collective-permute-start.18 = (bf16[192,256]{1,0:T(8,128)(2,1)S(1)}, bf16[192,256]{1,0:T(8,128)(2,1)S(1)}, u32[]{:S(2)}, u32[]{:S(2)}) collective-permute-start(bf16[192,256]{1,0:T(8,128)(2,1)S(1)} %get-tuple-element.120), channel_id=1, source_target_pairs={{0,16},{1,113},{16,0},{17,33},{32,48},{33,17},{48,32},{49,65},{64,... | collective-permute-start | bytes 294920 | tf_op jit(solution)/shard_map/ppermute | solution.py:422
  103.0 3.4 %collective-permute-start.22 = (bf16[64,512]{1,0:T(8,128)(2,1)S(1)}, bf16[64,512]{1,0:T(8,128)(2,1)S(1)}, u32[]{:S(2)}, u32[]{:S(2)}) collective-permute-start(bf16[64,512]{1,0:T(8,128)(2,1)S(1)} %get-tuple-element.130), channel_id=1, source_target_pairs={{0,1},{1,0},{2,3},{3,2},{4,5},{5,4},{6,7},{7,6},{8,9},{9,8},{10,11... | collective-permute-start | bytes 196616 | tf_op jit(solution)/shard_map/ppermute | solution.py:408
  106.4 4.1 %collective-permute-start.23 = (bf16[64,512]{1,0:T(8,128)(2,1)S(1)}, bf16[64,512]{1,0:T(8,128)(2,1)S(1)}, u32[]{:S(2)}, u32[]{:S(2)}) collective-permute-start(bf16[64,512]{1,0:T(8,128)(2,1)S(1)} %add_convert_fusion.2), channel_id=1, source_target_pairs={{0,2},{2,0},{1,3},{3,1},{4,6},{6,4},{5,7},{7,5},{8,10},{10,8},{9,1... | collective-permute-start | bytes 196616 | tf_op jit(solution)/shard_map/ppermute | solution.py:408
  110.5 4.5 %collective-permute-start.26 = (bf16[64,512]{1,0:T(8,128)(2,1)S(1)}, bf16[64,512]{1,0:T(8,128)(2,1)S(1)}, u32[]{:S(2)}, u32[]{:S(2)}) collective-permute-start(bf16[64,512]{1,0:T(8,128)(2,1)S(1)} %add_convert_fusion.1), channel_id=1, source_target_pairs={{0,12},{4,0},{8,4},{12,8},{1,13},{5,1},{9,5},{13,9},{2,14},{6,2},{... | collective-permute-start | bytes 196616 | tf_op jit(solution)/shard_map/ppermute | solution.py:413
  113.3 5.0 %collective-permute-start.25 = (bf16[64,512]{1,0:T(8,128)(2,1)S(1)}, bf16[64,512]{1,0:T(8,128)(2,1)S(1)}, u32[]{:S(2)}, u32[]{:S(2)}) collective-permute-start(bf16[64,512]{1,0:T(8,128)(2,1)S(1)} %add_convert_fusion.1), channel_id=1, source_target_pairs={{0,4},{4,8},{8,12},{12,0},{1,5},{5,9},{9,13},{13,1},{2,6},{6,10},{... | collective-permute-start | bytes 196616 | tf_op jit(solution)/shard_map/ppermute | solution.py:413
  113.3 5.0 %collective-permute-start.24 = (bf16[64,512]{1,0:T(8,128)(2,1)S(1)}, bf16[64,512]{1,0:T(8,128)(2,1)S(1)}, u32[]{:S(2)}, u32[]{:S(2)}) collective-permute-start(bf16[64,512]{1,0:T(8,128)(2,1)S(1)} %add_convert_fusion.1), channel_id=1, source_target_pairs={{0,8},{4,12},{8,0},{12,4},{1,9},{5,13},{9,1},{13,5},{2,10},{6,14},... | collective-permute-start | bytes 196616 | tf_op jit(solution)/shard_map/ppermute | solution.py:413
  118.4 3.8 %collective-permute-start.27 = (bf16[64,512]{1,0:T(8,128)(2,1)S(1)}, bf16[64,512]{1,0:T(8,128)(2,1)S(1)}, u32[]{:S(2)}, u32[]{:S(2)}) collective-permute-start(bf16[64,512]{1,0:T(8,128)(2,1)S(1)} %add_convert_fusion), channel_id=1, source_target_pairs={{0,1},{1,0},{2,3},{3,2},{4,5},{5,4},{6,7},{7,6},{8,9},{9,8},{10,11... | collective-permute-start | bytes 196616 | tf_op jit(solution)/shard_map/ppermute | solution.py:408

commit v12 on v11

--- a/solution.py
+++ b/solution.py
@@ -398,7 +398,7 @@
         compiler_params=pltpu.CompilerParams(vmem_limit_bytes=(56 if copies else 32) * 2**20),
         cost_estimate=pl.CostEstimate(
             flops=products * PROBS * LANES * HEAD_DIM * 4,
-            bytes_accessed=1_000_000,
+            bytes_accessed=1_000_000 * products,
             transcendentals=0,
         ),
     )(*scalars, *operands)
@@ -501,7 +501,6 @@
         forward_scratch(2),
         (info,),
         qt, left_a, left_b, right_a, right_b, shift1, total1, acc1,
-        products=4,
     )
     shift3, uplt, upl, delta, dqt, attn, far_ga, far_gb = call(
         far_kernel,

time: 123 us -> 126 us (1.024)
  starting transfers between devices: 51.5 us -> 62.2 us
  waiting for transfers between devices: 33.1 us -> 24.8 us
    ppermute x22, waiting for transfers between devices: 27.9 us -> 19.6 us  [local_permute(): return lax.ppermute(x, LOCAL, pairs)]
    ppermute x3, starting transfers between devices: 6.55 us -> 12.1 us  [swap(): return lax.ppermute(x, axis, [(0, 1), (1, 0)])]
    ppermute x22, starting transfers between devices: 40.4 us -> 45.7 us  [local_permute(): return lax.ppermute(x, LOCAL, pairs)]
  transfers between devices with their start and end apart: 28 -> 28, of which waited for: 11 -> 9; matrix products, arithmetic and copies ran while one was open for 1% -> 1% of each run, Pallas kernels for 21% -> 20%
where the time goes in v12:
time: 126 us; the launch traced here: 125 us
  starting transfers between devices  62.2 us (49%)
  Pallas kernels  33.4 us (27%)
  waiting for transfers between devices  24.8 us (20%)
  between operations  2.15 us (2%)
  other arithmetic  1.67 us (1%)
    ppermute x22, starting transfers between devices, local_permute(): return lax.ppermute(x, LOCAL, pairs)  45.7 us
    pallas_call x12, Pallas kernels, call(): pl.pallas_call(kernel, out_shape=tuple(outs), in_specs=[SMEM] * len(scala...  33.4 us
    ppermute x22, waiting for transfers between devices, local_permute(): return lax.ppermute(x, LOCAL, pairs)  19.6 us
    ppermute x3, starting transfers between devices, swap(): return lax.ppermute(x, axis, [(0, 1), (1, 0)])  12.1 us
    ppermute x3, starting transfers between devices, turn(): return lax.ppermute(x, axis, [(i, (i + step) % size) for i in range(size)])  4.45 us
    ppermute x3, waiting for transfers between devices, turn(): return lax.ppermute(x, axis, [(i, (i + step) % size) for i in range(size)])  3.38 us
  transfers between devices with their start and end apart: 28, of which 9 were waited for; matrix products, arithmetic and copies ran while one was open for 1% of the time, Pallas kernels for 20%

profile of v12, /device:TPU:1, one launch (start us, length us, event | category | flops | bytes accessed | tf_op | source)
XLA Modules:
  0.0 125.3 jit_solution(14460958609517998698)
XLA Ops:
  0.6 1.8 %shard_map.127 = (bf16[192,256]{1,0:T(8,128)(2,1)}, bf16[192,256]{1,0:T(8,128)(2,1)}, bf16[192,256]{1,0:T(8,128)(2,1)}, bf16[192,256]{1,0:T(8,128)(2,1)}) custom-call(s32[1]{0:T(128)} %bitcast.info, bf16[128,512]{1,0:T(8,128)(2,1)} %bitcast.17, bf16[128,512]{1,0:T(8,128)(2,1)} %bitcast.18, bf16[64,512]{1,0:T(8,128)(2,1)} %kp.1, bf16[64,512]{1,0:T(8,128)(2,1)} %vp.1), custom_call_target="tpu_custom_call" | custom-call | tf_op jit(solution)/shard_map/pallas_call | solution.py:392
  2.5 6.5 %collective-permute-start = (bf16[192,256]{1,0:T(8,128)(2,1)}, bf16[192,256]{1,0:T(8,128)(2,1)S(1)}, u32[]{:S(2)}, u32[]{:S(2)}) collective-permute-start(bf16[192,256]{1,0:T(8,128)(2,1)} %get-tuple-element.76), channel_id=1, source_target_pairs={{0,16},{1,113},{16,0},{17,33},{32,48},{33,17},{48,32},{49,65},{64,... | collective-permute-start | bytes 294920 | tf_op jit(solution)/shard_map/ppermute | solution.py:422
  9.0 2.7 %collective-permute-start.3 = (bf16[192,256]{1,0:T(8,128)(2,1)}, bf16[192,256]{1,0:T(8,128)(2,1)S(1)}, u32[]{:S(2)}, u32[]{:S(2)}) collective-permute-start(bf16[192,256]{1,0:T(8,128)(2,1)} %get-tuple-element.81), channel_id=1, source_target_pairs={{0,128},{1,129},{16,144},{17,145},{32,160},{33,161},{48,176},{49,1... | collective-permute-start | bytes 294920 | tf_op jit(solution)/shard_map/ppermute | solution.py:422
  11.8 0.9 pad_maximum_fusion.own_a
  12.7 1.9 %collective-permute-start.6 = (bf16[2,192,256]{2,1,0:T(8,128)(2,1)S(1)}, bf16[2,192,256]{2,1,0:T(8,128)(2,1)S(1)}, u32[]{:S(2)}, u32[]{:S(2)}) collective-permute-start(bf16[2,192,256]{2,1,0:T(8,128)(2,1)S(1)} %pad_maximum_fusion.own_a), channel_id=1, source_target_pairs={{0,96},{1,97},{16,112},{17,113},{32,0},{33,1},{48,16},{49,17},{64,... | collective-permute-start | bytes 589832 | tf_op jit(solution)/shard_map/ppermute | solution.py:422
  15.1 2.2 %shard_map.128 = (bf16[128,1024]{1,0:T(8,128)(2,1)}, bf16[128,1024]{1,0:T(8,128)(2,1)}, bf16[128,1024]{1,0:T(8,128)(2,1)}, bf16[128,1024]{1,0:T(8,128)(2,1)}) custom-call(s32[1]{0:T(128)} %bitcast.info, bf16[128,2048]{1,0:T(8,128)(2,1)} %bitcast.15, bf16[128,2048]{1,0:T(8,128)(2,1)} %bitcast.16), custom_call_target="tpu_custom_call" | custom-call | tf_op jit(solution)/shard_map/pallas_call | solution.py:392
  17.4 6.3 %collective-permute-start.8 = (bf16[128,1024]{1,0:T(8,128)(2,1)}, bf16[128,1024]{1,0:T(8,128)(2,1)S(1)}, u32[]{:S(2)}, u32[]{:S(2)}) collective-permute-start(bf16[128,1024]{1,0:T(8,128)(2,1)} %get-tuple-element.85), channel_id=1, source_target_pairs={{0,144},{1,241},{16,128},{17,161},{32,176},{33,145},{48,160},{49,1... | collective-permute-start | bytes 786440 | tf_op jit(solution)/shard_map/ppermute | solution.py:422
  24.1 6.1 %collective-permute-start.1 = (bf16[128,1024]{1,0:T(8,128)(2,1)}, bf16[128,1024]{1,0:T(8,128)(2,1)S(1)}, u32[]{:S(2)}, u32[]{:S(2)}) collective-permute-start(bf16[128,1024]{1,0:T(8,128)(2,1)} %get-tuple-element.79), channel_id=1, source_target_pairs={{0,16},{1,113},{16,0},{17,33},{32,48},{33,17},{48,32},{49,65},{64,... | collective-permute-start | bytes 786440 | tf_op jit(solution)/shard_map/ppermute | solution.py:422
  30.2 2.7 %collective-permute-start.2 = (bf16[128,1024]{1,0:T(8,128)(2,1)}, bf16[128,1024]{1,0:T(8,128)(2,1)S(1)}, u32[]{:S(2)}, u32[]{:S(2)}) collective-permute-start(bf16[128,1024]{1,0:T(8,128)(2,1)} %get-tuple-element.80), channel_id=1, source_target_pairs={{0,128},{1,129},{16,144},{17,145},{32,160},{33,161},{48,176},{49,1... | collective-permute-start | bytes 786440 | tf_op jit(solution)/shard_map/ppermute | solution.py:422
  33.5 3.3 %collective-permute-start.9 = (bf16[2,192,256]{2,1,0:T(8,128)(2,1)S(1)}, bf16[2,192,256]{2,1,0:T(8,128)(2,1)S(1)}, u32[]{:S(2)}, u32[]{:S(2)}) collective-permute-start(bf16[2,192,256]{2,1,0:T(8,128)(2,1)S(1)} %collective-permute-done.5.left_a), channel_id=1, source_target_pairs={{0,32},{1,33},{16,48},{17,49},{32,64},{33,65},{48,80},{49,81},{64,... | collective-permute-start | bytes 589832 | tf_op jit(solution)/shard_map/ppermute | solution.py:422
  38.9 0.9 copy-done
  39.9 3.4 %shard_map.129 = (bf16[2,128,1024]{2,1,0:T(8,128)(2,1)S(1)}, bf16[2,1024,128]{2,1,0:T(8,128)(2,1)S(1)}, bf16[2,128,1024]{2,1,0:T(8,128)(2,1)S(1)}, bf16[1,1280,1...) custom-call(s32[5]{0:T(128)S(1)} %stack.33.info, ...), custom_call_target="tpu_custom_call" | custom-call | flops 1342177280 | bytes 2000000 | tf_op jit(solution)/shard_map/pallas_call | solution.py:392
  43.3 5.8 %collective-permute-done.11.left_b = bf16[2,192,256]{2,1,0:T(8,128)(2,1)S(1)} collective-permute-done((bf16[2,192,256]{2,1,0:T(8,128)(2,1)S(1)}, bf16[2,192,256]{2,1,0:T(8,128)(2,1)S(1)}, u32[]{:S(2)}, u32[]{:S(2)}) %collective-permute-start.11) | collective-permute-done | bytes 196640 | tf_op jit(solution)/shard_map/ppermute | solution.py:422
  49.1 5.7 %shard_map.130 = (bf16[2,1280,1024]{2,1,0:T(8,128)(2,1)S(1)}, f32[2,1,1024]{2,1,0:T(1,128)S(1)}, f32[2,1,1024]{2,1,0:T(1,128)S(1)}, f32[2,128,1024]{2,1,0:T(8,128)S(1)}) custom-call(s32[5]{0:T(128)S(1)} %stack.33.info, bf16[2,128,1024]{2,1,0:T(8,128)(2,1)S(1)} %get-tuple-element.88.qt, bf16[2,192,256]{2,1,0:T(8,128)(2,1)S(1)} %collective-permute-done.5.left_a, ...), custom_call_target="tpu_custom_call" | custom-call | tf_op jit(solution)/shard_map/pallas_call | solution.py:392
  54.8 5.7 %shard_map.131 = (f32[2,1,1024]{2,1,0:T(1,128)S(1)}, bf16[2,128,1024]{2,1,0:T(8,128)(2,1)S(1)}, bf16[2,1024,128]{2,1,0:T(8,128)(2,1)S(1)}, f32[2,1,1024]{2,1,0:T...) custom-call(s32[5]{0:T(128)S(1)} %stack.33.info, ...), custom_call_target="tpu_custom_call" | custom-call | flops 4026531840 | bytes 6000000 | tf_op jit(solution)/shard_map/pallas_call | solution.py:392
  61.1 3.1 %collective-permute-start.13 = (bf16[2,192,256]{2,1,0:T(8,128)(2,1)S(1)}, bf16[2,192,256]{2,1,0:T(8,128)(2,1)S(1)}, u32[]{:S(2)}, u32[]{:S(2)}) collective-permute-start(bf16[2,192,256]{2,1,0:T(8,128)(2,1)S(1)} %get-tuple-element.112), channel_id=1, source_target_pairs={{0,96},{1,97},{16,112},{17,113},{32,0},{33,1},{48,16},{49,17},{64,... | collective-permute-start | bytes 589832 | tf_op jit(solution)/shard_map/ppermute | solution.py:422
  64.2 6.4 %shard_map.132 = (f32[2,128,1024]{2,1,0:T(8,128)S(1)}, bf16[4,192,256]{2,1,0:T(8,128)(2,1)S(1)}, bf16[4,192,256]{2,1,0:T(8,128)(2,1)S(1)}) custom-call(s32[5]{0:T(128)S(1)} %stack.33.info, bf16[2,1024,128]{2,1,0:T(8,128)(2,1)S(1)} %get-tuple-element.87.q, bf16[2,128,1024]{2,1,0:T(8,128)(2,1)S(1)} %get-tuple-element.99.uplt, ...), custom_call_target="tpu_custom_call" | custom-call | flops 5368709120 | bytes 8000000 | tf_op jit(solution)/shard_map/pallas_call | solution.py:392
  70.8 1.1 collective-permute-start.14
  71.9 1.7 %collective-permute-start.15 = (bf16[4,192,256]{2,1,0:T(8,128)(2,1)S(1)}, bf16[4,192,256]{2,1,0:T(8,128)(2,1)S(1)}, u32[]{:S(2)}, u32[]{:S(2)}) collective-permute-start(bf16[4,192,256]{2,1,0:T(8,128)(2,1)S(1)} %get-tuple-element.114), channel_id=1, source_target_pairs={{0,32},{1,33},{16,48},{17,49},{32,64},{33,65},{48,80},{49,81},{64,... | collective-permute-start | bytes 1179656 | tf_op jit(solution)/shard_map/ppermute | solution.py:422
  73.5 4.4 %shard_map.133 = (bf16[4,192,256]{2,1,0:T(8,128)(2,1)S(1)}, bf16[128,1024]{1,0:T(8,128)(2,1)S(1)}, bf16[128,1024]{1,0:T(8,128)(2,1)S(1)}, bf16[128,1024]{1,0:T(8,128)(2,1)S(1)}, bf16[128,1024]{1,0:T(8,128)(2,1)S(1)}) custom-call(s32[5]{0:T(128)S(1)} %stack.33.info, bf16[2,1024,128]{2,1,0:T(8,128)(2,1)S(1)} %get-tuple-element.87.q, ...), custom_call_target="tpu_custom_call" | custom-call | flops 2684354560 | bytes 4000000 | tf_op jit(solution)/shard_map/pallas_call | solution.py:392
  78.7 8.6 %collective-permute-done.14.left = bf16[4,192,256]{2,1,0:T(8,128)(2,1)S(1)} collective-permute-done((bf16[4,192,256]{2,1,0:T(8,128)(2,1)S(1)}, bf16[4,192,256]{2,1,0:T(8,128)(2,1)S(1)}, u32[]{:S(2)}, u32[]{:S(2)}) %collective-permute-start.14) | collective-permute-done | bytes 393248 | tf_op jit(solution)/shard_map/ppermute | solution.py:422
  87.7 5.1 %collective-permute-start.17 = (bf16[192,256]{1,0:T(8,128)(2,1)S(1)}, bf16[192,256]{1,0:T(8,128)(2,1)S(1)}, u32[]{:S(2)}, u32[]{:S(2)}) collective-permute-start(bf16[192,256]{1,0:T(8,128)(2,1)S(1)} %get-tuple-element.119), channel_id=1, source_target_pairs={{0,128},{1,129},{16,144},{17,145},{32,160},{33,161},{48,176},{49,1... | collective-permute-start | bytes 294920 | tf_op jit(solution)/shard_map/ppermute | solution.py:422
  92.9 2.3 %collective-permute-start.18 = (bf16[192,256]{1,0:T(8,128)(2,1)S(1)}, bf16[192,256]{1,0:T(8,128)(2,1)S(1)}, u32[]{:S(2)}, u32[]{:S(2)}) collective-permute-start(bf16[192,256]{1,0:T(8,128)(2,1)S(1)} %get-tuple-element.120), channel_id=1, source_target_pairs={{0,16},{1,113},{16,0},{17,33},{32,48},{33,17},{48,32},{49,65},{64,... | collective-permute-start | bytes 294920 | tf_op jit(solution)/shard_map/ppermute | solution.py:422
  95.2 4.1 %collective-permute-done.16.g3 = bf16[192,256]{1,0:T(8,128)(2,1)S(1)} collective-permute-done((bf16[192,256]{1,0:T(8,128)(2,1)S(1)}, bf16[192,256]{1,0:T(8,128)(2,1)S(1)}, u32[]{:S(2)}, u32[]{:S(2)}) %collective-permute-start.16) | collective-permute-done | bytes 98336 | tf_op jit(solution)/shard_map/ppermute | solution.py:422
  99.9 8.8 %collective-permute-start.22 = (bf16[64,512]{1,0:T(8,128)(2,1)S(1)}, bf16[64,512]{1,0:T(8,128)(2,1)S(1)}, u32[]{:S(2)}, u32[]{:S(2)}) collective-permute-start(bf16[64,512]{1,0:T(8,128)(2,1)S(1)} %get-tuple-element.130), channel_id=1, source_target_pairs={{0,1},{1,0},{2,3},{3,2},{4,5},{5,4},{6,7},{7,6},{8,9},{9,8},{10,11... | collective-permute-start | bytes 196616 | tf_op jit(solution)/shard_map/ppermute | solution.py:408
  108.7 0.9 collective-permute-done.22
  109.9 1.3 %shard_map.137 = (bf16[128,512]{1,0:T(8,128)(2,1)}, bf16[128,512]{1,0:T(8,128)(2,1)}) custom-call(s32[5]{0:T(128)S(1)} %stack.33.info, bf16[192,256]{1,0:T(8,128)(2,1)S(1)} %get-tuple-element.125.g0, bf16[192,256]{1,0:T(8,128)(2,1)S(1)} %collective-permute-done.18.g1, bf16[192,256]{1,0:T(8,128)(2,1)S(1)} %collective-permute-done.17.g2, ...), custom_call_target="tpu_custom_call" | custom-call | tf_op jit(solution)/shard_map/pallas_call | solution.py:392
  111.2 1.6 %shard_map.138 = (bf16[128,2048]{1,0:T(8,128)(2,1)}, bf16[128,2048]{1,0:T(8,128)(2,1)}) custom-call(s32[5]{0:T(128)S(1)} %stack.33.info, bf16[128,1024]{1,0:T(8,128)(2,1)S(1)} %get-tuple-element.133.od0, bf16[128,1024]{1,0:T(8,128)(2,1)S(1)} %collective-permute-done.21.od1, bf16[128,1024]{1,0:T(8,128)(2,1)S(1)} %collective-permute-done.20.od2, ...), custom_call_target="tpu_custom_call" | custom-call | tf_op jit(solution)/shard_map/pallas_call | solution.py:392
  112.9 2.8 %collective-permute-start.26 = (bf16[64,512]{1,0:T(8,128)(2,1)S(1)}, bf16[64,512]{1,0:T(8,128)(2,1)S(1)}, u32[]{:S(2)}, u32[]{:S(2)}) collective-permute-start(bf16[64,512]{1,0:T(8,128)(2,1)S(1)} %add_convert_fusion.1), channel_id=1, source_target_pairs={{0,12},{4,0},{8,4},{12,8},{1,13},{5,1},{9,5},{13,9},{2,14},{6,2},{... | collective-permute-start | bytes 196616 | tf_op jit(solution)/shard_map/ppermute | solution.py:413
  115.7 1.6 %collective-permute-start.24 = (bf16[64,512]{1,0:T(8,128)(2,1)S(1)}, bf16[64,512]{1,0:T(8,128)(2,1)S(1)}, u32[]{:S(2)}, u32[]{:S(2)}) collective-permute-start(bf16[64,512]{1,0:T(8,128)(2,1)S(1)} %add_convert_fusion.1), channel_id=1, source_target_pairs={{0,8},{4,12},{8,0},{12,4},{1,9},{5,13},{9,1},{13,5},{2,10},{6,14},... | collective-permute-start | bytes 196616 | tf_op jit(solution)/shard_map/ppermute | solution.py:413
  117.3 3.4 %collective-permute-done.25 = bf16[64,512]{1,0:T(8,128)(2,1)S(1)} collective-permute-done((bf16[64,512]{1,0:T(8,128)(2,1)S(1)}, bf16[64,512]{1,0:T(8,128)(2,1)S(1)}, u32[]{:S(2)}, u32[]{:S(2)}) %collective-permute-start.25) | collective-permute-done | bytes 65568 | tf_op jit(solution)/shard_map/ppermute | solution.py:413
  120.8 3.0 %collective-permute-start.27 = (bf16[64,512]{1,0:T(8,128)(2,1)S(1)}, bf16[64,512]{1,0:T(8,128)(2,1)S(1)}, u32[]{:S(2)}, u32[]{:S(2)}) collective-permute-start(bf16[64,512]{1,0:T(8,128)(2,1)S(1)} %add_convert_fusion), channel_id=1, source_target_pairs={{0,1},{1,0},{2,3},{3,2},{4,5},{5,4},{6,7},{7,6},{8,9},{9,8},{10,11... | collective-permute-start | bytes 196616 | tf_op jit(solution)/shard_map/ppermute | solution.py:408
  (45 shorter events, 6.7 us)
Async XLA Ops:
  2.5 9.3 %collective-permute-start = (bf16[192,256]{1,0:T(8,128)(2,1)}, bf16[192,256]{1,0:T(8,128)(2,1)S(1)}, u32[]{:S(2)}, u32[]{:S(2)}) collective-permute-start(bf16[192,256]{1,0:T(8,128)(2,1)} %get-tuple-element.76), channel_id=1, source_target_pairs={{0,16},{1,113},{16,0},{17,33},{32,48},{33,17},{48,32},{49,65},{64,... | collective-permute-start | bytes 294920 | tf_op jit(solution)/shard_map/ppermute | solution.py:422
  9.0 14.7 %collective-permute-start.3 = (bf16[192,256]{1,0:T(8,128)(2,1)}, bf16[192,256]{1,0:T(8,128)(2,1)S(1)}, u32[]{:S(2)}, u32[]{:S(2)}) collective-permute-start(bf16[192,256]{1,0:T(8,128)(2,1)} %get-tuple-element.81), channel_id=1, source_target_pairs={{0,128},{1,129},{16,144},{17,145},{32,160},{33,161},{48,176},{49,1... | collective-permute-start | bytes 294920 | tf_op jit(solution)/shard_map/ppermute | solution.py:422
  11.7 12.0 %collective-permute-start.4 = (bf16[192,256]{1,0:T(8,128)(2,1)}, bf16[192,256]{1,0:T(8,128)(2,1)S(1)}, u32[]{:S(2)}, u32[]{:S(2)}) collective-permute-start(bf16[192,256]{1,0:T(8,128)(2,1)} %get-tuple-element.82), channel_id=1, source_target_pairs={{0,144},{1,241},{16,128},{17,161},{32,176},{33,145},{48,160},{49,1... | collective-permute-start | bytes 294920 | tf_op jit(solution)/shard_map/ppermute | solution.py:422
  12.7 11.5 %collective-permute-start.6 = (bf16[2,192,256]{2,1,0:T(8,128)(2,1)S(1)}, bf16[2,192,256]{2,1,0:T(8,128)(2,1)S(1)}, u32[]{:S(2)}, u32[]{:S(2)}) collective-permute-start(bf16[2,192,256]{2,1,0:T(8,128)(2,1)S(1)} %pad_maximum_fusion.own_a), channel_id=1, source_target_pairs={{0,96},{1,97},{16,112},{17,113},{32,0},{33,1},{48,16},{49,17},{64,... | collective-permute-start | bytes 589832 | tf_op jit(solution)/shard_map/ppermute | solution.py:422
  14.6 9.6 %collective-permute-start.5 = (bf16[2,192,256]{2,1,0:T(8,128)(2,1)S(1)}, bf16[2,192,256]{2,1,0:T(8,128)(2,1)S(1)}, u32[]{:S(2)}, u32[]{:S(2)}) collective-permute-start(bf16[2,192,256]{2,1,0:T(8,128)(2,1)S(1)} %pad_maximum_fusion.own_a), channel_id=1, source_target_pairs={{0,32},{1,33},{16,48},{17,49},{32,64},{33,65},{48,80},{49,81},{64,... | collective-permute-start | bytes 589832 | tf_op jit(solution)/shard_map/ppermute | solution.py:422
  17.4 16.1 %collective-permute-start.8 = (bf16[128,1024]{1,0:T(8,128)(2,1)}, bf16[128,1024]{1,0:T(8,128)(2,1)S(1)}, u32[]{:S(2)}, u32[]{:S(2)}) collective-permute-start(bf16[128,1024]{1,0:T(8,128)(2,1)} %get-tuple-element.85), channel_id=1, source_target_pairs={{0,144},{1,241},{16,128},{17,161},{32,176},{33,145},{48,160},{49,1... | collective-permute-start | bytes 786440 | tf_op jit(solution)/shard_map/ppermute | solution.py:422
  24.1 12.7 %collective-permute-start.7 = (bf16[2,192,256]{2,1,0:T(8,128)(2,1)S(1)}, bf16[2,192,256]{2,1,0:T(8,128)(2,1)S(1)}, u32[]{:S(2)}, u32[]{:S(2)}) collective-permute-start(bf16[2,192,256]{2,1,0:T(8,128)(2,1)S(1)} %pad_maximum_fusion.1.own_b), channel_id=1, source_target_pairs={{0,96},{1,97},{16,112},{17,113},{32,0},{33,1},{48,16},{49,17},{64,... | collective-permute-start | bytes 589832 | tf_op jit(solution)/shard_map/ppermute | solution.py:422
  24.1 14.8 %collective-permute-start.1 = (bf16[128,1024]{1,0:T(8,128)(2,1)}, bf16[128,1024]{1,0:T(8,128)(2,1)S(1)}, u32[]{:S(2)}, u32[]{:S(2)}) collective-permute-start(bf16[128,1024]{1,0:T(8,128)(2,1)} %get-tuple-element.79), channel_id=1, source_target_pairs={{0,16},{1,113},{16,0},{17,33},{32,48},{33,17},{48,32},{49,65},{64,... | collective-permute-start | bytes 786440 | tf_op jit(solution)/shard_map/ppermute | solution.py:422
  30.2 8.7 %collective-permute-start.2 = (bf16[128,1024]{1,0:T(8,128)(2,1)}, bf16[128,1024]{1,0:T(8,128)(2,1)S(1)}, u32[]{:S(2)}, u32[]{:S(2)}) collective-permute-start(bf16[128,1024]{1,0:T(8,128)(2,1)} %get-tuple-element.80), channel_id=1, source_target_pairs={{0,128},{1,129},{16,144},{17,145},{32,160},{33,161},{48,176},{49,1... | collective-permute-start | bytes 786440 | tf_op jit(solution)/shard_map/ppermute | solution.py:422
  33.0 16.1 %collective-permute-start.11 = (bf16[2,192,256]{2,1,0:T(8,128)(2,1)S(1)}, bf16[2,192,256]{2,1,0:T(8,128)(2,1)S(1)}, u32[]{:S(2)}, u32[]{:S(2)}) collective-permute-start(bf16[2,192,256]{2,1,0:T(8,128)(2,1)S(1)} %pad_maximum_fusion.1.own_b), channel_id=1, source_target_pairs={{0,32},{1,33},{16,48},{17,49},{32,64},{33,65},{48,80},{49,81},{64,... | collective-permute-start | bytes 589832 | tf_op jit(solution)/shard_map/ppermute | solution.py:422
  33.5 21.3 %collective-permute-start.9 = (bf16[2,192,256]{2,1,0:T(8,128)(2,1)S(1)}, bf16[2,192,256]{2,1,0:T(8,128)(2,1)S(1)}, u32[]{:S(2)}, u32[]{:S(2)}) collective-permute-start(bf16[2,192,256]{2,1,0:T(8,128)(2,1)S(1)} %collective-permute-done.5.left_a), channel_id=1, source_target_pairs={{0,32},{1,33},{16,48},{17,49},{32,64},{33,65},{48,80},{49,81},{64,... | collective-permute-start | bytes 589832 | tf_op jit(solution)/shard_map/ppermute | solution.py:422
  36.8 18.0 %collective-permute-start.10 = (bf16[2,192,256]{2,1,0:T(8,128)(2,1)S(1)}, bf16[2,192,256]{2,1,0:T(8,128)(2,1)S(1)}, u32[]{:S(2)}, u32[]{:S(2)}) collective-permute-start(bf16[2,192,256]{2,1,0:T(8,128)(2,1)S(1)} %collective-permute-done.7.right_b), channel_id=1, source_target_pairs={{0,96},{1,97},{16,112},{17,113},{32,0},{33,1},{48,16},{49,17},{64,... | collective-permute-start | bytes 589832 | tf_op jit(solution)/shard_map/ppermute | solution.py:422
  38.9 1.0 copy-start
  60.5 10.1 %collective-permute-start.12 = (bf16[2,192,256]{2,1,0:T(8,128)(2,1)S(1)}, bf16[2,192,256]{2,1,0:T(8,128)(2,1)S(1)}, u32[]{:S(2)}, u32[]{:S(2)}) collective-permute-start(bf16[2,192,256]{2,1,0:T(8,128)(2,1)S(1)} %get-tuple-element.111), channel_id=1, source_target_pairs={{0,32},{1,33},{16,48},{17,49},{32,64},{33,65},{48,80},{49,81},{64,... | collective-permute-start | bytes 589832 | tf_op jit(solution)/shard_map/ppermute | solution.py:422
  61.1 9.6 %collective-permute-start.13 = (bf16[2,192,256]{2,1,0:T(8,128)(2,1)S(1)}, bf16[2,192,256]{2,1,0:T(8,128)(2,1)S(1)}, u32[]{:S(2)}, u32[]{:S(2)}) collective-permute-start(bf16[2,192,256]{2,1,0:T(8,128)(2,1)S(1)} %get-tuple-element.112), channel_id=1, source_target_pairs={{0,96},{1,97},{16,112},{17,113},{32,0},{33,1},{48,16},{49,17},{64,... | collective-permute-start | bytes 589832 | tf_op jit(solution)/shard_map/ppermute | solution.py:422
  70.8 16.5 %collective-permute-start.14 = (bf16[4,192,256]{2,1,0:T(8,128)(2,1)S(1)}, bf16[4,192,256]{2,1,0:T(8,128)(2,1)S(1)}, u32[]{:S(2)}, u32[]{:S(2)}) collective-permute-start(bf16[4,192,256]{2,1,0:T(8,128)(2,1)S(1)} %get-tuple-element.113), channel_id=1, source_target_pairs={{0,96},{1,97},{16,112},{17,113},{32,0},{33,1},{48,16},{49,17},{64,... | collective-permute-start | bytes 1179656 | tf_op jit(solution)/shard_map/ppermute | solution.py:422
  71.9 15.4 %collective-permute-start.15 = (bf16[4,192,256]{2,1,0:T(8,128)(2,1)S(1)}, bf16[4,192,256]{2,1,0:T(8,128)(2,1)S(1)}, u32[]{:S(2)}, u32[]{:S(2)}) collective-permute-start(bf16[4,192,256]{2,1,0:T(8,128)(2,1)S(1)} %get-tuple-element.114), channel_id=1, source_target_pairs={{0,32},{1,33},{16,48},{17,49},{32,64},{33,65},{48,80},{49,81},{64,... | collective-permute-start | bytes 1179656 | tf_op jit(solution)/shard_map/ppermute | solution.py:422
  77.9 14.9 %collective-permute-start.19 = (bf16[128,1024]{1,0:T(8,128)(2,1)S(1)}, bf16[128,1024]{1,0:T(8,128)(2,1)S(1)}, u32[]{:S(2)}, u32[]{:S(2)}) collective-permute-start(bf16[128,1024]{1,0:T(8,128)(2,1)S(1)} %get-tuple-element.122), channel_id=1, source_target_pairs={{0,144},{1,241},{16,128},{17,161},{32,176},{33,145},{48,160},{49,1... | collective-permute-start | bytes 786440 | tf_op jit(solution)/shard_map/ppermute | solution.py:422
  78.0 17.2 %collective-permute-start.20 = (bf16[128,1024]{1,0:T(8,128)(2,1)S(1)}, bf16[128,1024]{1,0:T(8,128)(2,1)S(1)}, u32[]{:S(2)}, u32[]{:S(2)}) collective-permute-start(bf16[128,1024]{1,0:T(8,128)(2,1)S(1)} %get-tuple-element.123), channel_id=1, source_target_pairs={{0,128},{1,129},{16,144},{17,145},{32,160},{33,161},{48,176},{49,1... | collective-permute-start | bytes 786440 | tf_op jit(solution)/shard_map/ppermute | solution.py:422
  87.3 12.1 %collective-permute-start.21 = (bf16[128,1024]{1,0:T(8,128)(2,1)S(1)}, bf16[128,1024]{1,0:T(8,128)(2,1)S(1)}, u32[]{:S(2)}, u32[]{:S(2)}) collective-permute-start(bf16[128,1024]{1,0:T(8,128)(2,1)S(1)} %get-tuple-element.124), channel_id=1, source_target_pairs={{0,16},{1,113},{16,0},{17,33},{32,48},{33,17},{48,32},{49,65},{64,... | collective-permute-start | bytes 786440 | tf_op jit(solution)/shard_map/ppermute | solution.py:422
  87.4 11.9 %collective-permute-start.16 = (bf16[192,256]{1,0:T(8,128)(2,1)S(1)}, bf16[192,256]{1,0:T(8,128)(2,1)S(1)}, u32[]{:S(2)}, u32[]{:S(2)}) collective-permute-start(bf16[192,256]{1,0:T(8,128)(2,1)S(1)} %get-tuple-element.118), channel_id=1, source_target_pairs={{0,144},{1,241},{16,128},{17,161},{32,176},{33,145},{48,160},{49,1... | collective-permute-start | bytes 294920 | tf_op jit(solution)/shard_map/ppermute | solution.py:422
  87.7 11.6 %collective-permute-start.17 = (bf16[192,256]{1,0:T(8,128)(2,1)S(1)}, bf16[192,256]{1,0:T(8,128)(2,1)S(1)}, u32[]{:S(2)}, u32[]{:S(2)}) collective-permute-start(bf16[192,256]{1,0:T(8,128)(2,1)S(1)} %get-tuple-element.119), channel_id=1, source_target_pairs={{0,128},{1,129},{16,144},{17,145},{32,160},{33,161},{48,176},{49,1... | collective-permute-start | bytes 294920 | tf_op jit(solution)/shard_map/ppermute | solution.py:422
  92.9 6.5 %collective-permute-start.18 = (bf16[192,256]{1,0:T(8,128)(2,1)S(1)}, bf16[192,256]{1,0:T(8,128)(2,1)S(1)}, u32[]{:S(2)}, u32[]{:S(2)}) collective-permute-start(bf16[192,256]{1,0:T(8,128)(2,1)S(1)} %get-tuple-element.120), channel_id=1, source_target_pairs={{0,16},{1,113},{16,0},{17,33},{32,48},{33,17},{48,32},{49,65},{64,... | collective-permute-start | bytes 294920 | tf_op jit(solution)/shard_map/ppermute | solution.py:422
  99.9 9.7 %collective-permute-start.22 = (bf16[64,512]{1,0:T(8,128)(2,1)S(1)}, bf16[64,512]{1,0:T(8,128)(2,1)S(1)}, u32[]{:S(2)}, u32[]{:S(2)}) collective-permute-start(bf16[64,512]{1,0:T(8,128)(2,1)S(1)} %get-tuple-element.130), channel_id=1, source_target_pairs={{0,1},{1,0},{2,3},{3,2},{4,5},{5,4},{6,7},{7,6},{8,9},{9,8},{10,11... | collective-permute-start | bytes 196616 | tf_op jit(solution)/shard_map/ppermute | solution.py:408
  109.7 3.2 %collective-permute-start.23 = (bf16[64,512]{1,0:T(8,128)(2,1)S(1)}, bf16[64,512]{1,0:T(8,128)(2,1)S(1)}, u32[]{:S(2)}, u32[]{:S(2)}) collective-permute-start(bf16[64,512]{1,0:T(8,128)(2,1)S(1)} %add_convert_fusion.2), channel_id=1, source_target_pairs={{0,2},{2,0},{1,3},{3,1},{4,6},{6,4},{5,7},{7,5},{8,10},{10,8},{9,1... | collective-permute-start | bytes 196616 | tf_op jit(solution)/shard_map/ppermute | solution.py:408
  112.9 4.5 %collective-permute-start.26 = (bf16[64,512]{1,0:T(8,128)(2,1)S(1)}, bf16[64,512]{1,0:T(8,128)(2,1)S(1)}, u32[]{:S(2)}, u32[]{:S(2)}) collective-permute-start(bf16[64,512]{1,0:T(8,128)(2,1)S(1)} %add_convert_fusion.1), channel_id=1, source_target_pairs={{0,12},{4,0},{8,4},{12,8},{1,13},{5,1},{9,5},{13,9},{2,14},{6,2},{... | collective-permute-start | bytes 196616 | tf_op jit(solution)/shard_map/ppermute | solution.py:413
  115.7 5.0 %collective-permute-start.25 = (bf16[64,512]{1,0:T(8,128)(2,1)S(1)}, bf16[64,512]{1,0:T(8,128)(2,1)S(1)}, u32[]{:S(2)}, u32[]{:S(2)}) collective-permute-start(bf16[64,512]{1,0:T(8,128)(2,1)S(1)} %add_convert_fusion.1), channel_id=1, source_target_pairs={{0,4},{4,8},{8,12},{12,0},{1,5},{5,9},{9,13},{13,1},{2,6},{6,10},{... | collective-permute-start | bytes 196616 | tf_op jit(solution)/shard_map/ppermute | solution.py:413
  115.7 5.0 %collective-permute-start.24 = (bf16[64,512]{1,0:T(8,128)(2,1)S(1)}, bf16[64,512]{1,0:T(8,128)(2,1)S(1)}, u32[]{:S(2)}, u32[]{:S(2)}) collective-permute-start(bf16[64,512]{1,0:T(8,128)(2,1)S(1)} %add_convert_fusion.1), channel_id=1, source_target_pairs={{0,8},{4,12},{8,0},{12,4},{1,9},{5,13},{9,1},{13,5},{2,10},{6,14},... | collective-permute-start | bytes 196616 | tf_op jit(solution)/shard_map/ppermute | solution.py:413
  120.8 3.9 %collective-permute-start.27 = (bf16[64,512]{1,0:T(8,128)(2,1)S(1)}, bf16[64,512]{1,0:T(8,128)(2,1)S(1)}, u32[]{:S(2)}, u32[]{:S(2)}) collective-permute-start(bf16[64,512]{1,0:T(8,128)(2,1)S(1)} %add_convert_fusion), channel_id=1, source_target_pairs={{0,1},{1,0},{2,3},{3,2},{4,5},{5,4},{6,7},{7,6},{8,9},{9,8},{10,11... | collective-permute-start | bytes 196616 | tf_op jit(solution)/shard_map/ppermute | solution.py:408
